TPU v7x, 32 devices: a whole 2x2x4 slice. The times are simulated.
32 devices in a mesh: ens: 4 (over y, x), horiz: 8 (over z, core).
Axes of the slice: x: 2, y: 2, z: 4, core: 2. Of those that a mesh axis runs over, the one named last changes fastest.
Arguments:
- prognostic: float32 [4, 128, 32, 128], P('ens', None, 'horiz'), may hold values from -6 to 6
- diffusivity: float32 [4, 32, 32, 128], P('ens', None, 'horiz'), may hold values from 0.1 to 10
- mixing: float32 [2, 32, 128], P(None, 'horiz'), may hold values from 0.03 to 0.24
- cotangent: float32 [4, 128, 32, 128], P('ens', None, 'horiz'), may hold values from -6 to 6
- tile_cols: int32 [4, 8, 3, 128], P('ens', 'horiz'), may hold values from 0 to 511, as said below
- pad_mask: int32 [4, 8, 3, 128], P('ens', 'horiz'), may hold values 0 or 1
- tile_count: int32 [4, 8], P('ens', 'horiz'), may hold values from 1 to 3, as said below
- w_in: bfloat16 [1024, 128], replicated, may hold values from -0.5 to 0.5
- w_mid: bfloat16 [1024, 1024], replicated, may hold values from -0.1875 to 0.1875
- w_out: bfloat16 [128, 1024], replicated, may hold values from -0.1875 to 0.1875
Outputs:
- state_next: float32 [4, 128, 32, 128], P('ens', None, 'horiz')
- state_grad: float32 [4, 128, 32, 128], P('ens', None, 'horiz')
- grad_in: float32 [1024, 128], replicated
- grad_mid: float32 [1024, 1024], replicated
- grad_out: float32 [128, 1024], replicated
Inputs may be any that keep to these rules, and one draw needn't show every extreme that they name: `tile_cols`: within one member and block all 3 x 128 entries name different columns. Tiles 0 to tile_count - 1 of a block are in use; in every member some block uses all 3.
All inputs are finite; a program needn't handle non-finite values. No bound on the sum of `pad_mask` on one device may be relied on, other than what follows from the above.
Results may differ from a plain program's by a relative error of at most 0.0071.
Values may be sent and summed in bfloat16 or wider, within the bound.
No kernel may reach another device: no remote copies, remote signals or barrier semaphores. Data moves between devices by JAX's collectives and lax.ppermute only.
A program may use at most 64 MiB of HBM per device.

v0:
```python
import math

import jax
import jax.numpy as jnp
from jax import lax
from jax.sharding import PartitionSpec as P

DYN_STEPS = 2


def shifted(block, axis, distance):
    devices = range(lax.axis_size(axis))
    route = [((i - distance) % len(devices), i) for i in devices]
    return lax.ppermute(block, axis, route)


def with_halo(block, sides, width):
    for axis, dim in sides:
        count = lax.axis_size(axis)
        forward = [(i, i + 1) for i in range(count - 1)]
        forward.append((count - 1, 0))
        backward = [(target, source) for source, target in forward]
        low = lax.ppermute(
            lax.slice_in_dim(block, block.shape[dim] - width, None, axis=dim), axis, forward
        )
        high = lax.ppermute(lax.slice_in_dim(block, 0, width, axis=dim), axis, backward)
        block = jnp.concatenate([low, block, high], axis=dim)
    return block


def silu_slope(pre_act):
    sigma_val = jax.nn.sigmoid(pre_act)
    return sigma_val * (1.0 + pre_act * (1.0 - sigma_val))


def vertical_solve(coefficient, right_side):
    coef_below = jnp.concatenate([jnp.zeros_like(coefficient[:1]), coefficient[:-1]], axis=0)
    coef_above = jnp.concatenate([coefficient[:-1], jnp.zeros_like(coefficient[:1])], axis=0)
    diag_term = 1.0 + coef_below + coefficient
    by_level = jnp.transpose(right_side, (1, 0, 2))

    def sweep_down(carried, inputs):
        prev_ratio, prev_value = carried
        below_now, above_now, diag_now, right_now = inputs
        divisor = diag_now + below_now * prev_ratio
        ratio_now = -above_now / divisor
        value_now = (right_now + below_now * prev_value) / divisor
        return ((ratio_now, value_now), (ratio_now, value_now))

    start_state = (jnp.zeros_like(coefficient[0]), jnp.zeros_like(by_level[0]))
    _, (ratios, values) = lax.scan(
        sweep_down, start_state, (coef_below, coef_above, diag_term, by_level)
    )

    def sweep_up(carried, inputs):
        ratio_now, value_now = inputs
        result = value_now - ratio_now * carried
        return (result, result)

    _, solved = lax.scan(sweep_up, jnp.zeros_like(by_level[0]), (ratios, values), reverse=True)
    return jnp.transpose(solved, (1, 0, 2))


def column_physics(x_tile, coef_tile, cot_tile, w_in, w_mid, w_out):
    fields = x_tile.shape[0]
    levels = coef_tile.shape[0]
    var_count = fields // levels
    contract_cols = (((1,), (1,)), ((), ()))
    contract_rows = (((0,), (0,)), ((), ()))
    pre_one = jnp.dot(w_in, x_tile, preferred_element_type=jnp.float32)
    act_one = jax.nn.silu(pre_one).astype(jnp.bfloat16)
    pre_two = jnp.dot(w_mid, act_one, preferred_element_type=jnp.float32)
    act_two = jax.nn.silu(pre_two).astype(jnp.bfloat16)
    tendency = jnp.dot(w_out, act_two, preferred_element_type=jnp.float32)
    coefficient = coef_tile.astype(jnp.float32)
    forced = (x_tile.astype(jnp.float32) + tendency).reshape(var_count, levels, -1)
    new_tile = vertical_solve(coefficient, forced).reshape(fields, -1)
    adjoint = vertical_solve(
        coefficient, cot_tile.astype(jnp.float32).reshape(var_count, levels, -1)
    ).reshape(fields, -1)
    adjoint_half = adjoint.astype(jnp.bfloat16)
    grad_out = lax.dot_general(
        adjoint_half, act_two, contract_cols, preferred_element_type=jnp.float32
    )
    back_two = lax.dot_general(
        w_out, adjoint_half, contract_rows, preferred_element_type=jnp.float32
    )
    delta_two = (back_two * silu_slope(pre_two)).astype(jnp.bfloat16)
    grad_mid = lax.dot_general(
        delta_two, act_one, contract_cols, preferred_element_type=jnp.float32
    )
    back_one = lax.dot_general(w_mid, delta_two, contract_rows, preferred_element_type=jnp.float32)
    delta_one = (back_one * silu_slope(pre_one)).astype(jnp.bfloat16)
    grad_in = lax.dot_general(delta_one, x_tile, contract_cols, preferred_element_type=jnp.float32)
    grad_x = adjoint + lax.dot_general(
        w_in, delta_one, contract_rows, preferred_element_type=jnp.float32
    )
    return (new_tile.astype(jnp.bfloat16), grad_x.astype(jnp.bfloat16), grad_in, grad_mid, grad_out)


def lat_flux(field_now, coef_lat):
    rising = jnp.concatenate(
        [field_now[..., 1:] - field_now[..., :-1], jnp.zeros_like(field_now[..., :1])], axis=-1
    )
    north_flux = coef_lat * rising
    south_flux = jnp.concatenate(
        [jnp.zeros_like(north_flux[..., :1]), north_flux[..., :-1]], axis=-1
    )
    return north_flux - south_flux


def padded_step(padded, lon_coef, lat_coef):
    inner_cells = padded[..., 1:-1, :]
    east_flux = lon_coef[1:-1] * (padded[..., 2:, :] - inner_cells)
    west_flux = lon_coef[:-2] * (inner_cells - padded[..., :-2, :])
    return inner_cells + east_flux - west_flux + lat_flux(inner_cells, lat_coef[1:-1])


def run_tiles(x_all, coef_all, cot_all, live_count, visit_order, w_in, w_mid, w_out):
    start_state = (
        jnp.zeros(x_all.shape, jnp.bfloat16),
        jnp.zeros(x_all.shape, jnp.bfloat16),
        jnp.zeros(w_in.shape, jnp.float32),
        jnp.zeros(w_mid.shape, jnp.float32),
        jnp.zeros(w_out.shape, jnp.float32),
    )

    def visit_tile(position, carried):
        state_acc, grad_acc, sum_in, sum_mid, sum_out = carried
        slot_now = visit_order[position]
        x_tile = lax.dynamic_index_in_dim(x_all, slot_now, 0, keepdims=False)
        coef_tile = lax.dynamic_index_in_dim(coef_all, slot_now, 0, keepdims=False)
        cot_tile = lax.dynamic_index_in_dim(cot_all, slot_now, 0, keepdims=False)
        new_tile, grad_x, grad_in, grad_mid, grad_out = column_physics(
            x_tile, coef_tile, cot_tile, w_in, w_mid, w_out
        )
        state_acc = lax.dynamic_update_index_in_dim(state_acc, new_tile, slot_now, 0)
        grad_acc = lax.dynamic_update_index_in_dim(grad_acc, grad_x, slot_now, 0)
        return (state_acc, grad_acc, sum_in + grad_in, sum_mid + grad_mid, sum_out + grad_out)

    finished = lax.fori_loop(0, live_count, visit_tile, start_state)
    return (finished[0], finished[1], (finished[2], finished[3], finished[4]))


def per_device(
    prognostic, diffusivity, mixing, cotangent, tile_cols, pad_mask, tile_count, w_in, w_mid, w_out
):
    fields = prognostic.shape[1]
    lon_local = prognostic.shape[2]
    latitudes = prognostic.shape[3]
    cells = lon_local * latitudes
    levels = diffusivity.shape[1]
    edge_coef = shifted(mixing[0, -1:, :], "horiz", 1)
    blank_row = jnp.zeros_like(edge_coef)
    lon_pad = jnp.concatenate([edge_coef, mixing[0], blank_row], axis=0)
    lat_pad = jnp.concatenate([blank_row, mixing[1], blank_row], axis=0)

    def advance(field_now):
        for repeat in range(DYN_STEPS):
            padded = with_halo(field_now, (("horiz", 2),), 1)
            field_now = padded_step(padded, lon_pad, lat_pad)
        return field_now

    moved = advance(prognostic)
    columns = tile_cols[0, 0].reshape(-1)
    tiles = tile_cols.shape[2]
    tile_width = tile_cols.shape[3]

    def to_tiles(field_flat):
        row_count = field_flat.shape[0]
        return jnp.transpose(
            field_flat[:, columns].reshape(row_count, tiles, tile_width), (1, 0, 2)
        )

    tile_total = tile_count[0, 0]
    active = (jnp.arange(tiles, dtype=jnp.int32) < tile_total).astype(jnp.int32)
    live_mask = pad_mask[0, 0] * active[:, None]
    moved_flat = moved[0].reshape(fields, cells)
    cot_flat = cotangent[0].reshape(fields, cells)
    x_tiles = to_tiles(moved_flat).astype(jnp.bfloat16)
    coef_tiles = to_tiles(diffusivity[0].reshape(levels, cells)).astype(jnp.bfloat16)
    cot_tiles = (to_tiles(cot_flat) * live_mask[:, None, :].astype(jnp.float32)).astype(
        jnp.bfloat16
    )
    state_tiles, grad_tiles, grad_sums = run_tiles(
        x_tiles,
        coef_tiles,
        cot_tiles,
        tile_total,
        jnp.arange(tiles, dtype=jnp.int32),
        w_in,
        w_mid,
        w_out,
    )
    live_flat = live_mask.reshape(-1)

    def place_back(field_flat, tile_vals):
        fresh_vals = jnp.transpose(tile_vals, (1, 0, 2)).reshape(fields, -1).astype(jnp.float32)
        kept_vals = field_flat[:, columns]
        return field_flat.at[:, columns].set(
            jnp.where(live_flat[None, :] > 0, fresh_vals, kept_vals)
        )

    state_next = place_back(moved_flat, state_tiles).reshape(prognostic.shape)
    grad_field = place_back(cot_flat, grad_tiles).reshape(prognostic.shape)
    state_grad = advance(grad_field)
    summed = lax.psum((grad_sums[0], grad_sums[1], grad_sums[2]), ("ens", "horiz"))
    column_total = lax.axis_size("ens") * lax.axis_size("horiz") * cells
    factor = 1.0 / math.sqrt(column_total)
    return (state_next, state_grad, summed[0] * factor, summed[1] * factor, summed[2] * factor)


def solution(mesh):
    placed = (
        P("ens", None, "horiz", None),
        P("ens", None, "horiz", None),
        P(None, "horiz", None),
        P("ens", None, "horiz", None),
        P("ens", "horiz", None, None),
        P("ens", "horiz", None, None),
        P("ens", "horiz"),
        P(),
        P(),
        P(),
    )
    return jax.shard_map(
        per_device,
        mesh=mesh,
        in_specs=placed,
        out_specs=(P("ens", None, "horiz", None), P("ens", None, "horiz", None), P(), P(), P()),
        check_vma=False,
    )
```

profile of v0, /device:TPU:0, one launch (start us, length us, event | category | flops | bytes accessed | tf_op | source)
XLA Modules:
  0.0 281.9 jit_solution(18334992509641621894)
XLA Ops:
  9.6 4.1 %collective-permute-start = (f32[1,128,1,128]{3,2,1,0:T(1,128)S(1)}, f32[1,128,1,128]{3,2,1,0:T(1,128)S(1)}, u32[]{:S(2)}, u32[]{:S(2)}) collective-permute-start(f32[1,128,1,128]{3,2,1,0:T(1,128)S(1)} %get-tuple-element.913), channel_id=1, source_target_pairs={{1,0},{2,1},{3,2},{4,3},{5,4},{6,5},{7,6},{0,7},{9,8},{10,9},{11,1... | collective-permute-start | bytes 196616 | tf_op jit(solution)/shard_map/ppermute | solution.py:26
  20.3 1.4 gather_fusion
  22.7 3.6 %collective-permute-start.3 = (f32[1,128,1,128]{3,2,1,0:T(1,128)S(1)}, f32[1,128,1,128]{3,2,1,0:T(1,128)S(1)}, u32[]{:S(2)}, u32[]{:S(2)}) collective-permute-start(f32[1,128,1,128]{3,2,1,0:T(1,128)S(1)} %get-tuple-element.911), channel_id=1, source_target_pairs={{1,0},{2,1},{3,2},{4,3},{5,4},{6,5},{7,6},{0,7},{9,8},{10,9},{11,1... | collective-permute-start | bytes 196616 | tf_op jit(solution)/shard_map/ppermute | solution.py:26
  26.4 1.8 collective-permute-done.3
  28.2 3.6 %collective-permute-done.4 = f32[1,128,1,128]{3,2,1,0:T(1,128)S(1)} collective-permute-done((f32[1,128,1,128]{3,2,1,0:T(1,128)S(1)}, f32[1,128,1,128]{3,2,1,0:T(1,128)S(1)}, u32[]{:S(2)}, u32[]{:S(2)}) %collective-permute-start.4) | collective-permute-done | bytes 65568 | tf_op jit(solution)/shard_map/ppermute | solution.py:23
  33.8 2.5 broadcast_in_dim.81
  36.4 56.5 %while.153 = (s32[]{:T(128)}, bf16[3,128,128]{2,1,0:T(8,128)(2,1)S(1)}, bf16[3,128,128]{1,2,0:T(8,128)(2,1)S(1)}, f32[1024,128]{1,0:T(8,128)S(1)}, f32[1024,1024...) while((s32[]{:T(128)}, ...), condition=%wide.region_9.10_spmd, body=%wide.region_0.9_spmd.sunk | while | flops 1013084416 | bytes 67982240 | solution.py:141
  40.0 2.4 convolution_bitcast_fusion.9
  43.3 3.8 %while.154 = (s32[]{:T(128)}, f32[128]{0:T(128)S(1)}, f32[4,128]{1,0:T(4,128)S(1)}, f32[32,128]{1,0:T(8,128)S(1)}, f32[32,4,128]{2,1,0:T(4,128)S(1)}, /*index=5*...) while((s32[]{:T(128)}, f32[128]{0:T(128)S(1)}, ...), condition=%wide.region_2.2_spmd.clone, body=%wide.region_1.1_spmd.clone.sunk | while | flops 2691 | bytes 14480 | solution.py:51
  47.1 2.0 while.155
  49.1 4.5 %while.156 = (s32[]{:T(128)}, f32[128]{0:T(128)S(1)}, f32[4,128]{1,0:T(4,128)S(1)}, f32[32,128]{1,0:T(8,128)S(1)}, f32[32,4,128]{2,1,0:T(4,128)S(1)}, /*index=5*...) while((s32[]{:T(128)}, f32[128]{0:T(128)S(1)}, ...), condition=%wide.region_6.6_spmd.clone, body=%wide.region_5.5_spmd.clone.sunk | while | flops 2691 | bytes 18580 | solution.py:51
  53.6 3.0 %while.157 = (s32[]{:T(128)}, f32[4,128]{1,0:T(4,128)S(1)}, f32[32,4,128]{2,0,1:T(8,128)S(1)}, f32[32,4,128]{2,1,0:T(4,128)S(1)}, f32[32,128]{1,0:T(8,128)S(1)}, /*index=5*/s32[]{:T(128)}, s32[]{:T(128)}, s32[]{:T(128)}) while((s32[]{:T(128)}, f32[4,128]{1,0:T(4,128)S(1)}, f32[32,4,128]{2,0,1:T(8,128)S(1)}, ...), condition=%wide.region_8.8_spmd.clone, body=%wide.region_7.7_spmd.clone.sunk | while | flops 1540 | bytes 11903 | solution.py:60
  56.8 1.6 fusion.127
  58.4 1.5 convolution_add_fusion.8
  62.3 2.0 copy-done.1
  67.9 2.4 convolution_bitcast_fusion.9
  71.2 3.8 %while.154 = (s32[]{:T(128)}, f32[128]{0:T(128)S(1)}, f32[4,128]{1,0:T(4,128)S(1)}, f32[32,128]{1,0:T(8,128)S(1)}, f32[32,4,128]{2,1,0:T(4,128)S(1)}, /*index=5*...) while((s32[]{:T(128)}, f32[128]{0:T(128)S(1)}, ...), condition=%wide.region_2.2_spmd.clone, body=%wide.region_1.1_spmd.clone.sunk | while | flops 2691 | bytes 14480 | solution.py:51
  75.0 2.0 while.155
  77.0 4.5 %while.156 = (s32[]{:T(128)}, f32[128]{0:T(128)S(1)}, f32[4,128]{1,0:T(4,128)S(1)}, f32[32,128]{1,0:T(8,128)S(1)}, f32[32,4,128]{2,1,0:T(4,128)S(1)}, /*index=5*...) while((s32[]{:T(128)}, f32[128]{0:T(128)S(1)}, ...), condition=%wide.region_6.6_spmd.clone, body=%wide.region_5.5_spmd.clone.sunk | while | flops 2691 | bytes 18580 | solution.py:51
  81.5 3.0 %while.157 = (s32[]{:T(128)}, f32[4,128]{1,0:T(4,128)S(1)}, f32[32,4,128]{2,0,1:T(8,128)S(1)}, f32[32,4,128]{2,1,0:T(4,128)S(1)}, f32[32,128]{1,0:T(8,128)S(1)}, /*index=5*/s32[]{:T(128)}, s32[]{:T(128)}, s32[]{:T(128)}) while((s32[]{:T(128)}, f32[4,128]{1,0:T(4,128)S(1)}, f32[32,4,128]{2,0,1:T(8,128)S(1)}, ...), condition=%wide.region_8.8_spmd.clone, body=%wide.region_7.7_spmd.clone.sunk | while | flops 1540 | bytes 11903 | solution.py:60
  84.7 1.6 fusion.127
  86.3 1.5 convolution_add_fusion.8
  90.2 2.0 copy-done.1
  94.3 1.6 scatter_custom_fusion.1
  96.2 23.7 %collective-permute-start.6 = (f32[1,128,1,128]{3,2,1,0:T(1,128)S(1)}, f32[1,128,1,128]{3,2,1,0:T(1,128)S(1)}, u32[]{:S(2)}, u32[]{:S(2)}) collective-permute-start(f32[1,128,1,128]{3,2,1,0:T(1,128)S(1)} %get-tuple-element.910), channel_id=1, source_target_pairs={{0,1},{1,2},{2,3},{3,4},{4,5},{5,6},{6,7},{7,0},{8,9},{9,10},{10,1... | collective-permute-start | bytes 196616 | tf_op jit(solution)/shard_map/ppermute | solution.py:23
  120.2 1.6 scatter_custom_fusion
  123.2 1.7 collective-permute-start.8
  126.4 3.7 %collective-permute-done.8 = f32[1,128,1,128]{3,2,1,0:T(1,128)S(1)} collective-permute-done((f32[1,128,1,128]{3,2,1,0:T(1,128)S(1)}, f32[1,128,1,128]{3,2,1,0:T(1,128)S(1)}, u32[]{:S(2)}, u32[]{:S(2)}) %collective-permute-start.8) | collective-permute-done | bytes 65568 | tf_op jit(solution)/shard_map/ppermute | solution.py:23
  131.2 135.1 %all-reduce.12.cloned.1.call-done = (f32[1024,128]{1,0:T(8,128)}, f32[1024,1024]{1,0:T(8,128)}, f32[128,1024]{1,0:T(8,128)}) async-done(((f32[1024,128]{1,0:T(8,128)}, f32[1024,1024]{1,0:T(8,128)}, f32[128,1024]{1,0:T(8,128)}), (f32[1024,128]{1,0:T(8,128)}, f32[1024,1024]{1,0:T(8,128)}, f32[128,1024]{1,0:T(8,128)})) %all-reduce.12.cloned.1.call-update) | async-done | bytes 5242896 | tf_op jit(solution)/shard_map/psum | solution.py:207
  266.3 1.9 broadcast_multiply_fusion.2
  268.1 1.9 broadcast_multiply_fusion.1
  270.0 5.0 %broadcast_multiply_fusion = f32[1024,1024]{1,0:T(8,128)} fusion(f32[1024,1024]{1,0:T(8,128)} %get-tuple-element.890), kind=kLoop, calls=%fused_computation.83 | loop fusion | flops 1048576 | bytes 8388608 | tf_op jit(solution)/shard_map/mul | solution.py:210
  (1041 shorter events, 44.1 us)
Async XLA Ops:
  7.2 14.8 %copy-start.4 = (f32[1,128,4,128]{3,2,1,0:T(4,128)S(1)}, f32[1,128,4,128]{3,2,1,0:T(4,128)}, u32[]{:S(2)}) copy-start(f32[1,128,4,128]{3,2,1,0:T(4,128)} %param.20) | copy-start | bytes 786436
  7.2 13.0 %copy-start.6 = (f32[1,32,4,128]{3,2,1,0:T(4,128)S(1)}, f32[1,32,4,128]{3,2,1,0:T(4,128)}, u32[]{:S(2)}) copy-start(f32[1,32,4,128]{3,2,1,0:T(4,128)} %param.21) | copy-start | bytes 196612
  7.2 259.1 %all-reduce.12.cloned.1.call-start = ((), (), s32[]{:S(2)}) async-start(), calls=%async_computation | async-start | bytes 10485760 | tf_op jit(solution)/shard_map/psum | solution.py:207
  8.0 13.9 %collective-permute-start.1 = (f32[1,128]{1,0:T(1,128)S(1)}, f32[1,128]{1,0:T(1,128)S(1)}, u32[]{:S(2)}, u32[]{:S(2)}) collective-permute-start(f32[1,128]{1,0:T(1,128)S(1)} %slice_bitcast_fusion.3), channel_id=1, source_target_pairs={{7,0},{0,1},{1,2},{2,3},{3,4},{4,5},{5,6},{6,7},{15,8},{8,9},{9,10... | collective-permute-start | bytes 1544 | tf_op jit(solution)/shard_map/ppermute | solution.py:14
  9.6 12.4 %collective-permute-start = (f32[1,128,1,128]{3,2,1,0:T(1,128)S(1)}, f32[1,128,1,128]{3,2,1,0:T(1,128)S(1)}, u32[]{:S(2)}, u32[]{:S(2)}) collective-permute-start(f32[1,128,1,128]{3,2,1,0:T(1,128)S(1)} %get-tuple-element.913), channel_id=1, source_target_pairs={{1,0},{2,1},{3,2},{4,3},{5,4},{6,5},{7,6},{0,7},{9,8},{10,9},{11,1... | collective-permute-start | bytes 196616 | tf_op jit(solution)/shard_map/ppermute | solution.py:26
  13.7 8.3 %collective-permute-start.2 = (f32[1,128,1,128]{3,2,1,0:T(1,128)S(1)}, f32[1,128,1,128]{3,2,1,0:T(1,128)S(1)}, u32[]{:S(2)}, u32[]{:S(2)}) collective-permute-start(f32[1,128,1,128]{3,2,1,0:T(1,128)S(1)} %get-tuple-element.914), channel_id=1, source_target_pairs={{0,1},{1,2},{2,3},{3,4},{4,5},{5,6},{6,7},{7,0},{8,9},{9,10},{10,1... | collective-permute-start | bytes 196616 | tf_op jit(solution)/shard_map/ppermute | solution.py:23
  22.7 5.5 %collective-permute-start.3 = (f32[1,128,1,128]{3,2,1,0:T(1,128)S(1)}, f32[1,128,1,128]{3,2,1,0:T(1,128)S(1)}, u32[]{:S(2)}, u32[]{:S(2)}) collective-permute-start(f32[1,128,1,128]{3,2,1,0:T(1,128)S(1)} %get-tuple-element.911), channel_id=1, source_target_pairs={{1,0},{2,1},{3,2},{4,3},{5,4},{6,5},{7,6},{0,7},{9,8},{10,9},{11,1... | collective-permute-start | bytes 196616 | tf_op jit(solution)/shard_map/ppermute | solution.py:26
  26.3 5.5 %collective-permute-start.4 = (f32[1,128,1,128]{3,2,1,0:T(1,128)S(1)}, f32[1,128,1,128]{3,2,1,0:T(1,128)S(1)}, u32[]{:S(2)}, u32[]{:S(2)}) collective-permute-start(f32[1,128,1,128]{3,2,1,0:T(1,128)S(1)} %get-tuple-element.912), channel_id=1, source_target_pairs={{0,1},{1,2},{2,3},{3,4},{4,5},{5,6},{6,7},{7,0},{8,9},{9,10},{10,1... | collective-permute-start | bytes 196616 | tf_op jit(solution)/shard_map/ppermute | solution.py:23
  32.2 4.1 %copy-start.2 = (bf16[1024,128]{1,0:T(8,128)(2,1)S(1)}, bf16[1024,128]{1,0:T(8,128)(2,1)}, u32[]{:S(2)}) copy-start(bf16[1024,128]{1,0:T(8,128)(2,1)} %param.27) | copy-start | bytes 786436
  32.2 4.1 %copy-start.7 = (pred[32]{0:T(512)(128)(4,1)S(1)}, pred[32]{0:T(512)(128)(4,1)}, u32[]{:S(2)}) copy-start(pred[32]{0:T(512)(128)(4,1)} %constant.183.clone.1) | copy-start | bytes 100
  39.6 2.8 %copy-start.10 = (bf16[128,1024]{1,0:T(8,128)(2,1)S(1)}, bf16[128,1024]{1,0:T(8,128)(2,1)}, u32[]{:S(2)}) copy-start(bf16[128,1024]{1,0:T(8,128)(2,1)} %get-tuple-element.1460) | copy-start | bytes 786436 | tf_op jit(solution)/shard_map/while
  42.5 0.8 copy-start.11
  56.7 3.1 %copy-start.9 = (bf16[1024,1024]{1,0:T(8,128)(2,1)S(1)}, bf16[1024,1024]{1,0:T(8,128)(2,1)}, u32[]{:S(2)}) copy-start(bf16[1024,1024]{1,0:T(8,128)(2,1)} %get-tuple-element.1459) | copy-start | bytes 6291460 | tf_op jit(solution)/shard_map/while
  58.3 2.7 copy-start
  62.3 2.0 copy-start.1
  67.6 2.8 %copy-start.10 = (bf16[128,1024]{1,0:T(8,128)(2,1)S(1)}, bf16[128,1024]{1,0:T(8,128)(2,1)}, u32[]{:S(2)}) copy-start(bf16[128,1024]{1,0:T(8,128)(2,1)} %get-tuple-element.1460) | copy-start | bytes 786436 | tf_op jit(solution)/shard_map/while
  70.4 0.8 copy-start.11
  84.7 3.1 %copy-start.9 = (bf16[1024,1024]{1,0:T(8,128)(2,1)S(1)}, bf16[1024,1024]{1,0:T(8,128)(2,1)}, u32[]{:S(2)}) copy-start(bf16[1024,1024]{1,0:T(8,128)(2,1)} %get-tuple-element.1459) | copy-start | bytes 6291460 | tf_op jit(solution)/shard_map/while
  86.3 2.7 copy-start
  90.2 2.0 copy-start.1
  92.9 0.8 copy-start.3
  92.9 1.0 copy-start.5
  92.9 1.0 copy-start.8
  96.1 26.5 %collective-permute-start.5 = (f32[1,128,1,128]{3,2,1,0:T(1,128)S(1)}, f32[1,128,1,128]{3,2,1,0:T(1,128)S(1)}, u32[]{:S(2)}, u32[]{:S(2)}) collective-permute-start(f32[1,128,1,128]{3,2,1,0:T(1,128)S(1)} %get-tuple-element.909), channel_id=1, source_target_pairs={{1,0},{2,1},{3,2},{4,3},{5,4},{6,5},{7,6},{0,7},{9,8},{10,9},{11,1... | collective-permute-start | bytes 196616 | tf_op jit(solution)/shard_map/ppermute | solution.py:26
  96.2 26.4 %collective-permute-start.6 = (f32[1,128,1,128]{3,2,1,0:T(1,128)S(1)}, f32[1,128,1,128]{3,2,1,0:T(1,128)S(1)}, u32[]{:S(2)}, u32[]{:S(2)}) collective-permute-start(f32[1,128,1,128]{3,2,1,0:T(1,128)S(1)} %get-tuple-element.910), channel_id=1, source_target_pairs={{0,1},{1,2},{2,3},{3,4},{4,5},{5,6},{6,7},{7,0},{8,9},{9,10},{10,1... | collective-permute-start | bytes 196616 | tf_op jit(solution)/shard_map/ppermute | solution.py:23
  123.2 3.2 %collective-permute-start.7 = (f32[1,128,1,128]{3,2,1,0:T(1,128)S(1)}, f32[1,128,1,128]{3,2,1,0:T(1,128)S(1)}, u32[]{:S(2)}, u32[]{:S(2)}) collective-permute-start(f32[1,128,1,128]{3,2,1,0:T(1,128)S(1)} %get-tuple-element.907), channel_id=1, source_target_pairs={{1,0},{2,1},{3,2},{4,3},{5,4},{6,5},{7,6},{0,7},{9,8},{10,9},{11,1... | collective-permute-start | bytes 196616 | tf_op jit(solution)/shard_map/ppermute | solution.py:26
  123.2 6.8 %collective-permute-start.8 = (f32[1,128,1,128]{3,2,1,0:T(1,128)S(1)}, f32[1,128,1,128]{3,2,1,0:T(1,128)S(1)}, u32[]{:S(2)}, u32[]{:S(2)}) collective-permute-start(f32[1,128,1,128]{3,2,1,0:T(1,128)S(1)} %get-tuple-element.908), channel_id=1, source_target_pairs={{0,1},{1,2},{2,3},{3,4},{4,5},{5,6},{6,7},{7,0},{8,9},{9,10},{10,1... | collective-permute-start | bytes 196616 | tf_op jit(solution)/shard_map/ppermute | solution.py:23
Sparse Core Ops, SparseCore 0:
  94.0 172.2 all-reduce.11
where the time goes:
time: 283 us; the launch traced here: 282 us
  waiting for transfers between devices  145 us (51%)
  starting transfers between devices  33.8 us (12%)
  local copies, waits for them, and re-layouts  33.6 us (12%)
  other arithmetic  22.9 us (8%)
  matrix products  16.9 us (6%)
  between operations  15.1 us (5%)
  loops' own time  14.3 us (5%)
    psum x1, waiting for transfers between devices, per_device(): lax.psum((grad_sums[0], grad_sums[1], grad_sums[2]), ('ens', 'horiz'))  135 us
    ppermute x4, starting transfers between devices, with_halo(): lax.ppermute(lax.slice_in_dim(block, block.shape[dim] - width, None, axis...  25.5 us
    ppermute x4, starting transfers between devices, with_halo(): lax.ppermute(lax.slice_in_dim(block, 0, width, axis=dim), axis, backward)  7.8 us
    dynamic_update_slice x192, local copies, waits for them, and re-layouts, vertical_solve(): lax.scan(sweep_down, start_state, (coef_below, coef_above, diag_term, by_...  7.31 us
    ppermute x4, waiting for transfers between devices, with_halo(): lax.ppermute(lax.slice_in_dim(block, block.shape[dim] - width, None, axis...  7.25 us
    another operation x1, loops' own time, run_tiles(): finished = lax.fori_loop(0, live_count, visit_tile, start_state)  6.46 us
  transfers between devices with their start and end apart: 10, of which 5 were waited for; matrix products, arithmetic and copies ran while one was open for 6% of the time, Pallas kernels for 0%

commit v1 on v0

v1 whole, which is shorter than its diff:
```python
import functools
import math

import jax
import jax.numpy as jnp
from jax import lax
from jax.experimental import pallas as pl
from jax.experimental.pallas import tpu as pltpu
from jax.sharding import PartitionSpec as P

DYN_STEPS = 2
BLOCK = 256
VMEM_LIMIT = 40 * 1024 * 1024
F32 = jnp.float32
BF16 = jnp.bfloat16
CONTRACT_LAST = (((1,), (1,)), ((), ()))
CONTRACT_FIRST = (((0,), (0,)), ((), ()))


def call(kernel, outs, scratch=(), smem=(), flops=0, moved=0, **names):
    def run(*operands):
        specs = [
            pl.BlockSpec(memory_space=pltpu.SMEM if place in smem else pltpu.VMEM)
            for place in range(len(operands))
        ]
        return pl.pallas_call(
            functools.partial(kernel, **names),
            out_shape=[jax.ShapeDtypeStruct(shape, dtype) for shape, dtype in outs],
            in_specs=specs,
            out_specs=[pl.BlockSpec(memory_space=pltpu.VMEM)] * len(outs),
            scratch_shapes=list(scratch),
            compiler_params=pltpu.CompilerParams(vmem_limit_bytes=VMEM_LIMIT),
            cost_estimate=pl.CostEstimate(flops=flops, bytes_accessed=moved, transcendentals=0),
        )(*operands)

    return run


def lat_term(field_now, coef_masked):
    lats = field_now.shape[1]
    north_flux = coef_masked * (pltpu.roll(field_now, lats - 1, 1) - field_now)
    return north_flux - pltpu.roll(north_flux, 1, 1)


def two_steps(rows, lon_coef, lat_coef):
    for repeat in range(DYN_STEPS):
        count = len(rows)
        fluxes = [
            lon_coef[place + repeat] * (rows[place + 1] - rows[place]) for place in range(count - 1)
        ]
        rows = [
            rows[place]
            + fluxes[place]
            - fluxes[place - 1]
            + lat_term(rows[place], lat_coef[place + repeat])
            for place in range(1, count - 1)
        ]
    return rows


def coefficients(mix_ref, low_mix, high_mix, lons):
    lats = mix_ref.shape[1]
    lane = lax.broadcasted_iota(jnp.int32, (1, lats), 1)
    inside = lane < lats - 1
    own_lon = [mix_ref[lon : lon + 1, :] for lon in range(lons)]
    own_lat = [mix_ref[lons + lon : lons + lon + 1, :] for lon in range(lons)]
    lon_coef = [low_mix[0:1, :], low_mix[1:2, :]] + own_lon + [high_mix[0:1, :], high_mix[1:2, :]]
    lat_coef = [low_mix[2:3, :], low_mix[3:4, :]] + own_lat + [high_mix[2:3, :], high_mix[3:4, :]]
    return lon_coef, [jnp.where(inside, coef, 0.0) for coef in lat_coef]


def pack_kernel(prog_ref, mix_ref, up_ref, down_ref, *, lons):
    fields = prog_ref.shape[0] // lons
    for out_ref, first in ((up_ref, lons - 2), (down_ref, 0)):
        for side in range(2):
            out_ref[side * fields : (side + 1) * fields, :] = prog_ref[
                pl.ds(first + side, fields, stride=lons), :
            ]
        out_ref[2 * fields : 2 * fields + 2, :] = mix_ref[first : first + 2, :]
        out_ref[2 * fields + 2 : 2 * fields + 4, :] = mix_ref[lons + first : lons + first + 2, :]
        out_ref[2 * fields + 4 :, :] = jnp.zeros_like(out_ref[2 * fields + 4 :, :])


def one_hot(cols_ref, cells):
    parts = []
    for tile in range(cols_ref.shape[0]):
        place = lax.broadcasted_iota(jnp.int32, (cells, cols_ref.shape[1]), 0)
        parts.append(jnp.where(place == cols_ref[tile : tile + 1, :], 1.0, 0.0))
    return jnp.concatenate(parts, axis=1).astype(BF16)


def live_row(count_ref, mask_ref):
    parts = []
    for tile in range(mask_ref.shape[0]):
        used = jnp.where(tile < count_ref[0, 0], 1, 0)
        parts.append((mask_ref[tile : tile + 1, :] * used).astype(F32))
    return jnp.concatenate(parts, axis=1)


def level_rows(levels, level, variables):
    return pl.ds(level, variables, stride=levels)


def solve(levels, variables, coef_ref, ratio_ref, inverse_ref, right_ref, out_ref):
    tiles, _, width = right_ref.shape
    spans = [slice(tile * width, (tile + 1) * width) for tile in range(tiles)]
    values = []
    for level in range(levels):
        inverse_now = inverse_ref[level : level + 1, :]
        if level > 0:
            carry_now = coef_ref[level - 1 : level, :] * inverse_now
        step = []
        for tile, span in enumerate(spans):
            right_now = right_ref[tile, level_rows(levels, level, variables), :]
            value_now = right_now * inverse_now[:, span]
            if level > 0:
                value_now = value_now + carry_now[:, span] * values[-1][tile]
            step.append(value_now)
        values.append(step)
    results = values[-1]
    for level in range(levels - 1, -1, -1):
        if level < levels - 1:
            ratio_now = ratio_ref[level : level + 1, :]
            results = [
                values[level][tile] - ratio_now[:, span] * results[tile]
                for tile, span in enumerate(spans)
            ]
        for tile in range(tiles):
            out_ref[tile, level_rows(levels, level, variables), :] = results[tile]


def split_tiles(ref, value):
    width = ref.shape[2]
    for tile in range(ref.shape[0]):
        ref[tile] = value[:, tile * width : (tile + 1) * width]


def join_tiles(ref):
    return jnp.concatenate([ref[tile] for tile in range(ref.shape[0])], axis=1)


def factorise(levels, coef_ref, ratio_ref, inverse_ref):
    ratio_prev = None
    for level in range(levels):
        coef_now = coef_ref[level : level + 1, :]
        divisor = 1.0 + coef_now
        if level > 0:
            below_now = coef_ref[level - 1 : level, :]
            divisor = divisor + below_now + below_now * ratio_prev
        inverse_now = 1.0 / divisor
        ratio_prev = -coef_now * inverse_now
        inverse_ref[level : level + 1, :] = inverse_now
        ratio_ref[level : level + 1, :] = ratio_prev


def by_cell(ref, rows, lons):
    return jnp.concatenate(
        [ref[pl.ds(lon, rows, stride=lons), :] for lon in range(lons)], axis=1
    )


def adjoint_kernel(
    count_ref,
    diff_ref,
    cot_ref,
    cols_ref,
    mask_ref,
    adj_ref,
    coef_ref,
    ratio_ref,
    inverse_ref,
    right_ref,
    *,
    lons,
):
    levels = diff_ref.shape[0] // lons
    fields = cot_ref.shape[0] // lons
    cells = lons * cot_ref.shape[1]
    spread = one_hot(cols_ref, cells)
    sources = jnp.concatenate(
        [by_cell(cot_ref, fields, lons), by_cell(diff_ref, levels, lons)], axis=0
    ).astype(BF16)
    picked = jnp.dot(sources, spread, preferred_element_type=F32)
    split_tiles(right_ref, picked[:fields] * live_row(count_ref, mask_ref))
    coef_ref[...] = picked[fields:]
    factorise(levels, coef_ref, ratio_ref, inverse_ref)
    solve(levels, fields // levels, coef_ref, ratio_ref, inverse_ref, right_ref, adj_ref)


def sigmoid(pre_act):
    return 0.5 * jnp.tanh(0.5 * pre_act) + 0.5


def forward_kernel(
    prog_ref,
    low_ref,
    high_ref,
    mix_ref,
    cols_ref,
    adj_ref,
    w_in_ref,
    w_mid_ref,
    w_out_ref,
    moved_ref,
    x_ref,
    act_two_ref,
    delta_two_ref,
    grad_ref,
    act_one_ref,
    *,
    lons,
):
    fields = prog_ref.shape[0] // lons
    units = w_mid_ref.shape[0]
    cells = lons * prog_ref.shape[1]
    lon_coef, lat_coef = coefficients(
        mix_ref,
        low_ref[2 * fields : 2 * fields + 4, :],
        high_ref[2 * fields : 2 * fields + 4, :],
        lons,
    )
    rows = [low_ref[side * fields : (side + 1) * fields, :] for side in range(2)]
    rows += [prog_ref[pl.ds(lon, fields, stride=lons), :] for lon in range(lons)]
    rows += [high_ref[side * fields : (side + 1) * fields, :] for side in range(2)]
    rows = two_steps(rows, lon_coef, lat_coef)
    for lon in range(lons):
        moved_ref[lon] = rows[lon]
    spread = one_hot(cols_ref, cells)
    sources = jnp.concatenate(rows, axis=1).astype(BF16)
    x_now = jnp.dot(sources, spread, preferred_element_type=F32).astype(BF16)
    x_ref[...] = x_now
    for start in range(0, units, BLOCK):
        pre_one = jnp.dot(w_in_ref[start : start + BLOCK, :], x_now, preferred_element_type=F32)
        act_one_ref[start : start + BLOCK, :] = (pre_one * sigmoid(pre_one)).astype(BF16)
    adj_half = join_tiles(adj_ref).astype(BF16)
    for start in range(0, units, BLOCK):
        pre_two = jnp.dot(
            w_mid_ref[start : start + BLOCK, :], act_one_ref[...], preferred_element_type=F32
        )
        sigma_val = sigmoid(pre_two)
        act_two_ref[start : start + BLOCK, :] = (pre_two * sigma_val).astype(BF16)
        back_two = lax.dot_general(
            w_out_ref[:, start : start + BLOCK],
            adj_half,
            CONTRACT_FIRST,
            preferred_element_type=F32,
        )
        slope = sigma_val * (1.0 + pre_two * (1.0 - sigma_val))
        delta_two_ref[start : start + BLOCK, :] = (back_two * slope).astype(BF16)
    for start in range(0, units, BLOCK):
        grad_ref[start : start + BLOCK, :] = lax.dot_general(
            delta_two_ref[start : start + BLOCK, :],
            act_one_ref[...],
            CONTRACT_LAST,
            preferred_element_type=F32,
        ).astype(BF16)


def backward_kernel(
    count_ref,
    moved_ref,
    cot_ref,
    cols_ref,
    mask_ref,
    x_ref,
    act_two_ref,
    delta_two_ref,
    adj_ref,
    coef_ref,
    ratio_ref,
    inverse_ref,
    w_in_ref,
    w_mid_ref,
    w_out_ref,
    small_ref,
    state_ref,
    field_ref,
    up_ref,
    down_ref,
    delta_one_ref,
    forced_ref,
    solved_ref,
    *,
    lons,
):
    fields = x_ref.shape[0]
    units = w_mid_ref.shape[0]
    levels = coef_ref.shape[0]
    lats = moved_ref.shape[2]
    x_now = x_ref[...]
    adj_now = join_tiles(adj_ref)
    for start in range(0, units, BLOCK):
        back_one = lax.dot_general(
            w_mid_ref[:, start : start + BLOCK],
            delta_two_ref[...],
            CONTRACT_FIRST,
            preferred_element_type=F32,
        )
        pre_one = jnp.dot(w_in_ref[start : start + BLOCK, :], x_now, preferred_element_type=F32)
        sigma_val = sigmoid(pre_one)
        slope = sigma_val * (1.0 + pre_one * (1.0 - sigma_val))
        delta_one_ref[start : start + BLOCK, :] = (back_one * slope).astype(BF16)
    adj_half = adj_now.astype(BF16)
    small_ref[:, :fields] = lax.dot_general(
        delta_one_ref[...], x_now, CONTRACT_LAST, preferred_element_type=F32
    ).astype(BF16)
    small_ref[:, fields:] = lax.dot_general(
        act_two_ref[...], adj_half, CONTRACT_LAST, preferred_element_type=F32
    ).astype(BF16)
    grad_x = adj_now + lax.dot_general(
        w_in_ref[...], delta_one_ref[...], CONTRACT_FIRST, preferred_element_type=F32
    )
    tendency = jnp.dot(w_out_ref[...], act_two_ref[...], preferred_element_type=F32)
    split_tiles(forced_ref, x_now.astype(F32) + tendency)
    solve(levels, fields // levels, coef_ref, ratio_ref, inverse_ref, forced_ref, solved_ref)
    live = live_row(count_ref, mask_ref)
    fresh = jnp.concatenate(
        [
            join_tiles(solved_ref) * live,
            grad_x * live,
            jnp.broadcast_to(live, (16, live.shape[1])),
        ],
        axis=0,
    ).astype(BF16)
    spread = one_hot(cols_ref, lons * lats)
    placed = lax.dot_general(fresh, spread, CONTRACT_LAST, preferred_element_type=F32)
    for lon in range(lons):
        here = slice(lon * lats, (lon + 1) * lats)
        taken = placed[2 * fields : 2 * fields + 1, here] > 0.5
        state_ref[pl.ds(lon, fields, stride=lons), :] = jnp.where(
            taken, placed[:fields, here], moved_ref[lon]
        )
        field_now = jnp.where(
            taken, placed[fields : 2 * fields, here], cot_ref[pl.ds(lon, fields, stride=lons), :]
        )
        field_ref[lon] = field_now
        if lon < 2:
            down_ref[lon] = field_now
        if lon >= lons - 2:
            up_ref[lon - (lons - 2)] = field_now


def last_kernel(field_ref, low_ref, high_ref, low_mix_ref, high_mix_ref, mix_ref, out_ref, *, lons):
    fields = field_ref.shape[1]
    lon_coef, lat_coef = coefficients(
        mix_ref,
        low_mix_ref[2 * fields : 2 * fields + 4, :],
        high_mix_ref[2 * fields : 2 * fields + 4, :],
        lons,
    )
    rows = [low_ref[0], low_ref[1]]
    rows += [field_ref[lon] for lon in range(lons)]
    rows += [high_ref[0], high_ref[1]]
    rows = two_steps(rows, lon_coef, lat_coef)
    for lon in range(lons):
        out_ref[pl.ds(lon, fields, stride=lons), :] = rows[lon]


def to_neighbours(upward, downward, axis):
    count = lax.axis_size(axis)
    forward = [(i, (i + 1) % count) for i in range(count)]
    backward = [(target, source) for source, target in forward]
    return lax.ppermute(upward, axis, forward), lax.ppermute(downward, axis, backward)


def per_device(
    prognostic, diffusivity, mixing, cotangent, tile_cols, pad_mask, tile_count, w_in, w_mid, w_out
):
    fields, lons, lats = prognostic.shape[1:]
    levels = diffusivity.shape[1]
    units = w_mid.shape[0]
    tiles, width = tile_cols.shape[2:]
    slots = tiles * width
    prog_rows = prognostic.reshape(fields * lons, lats)
    cot_rows = cotangent.reshape(fields * lons, lats)
    diff_rows = diffusivity.reshape(levels * lons, lats)
    mix_rows = mixing.reshape(2 * lons, lats)
    cols, mask = tile_cols[0, 0], pad_mask[0, 0]

    packed = ((2 * fields + 8, lats), F32)
    up_pack, down_pack = call(pack_kernel, [packed, packed], lons=lons)(prog_rows, mix_rows)
    low_pack, high_pack = to_neighbours(up_pack, down_pack, "horiz")

    adjoint, coef, ratio, inverse = call(
        adjoint_kernel,
        [((tiles, fields, width), F32)] + [((levels, slots), F32)] * 3,
        scratch=[pltpu.VMEM((tiles, fields, width), F32)],
        smem=(0,),
        flops=10**9,
        moved=10**6,
        lons=lons,
    )(tile_count, diff_rows, cot_rows, cols, mask)

    moved, x_now, act_two, delta_two, grad_mid = call(
        forward_kernel,
        [
            ((lons, fields, lats), F32),
            ((fields, slots), BF16),
            ((units, slots), BF16),
            ((units, slots), BF16),
            ((units, units), BF16),
        ],
        scratch=[pltpu.VMEM((units, slots), BF16)],
        flops=2 * 10**9,
        moved=6 * 10**6,
        lons=lons,
    )(prog_rows, low_pack, high_pack, mix_rows, cols, adjoint, w_in, w_mid, w_out)

    small, state_rows, grad_field, up_rows, down_rows = call(
        backward_kernel,
        [
            ((units, 2 * fields), BF16),
            ((fields * lons, lats), F32),
            ((lons, fields, lats), F32),
            ((2, fields, lats), F32),
            ((2, fields, lats), F32),
        ],
        scratch=[
            pltpu.VMEM((units, slots), BF16),
            pltpu.VMEM((tiles, fields, width), F32),
            pltpu.VMEM((tiles, fields, width), F32),
        ],
        smem=(0,),
        flops=2 * 10**9,
        moved=6 * 10**6,
        lons=lons,
    )(
        tile_count,
        moved,
        cot_rows,
        cols,
        mask,
        x_now,
        act_two,
        delta_two,
        adjoint,
        coef,
        ratio,
        inverse,
        w_in,
        w_mid,
        w_out,
    )
    low_rows, high_rows = to_neighbours(up_rows, down_rows, "horiz")
    (grad_rows,) = call(last_kernel, [((fields * lons, lats), F32)], lons=lons)(
        grad_field, low_rows, high_rows, low_pack, high_pack, mix_rows
    )

    sum_mid, sum_small = lax.psum((grad_mid, small), ("ens", "horiz"))
    column_total = lax.axis_size("ens") * lax.axis_size("horiz") * lons * lats
    factor = 1.0 / math.sqrt(column_total)
    return (
        state_rows.reshape(prognostic.shape),
        grad_rows.reshape(prognostic.shape),
        sum_small[:, :fields].astype(F32) * factor,
        sum_mid.astype(F32) * factor,
        sum_small[:, fields:].astype(F32).T * factor,
    )


def solution(mesh):
    placed = (
        P("ens", None, "horiz", None),
        P("ens", None, "horiz", None),
        P(None, "horiz", None),
        P("ens", None, "horiz", None),
        P("ens", "horiz", None, None),
        P("ens", "horiz", None, None),
        P("ens", "horiz"),
        P(),
        P(),
        P(),
    )
    return jax.shard_map(
        per_device,
        mesh=mesh,
        in_specs=placed,
        out_specs=(P("ens", None, "horiz", None), P("ens", None, "horiz", None), P(), P(), P()),
        check_vma=False,
    )
```

time: 283 us -> 183 us (0.65)
  starting transfers between devices: 33.8 us -> 8.23 us
  local copies, waits for them, and re-layouts: 33.6 us -> 10.3 us
  matrix products: 16.9 us -> 0 us
  other arithmetic: 22.9 us -> 6.09 us
  loops' own time: 14.3 us -> 0 us
  waiting for transfers between devices: 145 us -> 132 us
  Pallas kernels: 0 us -> 11.1 us
    ppermute x9 -> x4, starting transfers between devices: 33.7 us -> 8.2 us  [the longest x2 7.63 us: to_neighbours(): lax.ppermute(downward, axis, backward)]
    dot_general x18 -> x0, matrix products: 16.9 us -> none  [the longest x2 4.86 us: column_physics(): pre_two = jnp.dot(w_mid, act_one, preferred_element_type=jnp.float32)]
    another operation x9 -> x0, loops' own time: 14.3 us -> none  [the longest x1 6.46 us: run_tiles(): finished = lax.fori_loop(0, live_count, visit_tile, start_state)]
    pallas_call x0 -> x5, Pallas kernels: none -> 11.1 us  [run(): pl.pallas_call(functools.partial(kernel, **names), out_shape=[jax.ShapeDt...]
    dynamic_update_slice x194 -> x0, local copies, waits for them, and re-layouts: 7.34 us -> none  [the longest x192 7.31 us: vertical_solve(): lax.scan(sweep_down, start_state, (coef_below, coef_above, diag_term, by_...]
    unnamed x17 -> x30, local copies, waits for them, and re-layouts: 3.01 us -> 10.3 us
    ppermute x9 -> x4, waiting for transfers between devices: 10.2 us -> 3.36 us  [the longest x2 3.35 us: to_neighbours(): lax.ppermute(upward, axis, forward)]
    psum x1, waiting for transfers between devices: 135 us -> 129 us  [per_device(): sum_mid, sum_small = lax.psum((grad_mid, small), ('ens', 'horiz'))]
  transfers between devices with their start and end apart: 10 -> 5, of which waited for: 5 -> 2; matrix products, arithmetic and copies ran while one was open for 6% -> 0% of each run, Pallas kernels for 0% -> 1%
where the time goes in v1:
time: 183 us; the launch traced here: 182 us
  waiting for transfers between devices  132 us (72%)
  between operations  14.8 us (8%)
  Pallas kernels  11.1 us (6%)
  local copies, waits for them, and re-layouts  10.3 us (6%)
  starting transfers between devices  8.23 us (4%)
  other arithmetic  6.09 us (3%)
    psum x1, waiting for transfers between devices, per_device(): sum_mid, sum_small = lax.psum((grad_mid, small), ('ens', 'horiz'))  129 us
    pallas_call x5, Pallas kernels, run(): pl.pallas_call(functools.partial(kernel, **names), out_shape=[jax.ShapeDt...  11.1 us
    unnamed x30, local copies, waits for them, and re-layouts  10.3 us
    ppermute x2, starting transfers between devices, to_neighbours(): lax.ppermute(downward, axis, backward)  7.63 us
    mul x1, other arithmetic, per_device(): sum_mid.astype(F32) * factor  4.2 us
  transfers between devices with their start and end apart: 5, of which 2 were waited for; matrix products, arithmetic and copies ran while one was open for 0% of the time, Pallas kernels for 1%

profile of v1, /device:TPU:0, one launch (start us, length us, event | category | flops | bytes accessed | tf_op | source)
XLA Modules:
  0.0 182.4 jit_solution(12343020772578092450)
XLA Ops:
  7.2 0.0 all-reduce.3.cloned.1.call-start
  7.2 0.0 copy-start
  7.2 0.9 copy-done
  8.2 0.7 copy-done.2
  8.9 0.5 collective-permute-start
  9.4 4.1 %collective-permute-start.1 = (f32[264,128]{1,0:T(8,128)S(1)}, f32[264,128]{1,0:T(8,128)S(1)}, u32[]{:S(2)}, u32[]{:S(2)}) collective-permute-start(f32[264,128]{1,0:T(8,128)S(1)} %get-tuple-element.22), channel_id=1, source_target_pairs={{1,0},{2,1},{3,2},{4,3},{5,4},{6,5},{7,6},{0,7},{9,8},{10,9},{11,1... | collective-permute-start | bytes 405512 | tf_op jit(solution)/shard_map/ppermute | solution.py:363
  13.5 0.7 copy_bitcast_fusion
  14.8 0.0 copy-start.7
  14.8 0.9 copy-done.7
  15.8 0.8 copy-done.13
  16.6 0.8 shard_map.138
  17.4 0.0 collective-permute-done.low_ref.low_mix_ref
  17.4 0.0 collective-permute-done.1.high_ref.high_mix_ref
  17.4 0.0 copy-start.1
  17.4 1.0 copy-done.1
  18.4 0.7 copy-done.3
  19.1 1.6 copy-done.5
  20.7 0.9 copy-done.9
  21.7 0.9 copy-done.11
  22.6 4.9 %shard_map.139 = (f32[4,128,128]{2,1,0:T(8,128)S(1)}, bf16[128,384]{1,0:T(8,128)(2,1)S(1)}, bf16[1024,384]{1,0:T(8,128)(2,1)S(1)}, bf16[1024,384]{1,0:T(8,128)(2,1)S(1)}, bf16[1024,1024]{1,0:T(8,128)(2,1)}) custom-call(f32[512,128]{1,0:T(8,128)S(1)} %bitcast.13, f32[264,128]{1,0:T(8,128)S(1)} %collective-permute-done.low_ref.low_mix_ref, ...), custom_call_target="tpu_custom_call" | custom-call | flops 2000000000 | bytes 6000000 | tf_op jit(solution)/shard_map/pallas_call | solution.py:26
  27.6 0.0 copy-start.4
  27.6 3.9 %shard_map.140 = (bf16[1024,256]{1,0:T(8,128)(2,1)}, f32[512,128]{1,0:T(8,128)}, f32[4,128,128]{2,1,0:T(8,128)S(1)}, f32[2,128,128]{2,1,0:T(8,128)S(1)}, f32[2,128,128]{2,1,0:T(8,128)S(1)}) custom-call(s32[1,1]{1,0:T(1,128)S(6)} %copy.22.count_ref, f32[4,128,128]{2,1,0:T(8,128)S(1)} %get-tuple-element.24.moved_ref, f32[512,128]{1,0:T(8,128)S(1)} %bitcast.18, ...), custom_call_target="tpu_custom_call" | custom-call | flops 2000000000 | bytes 6000000 | tf_op jit(solution)/shard_map/pallas_call | solution.py:26
  31.5 0.0 all-reduce.3.cloned.1.call-update
  31.5 0.1 collective-permute-start.2
  31.6 3.5 %collective-permute-start.3 = (f32[2,128,128]{2,1,0:T(8,128)S(1)}, f32[2,128,128]{2,1,0:T(8,128)S(1)}, u32[]{:S(2)}, u32[]{:S(2)}) collective-permute-start(f32[2,128,128]{2,1,0:T(8,128)S(1)} %get-tuple-element.34), channel_id=1, source_target_pairs={{1,0},{2,1},{3,2},{4,3},{5,4},{6,5},{7,6},{0,7},{9,8},{10,9},{11,1... | collective-permute-start | bytes 393224 | tf_op jit(solution)/shard_map/ppermute | solution.py:363
  35.1 3.4 %collective-permute-done.2.low_ref = f32[2,128,128]{2,1,0:T(8,128)S(1)} collective-permute-done((f32[2,128,128]{2,1,0:T(8,128)S(1)}, f32[2,128,128]{2,1,0:T(8,128)S(1)}, u32[]{:S(2)}, u32[]{:S(2)}) %collective-permute-start.2) | collective-permute-done | bytes 131104 | tf_op jit(solution)/shard_map/ppermute | solution.py:363
  38.5 0.0 collective-permute-done.3.high_ref
  38.5 1.5 shard_map.141
  40.0 128.5 %all-reduce.3.cloned.1.call-done = (bf16[1024,256]{1,0:T(8,128)(2,1)}, bf16[1024,1024]{1,0:T(8,128)(2,1)}) async-done(((bf16[1024,256]{1,0:T(8,128)(2,1)}, bf16[1024,1024]{1,0:T(8,128)(2,1)}), (bf16[1024,256]{1,0:T(8,128)(2,1)}, bf16[1024,1024]{1,0:T(8,128)(2,1)})) %all-reduce.3.cloned.1.call-update) | async-done | bytes 2621456 | tf_op jit(solution)/shard_map/psum | solution.py:449
  168.5 1.9 %multiply_bitcast_fusion = (f32[128,1024]{0,1:T(8,128)S(1)}, f32[1024,128]{1,0:T(8,128)}) fusion(bf16[1024,256]{1,0:T(8,128)(2,1)} %get-tuple-element.42), kind=kLoop, calls=%fused_computation.1 | loop fusion | flops 524288 | bytes 1572864 | tf_op jit(solution)/shard_map/mul | solution.py:457
  170.4 1.0 copy.15
  171.4 4.2 %convert_multiply_fusion = f32[1024,1024]{1,0:T(8,128)} fusion(bf16[1024,1024]{1,0:T(8,128)(2,1)} %get-tuple-element.43), kind=kLoop, calls=%fused_computation | loop fusion | flops 2097152 | bytes 6291456 | tf_op jit(solution)/shard_map/mul | solution.py:456
  (16 shorter events, 0.0 us)
Async XLA Ops:
  7.2 161.3 %all-reduce.3.cloned.1.call-start = ((), (), s32[]{:S(2)}) async-start(), calls=%async_computation | async-start | bytes 5242880 | tf_op jit(solution)/shard_map/psum | solution.py:449
  7.2 1.0 copy-start
  8.2 0.7 copy-start.2
  8.9 8.5 %collective-permute-start = (f32[264,128]{1,0:T(8,128)S(1)}, f32[264,128]{1,0:T(8,128)S(1)}, u32[]{:S(2)}, u32[]{:S(2)}) collective-permute-start(f32[264,128]{1,0:T(8,128)S(1)} %get-tuple-element.21), channel_id=1, source_target_pairs={{0,1},{1,2},{2,3},{3,4},{4,5},{5,6},{6,7},{7,0},{8,9},{9,10},{10,1... | collective-permute-start | bytes 405512 | tf_op jit(solution)/shard_map/ppermute | solution.py:363
  9.4 8.0 %collective-permute-start.1 = (f32[264,128]{1,0:T(8,128)S(1)}, f32[264,128]{1,0:T(8,128)S(1)}, u32[]{:S(2)}, u32[]{:S(2)}) collective-permute-start(f32[264,128]{1,0:T(8,128)S(1)} %get-tuple-element.22), channel_id=1, source_target_pairs={{1,0},{2,1},{3,2},{4,3},{5,4},{6,5},{7,6},{0,7},{9,8},{10,9},{11,1... | collective-permute-start | bytes 405512 | tf_op jit(solution)/shard_map/ppermute | solution.py:363
  14.8 1.0 copy-start.7
  15.8 0.8 copy-start.13
  16.6 10.9 %copy-start.6 = (bf16[1024,1024]{1,0:T(8,128)(2,1)S(1)}, bf16[1024,1024]{1,0:T(8,128)(2,1)}, u32[]{:S(2)}) copy-start(bf16[1024,1024]{1,0:T(8,128)(2,1)} %w_mid_ref.3) | copy-start | bytes 6291460
  16.6 10.9 %copy-start.8 = (f32[1,128,4,128]{3,2,1,0:T(4,128)S(1)}, f32[1,128,4,128]{3,2,1,0:T(4,128)}, u32[]{:S(2)}) copy-start(f32[1,128,4,128]{3,2,1,0:T(4,128)} %param.13) | copy-start | bytes 786436
  16.6 10.9 %copy-start.10 = (bf16[1024,128]{1,0:T(8,128)(2,1)S(1)}, bf16[1024,128]{1,0:T(8,128)(2,1)}, u32[]{:S(2)}) copy-start(bf16[1024,128]{1,0:T(8,128)(2,1)} %w_in_ref.3) | copy-start | bytes 786436
  16.6 10.9 %copy-start.12 = (bf16[128,1024]{1,0:T(8,128)(2,1)S(1)}, bf16[128,1024]{1,0:T(8,128)(2,1)}, u32[]{:S(2)}) copy-start(bf16[128,1024]{1,0:T(8,128)(2,1)} %w_out_ref.3) | copy-start | bytes 786436
  17.4 1.0 copy-start.1
  18.4 0.7 copy-start.3
  19.1 1.6 copy-start.5
  20.7 0.9 copy-start.9
  21.7 0.9 copy-start.11
  27.6 10.9 %copy-start.4 = (f32[2,4,128]{2,1,0:T(4,128)S(1)}, f32[2,4,128]{2,1,0:T(4,128)}, u32[]{:S(2)}) copy-start(f32[2,4,128]{2,1,0:T(4,128)} %param.12) | copy-start | bytes 12292
  31.5 6.9 %collective-permute-start.2 = (f32[2,128,128]{2,1,0:T(8,128)S(1)}, f32[2,128,128]{2,1,0:T(8,128)S(1)}, u32[]{:S(2)}, u32[]{:S(2)}) collective-permute-start(f32[2,128,128]{2,1,0:T(8,128)S(1)} %get-tuple-element.33), channel_id=1, source_target_pairs={{0,1},{1,2},{2,3},{3,4},{4,5},{5,6},{6,7},{7,0},{8,9},{9,10},{10,1... | collective-permute-start | bytes 393224 | tf_op jit(solution)/shard_map/ppermute | solution.py:363
  31.6 6.9 %collective-permute-start.3 = (f32[2,128,128]{2,1,0:T(8,128)S(1)}, f32[2,128,128]{2,1,0:T(8,128)S(1)}, u32[]{:S(2)}, u32[]{:S(2)}) collective-permute-start(f32[2,128,128]{2,1,0:T(8,128)S(1)} %get-tuple-element.34), channel_id=1, source_target_pairs={{1,0},{2,1},{3,2},{4,3},{5,4},{6,5},{7,6},{0,7},{9,8},{10,9},{11,1... | collective-permute-start | bytes 393224 | tf_op jit(solution)/shard_map/ppermute | solution.py:363
Sparse Core Ops, SparseCore 0:
  31.6 136.8 all-reduce.2

commit v2 on v1

--- a/solution.py
+++ b/solution.py
@@ -201,11 +201,13 @@
     w_in_ref,
     w_mid_ref,
     w_out_ref,
+    place_ref,
     moved_ref,
     x_ref,
     act_two_ref,
     delta_two_ref,
-    grad_ref,
+    keep_ref,
+    send_ref,
     act_one_ref,
     *,
     lons,
@@ -247,13 +249,14 @@
         )
         slope = sigma_val * (1.0 + pre_two * (1.0 - sigma_val))
         delta_two_ref[start : start + BLOCK, :] = (back_two * slope).astype(BF16)
-    for start in range(0, units, BLOCK):
-        grad_ref[start : start + BLOCK, :] = lax.dot_general(
-            delta_two_ref[start : start + BLOCK, :],
-            act_one_ref[...],
-            CONTRACT_LAST,
-            preferred_element_type=F32,
-        ).astype(BF16)
+    for out_ref, half in ((send_ref, 1 - place_ref[0, 0]), (keep_ref, place_ref[0, 0])):
+        for start in range(0, units // 2, BLOCK):
+            out_ref[start : start + BLOCK, :] = lax.dot_general(
+                delta_two_ref[pl.ds(half * (units // 2) + start, BLOCK), :],
+                act_one_ref[...],
+                CONTRACT_LAST,
+                preferred_element_type=F32,
+            ).astype(BF16)
 
 
 def backward_kernel(
@@ -272,7 +275,9 @@
     w_in_ref,
     w_mid_ref,
     w_out_ref,
-    small_ref,
+    place_ref,
+    keep_ref,
+    send_ref,
     state_ref,
     field_ref,
     up_ref,
@@ -301,12 +306,14 @@
         slope = sigma_val * (1.0 + pre_one * (1.0 - sigma_val))
         delta_one_ref[start : start + BLOCK, :] = (back_one * slope).astype(BF16)
     adj_half = adj_now.astype(BF16)
-    small_ref[:, :fields] = lax.dot_general(
-        delta_one_ref[...], x_now, CONTRACT_LAST, preferred_element_type=F32
-    ).astype(BF16)
-    small_ref[:, fields:] = lax.dot_general(
-        act_two_ref[...], adj_half, CONTRACT_LAST, preferred_element_type=F32
-    ).astype(BF16)
+    for out_ref, half in ((send_ref, 1 - place_ref[0, 0]), (keep_ref, place_ref[0, 0])):
+        here = pl.ds(half * (units // 2), units // 2)
+        out_ref[:, :fields] = lax.dot_general(
+            delta_one_ref[here, :], x_now, CONTRACT_LAST, preferred_element_type=F32
+        ).astype(BF16)
+        out_ref[:, fields:] = lax.dot_general(
+            act_two_ref[here, :], adj_half, CONTRACT_LAST, preferred_element_type=F32
+        ).astype(BF16)
     grad_x = adj_now + lax.dot_general(
         w_in_ref[...], delta_one_ref[...], CONTRACT_FIRST, preferred_element_type=F32
     )
@@ -356,6 +363,122 @@
         out_ref[pl.ds(lon, fields, stride=lons), :] = rows[lon]
 
 
+def core_sum_kernel(place_ref, *refs, parts):
+    keeps, gots, outs = refs[: len(refs[:-parts]) // 2], refs[len(refs[:-parts]) // 2 : -parts], refs[-parts:]
+    rows = outs[0].shape[0]
+    for k in range(parts):
+        start = pl.multiple_of((place_ref[0, 1] ^ k) * rows, rows)
+        first = 0
+        for keep_ref, got_ref in zip(keeps, gots):
+            here = pl.ds(start, rows)
+            columns = keep_ref.shape[1]
+            outs[k][:, first : first + columns] = (
+                keep_ref[here, :].astype(F32) + got_ref[here, :].astype(F32)
+            ).astype(BF16)
+            first += columns
+
+
+def chip_sum_kernel(place_ref, *refs, terms, parts, which, factor):
+    ins, outs = refs[:terms], refs[terms:]
+    rows = outs[0].shape[0]
+    for k in range(parts):
+        start = pl.multiple_of((place_ref[0, which] ^ k) * rows, rows) if parts > 1 else 0
+        total = None
+        for ref in ins:
+            term = ref[pl.ds(start, rows), :].astype(F32)
+            total = term if total is None else total + term
+        outs[k][...] = (total * factor).astype(BF16)
+
+
+def join_kernel(place_ref, *refs, which):
+    ins, out_ref = refs[:-1], refs[-1]
+    rows = ins[0].shape[0]
+    for k, ref in enumerate(ins):
+        out_ref[pl.ds(pl.multiple_of((place_ref[0, which] ^ k) * rows, rows), rows), :] = ref[...]
+
+
+def final_kernel(place_ref, own_ref, got_ref, mid_ref, in_ref, out_ref, *, factor):
+    rows = own_ref.shape[0]
+    mids, fields = mid_ref.shape[1], in_ref.shape[1]
+    for ref, half in ((own_ref, place_ref[0, 0]), (got_ref, 1 - place_ref[0, 0])):
+        start = pl.multiple_of(half * rows, rows)
+        mid_ref[pl.ds(start, rows), :] = ref[:, :mids].astype(F32) * factor
+        in_ref[pl.ds(start, rows), :] = ref[:, mids : mids + fields].astype(F32) * factor
+        out_ref[:, pl.ds(start, rows)] = ref[:, mids + fields :].astype(F32).T * factor
+
+
+def exchange(arrays, axis, stride):
+    count = lax.axis_size(axis)
+    return [
+        lax.ppermute(array, axis, [(i, i ^ (k * stride)) for i in range(count)])
+        for k, array in enumerate(arrays, 1)
+    ]
+
+
+def sum_over_all(place, keeps, sends, factor):
+    members = lax.axis_size("ens")
+    chips = lax.axis_size("horiz") // 2
+    half = keeps[0].shape[0]
+    columns = sum(keep.shape[1] for keep in keeps)
+    quarter = half // members
+    eighth = quarter // chips
+    size = quarter * columns
+    gots = [exchange([send], "horiz", 1)[0] for send in sends]
+    parts = call(
+        core_sum_kernel,
+        [((quarter, columns), BF16)] * members,
+        smem=(0,),
+        flops=size * members,
+        moved=size * members * 6,
+        parts=members,
+    )(place, *keeps, *gots)
+    terms = [parts[0]] + exchange(parts[1:], "ens", 1)
+    if eighth % 16 == 0 and chips <= 8:
+        parts = call(
+            chip_sum_kernel,
+            [((eighth, columns), BF16)] * chips,
+            smem=(0,),
+            flops=size * members,
+            moved=size * members * 2,
+            terms=members,
+            parts=chips,
+            which=2,
+            factor=1.0,
+        )(place, *terms)
+        terms = [parts[0]] + exchange(parts[1:], "horiz", 2)
+        (own,) = call(
+            chip_sum_kernel,
+            [((eighth, columns), BF16)],
+            smem=(0,),
+            flops=size,
+            moved=size * 2,
+            terms=chips,
+            parts=1,
+            which=2,
+            factor=factor,
+        )(place, *terms)
+        (own,) = call(
+            join_kernel, [((quarter, columns), BF16)], smem=(0,), moved=size * 4, which=2
+        )(place, own, *exchange([own] * (chips - 1), "horiz", 2))
+    else:
+        (own,) = call(
+            chip_sum_kernel,
+            [((quarter, columns), BF16)],
+            smem=(0,),
+            terms=members,
+            parts=1,
+            which=2,
+            factor=1.0,
+        )(place, *terms)
+        core = place[0, 0]
+        both = jnp.stack([jnp.where(core == side, own, 0.0).astype(F32) for side in range(2)])
+        own = (lax.psum(both, "horiz")[core] * factor).astype(BF16)
+    (own,) = call(
+        join_kernel, [((half, columns), BF16)], smem=(0,), moved=size * 16, which=1
+    )(place, own, *exchange([own] * (members - 1), "ens", 1))
+    return own, exchange([own], "horiz", 1)[0]
+
+
 def to_neighbours(upward, downward, axis):
     count = lax.axis_size(axis)
     forward = [(i, (i + 1) % count) for i in range(count)]
@@ -376,6 +499,8 @@
     diff_rows = diffusivity.reshape(levels * lons, lats)
     mix_rows = mixing.reshape(2 * lons, lats)
     cols, mask = tile_cols[0, 0], pad_mask[0, 0]
+    horiz = lax.axis_index("horiz")
+    place = jnp.stack([horiz % 2, lax.axis_index("ens"), horiz // 2]).reshape(1, 3)
 
     packed = ((2 * fields + 8, lats), F32)
     up_pack, down_pack = call(pack_kernel, [packed, packed], lons=lons)(prog_rows, mix_rows)
@@ -391,25 +516,28 @@
         lons=lons,
     )(tile_count, diff_rows, cot_rows, cols, mask)
 
-    moved, x_now, act_two, delta_two, grad_mid = call(
+    moved, x_now, act_two, delta_two, keep_mid, send_mid = call(
         forward_kernel,
         [
             ((lons, fields, lats), F32),
             ((fields, slots), BF16),
             ((units, slots), BF16),
             ((units, slots), BF16),
-            ((units, units), BF16),
+            ((units // 2, units), BF16),
+            ((units // 2, units), BF16),
         ],
         scratch=[pltpu.VMEM((units, slots), BF16)],
         flops=2 * 10**9,
         moved=6 * 10**6,
+        smem=(9,),
         lons=lons,
-    )(prog_rows, low_pack, high_pack, mix_rows, cols, adjoint, w_in, w_mid, w_out)
-
-    small, state_rows, grad_field, up_rows, down_rows = call(
+    )(prog_rows, low_pack, high_pack, mix_rows, cols, adjoint, w_in, w_mid, w_out, place)
+
+    keep_small, send_small, state_rows, grad_field, up_rows, down_rows = call(
         backward_kernel,
         [
-            ((units, 2 * fields), BF16),
+            ((units // 2, 2 * fields), BF16),
+            ((units // 2, 2 * fields), BF16),
             ((fields * lons, lats), F32),
             ((lons, fields, lats), F32),
             ((2, fields, lats), F32),
@@ -420,7 +548,7 @@
             pltpu.VMEM((tiles, fields, width), F32),
             pltpu.VMEM((tiles, fields, width), F32),
         ],
-        smem=(0,),
+        smem=(0, 15),
         flops=2 * 10**9,
         moved=6 * 10**6,
         lons=lons,
@@ -440,21 +568,28 @@
         w_in,
         w_mid,
         w_out,
+        place,
     )
     low_rows, high_rows = to_neighbours(up_rows, down_rows, "horiz")
     (grad_rows,) = call(last_kernel, [((fields * lons, lats), F32)], lons=lons)(
         grad_field, low_rows, high_rows, low_pack, high_pack, mix_rows
     )
 
-    sum_mid, sum_small = lax.psum((grad_mid, small), ("ens", "horiz"))
     column_total = lax.axis_size("ens") * lax.axis_size("horiz") * lons * lats
     factor = 1.0 / math.sqrt(column_total)
+    own, got = sum_over_all(place, [keep_mid, keep_small], [send_mid, send_small], factor)
+    grad_mid, grad_in, grad_out = call(
+        final_kernel,
+        [((units, units), F32), ((units, fields), F32), ((fields, units), F32)],
+        smem=(0,),
+        factor=1.0,
+    )(place, own, got)
     return (
         state_rows.reshape(prognostic.shape),
         grad_rows.reshape(prognostic.shape),
-        sum_small[:, :fields].astype(F32) * factor,
-        sum_mid.astype(F32) * factor,
-        sum_small[:, fields:].astype(F32).T * factor,
+        grad_in,
+        grad_mid,
+        grad_out,
     )
 
 

time: 183 us -> 92.2 us (0.50)
  waiting for transfers between devices: 132 us -> 41.4 us
  starting transfers between devices: 8.23 us -> 25 us
  between operations: 14.8 us -> 1.47 us
  Pallas kernels: 11.1 us -> 17.6 us
  other arithmetic: 6.09 us -> 0.08 us
  local copies, waits for them, and re-layouts: 10.3 us -> 6.36 us
    psum x1 -> x0, waiting for transfers between devices: 129 us -> none  [per_device(): sum_mid, sum_small = lax.psum((grad_mid, small), ('ens', 'horiz'))]
    ppermute x0 -> x15, waiting for transfers between devices: none -> 37.6 us  [exchange(): lax.ppermute(array, axis, [(i, i ^ k * stride) for i in range(count)])]
    ppermute x0 -> x15, starting transfers between devices: none -> 16.8 us  [exchange(): lax.ppermute(array, axis, [(i, i ^ k * stride) for i in range(count)])]
    pallas_call x5 -> x11, Pallas kernels: 11.1 us -> 17.6 us  [run(): pl.pallas_call(functools.partial(kernel, **names), out_shape=[jax.ShapeDt...]
    mul x2 -> x0, other arithmetic: 6.09 us -> none  [the longest x1 4.2 us: per_device(): sum_mid.astype(F32) * factor]
    unnamed x30 -> x29, local copies, waits for them, and re-layouts: 10.3 us -> 6.36 us
  transfers between devices with their start and end apart: 5 -> 19, of which waited for: 2 -> 11; matrix products, arithmetic and copies ran while one was open for 0% -> 1% of each run, Pallas kernels for 1% -> 7%
where the time goes in v2:
time: 92.2 us; the launch traced here: 91.9 us
  waiting for transfers between devices  41.4 us (45%)
  starting transfers between devices  25 us (27%)
  Pallas kernels  17.6 us (19%)
  local copies, waits for them, and re-layouts  6.36 us (7%)
  between operations  1.47 us (2%)
    ppermute x15, waiting for transfers between devices, exchange(): lax.ppermute(array, axis, [(i, i ^ k * stride) for i in range(count)])  37.6 us
    pallas_call x11, Pallas kernels, run(): pl.pallas_call(functools.partial(kernel, **names), out_shape=[jax.ShapeDt...  17.6 us
    ppermute x15, starting transfers between devices, exchange(): lax.ppermute(array, axis, [(i, i ^ k * stride) for i in range(count)])  16.8 us
    ppermute x2, starting transfers between devices, to_neighbours(): lax.ppermute(downward, axis, backward)  7.2 us
    unnamed x29, local copies, waits for them, and re-layouts  6.36 us
    ppermute x2, waiting for transfers between devices, to_neighbours(): lax.ppermute(upward, axis, forward)  3.73 us
  transfers between devices with their start and end apart: 19, of which 11 were waited for; matrix products, arithmetic and copies ran while one was open for 1% of the time, Pallas kernels for 7%

profile of v2, /device:TPU:0, one launch (start us, length us, event | category | flops | bytes accessed | tf_op | source)
XLA Modules:
  0.0 91.9 jit_solution(4589027960934673569)
XLA Ops:
  0.6 0.9 %copy-done = f32[1,128,4,128]{3,2,1,0:T(4,128)S(1)} copy-done((f32[1,128,4,128]{3,2,1,0:T(4,128)S(1)}, f32[1,128,4,128]{3,2,1,0:T(4,128)}, u32[]{:S(2)}) %copy-start) | copy-done | bytes 262168
  2.8 4.1 %collective-permute-start.1 = (f32[264,128]{1,0:T(8,128)S(1)}, f32[264,128]{1,0:T(8,128)S(1)}, u32[]{:S(2)}, u32[]{:S(2)}) collective-permute-start(f32[264,128]{1,0:T(8,128)S(1)} %get-tuple-element.35), channel_id=1, source_target_pairs={{1,0},{2,1},{3,2},{4,3},{5,4},{6,5},{7,6},{0,7},{9,8},{10,9},{11,1... | collective-permute-start | bytes 405512 | tf_op jit(solution)/shard_map/ppermute | solution.py:486
  8.3 0.9 %copy-done.5 = f32[1,128,4,128]{3,2,1,0:T(4,128)S(1)} copy-done((f32[1,128,4,128]{3,2,1,0:T(4,128)S(1)}, f32[1,128,4,128]{3,2,1,0:T(4,128)}, u32[]{:S(2)}) %copy-start.5) | copy-done | bytes 262168
  9.2 0.8 copy-done.9
  10.1 0.7 shard_map.138
  12.3 0.9 copy-done.11
  13.2 4.4 %shard_map.139 = (f32[4,128,128]{2,1,0:T(8,128)S(1)}, bf16[128,384]{1,0:T(8,128)(2,1)S(1)}, bf16[1024,384]{1,0:T(8,128)(2,1)S(1)}, bf16[1024,384]{1,0:T(8,128)(2...) custom-call(f32[512,128]{1,0:T(8,128)S(1)} %bitcast.16, ...), custom_call_target="tpu_custom_call" | custom-call | flops 2000000000 | bytes 6000000 | tf_op jit(solution)/shard_map/pallas_call | solution.py:26
  17.7 4.6 %shard_map.140 = (bf16[512,256]{1,0:T(8,128)(2,1)S(1)}, bf16[512,256]{1,0:T(8,128)(2,1)S(1)}, f32[512,128]{1,0:T(8,128)}, f32[4,128,128]{2,1,0:T(8,128)S(1)}, f3...) custom-call(s32[1,1]{1,0:T(1,128)S(6)} %copy.19.count_ref, f32[4,128,128]{2,1,0:T(8,128)S(1)} %get-tuple-element.37.moved_ref, ...), custom_call_target="tpu_custom_call" | custom-call | flops 2000000000 | bytes 6000000 | tf_op jit(solution)/shard_map/pallas_call | solution.py:26
  22.8 1.2 %collective-permute-done.5.refs_3_ = bf16[512,256]{1,0:T(8,128)(2,1)S(1)} collective-permute-done((bf16[512,256]{1,0:T(8,128)(2,1)S(1)}, bf16[512,256]{1,0:T(8,128)(2,1)S(1)}, u32[]{:S(2)}, u32[]{:S(2)}) %collective-permute-start.5) | collective-permute-done | bytes 262176 | tf_op jit(solution)/shard_map/ppermute | solution.py:413
  23.9 0.8 shard_map.142
  24.8 2.0 %collective-permute-start.6 = (bf16[128,1280]{1,0:T(8,128)(2,1)S(1)}, bf16[128,1280]{1,0:T(8,128)(2,1)S(1)}, u32[]{:S(2)}, u32[]{:S(2)}) collective-permute-start(bf16[128,1280]{1,0:T(8,128)(2,1)S(1)} %get-tuple-element.53), channel_id=1, source_target_pairs={{0,8},{8,0},{16,24},{24,16},{1,9},{9,1},{17,25},{25,17},{2,10},{10... | collective-permute-start | bytes 983048 | tf_op jit(solution)/shard_map/ppermute | solution.py:413
  26.8 1.5 %collective-permute-start.7 = (bf16[128,1280]{1,0:T(8,128)(2,1)S(1)}, bf16[128,1280]{1,0:T(8,128)(2,1)S(1)}, u32[]{:S(2)}, u32[]{:S(2)}) collective-permute-start(bf16[128,1280]{1,0:T(8,128)(2,1)S(1)} %get-tuple-element.54), channel_id=1, source_target_pairs={{0,16},{8,24},{16,0},{24,8},{1,17},{9,25},{17,1},{25,9},{2,18},{10... | collective-permute-start | bytes 983048 | tf_op jit(solution)/shard_map/ppermute | solution.py:413
  28.3 7.0 %collective-permute-done.6.refs_1_ = bf16[128,1280]{1,0:T(8,128)(2,1)S(1)} collective-permute-done((bf16[128,1280]{1,0:T(8,128)(2,1)S(1)}, bf16[128,1280]{1,0:T(8,128)(2,1)S(1)}, u32[]{:S(2)}, u32[]{:S(2)}) %collective-permute-start.6) | collective-permute-done | bytes 327712 | tf_op jit(solution)/shard_map/ppermute | solution.py:413
  35.4 8.1 %collective-permute-done.7.refs_2_ = bf16[128,1280]{1,0:T(8,128)(2,1)S(1)} collective-permute-done((bf16[128,1280]{1,0:T(8,128)(2,1)S(1)}, bf16[128,1280]{1,0:T(8,128)(2,1)S(1)}, u32[]{:S(2)}, u32[]{:S(2)}) %collective-permute-start.7) | collective-permute-done | bytes 327712 | tf_op jit(solution)/shard_map/ppermute | solution.py:413
  43.5 0.7 shard_map.143
  44.3 2.4 %collective-permute-start.10 = (bf16[32,1280]{1,0:T(8,128)(2,1)S(1)}, bf16[32,1280]{1,0:T(8,128)(2,1)S(1)}, u32[]{:S(2)}, u32[]{:S(2)}) collective-permute-start(bf16[32,1280]{1,0:T(8,128)(2,1)S(1)} %get-tuple-element.58), channel_id=1, source_target_pairs={{0,4},{1,5},{2,6},{3,7},{4,0},{5,1},{6,2},{7,3},{8,12},{9,13},{10,... | collective-permute-start | bytes 245768 | tf_op jit(solution)/shard_map/ppermute | solution.py:413
  46.6 2.0 %collective-permute-start.11 = (bf16[32,1280]{1,0:T(8,128)(2,1)S(1)}, bf16[32,1280]{1,0:T(8,128)(2,1)S(1)}, u32[]{:S(2)}, u32[]{:S(2)}) collective-permute-start(bf16[32,1280]{1,0:T(8,128)(2,1)S(1)} %get-tuple-element.59), channel_id=1, source_target_pairs={{0,6},{1,7},{2,4},{3,5},{4,2},{5,3},{6,0},{7,1},{8,14},{9,15},{10,... | collective-permute-start | bytes 245768 | tf_op jit(solution)/shard_map/ppermute | solution.py:413
  48.9 4.4 %collective-permute-done.10.refs_2_ = bf16[32,1280]{1,0:T(8,128)(2,1)S(1)} collective-permute-done((bf16[32,1280]{1,0:T(8,128)(2,1)S(1)}, bf16[32,1280]{1,0:T(8,128)(2,1)S(1)}, u32[]{:S(2)}, u32[]{:S(2)}) %collective-permute-start.10) | collective-permute-done | bytes 81952 | tf_op jit(solution)/shard_map/ppermute | solution.py:413
  53.9 2.0 %collective-permute-start.14 = (bf16[32,1280]{1,0:T(8,128)(2,1)S(1)}, bf16[32,1280]{1,0:T(8,128)(2,1)S(1)}, u32[]{:S(2)}, u32[]{:S(2)}) collective-permute-start(bf16[32,1280]{1,0:T(8,128)(2,1)S(1)} %shard_map.144.refs_0_), channel_id=1, source_target_pairs={{0,6},{1,7},{2,4},{3,5},{4,2},{5,3},{6,0},{7,1},{8,14},{9,15},{10,... | collective-permute-start | bytes 245768 | tf_op jit(solution)/shard_map/ppermute | solution.py:413
  55.9 1.0 %collective-permute-start.13 = (bf16[32,1280]{1,0:T(8,128)(2,1)S(1)}, bf16[32,1280]{1,0:T(8,128)(2,1)S(1)}, u32[]{:S(2)}, u32[]{:S(2)}) collective-permute-start(bf16[32,1280]{1,0:T(8,128)(2,1)S(1)} %shard_map.144.refs_0_), channel_id=1, source_target_pairs={{0,4},{1,5},{2,6},{3,7},{4,0},{5,1},{6,2},{7,3},{8,12},{9,13},{10,... | collective-permute-start | bytes 245768 | tf_op jit(solution)/shard_map/ppermute | solution.py:413
  56.9 1.5 %collective-permute-start.12 = (bf16[32,1280]{1,0:T(8,128)(2,1)S(1)}, bf16[32,1280]{1,0:T(8,128)(2,1)S(1)}, u32[]{:S(2)}, u32[]{:S(2)}) collective-permute-start(bf16[32,1280]{1,0:T(8,128)(2,1)S(1)} %shard_map.144.refs_0_), channel_id=1, source_target_pairs={{0,2},{1,3},{2,0},{3,1},{4,6},{5,7},{6,4},{7,5},{8,10},{9,11},{10,... | collective-permute-start | bytes 245768 | tf_op jit(solution)/shard_map/ppermute | solution.py:413
  58.4 2.0 %collective-permute-done.14.refs_3_ = bf16[32,1280]{1,0:T(8,128)(2,1)S(1)} collective-permute-done((bf16[32,1280]{1,0:T(8,128)(2,1)S(1)}, bf16[32,1280]{1,0:T(8,128)(2,1)S(1)}, u32[]{:S(2)}, u32[]{:S(2)}) %collective-permute-start.14) | collective-permute-done | bytes 81952 | tf_op jit(solution)/shard_map/ppermute | solution.py:413
  60.3 1.9 %collective-permute-done.13.refs_2_ = bf16[32,1280]{1,0:T(8,128)(2,1)S(1)} collective-permute-done((bf16[32,1280]{1,0:T(8,128)(2,1)S(1)}, bf16[32,1280]{1,0:T(8,128)(2,1)S(1)}, u32[]{:S(2)}, u32[]{:S(2)}) %collective-permute-start.13) | collective-permute-done | bytes 81952 | tf_op jit(solution)/shard_map/ppermute | solution.py:413
  62.8 1.6 %collective-permute-start.17 = (bf16[128,1280]{1,0:T(8,128)(2,1)S(1)}, bf16[128,1280]{1,0:T(8,128)(2,1)S(1)}, u32[]{:S(2)}, u32[]{:S(2)}) collective-permute-start(bf16[128,1280]{1,0:T(8,128)(2,1)S(1)} %shard_map.145.refs_0_), channel_id=1, source_target_pairs={{0,24},{8,16},{16,8},{24,0},{1,25},{9,17},{17,9},{25,1},{2,26},{10... | collective-permute-start | bytes 983048 | tf_op jit(solution)/shard_map/ppermute | solution.py:413
  64.4 2.2 %collective-permute-start.16 = (bf16[128,1280]{1,0:T(8,128)(2,1)S(1)}, bf16[128,1280]{1,0:T(8,128)(2,1)S(1)}, u32[]{:S(2)}, u32[]{:S(2)}) collective-permute-start(bf16[128,1280]{1,0:T(8,128)(2,1)S(1)} %shard_map.145.refs_0_), channel_id=1, source_target_pairs={{0,16},{8,24},{16,0},{24,8},{1,17},{9,25},{17,1},{25,9},{2,18},{10... | collective-permute-start | bytes 983048 | tf_op jit(solution)/shard_map/ppermute | solution.py:413
  66.6 7.5 %collective-permute-done.17.refs_3_ = bf16[128,1280]{1,0:T(8,128)(2,1)S(1)} collective-permute-done((bf16[128,1280]{1,0:T(8,128)(2,1)S(1)}, bf16[128,1280]{1,0:T(8,128)(2,1)S(1)}, u32[]{:S(2)}, u32[]{:S(2)}) %collective-permute-start.17) | collective-permute-done | bytes 327712 | tf_op jit(solution)/shard_map/ppermute | solution.py:413
  74.1 4.2 %collective-permute-done.16.refs_2_ = bf16[128,1280]{1,0:T(8,128)(2,1)S(1)} collective-permute-done((bf16[128,1280]{1,0:T(8,128)(2,1)S(1)}, bf16[128,1280]{1,0:T(8,128)(2,1)S(1)}, u32[]{:S(2)}, u32[]{:S(2)}) %collective-permute-start.16) | collective-permute-done | bytes 327712 | tf_op jit(solution)/shard_map/ppermute | solution.py:413
  78.3 1.1 %collective-permute-done.15.refs_1_ = bf16[128,1280]{1,0:T(8,128)(2,1)S(1)} collective-permute-done((bf16[128,1280]{1,0:T(8,128)(2,1)S(1)}, bf16[128,1280]{1,0:T(8,128)(2,1)S(1)}, u32[]{:S(2)}, u32[]{:S(2)}) %collective-permute-start.15) | collective-permute-done | bytes 327712 | tf_op jit(solution)/shard_map/ppermute | solution.py:413
  80.6 3.1 %collective-permute-start.3 = (f32[2,128,128]{2,1,0:T(8,128)S(1)}, f32[2,128,128]{2,1,0:T(8,128)S(1)}, u32[]{:S(2)}, u32[]{:S(2)}) collective-permute-start(f32[2,128,128]{2,1,0:T(8,128)S(1)} %get-tuple-element.47), channel_id=1, source_target_pairs={{1,0},{2,1},{3,2},{4,3},{5,4},{6,5},{7,6},{0,7},{9,8},{10,9},{11,1... | collective-permute-start | bytes 393224 | tf_op jit(solution)/shard_map/ppermute | solution.py:486
  83.7 3.7 %collective-permute-done.2.low_ref = f32[2,128,128]{2,1,0:T(8,128)S(1)} collective-permute-done((f32[2,128,128]{2,1,0:T(8,128)S(1)}, f32[2,128,128]{2,1,0:T(8,128)S(1)}, u32[]{:S(2)}, u32[]{:S(2)}) %collective-permute-start.2) | collective-permute-done | bytes 131104 | tf_op jit(solution)/shard_map/ppermute | solution.py:486
  87.4 1.5 %shard_map.141 = f32[512,128]{1,0:T(8,128)} custom-call(f32[4,128,128]{2,1,0:T(8,128)S(1)} %get-tuple-element.45.field_ref, f32[2,128,128]{2,1,0:T(8,128)S(1)} %collective-permute-done.2.low_ref, f32[2,128,128]{2,1,0:T(8,128)S(1)} %collective-permute-done.3.high_ref, f32[264,128]{1,0:T(8,128)S(1)} %collective-permute-done.low_ref.low_mix_ref, ...), custom_call_target="tpu_custom_call" | custom-call | tf_op jit(solution)/shard_map/pallas_call | solution.py:26
  88.9 3.0 %shard_map.147 = (f32[1024,1024]{1,0:T(8,128)}, f32[1024,128]{1,0:T(8,128)}, f32[128,1024]{1,0:T(8,128)}) custom-call(s32[1,3]{1,0:T(1,128)S(1)} %add_bitcast_fusion.place_ref, bf16[512,1280]{1,0:T(8,128)(2,1)S(1)} %shard_map.146.own_ref, bf16[512,1280]{1,0:T(8,128)(2,1)S(1)} %collective-permute-done.18.got_ref), custom_call_target="tpu_custom_call" | custom-call | tf_op jit(solution)/shard_map/pallas_call | solution.py:26
  (47 shorter events, 6.6 us)
Async XLA Ops:
  0.6 1.0 %copy-start = (f32[1,128,4,128]{3,2,1,0:T(4,128)S(1)}, f32[1,128,4,128]{3,2,1,0:T(4,128)}, u32[]{:S(2)}) copy-start(f32[1,128,4,128]{3,2,1,0:T(4,128)} %param.10) | copy-start | bytes 786436
  1.6 0.7 copy-start.2
  2.3 9.9 %copy-start.1 = (f32[1,128,4,128]{3,2,1,0:T(4,128)S(1)}, f32[1,128,4,128]{3,2,1,0:T(4,128)}, u32[]{:S(2)}) copy-start(f32[1,128,4,128]{3,2,1,0:T(4,128)} %param.10) | copy-start | bytes 786436
  2.3 9.9 %copy-start.3 = (f32[2,4,128]{2,1,0:T(4,128)S(1)}, f32[2,4,128]{2,1,0:T(4,128)}, u32[]{:S(2)}) copy-start(f32[2,4,128]{2,1,0:T(4,128)} %param.12) | copy-start | bytes 12292
  2.3 9.9 %copy-start.4 = (bf16[1024,1024]{1,0:T(8,128)(2,1)S(1)}, bf16[1024,1024]{1,0:T(8,128)(2,1)}, u32[]{:S(2)}) copy-start(bf16[1024,1024]{1,0:T(8,128)(2,1)} %w_mid_ref.3) | copy-start | bytes 6291460
  2.3 9.9 %collective-permute-start = (f32[264,128]{1,0:T(8,128)S(1)}, f32[264,128]{1,0:T(8,128)S(1)}, u32[]{:S(2)}, u32[]{:S(2)}) collective-permute-start(f32[264,128]{1,0:T(8,128)S(1)} %get-tuple-element.34), channel_id=1, source_target_pairs={{0,1},{1,2},{2,3},{3,4},{4,5},{5,6},{6,7},{7,0},{8,9},{9,10},{10,1... | collective-permute-start | bytes 405512 | tf_op jit(solution)/shard_map/ppermute | solution.py:486
  2.8 9.4 %collective-permute-start.1 = (f32[264,128]{1,0:T(8,128)S(1)}, f32[264,128]{1,0:T(8,128)S(1)}, u32[]{:S(2)}, u32[]{:S(2)}) collective-permute-start(f32[264,128]{1,0:T(8,128)S(1)} %get-tuple-element.35), channel_id=1, source_target_pairs={{1,0},{2,1},{3,2},{4,3},{5,4},{6,5},{7,6},{0,7},{9,8},{10,9},{11,1... | collective-permute-start | bytes 405512 | tf_op jit(solution)/shard_map/ppermute | solution.py:486
  8.3 0.9 %copy-start.5 = (f32[1,128,4,128]{3,2,1,0:T(4,128)S(1)}, f32[1,128,4,128]{3,2,1,0:T(4,128)}, u32[]{:S(2)}) copy-start(f32[1,128,4,128]{3,2,1,0:T(4,128)} %param.13) | copy-start | bytes 786436
  9.2 0.8 copy-start.9
  10.1 2.2 %copy-start.7 = (bf16[1024,128]{1,0:T(8,128)(2,1)S(1)}, bf16[1024,128]{1,0:T(8,128)(2,1)}, u32[]{:S(2)}) copy-start(bf16[1024,128]{1,0:T(8,128)(2,1)} %w_in_ref.3) | copy-start | bytes 786436
  10.1 2.2 %copy-start.8 = (bf16[128,1024]{1,0:T(8,128)(2,1)S(1)}, bf16[128,1024]{1,0:T(8,128)(2,1)}, u32[]{:S(2)}) copy-start(bf16[128,1024]{1,0:T(8,128)(2,1)} %w_out_ref.3) | copy-start | bytes 786436
  10.8 0.7 copy-start.10
  12.2 0.9 %copy-start.11 = (f32[3,128,128]{2,1,0:T(8,128)S(1)}, f32[3,128,128]{2,1,0:T(8,128)}, u32[]{:S(2)}) copy-start(f32[3,128,128]{2,1,0:T(8,128)} %copy-done.10) | copy-start | bytes 589828
  13.2 4.5 %copy-start.6 = (f32[1,128,4,128]{3,2,1,0:T(4,128)S(1)}, f32[1,128,4,128]{3,2,1,0:T(4,128)}, u32[]{:S(2)}) copy-start(f32[1,128,4,128]{3,2,1,0:T(4,128)} %param.13) | copy-start | bytes 786436
  13.2 4.5 %copy-start.13 = (f32[32,384]{1,0:T(8,128)S(1)}, f32[32,384]{1,0:T(8,128)}, u32[]{:S(2)}) copy-start(f32[32,384]{1,0:T(8,128)} %copy-done.12) | copy-start | bytes 147460
  17.6 6.3 %collective-permute-start.4 = (bf16[512,1024]{1,0:T(8,128)(2,1)S(1)}, bf16[512,1024]{1,0:T(8,128)(2,1)S(1)}, u32[]{:S(2)}, u32[]{:S(2)}) collective-permute-start(bf16[512,1024]{1,0:T(8,128)(2,1)S(1)} %get-tuple-element.50), channel_id=1, source_target_pairs={{0,1},{1,0},{2,3},{3,2},{4,5},{5,4},{6,7},{7,6},{8,9},{9,8},{10,11... | collective-permute-start | bytes 3145736 | tf_op jit(solution)/shard_map/ppermute | solution.py:413
  22.3 1.6 %collective-permute-start.5 = (bf16[512,256]{1,0:T(8,128)(2,1)S(1)}, bf16[512,256]{1,0:T(8,128)(2,1)S(1)}, u32[]{:S(2)}, u32[]{:S(2)}) collective-permute-start(bf16[512,256]{1,0:T(8,128)(2,1)S(1)} %get-tuple-element.51), channel_id=1, source_target_pairs={{0,1},{1,0},{2,3},{3,2},{4,5},{5,4},{6,7},{7,6},{8,9},{9,8},{10,11... | collective-permute-start | bytes 786440 | tf_op jit(solution)/shard_map/ppermute | solution.py:413
  24.8 10.6 %collective-permute-start.6 = (bf16[128,1280]{1,0:T(8,128)(2,1)S(1)}, bf16[128,1280]{1,0:T(8,128)(2,1)S(1)}, u32[]{:S(2)}, u32[]{:S(2)}) collective-permute-start(bf16[128,1280]{1,0:T(8,128)(2,1)S(1)} %get-tuple-element.53), channel_id=1, source_target_pairs={{0,8},{8,0},{16,24},{24,16},{1,9},{9,1},{17,25},{25,17},{2,10},{10... | collective-permute-start | bytes 983048 | tf_op jit(solution)/shard_map/ppermute | solution.py:413
  26.8 16.7 %collective-permute-start.7 = (bf16[128,1280]{1,0:T(8,128)(2,1)S(1)}, bf16[128,1280]{1,0:T(8,128)(2,1)S(1)}, u32[]{:S(2)}, u32[]{:S(2)}) collective-permute-start(bf16[128,1280]{1,0:T(8,128)(2,1)S(1)} %get-tuple-element.54), channel_id=1, source_target_pairs={{0,16},{8,24},{16,0},{24,8},{1,17},{9,25},{17,1},{25,9},{2,18},{10... | collective-permute-start | bytes 983048 | tf_op jit(solution)/shard_map/ppermute | solution.py:413
  28.3 15.2 %collective-permute-start.8 = (bf16[128,1280]{1,0:T(8,128)(2,1)S(1)}, bf16[128,1280]{1,0:T(8,128)(2,1)S(1)}, u32[]{:S(2)}, u32[]{:S(2)}) collective-permute-start(bf16[128,1280]{1,0:T(8,128)(2,1)S(1)} %get-tuple-element.55), channel_id=1, source_target_pairs={{0,24},{8,16},{16,8},{24,0},{1,25},{9,17},{17,9},{25,1},{2,26},{10... | collective-permute-start | bytes 983048 | tf_op jit(solution)/shard_map/ppermute | solution.py:413
  44.2 4.7 %collective-permute-start.9 = (bf16[32,1280]{1,0:T(8,128)(2,1)S(1)}, bf16[32,1280]{1,0:T(8,128)(2,1)S(1)}, u32[]{:S(2)}, u32[]{:S(2)}) collective-permute-start(bf16[32,1280]{1,0:T(8,128)(2,1)S(1)} %get-tuple-element.57), channel_id=1, source_target_pairs={{0,2},{1,3},{2,0},{3,1},{4,6},{5,7},{6,4},{7,5},{8,10},{9,11},{10,... | collective-permute-start | bytes 245768 | tf_op jit(solution)/shard_map/ppermute | solution.py:413
  44.3 9.0 %collective-permute-start.10 = (bf16[32,1280]{1,0:T(8,128)(2,1)S(1)}, bf16[32,1280]{1,0:T(8,128)(2,1)S(1)}, u32[]{:S(2)}, u32[]{:S(2)}) collective-permute-start(bf16[32,1280]{1,0:T(8,128)(2,1)S(1)} %get-tuple-element.58), channel_id=1, source_target_pairs={{0,4},{1,5},{2,6},{3,7},{4,0},{5,1},{6,2},{7,3},{8,12},{9,13},{10,... | collective-permute-start | bytes 245768 | tf_op jit(solution)/shard_map/ppermute | solution.py:413
  46.6 6.7 %collective-permute-start.11 = (bf16[32,1280]{1,0:T(8,128)(2,1)S(1)}, bf16[32,1280]{1,0:T(8,128)(2,1)S(1)}, u32[]{:S(2)}, u32[]{:S(2)}) collective-permute-start(bf16[32,1280]{1,0:T(8,128)(2,1)S(1)} %get-tuple-element.59), channel_id=1, source_target_pairs={{0,6},{1,7},{2,4},{3,5},{4,2},{5,3},{6,0},{7,1},{8,14},{9,15},{10,... | collective-permute-start | bytes 245768 | tf_op jit(solution)/shard_map/ppermute | solution.py:413
  53.9 6.4 %collective-permute-start.14 = (bf16[32,1280]{1,0:T(8,128)(2,1)S(1)}, bf16[32,1280]{1,0:T(8,128)(2,1)S(1)}, u32[]{:S(2)}, u32[]{:S(2)}) collective-permute-start(bf16[32,1280]{1,0:T(8,128)(2,1)S(1)} %shard_map.144.refs_0_), channel_id=1, source_target_pairs={{0,6},{1,7},{2,4},{3,5},{4,2},{5,3},{6,0},{7,1},{8,14},{9,15},{10,... | collective-permute-start | bytes 245768 | tf_op jit(solution)/shard_map/ppermute | solution.py:413
  55.9 6.4 %collective-permute-start.13 = (bf16[32,1280]{1,0:T(8,128)(2,1)S(1)}, bf16[32,1280]{1,0:T(8,128)(2,1)S(1)}, u32[]{:S(2)}, u32[]{:S(2)}) collective-permute-start(bf16[32,1280]{1,0:T(8,128)(2,1)S(1)} %shard_map.144.refs_0_), channel_id=1, source_target_pairs={{0,4},{1,5},{2,6},{3,7},{4,0},{5,1},{6,2},{7,3},{8,12},{9,13},{10,... | collective-permute-start | bytes 245768 | tf_op jit(solution)/shard_map/ppermute | solution.py:413
  56.9 5.4 %collective-permute-start.12 = (bf16[32,1280]{1,0:T(8,128)(2,1)S(1)}, bf16[32,1280]{1,0:T(8,128)(2,1)S(1)}, u32[]{:S(2)}, u32[]{:S(2)}) collective-permute-start(bf16[32,1280]{1,0:T(8,128)(2,1)S(1)} %shard_map.144.refs_0_), channel_id=1, source_target_pairs={{0,2},{1,3},{2,0},{3,1},{4,6},{5,7},{6,4},{7,5},{8,10},{9,11},{10,... | collective-permute-start | bytes 245768 | tf_op jit(solution)/shard_map/ppermute | solution.py:413
  62.8 11.3 %collective-permute-start.17 = (bf16[128,1280]{1,0:T(8,128)(2,1)S(1)}, bf16[128,1280]{1,0:T(8,128)(2,1)S(1)}, u32[]{:S(2)}, u32[]{:S(2)}) collective-permute-start(bf16[128,1280]{1,0:T(8,128)(2,1)S(1)} %shard_map.145.refs_0_), channel_id=1, source_target_pairs={{0,24},{8,16},{16,8},{24,0},{1,25},{9,17},{17,9},{25,1},{2,26},{10... | collective-permute-start | bytes 983048 | tf_op jit(solution)/shard_map/ppermute | solution.py:413
  64.4 13.9 %collective-permute-start.16 = (bf16[128,1280]{1,0:T(8,128)(2,1)S(1)}, bf16[128,1280]{1,0:T(8,128)(2,1)S(1)}, u32[]{:S(2)}, u32[]{:S(2)}) collective-permute-start(bf16[128,1280]{1,0:T(8,128)(2,1)S(1)} %shard_map.145.refs_0_), channel_id=1, source_target_pairs={{0,16},{8,24},{16,0},{24,8},{1,17},{9,25},{17,1},{25,9},{2,18},{10... | collective-permute-start | bytes 983048 | tf_op jit(solution)/shard_map/ppermute | solution.py:413
  66.6 12.8 %collective-permute-start.15 = (bf16[128,1280]{1,0:T(8,128)(2,1)S(1)}, bf16[128,1280]{1,0:T(8,128)(2,1)S(1)}, u32[]{:S(2)}, u32[]{:S(2)}) collective-permute-start(bf16[128,1280]{1,0:T(8,128)(2,1)S(1)} %shard_map.145.refs_0_), channel_id=1, source_target_pairs={{0,8},{8,0},{16,24},{24,16},{1,9},{9,1},{17,25},{25,17},{2,10},{10... | collective-permute-start | bytes 983048 | tf_op jit(solution)/shard_map/ppermute | solution.py:413
  80.0 8.9 %collective-permute-start.18 = (bf16[512,1280]{1,0:T(8,128)(2,1)S(1)}, bf16[512,1280]{1,0:T(8,128)(2,1)S(1)}, u32[]{:S(2)}, u32[]{:S(2)}) collective-permute-start(bf16[512,1280]{1,0:T(8,128)(2,1)S(1)} %shard_map.146.own_ref), channel_id=1, source_target_pairs={{0,1},{1,0},{2,3},{3,2},{4,5},{5,4},{6,7},{7,6},{8,9},{9,8},{10,11... | collective-permute-start | bytes 3932168 | tf_op jit(solution)/shard_map/ppermute | solution.py:413
  80.1 7.3 %collective-permute-start.2 = (f32[2,128,128]{2,1,0:T(8,128)S(1)}, f32[2,128,128]{2,1,0:T(8,128)S(1)}, u32[]{:S(2)}, u32[]{:S(2)}) collective-permute-start(f32[2,128,128]{2,1,0:T(8,128)S(1)} %get-tuple-element.46), channel_id=1, source_target_pairs={{0,1},{1,2},{2,3},{3,4},{4,5},{5,6},{6,7},{7,0},{8,9},{9,10},{10,1... | collective-permute-start | bytes 393224 | tf_op jit(solution)/shard_map/ppermute | solution.py:486
  80.6 6.8 %collective-permute-start.3 = (f32[2,128,128]{2,1,0:T(8,128)S(1)}, f32[2,128,128]{2,1,0:T(8,128)S(1)}, u32[]{:S(2)}, u32[]{:S(2)}) collective-permute-start(f32[2,128,128]{2,1,0:T(8,128)S(1)} %get-tuple-element.47), channel_id=1, source_target_pairs={{1,0},{2,1},{3,2},{4,3},{5,4},{6,5},{7,6},{0,7},{9,8},{10,9},{11,1... | collective-permute-start | bytes 393224 | tf_op jit(solution)/shard_map/ppermute | solution.py:486
  (1 other events, 0.6 us)

commit v3 on v1

--- a/solution.py
+++ b/solution.py
@@ -201,11 +201,13 @@
     w_in_ref,
     w_mid_ref,
     w_out_ref,
+    place_ref,
     moved_ref,
     x_ref,
     act_two_ref,
     delta_two_ref,
-    grad_ref,
+    keep_ref,
+    send_ref,
     act_one_ref,
     *,
     lons,
@@ -247,13 +249,14 @@
         )
         slope = sigma_val * (1.0 + pre_two * (1.0 - sigma_val))
         delta_two_ref[start : start + BLOCK, :] = (back_two * slope).astype(BF16)
-    for start in range(0, units, BLOCK):
-        grad_ref[start : start + BLOCK, :] = lax.dot_general(
-            delta_two_ref[start : start + BLOCK, :],
-            act_one_ref[...],
-            CONTRACT_LAST,
-            preferred_element_type=F32,
-        ).astype(BF16)
+    for out_ref, half in ((send_ref, 1 - place_ref[0, 0]), (keep_ref, place_ref[0, 0])):
+        for start in range(0, units // 2, BLOCK):
+            out_ref[start : start + BLOCK, :] = lax.dot_general(
+                delta_two_ref[pl.ds(half * (units // 2) + start, BLOCK), :],
+                act_one_ref[...],
+                CONTRACT_LAST,
+                preferred_element_type=F32,
+            ).astype(BF16)
 
 
 def backward_kernel(
@@ -272,7 +275,9 @@
     w_in_ref,
     w_mid_ref,
     w_out_ref,
-    small_ref,
+    place_ref,
+    keep_ref,
+    send_ref,
     state_ref,
     field_ref,
     up_ref,
@@ -301,12 +306,14 @@
         slope = sigma_val * (1.0 + pre_one * (1.0 - sigma_val))
         delta_one_ref[start : start + BLOCK, :] = (back_one * slope).astype(BF16)
     adj_half = adj_now.astype(BF16)
-    small_ref[:, :fields] = lax.dot_general(
-        delta_one_ref[...], x_now, CONTRACT_LAST, preferred_element_type=F32
-    ).astype(BF16)
-    small_ref[:, fields:] = lax.dot_general(
-        act_two_ref[...], adj_half, CONTRACT_LAST, preferred_element_type=F32
-    ).astype(BF16)
+    for out_ref, half in ((send_ref, 1 - place_ref[0, 0]), (keep_ref, place_ref[0, 0])):
+        here = pl.ds(half * (units // 2), units // 2)
+        out_ref[:, :fields] = lax.dot_general(
+            delta_one_ref[here, :], x_now, CONTRACT_LAST, preferred_element_type=F32
+        ).astype(BF16)
+        out_ref[:, fields:] = lax.dot_general(
+            act_two_ref[here, :], adj_half, CONTRACT_LAST, preferred_element_type=F32
+        ).astype(BF16)
     grad_x = adj_now + lax.dot_general(
         w_in_ref[...], delta_one_ref[...], CONTRACT_FIRST, preferred_element_type=F32
     )
@@ -356,6 +363,94 @@
         out_ref[pl.ds(lon, fields, stride=lons), :] = rows[lon]
 
 
+def core_sum_kernel(*refs):
+    keeps, gots, out_ref = refs[: len(refs) // 2], refs[len(refs) // 2 : -1], refs[-1]
+    first = 0
+    for keep_ref, got_ref in zip(keeps, gots):
+        columns = keep_ref.shape[1]
+        out_ref[:, first : first + columns] = (
+            keep_ref[...].astype(F32) + got_ref[...].astype(F32)
+        ).astype(BF16)
+        first += columns
+
+
+def sum_kernel(terms_ref, *outs, factor):
+    total = terms_ref[0].astype(F32)
+    for place in range(1, terms_ref.shape[0]):
+        total = total + terms_ref[place].astype(F32)
+    for out_ref in outs:
+        result = (total * factor).astype(BF16)
+        if len(out_ref.shape) == 2:
+            out_ref[...] = result
+        else:
+            for place in range(out_ref.shape[0]):
+                out_ref[place] = result
+
+
+def repeat_kernel(value_ref, out_ref):
+    for place in range(out_ref.shape[0]):
+        out_ref[place] = value_ref[...]
+
+
+def final_kernel(place_ref, own_ref, got_ref, mid_ref, in_ref, out_ref, *, factor):
+    rows = own_ref.shape[0]
+    mids, fields = mid_ref.shape[1], in_ref.shape[1]
+    for ref, half in ((own_ref, place_ref[0, 0]), (got_ref, 1 - place_ref[0, 0])):
+        start = pl.multiple_of(half * rows, rows)
+        mid_ref[pl.ds(start, rows), :] = ref[:, :mids].astype(F32) * factor
+        in_ref[pl.ds(start, rows), :] = ref[:, mids : mids + fields].astype(F32) * factor
+        out_ref[:, pl.ds(start, rows)] = ref[:, mids + fields :].astype(F32).T * factor
+
+
+def other_core(array):
+    count = lax.axis_size("horiz")
+    return lax.ppermute(array, "horiz", [(i, i ^ 1) for i in range(count)])
+
+
+def over_chips(array):
+    count = lax.axis_size("horiz")
+    groups = [list(range(core, count, 2)) for core in range(2)]
+    return lax.all_to_all(array, "horiz", 0, 0, axis_index_groups=groups)
+
+
+def over_members(array):
+    return lax.all_to_all(array, "ens", 0, 0)
+
+
+def sum_over_all(core, keeps, sends, factor, beside):
+    members = lax.axis_size("ens")
+    chips = lax.axis_size("horiz") // 2
+    half = keeps[0].shape[0]
+    columns = sum(keep.shape[1] for keep in keeps)
+    quarter = half // members
+    eighth = quarter // chips
+    size = half * columns
+    gots = [other_core(send) for send in sends]
+    (summed,) = call(
+        core_sum_kernel, [((half, columns), BF16)], flops=size, moved=size * 6
+    )(*keeps, *gots)
+    terms = over_members(summed.reshape(members, quarter, columns))
+    terms, beside = lax.optimization_barrier((terms, beside))
+    if eighth % 16 == 0 and chips <= 8:
+        (summed,) = call(
+            sum_kernel, [((quarter, columns), BF16)], flops=size, moved=size * 2, factor=1.0
+        )(terms)
+        terms = over_chips(summed.reshape(chips, eighth, columns))
+        (repeated,) = call(
+            sum_kernel, [((chips, eighth, columns), BF16)], flops=size, moved=size, factor=factor
+        )(terms)
+        own = over_chips(repeated).reshape(quarter, columns)
+    else:
+        (summed,) = call(sum_kernel, [((quarter, columns), BF16)], factor=1.0)(terms)
+        both = jnp.stack([jnp.where(core == side, summed, 0.0).astype(F32) for side in range(2)])
+        own = (lax.psum(both, "horiz")[core] * factor).astype(BF16)
+    (repeated,) = call(
+        repeat_kernel, [((members, quarter, columns), BF16)], flops=size, moved=size * 2
+    )(own)
+    own = over_members(repeated).reshape(half, columns)
+    return own, other_core(own), beside
+
+
 def to_neighbours(upward, downward, axis):
     count = lax.axis_size(axis)
     forward = [(i, (i + 1) % count) for i in range(count)]
@@ -376,6 +471,8 @@
     diff_rows = diffusivity.reshape(levels * lons, lats)
     mix_rows = mixing.reshape(2 * lons, lats)
     cols, mask = tile_cols[0, 0], pad_mask[0, 0]
+    horiz = lax.axis_index("horiz")
+    place = (horiz % 2).reshape(1, 1)
 
     packed = ((2 * fields + 8, lats), F32)
     up_pack, down_pack = call(pack_kernel, [packed, packed], lons=lons)(prog_rows, mix_rows)
@@ -391,25 +488,28 @@
         lons=lons,
     )(tile_count, diff_rows, cot_rows, cols, mask)
 
-    moved, x_now, act_two, delta_two, grad_mid = call(
+    moved, x_now, act_two, delta_two, keep_mid, send_mid = call(
         forward_kernel,
         [
             ((lons, fields, lats), F32),
             ((fields, slots), BF16),
             ((units, slots), BF16),
             ((units, slots), BF16),
-            ((units, units), BF16),
+            ((units // 2, units), BF16),
+            ((units // 2, units), BF16),
         ],
         scratch=[pltpu.VMEM((units, slots), BF16)],
         flops=2 * 10**9,
         moved=6 * 10**6,
+        smem=(9,),
         lons=lons,
-    )(prog_rows, low_pack, high_pack, mix_rows, cols, adjoint, w_in, w_mid, w_out)
-
-    small, state_rows, grad_field, up_rows, down_rows = call(
+    )(prog_rows, low_pack, high_pack, mix_rows, cols, adjoint, w_in, w_mid, w_out, place)
+
+    keep_small, send_small, state_rows, grad_field, up_rows, down_rows = call(
         backward_kernel,
         [
-            ((units, 2 * fields), BF16),
+            ((units // 2, 2 * fields), BF16),
+            ((units // 2, 2 * fields), BF16),
             ((fields * lons, lats), F32),
             ((lons, fields, lats), F32),
             ((2, fields, lats), F32),
@@ -420,7 +520,7 @@
             pltpu.VMEM((tiles, fields, width), F32),
             pltpu.VMEM((tiles, fields, width), F32),
         ],
-        smem=(0,),
+        smem=(0, 15),
         flops=2 * 10**9,
         moved=6 * 10**6,
         lons=lons,
@@ -440,21 +540,30 @@
         w_in,
         w_mid,
         w_out,
+        place,
     )
     low_rows, high_rows = to_neighbours(up_rows, down_rows, "horiz")
     (grad_rows,) = call(last_kernel, [((fields * lons, lats), F32)], lons=lons)(
         grad_field, low_rows, high_rows, low_pack, high_pack, mix_rows
     )
 
-    sum_mid, sum_small = lax.psum((grad_mid, small), ("ens", "horiz"))
     column_total = lax.axis_size("ens") * lax.axis_size("horiz") * lons * lats
     factor = 1.0 / math.sqrt(column_total)
+    own, got, grad_rows = sum_over_all(
+        place[0, 0], [keep_mid, keep_small], [send_mid, send_small], factor, grad_rows
+    )
+    grad_mid, grad_in, grad_out = call(
+        final_kernel,
+        [((units, units), F32), ((units, fields), F32), ((fields, units), F32)],
+        smem=(0,),
+        factor=1.0,
+    )(place, own, got)
     return (
         state_rows.reshape(prognostic.shape),
         grad_rows.reshape(prognostic.shape),
-        sum_small[:, :fields].astype(F32) * factor,
-        sum_mid.astype(F32) * factor,
-        sum_small[:, fields:].astype(F32).T * factor,
+        grad_in,
+        grad_mid,
+        grad_out,
     )
 
 

time: 183 us -> 93 us (0.51)
  waiting for transfers between devices: 132 us -> 16.1 us
  blocking collectives: 0 us -> 42.7 us
  between operations: 14.8 us -> 1.39 us
  other arithmetic: 6.09 us -> 0 us
  local copies, waits for them, and re-layouts: 10.3 us -> 5.08 us
  starting transfers between devices: 8.23 us -> 12.9 us
  Pallas kernels: 11.1 us -> 14.3 us
    psum x1 -> x0, waiting for transfers between devices: 129 us -> none  [per_device(): sum_mid, sum_small = lax.psum((grad_mid, small), ('ens', 'horiz'))]
    all_to_all x0 -> x3, blocking collectives: none -> 42.7 us  [the longest x2 24.8 us: over_chips(): return lax.all_to_all(array, 'horiz', 0, 0, axis_index_groups=groups)]
    all_to_all x0 -> x1, waiting for transfers between devices: none -> 8.18 us  [over_members(): return lax.all_to_all(array, 'ens', 0, 0)]
    mul x2 -> x0, other arithmetic: 6.09 us -> none  [the longest x1 4.2 us: per_device(): sum_mid.astype(F32) * factor]
    unnamed x30 -> x21, local copies, waits for them, and re-layouts: 10.3 us -> 5.08 us
    ppermute x0 -> x3, waiting for transfers between devices: none -> 4.2 us  [other_core(): return lax.ppermute(array, 'horiz', [(i, i ^ 1) for i in range(count)])]
    all_to_all x0 -> x1, starting transfers between devices: none -> 4.16 us  [over_members(): return lax.all_to_all(array, 'ens', 0, 0)]
    pallas_call x5 -> x10, Pallas kernels: 11.1 us -> 14.3 us  [run(): pl.pallas_call(functools.partial(kernel, **names), out_shape=[jax.ShapeDt...]
  transfers between devices with their start and end apart: 5 -> 8, of which waited for: 2 -> 4; matrix products, arithmetic and copies ran while one was open for 0% -> 1% of each run, Pallas kernels for 1% -> 7%
where the time goes in v3:
time: 93 us; the launch traced here: 92.5 us
  blocking collectives  42.7 us (46%)
  waiting for transfers between devices  16.1 us (17%)
  Pallas kernels  14.3 us (15%)
  starting transfers between devices  12.9 us (14%)
  local copies, waits for them, and re-layouts  5.08 us (5%)
  between operations  1.39 us (1%)
    all_to_all x2, blocking collectives, over_chips(): return lax.all_to_all(array, 'horiz', 0, 0, axis_index_groups=groups)  24.8 us
    all_to_all x1, blocking collectives, over_members(): return lax.all_to_all(array, 'ens', 0, 0)  17.9 us
    pallas_call x10, Pallas kernels, run(): pl.pallas_call(functools.partial(kernel, **names), out_shape=[jax.ShapeDt...  14.3 us
    all_to_all x1, waiting for transfers between devices, over_members(): return lax.all_to_all(array, 'ens', 0, 0)  8.18 us
    ppermute x2, starting transfers between devices, to_neighbours(): lax.ppermute(downward, axis, backward)  7.57 us
    unnamed x21, local copies, waits for them, and re-layouts  5.08 us
    ppermute x3, waiting for transfers between devices, other_core(): return lax.ppermute(array, 'horiz', [(i, i ^ 1) for i in range(count)])  4.2 us
    all_to_all x1, starting transfers between devices, over_members(): return lax.all_to_all(array, 'ens', 0, 0)  4.16 us
  transfers between devices with their start and end apart: 8, of which 4 were waited for; matrix products, arithmetic and copies ran while one was open for 1% of the time, Pallas kernels for 7%

profile of v3, /device:TPU:0, one launch (start us, length us, event | category | flops | bytes accessed | tf_op | source)
XLA Modules:
  0.0 92.5 jit_solution(9199318512031643424)
XLA Ops:
  0.6 0.0 copy-start
  0.6 0.9 %copy-done = f32[1,128,4,128]{3,2,1,0:T(4,128)S(1)} copy-done((f32[1,128,4,128]{3,2,1,0:T(4,128)S(1)}, f32[1,128,4,128]{3,2,1,0:T(4,128)}, u32[]{:S(2)}) %copy-start) | copy-done | bytes 262168
  1.6 0.7 copy-done.2
  2.3 0.5 collective-permute-start
  2.8 4.1 %collective-permute-start.1 = (f32[264,128]{1,0:T(8,128)S(1)}, f32[264,128]{1,0:T(8,128)S(1)}, u32[]{:S(2)}, u32[]{:S(2)}) collective-permute-start(f32[264,128]{1,0:T(8,128)S(1)} %get-tuple-element.29), channel_id=1, source_target_pairs={{1,0},{2,1},{3,2},{4,3},{5,4},{6,5},{7,6},{0,7},{9,8},{10,9},{11,1... | collective-permute-start | bytes 405512 | tf_op jit(solution)/shard_map/ppermute | solution.py:458
  6.9 0.7 copy_bitcast_fusion
  8.3 0.9 %copy-done.5 = f32[1,128,4,128]{3,2,1,0:T(4,128)S(1)} copy-done((f32[1,128,4,128]{3,2,1,0:T(4,128)S(1)}, f32[1,128,4,128]{3,2,1,0:T(4,128)}, u32[]{:S(2)}) %copy-start.5) | copy-done | bytes 262168
  9.2 0.8 copy-done.9
  10.1 0.8 shard_map.138
  10.9 0.1 copy-done.1
  11.0 0.8 copy-done.4
  11.8 0.0 copy-done.8
  11.8 3.9 %shard_map.139 = (f32[4,128,128]{2,1,0:T(8,128)S(1)}, bf16[128,384]{1,0:T(8,128)(2,1)S(1)}, bf16[1024,384]{1,0:T(8,128)(2,1)S(1)}, bf16[1024,384]{1,0:T(8,128)(2...) custom-call(f32[512,128]{1,0:T(8,128)S(1)} %bitcast.20, ...), custom_call_target="tpu_custom_call" | custom-call | flops 2000000000 | bytes 6000000 | tf_op jit(solution)/shard_map/pallas_call | solution.py:26
  15.7 0.1 collective-permute-start.2
  15.8 4.1 %shard_map.140 = (bf16[512,256]{1,0:T(8,128)(2,1)S(1)}, bf16[512,256]{1,0:T(8,128)(2,1)S(1)}, f32[512,128]{1,0:T(8,128)}, f32[4,128,128]{2,1,0:T(8,128)S(1)}, f3...) custom-call(s32[1,1]{1,0:T(1,128)S(6)} %copy.19.count_ref, f32[4,128,128]{2,1,0:T(8,128)S(1)} %get-tuple-element.31.moved_ref, ...), custom_call_target="tpu_custom_call" | custom-call | flops 2000000000 | bytes 6000000 | tf_op jit(solution)/shard_map/pallas_call | solution.py:26
  19.9 0.5 collective-permute-start.3
  20.3 1.2 %collective-permute-done.3.refs_3_ = bf16[512,256]{1,0:T(8,128)(2,1)S(1)} collective-permute-done((bf16[512,256]{1,0:T(8,128)(2,1)S(1)}, bf16[512,256]{1,0:T(8,128)(2,1)S(1)}, u32[]{:S(2)}, u32[]{:S(2)}) %collective-permute-start.3) | collective-permute-done | bytes 262176 | tf_op jit(solution)/shard_map/ppermute | solution.py:407
  21.5 1.4 %shard_map.141 = bf16[512,1280]{1,0:T(8,128)(2,1)} custom-call(bf16[512,1024]{1,0:T(8,128)(2,1)S(1)} %get-tuple-element.39.refs_0_, bf16[512,256]{1,0:T(8,128)(2,1)S(1)} %get-tuple-element.40.refs_1_, bf16[512,1024]{1,0:T(8,128)(2,1)S(1)} %collective-permute-done.2.refs_2_, bf16[512,256]{1,0:T(8,128)(2,1)S(1)} %collective-permute-done.3.refs_3_), custom_call_target="tpu_custom_call" | custom-call | flops 655360 | bytes 3932160 | tf_op jit(solution)/shard_map/pallas_call | solution.py:26
  22.9 4.2 %all-to-all-start = ((bf16[4,128,1280]{2,1,0:T(8,128)(2,1)}), bf16[4,128,1280]{2,1,0:T(8,128)(2,1)S(1)}, u32[]{:S(2)}, u32[]{:S(2)}) async-start(bf16[4,128,1280]{2,1,0:T(8,128)(2,1)} %bitcast.6), calls=%async_computation | async-start | bytes 2621440 | tf_op jit(solution)/shard_map/all_to_all | solution.py:417
  27.0 0.1 collective-permute-start.4
  27.1 3.5 %collective-permute-start.5 = (f32[2,128,128]{2,1,0:T(8,128)S(1)}, f32[2,128,128]{2,1,0:T(8,128)S(1)}, u32[]{:S(2)}, u32[]{:S(2)}) collective-permute-start(f32[2,128,128]{2,1,0:T(8,128)S(1)} %get-tuple-element.45), channel_id=1, source_target_pairs={{1,0},{2,1},{3,2},{4,3},{5,4},{6,5},{7,6},{0,7},{9,8},{10,9},{11,1... | collective-permute-start | bytes 393224 | tf_op jit(solution)/shard_map/ppermute | solution.py:458
  30.6 3.7 %collective-permute-done.4.low_ref = f32[2,128,128]{2,1,0:T(8,128)S(1)} collective-permute-done((f32[2,128,128]{2,1,0:T(8,128)S(1)}, f32[2,128,128]{2,1,0:T(8,128)S(1)}, u32[]{:S(2)}, u32[]{:S(2)}) %collective-permute-start.4) | collective-permute-done | bytes 131104 | tf_op jit(solution)/shard_map/ppermute | solution.py:458
  34.3 1.5 %shard_map.142 = f32[512,128]{1,0:T(8,128)} custom-call(f32[4,128,128]{2,1,0:T(8,128)S(1)} %get-tuple-element.43.field_ref, f32[2,128,128]{2,1,0:T(8,128)S(1)} %collective-permute-done.4.low_ref, f32[2,128,128]{2,1,0:T(8,128)S(1)} %collective-permute-done.5.high_ref, f32[264,128]{1,0:T(8,128)S(1)} %collective-permute-done.low_ref.low_mix_ref, ...), custom_call_target="tpu_custom_call" | custom-call | tf_op jit(solution)/shard_map/pallas_call | solution.py:26
  35.8 8.2 %all-to-all-done.terms_ref = bf16[4,128,1280]{2,1,0:T(8,128)(2,1)S(1)} async-done(((bf16[4,128,1280]{2,1,0:T(8,128)(2,1)}), bf16[4,128,1280]{2,1,0:T(8,128)(2,1)S(1)}, u32[]{:S(2)}, u32[]{:S(2)}) %all-to-all-start) | async-done | bytes 1310752 | tf_op jit(solution)/shard_map/all_to_all | solution.py:417
  44.0 0.2 shard_map.143
  44.2 12.7 %all_to_all.20.terms_ref = bf16[4,32,1280]{2,1,0:T(8,128)(2,1)S(1)} all-to-all(bf16[4,32,1280]{2,1,0:T(8,128)(2,1)S(1)} %bitcast.17), channel_id=1, replica_groups={{0,2,4,6},{1,3,5,7},{8,10,12,14},{9,11,13,15},{16,18,20,22},{17,19,21,2..., dimensions={0} | all-to-all | bytes 655360 | tf_op jit(solution)/shard_map/all_to_all | solution.py:413
  56.9 0.1 shard_map.144
  56.9 12.1 %all_to_all.21 = bf16[4,32,1280]{2,1,0:T(8,128)(2,1)S(1)} all-to-all(bf16[4,32,1280]{2,1,0:T(8,128)(2,1)S(1)} %shard_map.144), channel_id=1, replica_groups={{0,2,4,6},{1,3,5,7},{8,10,12,14},{9,11,13,15},{16,18,20,22},{17,19,21,2..., dimensions={0} | all-to-all | bytes 655360 | tf_op jit(solution)/shard_map/all_to_all | solution.py:413
  69.0 0.1 shard_map.145
  69.1 17.9 %all_to_all.22 = bf16[4,128,1280]{2,1,0:T(8,128)(2,1)S(1)} all-to-all(bf16[4,128,1280]{2,1,0:T(8,128)(2,1)S(1)} %shard_map.145), channel_id=1, replica_groups=mesh['ens'=4,'horiz'=8] {'ens'}, dimensions={0} | all-to-all | bytes 2621440 | tf_op jit(solution)/shard_map/all_to_all | solution.py:417
  87.0 3.0 %collective-permute-done.6.got_ref = bf16[512,1280]{1,0:T(8,128)(2,1)S(1)} collective-permute-done((bf16[512,1280]{1,0:T(8,128)(2,1)S(1)}, bf16[512,1280]{1,0:T(8,128)(2,1)S(1)}, u32[]{:S(2)}, u32[]{:S(2)}) %collective-permute-start.6) | collective-permute-done | bytes 1310752 | tf_op jit(solution)/shard_map/ppermute | solution.py:407
  90.0 2.5 %shard_map.146 = (f32[1024,1024]{1,0:T(8,128)}, f32[1024,128]{1,0:T(8,128)}, f32[128,1024]{1,0:T(8,128)}) custom-call(s32[1,1]{1,0:T(1,128)} %bitcast.4.place_ref, bf16[512,1280]{1,0:T(8,128)(2,1)S(1)} %bitcast.16, bf16[512,1280]{1,0:T(8,128)(2,1)S(1)} %collective-permute-done.6.got_ref), custom_call_target="tpu_custom_call" | custom-call | tf_op jit(solution)/shard_map/pallas_call | solution.py:26
  (18 shorter events, 0.1 us)
Async XLA Ops:
  0.6 1.0 %copy-start = (f32[1,128,4,128]{3,2,1,0:T(4,128)S(1)}, f32[1,128,4,128]{3,2,1,0:T(4,128)}, u32[]{:S(2)}) copy-start(f32[1,128,4,128]{3,2,1,0:T(4,128)} %param.10) | copy-start | bytes 786436
  1.6 0.7 copy-start.2
  2.3 8.5 %collective-permute-start = (f32[264,128]{1,0:T(8,128)S(1)}, f32[264,128]{1,0:T(8,128)S(1)}, u32[]{:S(2)}, u32[]{:S(2)}) collective-permute-start(f32[264,128]{1,0:T(8,128)S(1)} %get-tuple-element.28), channel_id=1, source_target_pairs={{0,1},{1,2},{2,3},{3,4},{4,5},{5,6},{6,7},{7,0},{8,9},{9,10},{10,1... | collective-permute-start | bytes 405512 | tf_op jit(solution)/shard_map/ppermute | solution.py:458
  2.8 8.0 %collective-permute-start.1 = (f32[264,128]{1,0:T(8,128)S(1)}, f32[264,128]{1,0:T(8,128)S(1)}, u32[]{:S(2)}, u32[]{:S(2)}) collective-permute-start(f32[264,128]{1,0:T(8,128)S(1)} %get-tuple-element.29), channel_id=1, source_target_pairs={{1,0},{2,1},{3,2},{4,3},{5,4},{6,5},{7,6},{0,7},{9,8},{10,9},{11,1... | collective-permute-start | bytes 405512 | tf_op jit(solution)/shard_map/ppermute | solution.py:458
  8.3 1.0 %copy-start.5 = (f32[1,128,4,128]{3,2,1,0:T(4,128)S(1)}, f32[1,128,4,128]{3,2,1,0:T(4,128)}, u32[]{:S(2)}) copy-start(f32[1,128,4,128]{3,2,1,0:T(4,128)} %param.13) | copy-start | bytes 786436
  9.2 0.8 copy-start.9
  10.1 0.9 %copy-start.1 = (f32[1,128,4,128]{3,2,1,0:T(4,128)S(1)}, f32[1,128,4,128]{3,2,1,0:T(4,128)}, u32[]{:S(2)}) copy-start(f32[1,128,4,128]{3,2,1,0:T(4,128)} %param.10) | copy-start | bytes 786436
  10.1 1.0 %copy-start.3 = (f32[2,4,128]{2,1,0:T(4,128)S(1)}, f32[2,4,128]{2,1,0:T(4,128)}, u32[]{:S(2)}) copy-start(f32[2,4,128]{2,1,0:T(4,128)} %param.12) | copy-start | bytes 12292
  10.1 1.7 %copy-start.4 = (bf16[1024,1024]{1,0:T(8,128)(2,1)S(1)}, bf16[1024,1024]{1,0:T(8,128)(2,1)}, u32[]{:S(2)}) copy-start(bf16[1024,1024]{1,0:T(8,128)(2,1)} %w_mid_ref.3) | copy-start | bytes 6291460
  10.1 1.7 %copy-start.7 = (bf16[1024,128]{1,0:T(8,128)(2,1)S(1)}, bf16[1024,128]{1,0:T(8,128)(2,1)}, u32[]{:S(2)}) copy-start(bf16[1024,128]{1,0:T(8,128)(2,1)} %w_in_ref.3) | copy-start | bytes 786436
  10.1 1.7 %copy-start.8 = (bf16[128,1024]{1,0:T(8,128)(2,1)S(1)}, bf16[128,1024]{1,0:T(8,128)(2,1)}, u32[]{:S(2)}) copy-start(bf16[128,1024]{1,0:T(8,128)(2,1)} %w_out_ref.3) | copy-start | bytes 786436
  11.8 4.0 %copy-start.6 = (f32[1,128,4,128]{3,2,1,0:T(4,128)S(1)}, f32[1,128,4,128]{3,2,1,0:T(4,128)}, u32[]{:S(2)}) copy-start(f32[1,128,4,128]{3,2,1,0:T(4,128)} %param.13) | copy-start | bytes 786436
  15.7 5.8 %collective-permute-start.2 = (bf16[512,1024]{1,0:T(8,128)(2,1)S(1)}, bf16[512,1024]{1,0:T(8,128)(2,1)S(1)}, u32[]{:S(2)}, u32[]{:S(2)}) collective-permute-start(bf16[512,1024]{1,0:T(8,128)(2,1)S(1)} %get-tuple-element.41), channel_id=1, source_target_pairs={{0,1},{1,0},{2,3},{3,2},{4,5},{5,4},{6,7},{7,6},{8,9},{9,8},{10,11... | collective-permute-start | bytes 3145736 | tf_op jit(solution)/shard_map/ppermute | solution.py:407
  19.9 1.6 %collective-permute-start.3 = (bf16[512,256]{1,0:T(8,128)(2,1)S(1)}, bf16[512,256]{1,0:T(8,128)(2,1)S(1)}, u32[]{:S(2)}, u32[]{:S(2)}) collective-permute-start(bf16[512,256]{1,0:T(8,128)(2,1)S(1)} %get-tuple-element.42), channel_id=1, source_target_pairs={{0,1},{1,0},{2,3},{3,2},{4,5},{5,4},{6,7},{7,6},{8,9},{9,8},{10,11... | collective-permute-start | bytes 786440 | tf_op jit(solution)/shard_map/ppermute | solution.py:407
  22.9 21.1 %all-to-all-start = ((bf16[4,128,1280]{2,1,0:T(8,128)(2,1)}), bf16[4,128,1280]{2,1,0:T(8,128)(2,1)S(1)}, u32[]{:S(2)}, u32[]{:S(2)}) async-start(bf16[4,128,1280]{2,1,0:T(8,128)(2,1)} %bitcast.6), calls=%async_computation | async-start | bytes 2621440 | tf_op jit(solution)/shard_map/all_to_all | solution.py:417
  27.0 7.3 %collective-permute-start.4 = (f32[2,128,128]{2,1,0:T(8,128)S(1)}, f32[2,128,128]{2,1,0:T(8,128)S(1)}, u32[]{:S(2)}, u32[]{:S(2)}) collective-permute-start(f32[2,128,128]{2,1,0:T(8,128)S(1)} %get-tuple-element.44), channel_id=1, source_target_pairs={{0,1},{1,2},{2,3},{3,4},{4,5},{5,6},{6,7},{7,0},{8,9},{9,10},{10,1... | collective-permute-start | bytes 393224 | tf_op jit(solution)/shard_map/ppermute | solution.py:458
  27.1 7.2 %collective-permute-start.5 = (f32[2,128,128]{2,1,0:T(8,128)S(1)}, f32[2,128,128]{2,1,0:T(8,128)S(1)}, u32[]{:S(2)}, u32[]{:S(2)}) collective-permute-start(f32[2,128,128]{2,1,0:T(8,128)S(1)} %get-tuple-element.45), channel_id=1, source_target_pairs={{1,0},{2,1},{3,2},{4,3},{5,4},{6,5},{7,6},{0,7},{9,8},{10,9},{11,1... | collective-permute-start | bytes 393224 | tf_op jit(solution)/shard_map/ppermute | solution.py:458
  87.0 3.0 %collective-permute-start.6 = (bf16[512,1280]{1,0:T(8,128)(2,1)S(1)}, bf16[512,1280]{1,0:T(8,128)(2,1)S(1)}, u32[]{:S(2)}, u32[]{:S(2)}) collective-permute-start(bf16[512,1280]{1,0:T(8,128)(2,1)S(1)} %bitcast.15), channel_id=1, source_target_pairs={{0,1},{1,0},{2,3},{3,2},{4,5},{5,4},{6,7},{7,6},{8,9},{9,8},{10,11... | collective-permute-start | bytes 3932168 | tf_op jit(solution)/shard_map/ppermute | solution.py:407

commit v4 on v2

--- a/solution.py
+++ b/solution.py
@@ -10,7 +10,8 @@
 
 DYN_STEPS = 2
 BLOCK = 256
-VMEM_LIMIT = 40 * 1024 * 1024
+PACK_ROWS = 16
+VMEM_LIMIT = 32 * 1024 * 1024
 F32 = jnp.float32
 BF16 = jnp.bfloat16
 CONTRACT_LAST = (((1,), (1,)), ((), ()))
@@ -75,10 +76,18 @@
         for side in range(2):
             out_ref[side * fields : (side + 1) * fields, :] = prog_ref[
                 pl.ds(first + side, fields, stride=lons), :
-            ]
-        out_ref[2 * fields : 2 * fields + 2, :] = mix_ref[first : first + 2, :]
-        out_ref[2 * fields + 2 : 2 * fields + 4, :] = mix_ref[lons + first : lons + first + 2, :]
-        out_ref[2 * fields + 4 :, :] = jnp.zeros_like(out_ref[2 * fields + 4 :, :])
+            ].astype(BF16)
+        mix_rows = [mix_ref[first : first + 2, :], mix_ref[lons + first : lons + first + 2, :]]
+        mix_rows.append(jnp.zeros((PACK_ROWS - 4, mix_ref.shape[1]), F32))
+        out_ref[2 * fields :, :] = jnp.concatenate(mix_rows, axis=0).astype(BF16)
+
+
+def halo_rows(pack_ref, fields):
+    return [pack_ref[side * fields : (side + 1) * fields, :].astype(F32) for side in range(2)]
+
+
+def halo_mixing(pack_ref, fields):
+    return pack_ref[2 * fields :, :].astype(F32)
 
 
 def one_hot(cols_ref, cells):
@@ -191,7 +200,21 @@
     return 0.5 * jnp.tanh(0.5 * pre_act) + 0.5
 
 
+def weight_product(left_ref, right, place_ref, keep_ref, send_ref, first, transposed=CONTRACT_LAST):
+    half = left_ref.shape[0] // 2
+    block = min(BLOCK, half)
+    for out_ref, side in ((send_ref, 1 - place_ref[0, 0]), (keep_ref, place_ref[0, 0])):
+        for start in range(0, half, block):
+            out_ref[start : start + block, first : first + right.shape[0]] = lax.dot_general(
+                left_ref[pl.ds(pl.multiple_of(side * half + start, block), block), :],
+                right,
+                transposed,
+                preferred_element_type=F32,
+            ).astype(BF16)
+
+
 def forward_kernel(
+    place_ref,
     prog_ref,
     low_ref,
     high_ref,
@@ -201,30 +224,25 @@
     w_in_ref,
     w_mid_ref,
     w_out_ref,
-    place_ref,
     moved_ref,
     x_ref,
+    act_one_ref,
     act_two_ref,
     delta_two_ref,
     keep_ref,
     send_ref,
-    act_one_ref,
     *,
     lons,
 ):
     fields = prog_ref.shape[0] // lons
     units = w_mid_ref.shape[0]
     cells = lons * prog_ref.shape[1]
+    low_rows, high_rows = halo_rows(low_ref, fields), halo_rows(high_ref, fields)
     lon_coef, lat_coef = coefficients(
-        mix_ref,
-        low_ref[2 * fields : 2 * fields + 4, :],
-        high_ref[2 * fields : 2 * fields + 4, :],
-        lons,
-    )
-    rows = [low_ref[side * fields : (side + 1) * fields, :] for side in range(2)]
-    rows += [prog_ref[pl.ds(lon, fields, stride=lons), :] for lon in range(lons)]
-    rows += [high_ref[side * fields : (side + 1) * fields, :] for side in range(2)]
-    rows = two_steps(rows, lon_coef, lat_coef)
+        mix_ref, halo_mixing(low_ref, fields), halo_mixing(high_ref, fields), lons
+    )
+    rows = [prog_ref[pl.ds(lon, fields, stride=lons), :] for lon in range(lons)]
+    rows = two_steps(low_rows + rows + high_rows, lon_coef, lat_coef)
     for lon in range(lons):
         moved_ref[lon] = rows[lon]
     spread = one_hot(cols_ref, cells)
@@ -249,51 +267,28 @@
         )
         slope = sigma_val * (1.0 + pre_two * (1.0 - sigma_val))
         delta_two_ref[start : start + BLOCK, :] = (back_two * slope).astype(BF16)
-    for out_ref, half in ((send_ref, 1 - place_ref[0, 0]), (keep_ref, place_ref[0, 0])):
-        for start in range(0, units // 2, BLOCK):
-            out_ref[start : start + BLOCK, :] = lax.dot_general(
-                delta_two_ref[pl.ds(half * (units // 2) + start, BLOCK), :],
-                act_one_ref[...],
-                CONTRACT_LAST,
-                preferred_element_type=F32,
-            ).astype(BF16)
+    weight_product(
+        delta_two_ref, act_one_ref[: keep_ref.shape[1], :], place_ref, keep_ref, send_ref, 0
+    )
 
 
 def backward_kernel(
-    count_ref,
-    moved_ref,
-    cot_ref,
-    cols_ref,
-    mask_ref,
+    place_ref,
     x_ref,
+    act_one_ref,
     act_two_ref,
     delta_two_ref,
     adj_ref,
-    coef_ref,
-    ratio_ref,
-    inverse_ref,
     w_in_ref,
     w_mid_ref,
-    w_out_ref,
-    place_ref,
+    delta_one_ref,
     keep_ref,
     send_ref,
-    state_ref,
-    field_ref,
-    up_ref,
-    down_ref,
-    delta_one_ref,
-    forced_ref,
-    solved_ref,
-    *,
-    lons,
 ):
     fields = x_ref.shape[0]
     units = w_mid_ref.shape[0]
-    levels = coef_ref.shape[0]
-    lats = moved_ref.shape[2]
+    done = units + 2 * fields - keep_ref.shape[1]
     x_now = x_ref[...]
-    adj_now = join_tiles(adj_ref)
     for start in range(0, units, BLOCK):
         back_one = lax.dot_general(
             w_mid_ref[:, start : start + BLOCK],
@@ -305,21 +300,45 @@
         sigma_val = sigmoid(pre_one)
         slope = sigma_val * (1.0 + pre_one * (1.0 - sigma_val))
         delta_one_ref[start : start + BLOCK, :] = (back_one * slope).astype(BF16)
-    adj_half = adj_now.astype(BF16)
-    for out_ref, half in ((send_ref, 1 - place_ref[0, 0]), (keep_ref, place_ref[0, 0])):
-        here = pl.ds(half * (units // 2), units // 2)
-        out_ref[:, :fields] = lax.dot_general(
-            delta_one_ref[here, :], x_now, CONTRACT_LAST, preferred_element_type=F32
-        ).astype(BF16)
-        out_ref[:, fields:] = lax.dot_general(
-            act_two_ref[here, :], adj_half, CONTRACT_LAST, preferred_element_type=F32
-        ).astype(BF16)
-    grad_x = adj_now + lax.dot_general(
+    weight_product(delta_two_ref, act_one_ref[done:, :], place_ref, keep_ref, send_ref, 0)
+    weight_product(delta_one_ref, x_now, place_ref, keep_ref, send_ref, units - done)
+    adj_half = join_tiles(adj_ref).astype(BF16)
+    weight_product(act_two_ref, adj_half, place_ref, keep_ref, send_ref, units - done + fields)
+
+
+def place_kernel(
+    count_ref,
+    moved_ref,
+    cot_ref,
+    cols_ref,
+    mask_ref,
+    x_ref,
+    act_two_ref,
+    delta_one_ref,
+    adj_ref,
+    coef_ref,
+    ratio_ref,
+    inverse_ref,
+    w_in_ref,
+    w_out_ref,
+    state_ref,
+    field_ref,
+    up_ref,
+    down_ref,
+    forced_ref,
+    solved_ref,
+    *,
+    lons,
+):
+    fields = x_ref.shape[0]
+    levels = coef_ref.shape[0]
+    lats = moved_ref.shape[2]
+    tendency = jnp.dot(w_out_ref[...], act_two_ref[...], preferred_element_type=F32)
+    split_tiles(forced_ref, x_ref[...].astype(F32) + tendency)
+    solve(levels, fields // levels, coef_ref, ratio_ref, inverse_ref, forced_ref, solved_ref)
+    grad_x = join_tiles(adj_ref) + lax.dot_general(
         w_in_ref[...], delta_one_ref[...], CONTRACT_FIRST, preferred_element_type=F32
     )
-    tendency = jnp.dot(w_out_ref[...], act_two_ref[...], preferred_element_type=F32)
-    split_tiles(forced_ref, x_now.astype(F32) + tendency)
-    solve(levels, fields // levels, coef_ref, ratio_ref, inverse_ref, forced_ref, solved_ref)
     live = live_row(count_ref, mask_ref)
     fresh = jnp.concatenate(
         [
@@ -342,52 +361,40 @@
         )
         field_ref[lon] = field_now
         if lon < 2:
-            down_ref[lon] = field_now
+            down_ref[lon * fields : (lon + 1) * fields, :] = field_now.astype(BF16)
         if lon >= lons - 2:
-            up_ref[lon - (lons - 2)] = field_now
+            side = lon - (lons - 2)
+            up_ref[side * fields : (side + 1) * fields, :] = field_now.astype(BF16)
 
 
 def last_kernel(field_ref, low_ref, high_ref, low_mix_ref, high_mix_ref, mix_ref, out_ref, *, lons):
     fields = field_ref.shape[1]
+    low_rows, high_rows = halo_rows(low_ref, fields), halo_rows(high_ref, fields)
     lon_coef, lat_coef = coefficients(
-        mix_ref,
-        low_mix_ref[2 * fields : 2 * fields + 4, :],
-        high_mix_ref[2 * fields : 2 * fields + 4, :],
-        lons,
-    )
-    rows = [low_ref[0], low_ref[1]]
-    rows += [field_ref[lon] for lon in range(lons)]
-    rows += [high_ref[0], high_ref[1]]
-    rows = two_steps(rows, lon_coef, lat_coef)
+        mix_ref, halo_mixing(low_mix_ref, fields), halo_mixing(high_mix_ref, fields), lons
+    )
+    rows = [field_ref[lon] for lon in range(lons)]
+    rows = two_steps(low_rows + rows + high_rows, lon_coef, lat_coef)
     for lon in range(lons):
         out_ref[pl.ds(lon, fields, stride=lons), :] = rows[lon]
 
 
-def core_sum_kernel(place_ref, *refs, parts):
-    keeps, gots, outs = refs[: len(refs[:-parts]) // 2], refs[len(refs[:-parts]) // 2 : -parts], refs[-parts:]
+def core_sum_kernel(place_ref, keep_ref, got_ref, *outs):
     rows = outs[0].shape[0]
-    for k in range(parts):
-        start = pl.multiple_of((place_ref[0, 1] ^ k) * rows, rows)
-        first = 0
-        for keep_ref, got_ref in zip(keeps, gots):
-            here = pl.ds(start, rows)
-            columns = keep_ref.shape[1]
-            outs[k][:, first : first + columns] = (
-                keep_ref[here, :].astype(F32) + got_ref[here, :].astype(F32)
-            ).astype(BF16)
-            first += columns
-
-
-def chip_sum_kernel(place_ref, *refs, terms, parts, which, factor):
+    for k, out_ref in enumerate(outs):
+        here = pl.ds(pl.multiple_of((place_ref[0, 1] ^ k) * rows, rows), rows)
+        out_ref[...] = (keep_ref[here, :].astype(F32) + got_ref[here, :].astype(F32)).astype(BF16)
+
+
+def sum_kernel(place_ref, *refs, terms, which, factor):
     ins, outs = refs[:terms], refs[terms:]
     rows = outs[0].shape[0]
-    for k in range(parts):
-        start = pl.multiple_of((place_ref[0, which] ^ k) * rows, rows) if parts > 1 else 0
-        total = None
-        for ref in ins:
-            term = ref[pl.ds(start, rows), :].astype(F32)
-            total = term if total is None else total + term
-        outs[k][...] = (total * factor).astype(BF16)
+    for k, out_ref in enumerate(outs):
+        start = pl.multiple_of((place_ref[0, which] ^ k) * rows, rows) if len(outs) > 1 else 0
+        total = ins[0][pl.ds(start, rows), :].astype(F32)
+        for ref in ins[1:]:
+            total = total + ref[pl.ds(start, rows), :].astype(F32)
+        out_ref[...] = (total * factor).astype(BF16)
 
 
 def join_kernel(place_ref, *refs, which):
@@ -397,14 +404,19 @@
         out_ref[pl.ds(pl.multiple_of((place_ref[0, which] ^ k) * rows, rows), rows), :] = ref[...]
 
 
-def final_kernel(place_ref, own_ref, got_ref, mid_ref, in_ref, out_ref, *, factor):
-    rows = own_ref.shape[0]
-    mids, fields = mid_ref.shape[1], in_ref.shape[1]
-    for ref, half in ((own_ref, place_ref[0, 0]), (got_ref, 1 - place_ref[0, 0])):
-        start = pl.multiple_of(half * rows, rows)
-        mid_ref[pl.ds(start, rows), :] = ref[:, :mids].astype(F32) * factor
-        in_ref[pl.ds(start, rows), :] = ref[:, mids : mids + fields].astype(F32) * factor
-        out_ref[:, pl.ds(start, rows)] = ref[:, mids + fields :].astype(F32).T * factor
+def final_kernel(place_ref, own_one, got_one, own_two, got_two, mid_ref, in_ref, out_ref):
+    rows, first = own_one.shape
+    fields = in_ref.shape[1]
+    rest = mid_ref.shape[1] - first
+    for one_ref, two_ref, half in (
+        (own_one, own_two, place_ref[0, 0]),
+        (got_one, got_two, 1 - place_ref[0, 0]),
+    ):
+        here = pl.ds(pl.multiple_of(half * rows, rows), rows)
+        mid_ref[here, :first] = one_ref[...].astype(F32)
+        mid_ref[here, first:] = two_ref[:, :rest].astype(F32)
+        in_ref[here, :] = two_ref[:, rest : rest + fields].astype(F32)
+        out_ref[:, here] = two_ref[:, rest + fields :].astype(F32).T
 
 
 def exchange(arrays, axis, stride):
@@ -415,58 +427,55 @@
     ]
 
 
-def sum_over_all(place, keeps, sends, factor):
+def sum_over_all(place, keep, send, factor, beside=None):
     members = lax.axis_size("ens")
     chips = lax.axis_size("horiz") // 2
-    half = keeps[0].shape[0]
-    columns = sum(keep.shape[1] for keep in keeps)
+    half, columns = keep.shape
     quarter = half // members
     eighth = quarter // chips
-    size = quarter * columns
-    gots = [exchange([send], "horiz", 1)[0] for send in sends]
+    size = half * columns
+    (got,) = exchange([send], "horiz", 1)
     parts = call(
         core_sum_kernel,
         [((quarter, columns), BF16)] * members,
         smem=(0,),
-        flops=size * members,
-        moved=size * members * 6,
-        parts=members,
-    )(place, *keeps, *gots)
+        flops=size,
+        moved=size * 6,
+    )(place, keep, got)
     terms = [parts[0]] + exchange(parts[1:], "ens", 1)
+    if beside is not None:
+        terms, beside = lax.optimization_barrier((terms, beside))
     if eighth % 16 == 0 and chips <= 8:
         parts = call(
-            chip_sum_kernel,
+            sum_kernel,
             [((eighth, columns), BF16)] * chips,
             smem=(0,),
-            flops=size * members,
-            moved=size * members * 2,
+            flops=size,
+            moved=size * 2,
             terms=members,
-            parts=chips,
             which=2,
             factor=1.0,
         )(place, *terms)
         terms = [parts[0]] + exchange(parts[1:], "horiz", 2)
         (own,) = call(
-            chip_sum_kernel,
+            sum_kernel,
             [((eighth, columns), BF16)],
             smem=(0,),
             flops=size,
-            moved=size * 2,
+            moved=size,
             terms=chips,
-            parts=1,
             which=2,
             factor=factor,
         )(place, *terms)
         (own,) = call(
-            join_kernel, [((quarter, columns), BF16)], smem=(0,), moved=size * 4, which=2
+            join_kernel, [((quarter, columns), BF16)], smem=(0,), moved=size, which=2
         )(place, own, *exchange([own] * (chips - 1), "horiz", 2))
     else:
         (own,) = call(
-            chip_sum_kernel,
+            sum_kernel,
             [((quarter, columns), BF16)],
             smem=(0,),
             terms=members,
-            parts=1,
             which=2,
             factor=1.0,
         )(place, *terms)
@@ -474,9 +483,9 @@
         both = jnp.stack([jnp.where(core == side, own, 0.0).astype(F32) for side in range(2)])
         own = (lax.psum(both, "horiz")[core] * factor).astype(BF16)
     (own,) = call(
-        join_kernel, [((half, columns), BF16)], smem=(0,), moved=size * 16, which=1
+        join_kernel, [((half, columns), BF16)], smem=(0,), moved=size * 4, which=1
     )(place, own, *exchange([own] * (members - 1), "ens", 1))
-    return own, exchange([own], "horiz", 1)[0]
+    return own, exchange([own], "horiz", 1)[0], beside
 
 
 def to_neighbours(upward, downward, axis):
@@ -502,7 +511,7 @@
     horiz = lax.axis_index("horiz")
     place = jnp.stack([horiz % 2, lax.axis_index("ens"), horiz // 2]).reshape(1, 3)
 
-    packed = ((2 * fields + 8, lats), F32)
+    packed = ((2 * fields + PACK_ROWS, lats), BF16)
     up_pack, down_pack = call(pack_kernel, [packed, packed], lons=lons)(prog_rows, mix_rows)
     low_pack, high_pack = to_neighbours(up_pack, down_pack, "horiz")
 
@@ -516,41 +525,43 @@
         lons=lons,
     )(tile_count, diff_rows, cot_rows, cols, mask)
 
-    moved, x_now, act_two, delta_two, keep_mid, send_mid = call(
+    hidden = ((units, slots), BF16)
+    first = (units + 2 * fields) // 2
+    chunk = ((units // 2, first), BF16)
+    moved, x_now, act_one, act_two, delta_two, keep, send = call(
         forward_kernel,
-        [
-            ((lons, fields, lats), F32),
-            ((fields, slots), BF16),
-            ((units, slots), BF16),
-            ((units, slots), BF16),
-            ((units // 2, units), BF16),
-            ((units // 2, units), BF16),
-        ],
-        scratch=[pltpu.VMEM((units, slots), BF16)],
+        [((lons, fields, lats), F32), ((fields, slots), BF16), hidden, hidden, hidden, chunk, chunk],
+        smem=(0,),
         flops=2 * 10**9,
         moved=6 * 10**6,
-        smem=(9,),
         lons=lons,
-    )(prog_rows, low_pack, high_pack, mix_rows, cols, adjoint, w_in, w_mid, w_out, place)
-
-    keep_small, send_small, state_rows, grad_field, up_rows, down_rows = call(
+    )(place, prog_rows, low_pack, high_pack, mix_rows, cols, adjoint, w_in, w_mid, w_out)
+    column_total = lax.axis_size("ens") * lax.axis_size("horiz") * lons * lats
+    factor = 1.0 / math.sqrt(column_total)
+    chunk_one = (keep, send)
+
+    chunk = ((units // 2, units + 2 * fields - first), BF16)
+    delta_one, keep, send = call(
         backward_kernel,
+        [hidden, chunk, chunk],
+        smem=(0,),
+        flops=2 * 10**9,
+        moved=6 * 10**6,
+    )(place, x_now, act_one, act_two, delta_two, adjoint, w_in, w_mid)
+    chunk_two = (keep, send)
+
+    state_rows, grad_field, up_rows, down_rows = call(
+        place_kernel,
         [
-            ((units // 2, 2 * fields), BF16),
-            ((units // 2, 2 * fields), BF16),
             ((fields * lons, lats), F32),
             ((lons, fields, lats), F32),
-            ((2, fields, lats), F32),
-            ((2, fields, lats), F32),
+            ((2 * fields, lats), BF16),
+            ((2 * fields, lats), BF16),
         ],
-        scratch=[
-            pltpu.VMEM((units, slots), BF16),
-            pltpu.VMEM((tiles, fields, width), F32),
-            pltpu.VMEM((tiles, fields, width), F32),
-        ],
-        smem=(0, 15),
-        flops=2 * 10**9,
-        moved=6 * 10**6,
+        scratch=[pltpu.VMEM((tiles, fields, width), F32)] * 2,
+        smem=(0,),
+        flops=10**9,
+        moved=3 * 10**6,
         lons=lons,
     )(
         tile_count,
@@ -560,30 +571,27 @@
         mask,
         x_now,
         act_two,
-        delta_two,
+        delta_one,
         adjoint,
         coef,
         ratio,
         inverse,
         w_in,
-        w_mid,
         w_out,
-        place,
     )
     low_rows, high_rows = to_neighbours(up_rows, down_rows, "horiz")
-    (grad_rows,) = call(last_kernel, [((fields * lons, lats), F32)], lons=lons)(
-        grad_field, low_rows, high_rows, low_pack, high_pack, mix_rows
-    )
-
-    column_total = lax.axis_size("ens") * lax.axis_size("horiz") * lons * lats
-    factor = 1.0 / math.sqrt(column_total)
-    own, got = sum_over_all(place, [keep_mid, keep_small], [send_mid, send_small], factor)
+    (grad_rows,) = call(
+        last_kernel, [((fields * lons, lats), F32)], flops=10**6, moved=10**6, lons=lons
+    )(grad_field, low_rows, high_rows, low_pack, high_pack, mix_rows)
+
+    own_one, got_one, grad_rows = sum_over_all(place, *chunk_one, factor, grad_rows)
+    own_two, got_two, _ = sum_over_all(place, *chunk_two, factor)
     grad_mid, grad_in, grad_out = call(
         final_kernel,
         [((units, units), F32), ((units, fields), F32), ((fields, units), F32)],
         smem=(0,),
-        factor=1.0,
-    )(place, own, got)
+        moved=8 * 10**6,
+    )(place, own_one, got_one, own_two, got_two)
     return (
         state_rows.reshape(prognostic.shape),
         grad_rows.reshape(prognostic.shape),

time: 92.2 us -> 93.8 us (1.017)
  waiting for transfers between devices: 41.4 us -> 27 us
  starting transfers between devices: 25 us -> 35 us
  local copies, waits for them, and re-layouts: 6.36 us -> 9.27 us
  Pallas kernels: 17.6 us -> 20.5 us
    ppermute x15 -> x28, waiting for transfers between devices: 37.6 us -> 19.6 us  [exchange(): lax.ppermute(array, axis, [(i, i ^ k * stride) for i in range(count)])]
    ppermute x15 -> x28, starting transfers between devices: 16.8 us -> 30.4 us  [exchange(): lax.ppermute(array, axis, [(i, i ^ k * stride) for i in range(count)])]
    ppermute x2, starting transfers between devices: 7.2 us -> 4.1 us  [to_neighbours(): lax.ppermute(downward, axis, backward)]
    unnamed x29, local copies, waits for them, and re-layouts: 6.36 us -> 9.27 us
    pallas_call x11 -> x17, Pallas kernels: 17.6 us -> 20.5 us  [run(): pl.pallas_call(functools.partial(kernel, **names), out_shape=[jax.ShapeDt...]
    ppermute x2, waiting for transfers between devices: 0.01 us -> 1.91 us  [to_neighbours(): lax.ppermute(downward, axis, backward)]
    ppermute x2, waiting for transfers between devices: 3.73 us -> 5.49 us  [to_neighbours(): lax.ppermute(upward, axis, forward)]
  transfers between devices with their start and end apart: 19 -> 32, of which waited for: 11 -> 13; matrix products, arithmetic and copies ran while one was open for 1% -> 1% of each run, Pallas kernels for 7% -> 14%
where the time goes in v4:
time: 93.8 us; the launch traced here: 93.4 us
  starting transfers between devices  35 us (37%)
  waiting for transfers between devices  27 us (29%)
  Pallas kernels  20.5 us (22%)
  local copies, waits for them, and re-layouts  9.27 us (10%)
  between operations  1.54 us (2%)
    ppermute x28, starting transfers between devices, exchange(): lax.ppermute(array, axis, [(i, i ^ k * stride) for i in range(count)])  30.4 us
    pallas_call x17, Pallas kernels, run(): pl.pallas_call(functools.partial(kernel, **names), out_shape=[jax.ShapeDt...  20.5 us
    ppermute x28, waiting for transfers between devices, exchange(): lax.ppermute(array, axis, [(i, i ^ k * stride) for i in range(count)])  19.6 us
    unnamed x29, local copies, waits for them, and re-layouts  9.27 us
    ppermute x2, waiting for transfers between devices, to_neighbours(): lax.ppermute(upward, axis, forward)  5.49 us
    ppermute x2, starting transfers between devices, to_neighbours(): lax.ppermute(downward, axis, backward)  4.1 us
    ppermute x2, waiting for transfers between devices, to_neighbours(): lax.ppermute(downward, axis, backward)  1.91 us
  transfers between devices with their start and end apart: 32, of which 13 were waited for; matrix products, arithmetic and copies ran while one was open for 1% of the time, Pallas kernels for 14%

profile of v4, /device:TPU:0, one launch (start us, length us, event | category | flops | bytes accessed | tf_op | source)
XLA Modules:
  0.0 93.4 jit_solution(11842443046092156707)
XLA Ops:
  2.8 4.1 %collective-permute-start.1 = (bf16[272,128]{1,0:T(8,128)(2,1)S(1)}, bf16[272,128]{1,0:T(8,128)(2,1)S(1)}, u32[]{:S(2)}, u32[]{:S(2)}) collective-permute-start(bf16[272,128]{1,0:T(8,128)(2,1)S(1)} %get-tuple-element.50), channel_id=1, source_target_pairs={{1,0},{2,1},{3,2},{4,3},{5,4},{6,5},{7,6},{0,7},{9,8},{10,9},{11,1... | collective-permute-start | bytes 208904 | tf_op jit(solution)/shard_map/ppermute | solution.py:495
  12.6 1.6 %copy-done.5 = bf16[1024,1024]{1,0:T(8,128)(2,1)S(1)} copy-done((bf16[1024,1024]{1,0:T(8,128)(2,1)S(1)}, bf16[1024,1024]{1,0:T(8,128)(2,1)}, u32[]{:S(2)}) %copy-start.5) | copy-done | bytes 2097176
  16.0 4.1 %shard_map.139 = (f32[4,128,128]{2,1,0:T(8,128)S(1)}, bf16[128,384]{1,0:T(8,128)(2,1)S(1)}, bf16[1024,384]{1,0:T(8,128)(2,1)S(1)}, bf16[1024,384]{1,0:T(8,128)(2...) custom-call(s32[1,3]{1,0:T(1,128)S(1)} %add_bitcast_fusion.place_ref, ...), custom_call_target="tpu_custom_call" | custom-call | flops 2000000000 | bytes 6000000 | tf_op jit(solution)/shard_map/pallas_call | solution.py:27
  20.2 3.2 %shard_map.140 = (bf16[1024,384]{1,0:T(8,128)(2,1)S(1)}, bf16[512,640]{1,0:T(8,128)(2,1)S(1)}, bf16[512,640]{1,0:T(8,128)(2,1)S(1)}) custom-call(s32[1,3]{1,0:T(1,128)S(1)} %add_bitcast_fusion.place_ref, bf16[128,384]{1,0:T(8,128)(2,1)S(1)} %get-tuple-element.53.x_ref, bf16[1024,384]{1,0:T(8,128)(2,1)S(1)} %get-tuple-element.55.act_one_ref, ...), custom_call_target="tpu_custom_call" | custom-call | flops 2000000000 | bytes 6000000 | tf_op jit(solution)/shard_map/pallas_call | solution.py:27
  24.8 2.0 %collective-permute-start.3 = (bf16[128,640]{1,0:T(8,128)(2,1)S(1)}, bf16[128,640]{1,0:T(8,128)(2,1)S(1)}, u32[]{:S(2)}, u32[]{:S(2)}) collective-permute-start(bf16[128,640]{1,0:T(8,128)(2,1)S(1)} %get-tuple-element.65), channel_id=1, source_target_pairs={{0,8},{8,0},{16,24},{24,16},{1,9},{9,1},{17,25},{25,17},{2,10},{10... | collective-permute-start | bytes 491528 | tf_op jit(solution)/shard_map/ppermute | solution.py:425
  26.7 1.5 %collective-permute-start.4 = (bf16[128,640]{1,0:T(8,128)(2,1)S(1)}, bf16[128,640]{1,0:T(8,128)(2,1)S(1)}, u32[]{:S(2)}, u32[]{:S(2)}) collective-permute-start(bf16[128,640]{1,0:T(8,128)(2,1)S(1)} %get-tuple-element.66), channel_id=1, source_target_pairs={{0,16},{8,24},{16,0},{24,8},{1,17},{9,25},{17,1},{25,9},{2,18},{10... | collective-permute-start | bytes 491528 | tf_op jit(solution)/shard_map/ppermute | solution.py:425
  28.3 1.7 %shard_map.141 = (f32[512,128]{1,0:T(8,128)}, f32[4,128,128]{2,1,0:T(8,128)S(1)}, bf16[256,128]{1,0:T(8,128)(2,1)S(1)}, bf16[256,128]{1,0:T(8,128)(2,1)S(1)}) custom-call(s32[1,1]{1,0:T(1,128)S(6)} %copy.19.count_ref, f32[4,128,128]{2,1,0:T(8,128)S(1)} %get-tuple-element.52.moved_ref, f32[512,128]{1,0:T(8,128)S(1)} %bitcast.21, ...), custom_call_target="tpu_custom_call" | custom-call | flops 1000000000 | bytes 3000000 | tf_op jit(solution)/shard_map/pallas_call | solution.py:27
  30.1 5.5 %collective-permute-done.6.low_ref = bf16[256,128]{1,0:T(8,128)(2,1)S(1)} collective-permute-done((bf16[256,128]{1,0:T(8,128)(2,1)S(1)}, bf16[256,128]{1,0:T(8,128)(2,1)S(1)}, u32[]{:S(2)}, u32[]{:S(2)}) %collective-permute-start.6) | collective-permute-done | bytes 65568 | tf_op jit(solution)/shard_map/ppermute | solution.py:495
  35.5 1.9 %collective-permute-done.7.high_ref = bf16[256,128]{1,0:T(8,128)(2,1)S(1)} collective-permute-done((bf16[256,128]{1,0:T(8,128)(2,1)S(1)}, bf16[256,128]{1,0:T(8,128)(2,1)S(1)}, u32[]{:S(2)}, u32[]{:S(2)}) %collective-permute-start.7) | collective-permute-done | bytes 65568 | tf_op jit(solution)/shard_map/ppermute | solution.py:495
  37.5 1.5 %shard_map.143 = f32[512,128]{1,0:T(8,128)} custom-call(f32[4,128,128]{2,1,0:T(8,128)S(1)} %get-tuple-element.68.field_ref, bf16[256,128]{1,0:T(8,128)(2,1)S(1)} %collective-permute-done.6.low_ref, bf16[256,128]{1,0:T(8,128)(2,1)S(1)} %collective-permute-done.7.high_ref, bf16[272,128]{1,0:T(8,128)(2,1)S(1)} %collective-permute-done.low_ref.low_mix_ref, ...), custom_call_target="tpu_custom_call" | custom-call | flops 1000000 | bytes 1000000 | tf_op jit(solution)/shard_map/pallas_call | solution.py:27
  39.7 1.0 %collective-permute-start.9 = (bf16[32,640]{1,0:T(8,128)(2,1)S(1)}, bf16[32,640]{1,0:T(8,128)(2,1)S(1)}, u32[]{:S(2)}, u32[]{:S(2)}) collective-permute-start(bf16[32,640]{1,0:T(8,128)(2,1)S(1)} %get-tuple-element.78), channel_id=1, source_target_pairs={{0,4},{1,5},{2,6},{3,7},{4,0},{5,1},{6,2},{7,3},{8,12},{9,13},{10,... | collective-permute-start | bytes 122888 | tf_op jit(solution)/shard_map/ppermute | solution.py:425
  40.7 3.4 %collective-permute-start.10 = (bf16[32,640]{1,0:T(8,128)(2,1)S(1)}, bf16[32,640]{1,0:T(8,128)(2,1)S(1)}, u32[]{:S(2)}, u32[]{:S(2)}) collective-permute-start(bf16[32,640]{1,0:T(8,128)(2,1)S(1)} %get-tuple-element.79), channel_id=1, source_target_pairs={{0,6},{1,7},{2,4},{3,5},{4,2},{5,3},{6,0},{7,1},{8,14},{9,15},{10,... | collective-permute-start | bytes 122888 | tf_op jit(solution)/shard_map/ppermute | solution.py:425
  44.8 2.0 %collective-permute-start.19 = (bf16[128,640]{1,0:T(8,128)(2,1)S(1)}, bf16[128,640]{1,0:T(8,128)(2,1)S(1)}, u32[]{:S(2)}, u32[]{:S(2)}) collective-permute-start(bf16[128,640]{1,0:T(8,128)(2,1)S(1)} %get-tuple-element.83), channel_id=1, source_target_pairs={{0,8},{8,0},{16,24},{24,16},{1,9},{9,1},{17,25},{25,17},{2,10},{10... | collective-permute-start | bytes 491528 | tf_op jit(solution)/shard_map/ppermute | solution.py:425
  46.9 1.5 %collective-permute-start.20 = (bf16[128,640]{1,0:T(8,128)(2,1)S(1)}, bf16[128,640]{1,0:T(8,128)(2,1)S(1)}, u32[]{:S(2)}, u32[]{:S(2)}) collective-permute-start(bf16[128,640]{1,0:T(8,128)(2,1)S(1)} %get-tuple-element.84), channel_id=1, source_target_pairs={{0,16},{8,24},{16,0},{24,8},{1,17},{9,25},{17,1},{25,9},{2,18},{10... | collective-permute-start | bytes 491528 | tf_op jit(solution)/shard_map/ppermute | solution.py:425
  49.0 1.5 %collective-permute-start.13 = (bf16[32,640]{1,0:T(8,128)(2,1)S(1)}, bf16[32,640]{1,0:T(8,128)(2,1)S(1)}, u32[]{:S(2)}, u32[]{:S(2)}) collective-permute-start(bf16[32,640]{1,0:T(8,128)(2,1)S(1)} %shard_map.145.refs_0_), channel_id=1, source_target_pairs={{0,6},{1,7},{2,4},{3,5},{4,2},{5,3},{6,0},{7,1},{8,14},{9,15},{10,... | collective-permute-start | bytes 122888 | tf_op jit(solution)/shard_map/ppermute | solution.py:425
  50.5 4.3 %collective-permute-done.13.refs_3_ = bf16[32,640]{1,0:T(8,128)(2,1)S(1)} collective-permute-done((bf16[32,640]{1,0:T(8,128)(2,1)S(1)}, bf16[32,640]{1,0:T(8,128)(2,1)S(1)}, u32[]{:S(2)}, u32[]{:S(2)}) %collective-permute-start.13) | collective-permute-done | bytes 40992 | tf_op jit(solution)/shard_map/ppermute | solution.py:425
  54.8 1.3 %collective-permute-done.12.refs_2_ = bf16[32,640]{1,0:T(8,128)(2,1)S(1)} collective-permute-done((bf16[32,640]{1,0:T(8,128)(2,1)S(1)}, bf16[32,640]{1,0:T(8,128)(2,1)S(1)}, u32[]{:S(2)}, u32[]{:S(2)}) %collective-permute-start.12) | collective-permute-done | bytes 40992 | tf_op jit(solution)/shard_map/ppermute | solution.py:425
  56.2 2.7 %collective-permute-done.11.refs_1_ = bf16[32,640]{1,0:T(8,128)(2,1)S(1)} collective-permute-done((bf16[32,640]{1,0:T(8,128)(2,1)S(1)}, bf16[32,640]{1,0:T(8,128)(2,1)S(1)}, u32[]{:S(2)}, u32[]{:S(2)}) %collective-permute-start.11) | collective-permute-done | bytes 40992 | tf_op jit(solution)/shard_map/ppermute | solution.py:425
  59.4 3.0 %collective-permute-start.16 = (bf16[128,640]{1,0:T(8,128)(2,1)S(1)}, bf16[128,640]{1,0:T(8,128)(2,1)S(1)}, u32[]{:S(2)}, u32[]{:S(2)}) collective-permute-start(bf16[128,640]{1,0:T(8,128)(2,1)S(1)} %shard_map.146.refs_0_), channel_id=1, source_target_pairs={{0,24},{8,16},{16,8},{24,0},{1,25},{9,17},{17,9},{25,1},{2,26},{10... | collective-permute-start | bytes 491528 | tf_op jit(solution)/shard_map/ppermute | solution.py:425
  63.1 2.5 %collective-permute-start.23 = (bf16[32,640]{1,0:T(8,128)(2,1)S(1)}, bf16[32,640]{1,0:T(8,128)(2,1)S(1)}, u32[]{:S(2)}, u32[]{:S(2)}) collective-permute-start(bf16[32,640]{1,0:T(8,128)(2,1)S(1)} %get-tuple-element.88), channel_id=1, source_target_pairs={{0,4},{1,5},{2,6},{3,7},{4,0},{5,1},{6,2},{7,3},{8,12},{9,13},{10,... | collective-permute-start | bytes 122888 | tf_op jit(solution)/shard_map/ppermute | solution.py:425
  65.7 1.8 %collective-permute-start.24 = (bf16[32,640]{1,0:T(8,128)(2,1)S(1)}, bf16[32,640]{1,0:T(8,128)(2,1)S(1)}, u32[]{:S(2)}, u32[]{:S(2)}) collective-permute-start(bf16[32,640]{1,0:T(8,128)(2,1)S(1)} %get-tuple-element.89), channel_id=1, source_target_pairs={{0,6},{1,7},{2,4},{3,5},{4,2},{5,3},{6,0},{7,1},{8,14},{9,15},{10,... | collective-permute-start | bytes 122888 | tf_op jit(solution)/shard_map/ppermute | solution.py:425
  67.5 1.0 %collective-permute-done.23.refs_2_ = bf16[32,640]{1,0:T(8,128)(2,1)S(1)} collective-permute-done((bf16[32,640]{1,0:T(8,128)(2,1)S(1)}, bf16[32,640]{1,0:T(8,128)(2,1)S(1)}, u32[]{:S(2)}, u32[]{:S(2)}) %collective-permute-start.23) | collective-permute-done | bytes 40992 | tf_op jit(solution)/shard_map/ppermute | solution.py:425
  68.5 2.9 %collective-permute-done.24.refs_3_ = bf16[32,640]{1,0:T(8,128)(2,1)S(1)} collective-permute-done((bf16[32,640]{1,0:T(8,128)(2,1)S(1)}, bf16[32,640]{1,0:T(8,128)(2,1)S(1)}, u32[]{:S(2)}, u32[]{:S(2)}) %collective-permute-start.24) | collective-permute-done | bytes 40992 | tf_op jit(solution)/shard_map/ppermute | solution.py:425
  72.0 1.9 %collective-permute-start.27 = (bf16[32,640]{1,0:T(8,128)(2,1)S(1)}, bf16[32,640]{1,0:T(8,128)(2,1)S(1)}, u32[]{:S(2)}, u32[]{:S(2)}) collective-permute-start(bf16[32,640]{1,0:T(8,128)(2,1)S(1)} %shard_map.150.refs_0_), channel_id=1, source_target_pairs={{0,6},{1,7},{2,4},{3,5},{4,2},{5,3},{6,0},{7,1},{8,14},{9,15},{10,... | collective-permute-start | bytes 122888 | tf_op jit(solution)/shard_map/ppermute | solution.py:425
  74.0 2.5 %collective-permute-start.25 = (bf16[32,640]{1,0:T(8,128)(2,1)S(1)}, bf16[32,640]{1,0:T(8,128)(2,1)S(1)}, u32[]{:S(2)}, u32[]{:S(2)}) collective-permute-start(bf16[32,640]{1,0:T(8,128)(2,1)S(1)} %shard_map.150.refs_0_), channel_id=1, source_target_pairs={{0,2},{1,3},{2,0},{3,1},{4,6},{5,7},{6,4},{7,5},{8,10},{9,11},{10,... | collective-permute-start | bytes 122888 | tf_op jit(solution)/shard_map/ppermute | solution.py:425
  79.5 1.1 %collective-permute-start.30 = (bf16[128,640]{1,0:T(8,128)(2,1)S(1)}, bf16[128,640]{1,0:T(8,128)(2,1)S(1)}, u32[]{:S(2)}, u32[]{:S(2)}) collective-permute-start(bf16[128,640]{1,0:T(8,128)(2,1)S(1)} %shard_map.151.refs_0_), channel_id=1, source_target_pairs={{0,24},{8,16},{16,8},{24,0},{1,25},{9,17},{17,9},{25,1},{2,26},{10... | collective-permute-start | bytes 491528 | tf_op jit(solution)/shard_map/ppermute | solution.py:425
  80.6 1.4 %collective-permute-start.29 = (bf16[128,640]{1,0:T(8,128)(2,1)S(1)}, bf16[128,640]{1,0:T(8,128)(2,1)S(1)}, u32[]{:S(2)}, u32[]{:S(2)}) collective-permute-start(bf16[128,640]{1,0:T(8,128)(2,1)S(1)} %shard_map.151.refs_0_), channel_id=1, source_target_pairs={{0,16},{8,24},{16,0},{24,8},{1,17},{9,25},{17,1},{25,9},{2,18},{10... | collective-permute-start | bytes 491528 | tf_op jit(solution)/shard_map/ppermute | solution.py:425
  82.0 1.0 %collective-permute-start.28 = (bf16[128,640]{1,0:T(8,128)(2,1)S(1)}, bf16[128,640]{1,0:T(8,128)(2,1)S(1)}, u32[]{:S(2)}, u32[]{:S(2)}) collective-permute-start(bf16[128,640]{1,0:T(8,128)(2,1)S(1)} %shard_map.151.refs_0_), channel_id=1, source_target_pairs={{0,8},{8,0},{16,24},{24,16},{1,9},{9,1},{17,25},{25,17},{2,10},{10... | collective-permute-start | bytes 491528 | tf_op jit(solution)/shard_map/ppermute | solution.py:425
  84.2 1.7 %collective-permute-done.30.refs_3_ = bf16[128,640]{1,0:T(8,128)(2,1)S(1)} collective-permute-done((bf16[128,640]{1,0:T(8,128)(2,1)S(1)}, bf16[128,640]{1,0:T(8,128)(2,1)S(1)}, u32[]{:S(2)}, u32[]{:S(2)}) %collective-permute-start.30) | collective-permute-done | bytes 163872 | tf_op jit(solution)/shard_map/ppermute | solution.py:425
  85.9 1.7 %collective-permute-done.29.refs_2_ = bf16[128,640]{1,0:T(8,128)(2,1)S(1)} collective-permute-done((bf16[128,640]{1,0:T(8,128)(2,1)S(1)}, bf16[128,640]{1,0:T(8,128)(2,1)S(1)}, u32[]{:S(2)}, u32[]{:S(2)}) %collective-permute-start.29) | collective-permute-done | bytes 163872 | tf_op jit(solution)/shard_map/ppermute | solution.py:425
  88.3 2.1 %collective-permute-done.31.got_two = bf16[512,640]{1,0:T(8,128)(2,1)S(1)} collective-permute-done((bf16[512,640]{1,0:T(8,128)(2,1)S(1)}, bf16[512,640]{1,0:T(8,128)(2,1)S(1)}, u32[]{:S(2)}, u32[]{:S(2)}) %collective-permute-start.31) | collective-permute-done | bytes 655392 | tf_op jit(solution)/shard_map/ppermute | solution.py:425
  90.3 3.0 %shard_map.153 = (f32[1024,1024]{1,0:T(8,128)}, f32[1024,128]{1,0:T(8,128)}, f32[128,1024]{1,0:T(8,128)}) custom-call(s32[1,3]{1,0:T(1,128)S(1)} %add_bitcast_fusion.place_ref, bf16[512,640]{1,0:T(8,128)(2,1)S(1)} %shard_map.147.own_one, bf16[512,640]{1,0:T(8,128)(2,1)S(1)} %collective-permute-done.17.got_one, bf16[512,640]{1,0:T(8,128)(2,1)S(1)} %shard_map.152.own_two, ...), custom_call_target="tpu_custom_call" | custom-call | bytes 8000000 | tf_op jit(solution)/shard_map/pallas_call | solution.py:27
  (79 shorter events, 19.1 us)
Async XLA Ops:
  2.3 8.6 %collective-permute-start = (bf16[272,128]{1,0:T(8,128)(2,1)S(1)}, bf16[272,128]{1,0:T(8,128)(2,1)S(1)}, u32[]{:S(2)}, u32[]{:S(2)}) collective-permute-start(bf16[272,128]{1,0:T(8,128)(2,1)S(1)} %get-tuple-element.49), channel_id=1, source_target_pairs={{0,1},{1,2},{2,3},{3,4},{4,5},{5,6},{6,7},{7,0},{8,9},{9,10},{10,1... | collective-permute-start | bytes 208904 | tf_op jit(solution)/shard_map/ppermute | solution.py:495
  2.8 8.1 %collective-permute-start.1 = (bf16[272,128]{1,0:T(8,128)(2,1)S(1)}, bf16[272,128]{1,0:T(8,128)(2,1)S(1)}, u32[]{:S(2)}, u32[]{:S(2)}) collective-permute-start(bf16[272,128]{1,0:T(8,128)(2,1)S(1)} %get-tuple-element.50), channel_id=1, source_target_pairs={{1,0},{2,1},{3,2},{4,3},{5,4},{6,5},{7,6},{0,7},{9,8},{10,9},{11,1... | collective-permute-start | bytes 208904 | tf_op jit(solution)/shard_map/ppermute | solution.py:495
  20.1 3.9 %collective-permute-start.2 = (bf16[512,640]{1,0:T(8,128)(2,1)S(1)}, bf16[512,640]{1,0:T(8,128)(2,1)S(1)}, u32[]{:S(2)}, u32[]{:S(2)}) collective-permute-start(bf16[512,640]{1,0:T(8,128)(2,1)S(1)} %get-tuple-element.63), channel_id=1, source_target_pairs={{0,1},{1,0},{2,3},{3,2},{4,5},{5,4},{6,7},{7,6},{8,9},{9,8},{10,11... | collective-permute-start | bytes 1966088 | tf_op jit(solution)/shard_map/ppermute | solution.py:425
  23.5 20.6 %collective-permute-start.18 = (bf16[512,640]{1,0:T(8,128)(2,1)S(1)}, bf16[512,640]{1,0:T(8,128)(2,1)S(1)}, u32[]{:S(2)}, u32[]{:S(2)}) collective-permute-start(bf16[512,640]{1,0:T(8,128)(2,1)S(1)} %get-tuple-element.81), channel_id=1, source_target_pairs={{0,1},{1,0},{2,3},{3,2},{4,5},{5,4},{6,7},{7,6},{8,9},{9,8},{10,11... | collective-permute-start | bytes 1966088 | tf_op jit(solution)/shard_map/ppermute | solution.py:425
  24.8 14.2 %collective-permute-start.3 = (bf16[128,640]{1,0:T(8,128)(2,1)S(1)}, bf16[128,640]{1,0:T(8,128)(2,1)S(1)}, u32[]{:S(2)}, u32[]{:S(2)}) collective-permute-start(bf16[128,640]{1,0:T(8,128)(2,1)S(1)} %get-tuple-element.65), channel_id=1, source_target_pairs={{0,8},{8,0},{16,24},{24,16},{1,9},{9,1},{17,25},{25,17},{2,10},{10... | collective-permute-start | bytes 491528 | tf_op jit(solution)/shard_map/ppermute | solution.py:425
  26.7 12.2 %collective-permute-start.4 = (bf16[128,640]{1,0:T(8,128)(2,1)S(1)}, bf16[128,640]{1,0:T(8,128)(2,1)S(1)}, u32[]{:S(2)}, u32[]{:S(2)}) collective-permute-start(bf16[128,640]{1,0:T(8,128)(2,1)S(1)} %get-tuple-element.66), channel_id=1, source_target_pairs={{0,16},{8,24},{16,0},{24,8},{1,17},{9,25},{17,1},{25,9},{2,18},{10... | collective-permute-start | bytes 491528 | tf_op jit(solution)/shard_map/ppermute | solution.py:425
  28.3 10.7 %collective-permute-start.5 = (bf16[128,640]{1,0:T(8,128)(2,1)S(1)}, bf16[128,640]{1,0:T(8,128)(2,1)S(1)}, u32[]{:S(2)}, u32[]{:S(2)}) collective-permute-start(bf16[128,640]{1,0:T(8,128)(2,1)S(1)} %get-tuple-element.67), channel_id=1, source_target_pairs={{0,24},{8,16},{16,8},{24,0},{1,25},{9,17},{17,9},{25,1},{2,26},{10... | collective-permute-start | bytes 491528 | tf_op jit(solution)/shard_map/ppermute | solution.py:425
  30.1 5.5 %collective-permute-start.6 = (bf16[256,128]{1,0:T(8,128)(2,1)S(1)}, bf16[256,128]{1,0:T(8,128)(2,1)S(1)}, u32[]{:S(2)}, u32[]{:S(2)}) collective-permute-start(bf16[256,128]{1,0:T(8,128)(2,1)S(1)} %get-tuple-element.69), channel_id=1, source_target_pairs={{0,1},{1,2},{2,3},{3,4},{4,5},{5,6},{6,7},{7,0},{8,9},{9,10},{10,1... | collective-permute-start | bytes 196616 | tf_op jit(solution)/shard_map/ppermute | solution.py:495
  35.5 1.9 %collective-permute-start.7 = (bf16[256,128]{1,0:T(8,128)(2,1)S(1)}, bf16[256,128]{1,0:T(8,128)(2,1)S(1)}, u32[]{:S(2)}, u32[]{:S(2)}) collective-permute-start(bf16[256,128]{1,0:T(8,128)(2,1)S(1)} %get-tuple-element.70), channel_id=1, source_target_pairs={{1,0},{2,1},{3,2},{4,3},{5,4},{6,5},{7,6},{0,7},{9,8},{10,9},{11,1... | collective-permute-start | bytes 196616 | tf_op jit(solution)/shard_map/ppermute | solution.py:495
  39.6 8.8 %collective-permute-start.8 = (bf16[32,640]{1,0:T(8,128)(2,1)S(1)}, bf16[32,640]{1,0:T(8,128)(2,1)S(1)}, u32[]{:S(2)}, u32[]{:S(2)}) collective-permute-start(bf16[32,640]{1,0:T(8,128)(2,1)S(1)} %get-tuple-element.77), channel_id=1, source_target_pairs={{0,2},{1,3},{2,0},{3,1},{4,6},{5,7},{6,4},{7,5},{8,10},{9,11},{10,... | collective-permute-start | bytes 122888 | tf_op jit(solution)/shard_map/ppermute | solution.py:425
  39.7 8.7 %collective-permute-start.9 = (bf16[32,640]{1,0:T(8,128)(2,1)S(1)}, bf16[32,640]{1,0:T(8,128)(2,1)S(1)}, u32[]{:S(2)}, u32[]{:S(2)}) collective-permute-start(bf16[32,640]{1,0:T(8,128)(2,1)S(1)} %get-tuple-element.78), channel_id=1, source_target_pairs={{0,4},{1,5},{2,6},{3,7},{4,0},{5,1},{6,2},{7,3},{8,12},{9,13},{10,... | collective-permute-start | bytes 122888 | tf_op jit(solution)/shard_map/ppermute | solution.py:425
  40.7 7.7 %collective-permute-start.10 = (bf16[32,640]{1,0:T(8,128)(2,1)S(1)}, bf16[32,640]{1,0:T(8,128)(2,1)S(1)}, u32[]{:S(2)}, u32[]{:S(2)}) collective-permute-start(bf16[32,640]{1,0:T(8,128)(2,1)S(1)} %get-tuple-element.79), channel_id=1, source_target_pairs={{0,6},{1,7},{2,4},{3,5},{4,2},{5,3},{6,0},{7,1},{8,14},{9,15},{10,... | collective-permute-start | bytes 122888 | tf_op jit(solution)/shard_map/ppermute | solution.py:425
  44.8 17.6 %collective-permute-start.19 = (bf16[128,640]{1,0:T(8,128)(2,1)S(1)}, bf16[128,640]{1,0:T(8,128)(2,1)S(1)}, u32[]{:S(2)}, u32[]{:S(2)}) collective-permute-start(bf16[128,640]{1,0:T(8,128)(2,1)S(1)} %get-tuple-element.83), channel_id=1, source_target_pairs={{0,8},{8,0},{16,24},{24,16},{1,9},{9,1},{17,25},{25,17},{2,10},{10... | collective-permute-start | bytes 491528 | tf_op jit(solution)/shard_map/ppermute | solution.py:425
  46.9 15.6 %collective-permute-start.20 = (bf16[128,640]{1,0:T(8,128)(2,1)S(1)}, bf16[128,640]{1,0:T(8,128)(2,1)S(1)}, u32[]{:S(2)}, u32[]{:S(2)}) collective-permute-start(bf16[128,640]{1,0:T(8,128)(2,1)S(1)} %get-tuple-element.84), channel_id=1, source_target_pairs={{0,16},{8,24},{16,0},{24,8},{1,17},{9,25},{17,1},{25,9},{2,18},{10... | collective-permute-start | bytes 491528 | tf_op jit(solution)/shard_map/ppermute | solution.py:425
  48.4 14.0 %collective-permute-start.21 = (bf16[128,640]{1,0:T(8,128)(2,1)S(1)}, bf16[128,640]{1,0:T(8,128)(2,1)S(1)}, u32[]{:S(2)}, u32[]{:S(2)}) collective-permute-start(bf16[128,640]{1,0:T(8,128)(2,1)S(1)} %get-tuple-element.85), channel_id=1, source_target_pairs={{0,24},{8,16},{16,8},{24,0},{1,25},{9,17},{17,9},{25,1},{2,26},{10... | collective-permute-start | bytes 491528 | tf_op jit(solution)/shard_map/ppermute | solution.py:425
  49.0 5.9 %collective-permute-start.13 = (bf16[32,640]{1,0:T(8,128)(2,1)S(1)}, bf16[32,640]{1,0:T(8,128)(2,1)S(1)}, u32[]{:S(2)}, u32[]{:S(2)}) collective-permute-start(bf16[32,640]{1,0:T(8,128)(2,1)S(1)} %shard_map.145.refs_0_), channel_id=1, source_target_pairs={{0,6},{1,7},{2,4},{3,5},{4,2},{5,3},{6,0},{7,1},{8,14},{9,15},{10,... | collective-permute-start | bytes 122888 | tf_op jit(solution)/shard_map/ppermute | solution.py:425
  50.5 5.7 %collective-permute-start.12 = (bf16[32,640]{1,0:T(8,128)(2,1)S(1)}, bf16[32,640]{1,0:T(8,128)(2,1)S(1)}, u32[]{:S(2)}, u32[]{:S(2)}) collective-permute-start(bf16[32,640]{1,0:T(8,128)(2,1)S(1)} %shard_map.145.refs_0_), channel_id=1, source_target_pairs={{0,4},{1,5},{2,6},{3,7},{4,0},{5,1},{6,2},{7,3},{8,12},{9,13},{10,... | collective-permute-start | bytes 122888 | tf_op jit(solution)/shard_map/ppermute | solution.py:425
  54.8 4.0 %collective-permute-start.11 = (bf16[32,640]{1,0:T(8,128)(2,1)S(1)}, bf16[32,640]{1,0:T(8,128)(2,1)S(1)}, u32[]{:S(2)}, u32[]{:S(2)}) collective-permute-start(bf16[32,640]{1,0:T(8,128)(2,1)S(1)} %shard_map.145.refs_0_), channel_id=1, source_target_pairs={{0,2},{1,3},{2,0},{3,1},{4,6},{5,7},{6,4},{7,5},{8,10},{9,11},{10,... | collective-permute-start | bytes 122888 | tf_op jit(solution)/shard_map/ppermute | solution.py:425
  59.4 22.6 %collective-permute-start.16 = (bf16[128,640]{1,0:T(8,128)(2,1)S(1)}, bf16[128,640]{1,0:T(8,128)(2,1)S(1)}, u32[]{:S(2)}, u32[]{:S(2)}) collective-permute-start(bf16[128,640]{1,0:T(8,128)(2,1)S(1)} %shard_map.146.refs_0_), channel_id=1, source_target_pairs={{0,24},{8,16},{16,8},{24,0},{1,25},{9,17},{17,9},{25,1},{2,26},{10... | collective-permute-start | bytes 491528 | tf_op jit(solution)/shard_map/ppermute | solution.py:425
  63.1 4.5 %collective-permute-start.22 = (bf16[32,640]{1,0:T(8,128)(2,1)S(1)}, bf16[32,640]{1,0:T(8,128)(2,1)S(1)}, u32[]{:S(2)}, u32[]{:S(2)}) collective-permute-start(bf16[32,640]{1,0:T(8,128)(2,1)S(1)} %get-tuple-element.87), channel_id=1, source_target_pairs={{0,2},{1,3},{2,0},{3,1},{4,6},{5,7},{6,4},{7,5},{8,10},{9,11},{10,... | collective-permute-start | bytes 122888 | tf_op jit(solution)/shard_map/ppermute | solution.py:425
  63.1 5.4 %collective-permute-start.23 = (bf16[32,640]{1,0:T(8,128)(2,1)S(1)}, bf16[32,640]{1,0:T(8,128)(2,1)S(1)}, u32[]{:S(2)}, u32[]{:S(2)}) collective-permute-start(bf16[32,640]{1,0:T(8,128)(2,1)S(1)} %get-tuple-element.88), channel_id=1, source_target_pairs={{0,4},{1,5},{2,6},{3,7},{4,0},{5,1},{6,2},{7,3},{8,12},{9,13},{10,... | collective-permute-start | bytes 122888 | tf_op jit(solution)/shard_map/ppermute | solution.py:425
  65.7 5.8 %collective-permute-start.24 = (bf16[32,640]{1,0:T(8,128)(2,1)S(1)}, bf16[32,640]{1,0:T(8,128)(2,1)S(1)}, u32[]{:S(2)}, u32[]{:S(2)}) collective-permute-start(bf16[32,640]{1,0:T(8,128)(2,1)S(1)} %get-tuple-element.89), channel_id=1, source_target_pairs={{0,6},{1,7},{2,4},{3,5},{4,2},{5,3},{6,0},{7,1},{8,14},{9,15},{10,... | collective-permute-start | bytes 122888 | tf_op jit(solution)/shard_map/ppermute | solution.py:425
  72.0 5.9 %collective-permute-start.27 = (bf16[32,640]{1,0:T(8,128)(2,1)S(1)}, bf16[32,640]{1,0:T(8,128)(2,1)S(1)}, u32[]{:S(2)}, u32[]{:S(2)}) collective-permute-start(bf16[32,640]{1,0:T(8,128)(2,1)S(1)} %shard_map.150.refs_0_), channel_id=1, source_target_pairs={{0,6},{1,7},{2,4},{3,5},{4,2},{5,3},{6,0},{7,1},{8,14},{9,15},{10,... | collective-permute-start | bytes 122888 | tf_op jit(solution)/shard_map/ppermute | solution.py:425
  74.0 5.0 %collective-permute-start.26 = (bf16[32,640]{1,0:T(8,128)(2,1)S(1)}, bf16[32,640]{1,0:T(8,128)(2,1)S(1)}, u32[]{:S(2)}, u32[]{:S(2)}) collective-permute-start(bf16[32,640]{1,0:T(8,128)(2,1)S(1)} %shard_map.150.refs_0_), channel_id=1, source_target_pairs={{0,4},{1,5},{2,6},{3,7},{4,0},{5,1},{6,2},{7,3},{8,12},{9,13},{10,... | collective-permute-start | bytes 122888 | tf_op jit(solution)/shard_map/ppermute | solution.py:425
  74.0 5.0 %collective-permute-start.25 = (bf16[32,640]{1,0:T(8,128)(2,1)S(1)}, bf16[32,640]{1,0:T(8,128)(2,1)S(1)}, u32[]{:S(2)}, u32[]{:S(2)}) collective-permute-start(bf16[32,640]{1,0:T(8,128)(2,1)S(1)} %shard_map.150.refs_0_), channel_id=1, source_target_pairs={{0,2},{1,3},{2,0},{3,1},{4,6},{5,7},{6,4},{7,5},{8,10},{9,11},{10,... | collective-permute-start | bytes 122888 | tf_op jit(solution)/shard_map/ppermute | solution.py:425
  76.5 7.0 %collective-permute-start.15 = (bf16[128,640]{1,0:T(8,128)(2,1)S(1)}, bf16[128,640]{1,0:T(8,128)(2,1)S(1)}, u32[]{:S(2)}, u32[]{:S(2)}) collective-permute-start(bf16[128,640]{1,0:T(8,128)(2,1)S(1)} %shard_map.146.refs_0_), channel_id=1, source_target_pairs={{0,16},{8,24},{16,0},{24,8},{1,17},{9,25},{17,1},{25,9},{2,18},{10... | collective-permute-start | bytes 491528 | tf_op jit(solution)/shard_map/ppermute | solution.py:425
  77.9 5.6 %collective-permute-start.14 = (bf16[128,640]{1,0:T(8,128)(2,1)S(1)}, bf16[128,640]{1,0:T(8,128)(2,1)S(1)}, u32[]{:S(2)}, u32[]{:S(2)}) collective-permute-start(bf16[128,640]{1,0:T(8,128)(2,1)S(1)} %shard_map.146.refs_0_), channel_id=1, source_target_pairs={{0,8},{8,0},{16,24},{24,16},{1,9},{9,1},{17,25},{25,17},{2,10},{10... | collective-permute-start | bytes 491528 | tf_op jit(solution)/shard_map/ppermute | solution.py:425
  79.5 6.4 %collective-permute-start.30 = (bf16[128,640]{1,0:T(8,128)(2,1)S(1)}, bf16[128,640]{1,0:T(8,128)(2,1)S(1)}, u32[]{:S(2)}, u32[]{:S(2)}) collective-permute-start(bf16[128,640]{1,0:T(8,128)(2,1)S(1)} %shard_map.151.refs_0_), channel_id=1, source_target_pairs={{0,24},{8,16},{16,8},{24,0},{1,25},{9,17},{17,9},{25,1},{2,26},{10... | collective-permute-start | bytes 491528 | tf_op jit(solution)/shard_map/ppermute | solution.py:425
  80.6 6.9 %collective-permute-start.29 = (bf16[128,640]{1,0:T(8,128)(2,1)S(1)}, bf16[128,640]{1,0:T(8,128)(2,1)S(1)}, u32[]{:S(2)}, u32[]{:S(2)}) collective-permute-start(bf16[128,640]{1,0:T(8,128)(2,1)S(1)} %shard_map.151.refs_0_), channel_id=1, source_target_pairs={{0,16},{8,24},{16,0},{24,8},{1,17},{9,25},{17,1},{25,9},{2,18},{10... | collective-permute-start | bytes 491528 | tf_op jit(solution)/shard_map/ppermute | solution.py:425
  82.0 5.5 %collective-permute-start.28 = (bf16[128,640]{1,0:T(8,128)(2,1)S(1)}, bf16[128,640]{1,0:T(8,128)(2,1)S(1)}, u32[]{:S(2)}, u32[]{:S(2)}) collective-permute-start(bf16[128,640]{1,0:T(8,128)(2,1)S(1)} %shard_map.151.refs_0_), channel_id=1, source_target_pairs={{0,8},{8,0},{16,24},{24,16},{1,9},{9,1},{17,25},{25,17},{2,10},{10... | collective-permute-start | bytes 491528 | tf_op jit(solution)/shard_map/ppermute | solution.py:425
  84.1 4.2 %collective-permute-start.17 = (bf16[512,640]{1,0:T(8,128)(2,1)S(1)}, bf16[512,640]{1,0:T(8,128)(2,1)S(1)}, u32[]{:S(2)}, u32[]{:S(2)}) collective-permute-start(bf16[512,640]{1,0:T(8,128)(2,1)S(1)} %shard_map.147.own_one), channel_id=1, source_target_pairs={{0,1},{1,0},{2,3},{3,2},{4,5},{5,4},{6,7},{7,6},{8,9},{9,8},{10,11... | collective-permute-start | bytes 1966088 | tf_op jit(solution)/shard_map/ppermute | solution.py:425
  88.2 2.2 %collective-permute-start.31 = (bf16[512,640]{1,0:T(8,128)(2,1)S(1)}, bf16[512,640]{1,0:T(8,128)(2,1)S(1)}, u32[]{:S(2)}, u32[]{:S(2)}) collective-permute-start(bf16[512,640]{1,0:T(8,128)(2,1)S(1)} %shard_map.152.own_two), channel_id=1, source_target_pairs={{0,1},{1,0},{2,3},{3,2},{4,5},{5,4},{6,7},{7,6},{8,9},{9,8},{10,11... | collective-permute-start | bytes 1966088 | tf_op jit(solution)/shard_map/ppermute | solution.py:425
  (14 other events, 56.9 us)

commit v5 on v4

--- a/solution.py
+++ b/solution.py
@@ -70,7 +70,7 @@
     return lon_coef, [jnp.where(inside, coef, 0.0) for coef in lat_coef]
 
 
-def pack_kernel(prog_ref, mix_ref, up_ref, down_ref, *, lons):
+def pack_kernel(prog_ref, mix_ref, up_ref, down_ref, prog_out, mix_out, *, lons):
     fields = prog_ref.shape[0] // lons
     for out_ref, first in ((up_ref, lons - 2), (down_ref, 0)):
         for side in range(2):
@@ -80,6 +80,8 @@
         mix_rows = [mix_ref[first : first + 2, :], mix_ref[lons + first : lons + first + 2, :]]
         mix_rows.append(jnp.zeros((PACK_ROWS - 4, mix_ref.shape[1]), F32))
         out_ref[2 * fields :, :] = jnp.concatenate(mix_rows, axis=0).astype(BF16)
+    prog_out[...] = prog_ref[...]
+    mix_out[...] = mix_ref[...]
 
 
 def halo_rows(pack_ref, fields):
@@ -174,14 +176,23 @@
     cot_ref,
     cols_ref,
     mask_ref,
+    w_in_ref,
+    w_mid_ref,
+    w_out_ref,
     adj_ref,
     coef_ref,
     ratio_ref,
     inverse_ref,
+    w_in_out,
+    w_mid_out,
+    w_out_out,
     right_ref,
     *,
     lons,
 ):
+    w_in_out[...] = w_in_ref[...]
+    w_mid_out[...] = w_mid_ref[...]
+    w_out_out[...] = w_out_ref[...]
     levels = diff_ref.shape[0] // lons
     fields = cot_ref.shape[0] // lons
     cells = lons * cot_ref.shape[1]
@@ -200,21 +211,21 @@
     return 0.5 * jnp.tanh(0.5 * pre_act) + 0.5
 
 
-def weight_product(left_ref, right, place_ref, keep_ref, send_ref, first, transposed=CONTRACT_LAST):
+def weight_product(left_ref, right, keep_ref, send_ref, first):
     half = left_ref.shape[0] // 2
     block = min(BLOCK, half)
-    for out_ref, side in ((send_ref, 1 - place_ref[0, 0]), (keep_ref, place_ref[0, 0])):
+    core = lax.axis_index("horiz") % 2
+    for out_ref, side in ((send_ref, 1 - core), (keep_ref, core)):
         for start in range(0, half, block):
             out_ref[start : start + block, first : first + right.shape[0]] = lax.dot_general(
                 left_ref[pl.ds(pl.multiple_of(side * half + start, block), block), :],
                 right,
-                transposed,
+                CONTRACT_LAST,
                 preferred_element_type=F32,
             ).astype(BF16)
 
 
 def forward_kernel(
-    place_ref,
     prog_ref,
     low_ref,
     high_ref,
@@ -267,15 +278,11 @@
         )
         slope = sigma_val * (1.0 + pre_two * (1.0 - sigma_val))
         delta_two_ref[start : start + BLOCK, :] = (back_two * slope).astype(BF16)
-    weight_product(
-        delta_two_ref, act_one_ref[: keep_ref.shape[1], :], place_ref, keep_ref, send_ref, 0
-    )
+    weight_product(delta_two_ref, act_one_ref[...], keep_ref, send_ref, 0)
 
 
 def backward_kernel(
-    place_ref,
     x_ref,
-    act_one_ref,
     act_two_ref,
     delta_two_ref,
     adj_ref,
@@ -287,7 +294,6 @@
 ):
     fields = x_ref.shape[0]
     units = w_mid_ref.shape[0]
-    done = units + 2 * fields - keep_ref.shape[1]
     x_now = x_ref[...]
     for start in range(0, units, BLOCK):
         back_one = lax.dot_general(
@@ -300,31 +306,34 @@
         sigma_val = sigmoid(pre_one)
         slope = sigma_val * (1.0 + pre_one * (1.0 - sigma_val))
         delta_one_ref[start : start + BLOCK, :] = (back_one * slope).astype(BF16)
-    weight_product(delta_two_ref, act_one_ref[done:, :], place_ref, keep_ref, send_ref, 0)
-    weight_product(delta_one_ref, x_now, place_ref, keep_ref, send_ref, units - done)
-    adj_half = join_tiles(adj_ref).astype(BF16)
-    weight_product(act_two_ref, adj_half, place_ref, keep_ref, send_ref, units - done + fields)
-
-
-def place_kernel(
+    weight_product(delta_one_ref, x_now, keep_ref, send_ref, 0)
+    weight_product(act_two_ref, join_tiles(adj_ref).astype(BF16), keep_ref, send_ref, fields)
+
+
+def place_back(fresh, live, cols_ref, cells):
+    marks = jnp.broadcast_to(live, (16, live.shape[1]))
+    placed = lax.dot_general(
+        jnp.concatenate([fresh * live, marks], axis=0).astype(BF16),
+        one_hot(cols_ref, cells),
+        CONTRACT_LAST,
+        preferred_element_type=F32,
+    )
+    rows = fresh.shape[0]
+    return placed[:rows], placed[rows : rows + 1] > 0.5
+
+
+def state_kernel(
     count_ref,
     moved_ref,
-    cot_ref,
     cols_ref,
     mask_ref,
     x_ref,
     act_two_ref,
-    delta_one_ref,
-    adj_ref,
     coef_ref,
     ratio_ref,
     inverse_ref,
-    w_in_ref,
     w_out_ref,
     state_ref,
-    field_ref,
-    up_ref,
-    down_ref,
     forced_ref,
     solved_ref,
     *,
@@ -336,28 +345,39 @@
     tendency = jnp.dot(w_out_ref[...], act_two_ref[...], preferred_element_type=F32)
     split_tiles(forced_ref, x_ref[...].astype(F32) + tendency)
     solve(levels, fields // levels, coef_ref, ratio_ref, inverse_ref, forced_ref, solved_ref)
+    placed, taken = place_back(
+        join_tiles(solved_ref), live_row(count_ref, mask_ref), cols_ref, lons * lats
+    )
+    for lon in range(lons):
+        here = slice(lon * lats, (lon + 1) * lats)
+        state_ref[pl.ds(lon, fields, stride=lons), :] = jnp.where(
+            taken[:, here], placed[:, here], moved_ref[lon]
+        )
+
+
+def grad_kernel(
+    count_ref,
+    cot_ref,
+    cols_ref,
+    mask_ref,
+    delta_one_ref,
+    adj_ref,
+    w_in_ref,
+    field_ref,
+    up_ref,
+    down_ref,
+    *,
+    lons,
+):
+    fields, lats = field_ref.shape[1:]
     grad_x = join_tiles(adj_ref) + lax.dot_general(
         w_in_ref[...], delta_one_ref[...], CONTRACT_FIRST, preferred_element_type=F32
     )
-    live = live_row(count_ref, mask_ref)
-    fresh = jnp.concatenate(
-        [
-            join_tiles(solved_ref) * live,
-            grad_x * live,
-            jnp.broadcast_to(live, (16, live.shape[1])),
-        ],
-        axis=0,
-    ).astype(BF16)
-    spread = one_hot(cols_ref, lons * lats)
-    placed = lax.dot_general(fresh, spread, CONTRACT_LAST, preferred_element_type=F32)
+    placed, taken = place_back(grad_x, live_row(count_ref, mask_ref), cols_ref, lons * lats)
     for lon in range(lons):
         here = slice(lon * lats, (lon + 1) * lats)
-        taken = placed[2 * fields : 2 * fields + 1, here] > 0.5
-        state_ref[pl.ds(lon, fields, stride=lons), :] = jnp.where(
-            taken, placed[:fields, here], moved_ref[lon]
-        )
         field_now = jnp.where(
-            taken, placed[fields : 2 * fields, here], cot_ref[pl.ds(lon, fields, stride=lons), :]
+            taken[:, here], placed[:, here], cot_ref[pl.ds(lon, fields, stride=lons), :]
         )
         field_ref[lon] = field_now
         if lon < 2:
@@ -379,113 +399,133 @@
         out_ref[pl.ds(lon, fields, stride=lons), :] = rows[lon]
 
 
-def core_sum_kernel(place_ref, keep_ref, got_ref, *outs):
-    rows = outs[0].shape[0]
-    for k, out_ref in enumerate(outs):
-        here = pl.ds(pl.multiple_of((place_ref[0, 1] ^ k) * rows, rows), rows)
-        out_ref[...] = (keep_ref[here, :].astype(F32) + got_ref[here, :].astype(F32)).astype(BF16)
-
-
-def sum_kernel(place_ref, *refs, terms, which, factor):
+CORE = ("horiz", 0, 2)
+NEAR, FAR = ("horiz", 1, 2), ("horiz", 2, 2)
+CHIPS = ("horiz", 1, 4)
+MEMBER_LOW, MEMBER_HIGH = ("ens", 0, 2), ("ens", 1, 2)
+MEMBERS = ("ens", 0, 4)
+
+
+def position(stage):
+    axis, shift, parts = stage
+    return lax.axis_index(axis) // (1 << shift) % parts
+
+
+def sum_kernel(*refs, terms, stage, factor):
     ins, outs = refs[:terms], refs[terms:]
     rows = outs[0].shape[0]
     for k, out_ref in enumerate(outs):
-        start = pl.multiple_of((place_ref[0, which] ^ k) * rows, rows) if len(outs) > 1 else 0
-        total = ins[0][pl.ds(start, rows), :].astype(F32)
+        here = pl.ds(0, rows)
+        if stage is not None:
+            here = pl.ds(pl.multiple_of((position(stage) ^ k) * rows, rows), rows)
+        total = ins[0][here, :].astype(F32)
         for ref in ins[1:]:
-            total = total + ref[pl.ds(start, rows), :].astype(F32)
+            total = total + ref[here, :].astype(F32)
         out_ref[...] = (total * factor).astype(BF16)
 
 
-def join_kernel(place_ref, *refs, which):
+def join_kernel(*refs, stage):
     ins, out_ref = refs[:-1], refs[-1]
     rows = ins[0].shape[0]
     for k, ref in enumerate(ins):
-        out_ref[pl.ds(pl.multiple_of((place_ref[0, which] ^ k) * rows, rows), rows), :] = ref[...]
-
-
-def final_kernel(place_ref, own_one, got_one, own_two, got_two, mid_ref, in_ref, out_ref):
-    rows, first = own_one.shape
+        here = pl.ds(pl.multiple_of((position(stage) ^ k) * rows, rows), rows)
+        out_ref[here, :] = ref[...]
+
+
+def merge_kernel(*refs, terms, factor):
+    out_ref = refs[-1]
+    first = 0
+    for group in (refs[:terms], refs[terms:-1]):
+        total = group[0][...].astype(F32)
+        for ref in group[1:]:
+            total = total + ref[...].astype(F32)
+        columns = total.shape[1]
+        out_ref[:, first : first + columns] = (total * factor).astype(BF16)
+        first += columns
+
+
+def final_kernel(
+    own_mid, got_mid, own_small, got_small, mid_ref, in_ref, out_ref, sorted_ref, *, swapped
+):
+    rows = own_mid.shape[0]
     fields = in_ref.shape[1]
-    rest = mid_ref.shape[1] - first
-    for one_ref, two_ref, half in (
-        (own_one, own_two, place_ref[0, 0]),
-        (got_one, got_two, 1 - place_ref[0, 0]),
+    core = lax.axis_index("horiz") % 2
+    outer, inner = swapped
+    block = rows // (outer * inner)
+    for mid_half, small_half, half in (
+        (own_mid, own_small, core),
+        (got_mid, got_small, 1 - core),
     ):
         here = pl.ds(pl.multiple_of(half * rows, rows), rows)
-        mid_ref[here, :first] = one_ref[...].astype(F32)
-        mid_ref[here, first:] = two_ref[:, :rest].astype(F32)
-        in_ref[here, :] = two_ref[:, rest : rest + fields].astype(F32)
-        out_ref[:, here] = two_ref[:, rest + fields :].astype(F32).T
-
-
-def exchange(arrays, axis, stride):
+        mid_ref[here, :] = mid_half[...].astype(F32)
+
+        @pl.when(pl.program_id(0) == 0)
+        def _():
+            for place in range(outer * inner):
+                target = (place % inner * outer + place // inner) * block
+                sorted_ref[target : target + block, :] = small_half[
+                    place * block : (place + 1) * block, :
+                ].astype(F32)
+            in_ref[here, :] = sorted_ref[:, :fields]
+            out_ref[:, here] = sorted_ref[:, fields:].T
+
+
+def exchange(arrays, stage):
+    axis, shift, _ = stage
     count = lax.axis_size(axis)
     return [
-        lax.ppermute(array, axis, [(i, i ^ (k * stride)) for i in range(count)])
+        lax.ppermute(array, axis, [(i, i ^ (k << shift)) for i in range(count)])
         for k, array in enumerate(arrays, 1)
     ]
 
 
-def sum_over_all(place, keep, send, factor, beside=None):
-    members = lax.axis_size("ens")
-    chips = lax.axis_size("horiz") // 2
-    half, columns = keep.shape
-    quarter = half // members
-    eighth = quarter // chips
-    size = half * columns
-    (got,) = exchange([send], "horiz", 1)
-    parts = call(
-        core_sum_kernel,
-        [((quarter, columns), BF16)] * members,
-        smem=(0,),
-        flops=size,
-        moved=size * 6,
-    )(place, keep, got)
-    terms = [parts[0]] + exchange(parts[1:], "ens", 1)
-    if beside is not None:
-        terms, beside = lax.optimization_barrier((terms, beside))
-    if eighth % 16 == 0 and chips <= 8:
-        parts = call(
-            sum_kernel,
-            [((eighth, columns), BF16)] * chips,
-            smem=(0,),
-            flops=size,
-            moved=size * 2,
-            terms=members,
-            which=2,
-            factor=1.0,
-        )(place, *terms)
-        terms = [parts[0]] + exchange(parts[1:], "horiz", 2)
-        (own,) = call(
-            sum_kernel,
-            [((eighth, columns), BF16)],
-            smem=(0,),
-            flops=size,
-            moved=size,
-            terms=chips,
-            which=2,
-            factor=factor,
-        )(place, *terms)
-        (own,) = call(
-            join_kernel, [((quarter, columns), BF16)], smem=(0,), moved=size, which=2
-        )(place, own, *exchange([own] * (chips - 1), "horiz", 2))
-    else:
-        (own,) = call(
-            sum_kernel,
-            [((quarter, columns), BF16)],
-            smem=(0,),
-            terms=members,
-            which=2,
-            factor=1.0,
-        )(place, *terms)
-        core = place[0, 0]
-        both = jnp.stack([jnp.where(core == side, own, 0.0).astype(F32) for side in range(2)])
-        own = (lax.psum(both, "horiz")[core] * factor).astype(BF16)
-    (own,) = call(
-        join_kernel, [((half, columns), BF16)], smem=(0,), moved=size * 4, which=1
-    )(place, own, *exchange([own] * (members - 1), "ens", 1))
-    return own, exchange([own], "horiz", 1)[0], beside
+def add(terms, stage, factor=1.0):
+    rows, columns = terms[0].shape
+    parts = 1 if stage is None else stage[2]
+    return call(
+        sum_kernel,
+        [((rows // parts, columns), BF16)] * parts,
+        terms=len(terms),
+        stage=stage,
+        factor=factor,
+    )(*terms)
+
+
+def join(pieces, stage):
+    rows, columns = pieces[0].shape
+    (joined,) = call(
+        join_kernel,
+        [((rows * len(pieces), columns), BF16)],
+        stage=stage,
+    )(*pieces)
+    return joined
+
+
+def reduce_to(terms, stage):
+    parts = add(terms, stage)
+    return [parts[0]] + exchange(parts[1:], stage)
+
+
+def collect(piece, stage):
+    return [piece] + exchange([piece] * (stage[2] - 1), stage)
+
+
+def merge(terms_mid, terms_small, factor):
+    rows = terms_mid[0].shape[0]
+    columns = terms_mid[0].shape[1] + terms_small[0].shape[1]
+    return call(
+        merge_kernel, [((rows, columns), BF16)], terms=len(terms_mid), factor=factor
+    )(*terms_mid, *terms_small)[0]
+
+
+def tie(*values):
+    return lax.optimization_barrier(values)
+
+
+def over_all_chips(piece, factor):
+    core = lax.axis_index("horiz") % 2
+    both = jnp.stack([jnp.where(core == side, piece, 0.0).astype(F32) for side in range(2)])
+    return (lax.psum(both, "horiz")[core] * factor).astype(BF16)
 
 
 def to_neighbours(upward, downward, axis):
@@ -508,90 +548,121 @@
     diff_rows = diffusivity.reshape(levels * lons, lats)
     mix_rows = mixing.reshape(2 * lons, lats)
     cols, mask = tile_cols[0, 0], pad_mask[0, 0]
-    horiz = lax.axis_index("horiz")
-    place = jnp.stack([horiz % 2, lax.axis_index("ens"), horiz // 2]).reshape(1, 3)
 
     packed = ((2 * fields + PACK_ROWS, lats), BF16)
-    up_pack, down_pack = call(pack_kernel, [packed, packed], lons=lons)(prog_rows, mix_rows)
+    up_pack, down_pack, prog_rows, mix_rows = call(
+        pack_kernel,
+        [packed, packed, (prog_rows.shape, F32), (mix_rows.shape, F32)],
+        moved=20 * 10**6,
+        lons=lons,
+    )(prog_rows, mix_rows)
     low_pack, high_pack = to_neighbours(up_pack, down_pack, "horiz")
 
-    adjoint, coef, ratio, inverse = call(
+    adjoint, coef, ratio, inverse, w_in, w_mid, w_out = call(
         adjoint_kernel,
-        [((tiles, fields, width), F32)] + [((levels, slots), F32)] * 3,
+        [((tiles, fields, width), F32)]
+        + [((levels, slots), F32)] * 3
+        + [(weight.shape, BF16) for weight in (w_in, w_mid, w_out)],
         scratch=[pltpu.VMEM((tiles, fields, width), F32)],
         smem=(0,),
-        flops=10**9,
-        moved=10**6,
+        moved=30 * 10**6,
         lons=lons,
-    )(tile_count, diff_rows, cot_rows, cols, mask)
+    )(tile_count, diff_rows, cot_rows, cols, mask, w_in, w_mid, w_out)
 
     hidden = ((units, slots), BF16)
-    first = (units + 2 * fields) // 2
-    chunk = ((units // 2, first), BF16)
-    moved, x_now, act_one, act_two, delta_two, keep, send = call(
+    half = ((units // 2, units), BF16)
+    moved, x_now, act_one, act_two, delta_two, keep_mid, send_mid = call(
         forward_kernel,
-        [((lons, fields, lats), F32), ((fields, slots), BF16), hidden, hidden, hidden, chunk, chunk],
-        smem=(0,),
-        flops=2 * 10**9,
-        moved=6 * 10**6,
+        [((lons, fields, lats), F32), ((fields, slots), BF16), hidden, hidden, hidden, half, half],
+        moved=15 * 10**6,
         lons=lons,
-    )(place, prog_rows, low_pack, high_pack, mix_rows, cols, adjoint, w_in, w_mid, w_out)
+    )(prog_rows, low_pack, high_pack, mix_rows, cols, adjoint, w_in, w_mid, w_out)
     column_total = lax.axis_size("ens") * lax.axis_size("horiz") * lons * lats
     factor = 1.0 / math.sqrt(column_total)
-    chunk_one = (keep, send)
-
-    chunk = ((units // 2, units + 2 * fields - first), BF16)
-    delta_one, keep, send = call(
-        backward_kernel,
-        [hidden, chunk, chunk],
-        smem=(0,),
-        flops=2 * 10**9,
-        moved=6 * 10**6,
-    )(place, x_now, act_one, act_two, delta_two, adjoint, w_in, w_mid)
-    chunk_two = (keep, send)
-
-    state_rows, grad_field, up_rows, down_rows = call(
-        place_kernel,
-        [
-            ((fields * lons, lats), F32),
-            ((lons, fields, lats), F32),
-            ((2 * fields, lats), BF16),
-            ((2 * fields, lats), BF16),
+    (got_mid,) = exchange([send_mid], CORE)
+
+    half = ((units // 2, 2 * fields), BF16)
+    delta_one, keep_small, send_small = call(
+        backward_kernel, [hidden, half, half], moved=4 * 10**6
+    )(x_now, act_two, delta_two, adjoint, w_in, w_mid)
+    got_mid, keep_small = tie(got_mid, keep_small)
+    (got_small,) = exchange([send_small], CORE)
+
+    def new_state(act_two):
+        return call(
+            state_kernel,
+            [((fields * lons, lats), F32)],
+            scratch=[pltpu.VMEM((tiles, fields, width), F32)] * 2,
+            smem=(0,),
+            lons=lons,
+        )(tile_count, moved, cols, mask, x_now, act_two, coef, ratio, inverse, w_out)[0]
+
+    def new_field(delta_one):
+        packed = ((2 * fields, lats), BF16)
+        return call(
+            grad_kernel,
+            [((lons, fields, lats), F32), packed, packed],
+            smem=(0,),
+            lons=lons,
+        )(tile_count, cot_rows, cols, mask, delta_one, adjoint, w_in)
+
+    def finish(field, halos):
+        return call(last_kernel, [((fields * lons, lats), F32)], lons=lons)(
+            field, *halos, low_pack, high_pack, mix_rows
+        )[0]
+
+    terms_mid = reduce_to([keep_mid, got_mid], MEMBERS)
+    fast = lax.axis_size("ens") == 4 and lax.axis_size("horiz") == 8
+    if fast:
+        terms_small = reduce_to([keep_small, got_small], FAR)
+        terms_small, delta_one = tie(terms_small, delta_one)
+        terms_small = reduce_to(terms_small, NEAR)
+        field, up_rows, down_rows = new_field(delta_one)
+        terms_mid, terms_small, field = tie(terms_mid, terms_small, field)
+
+        terms_mid = reduce_to(terms_mid, CHIPS)
+        terms_small = reduce_to(terms_small, MEMBER_HIGH)
+        terms_small, act_two = tie(terms_small, act_two)
+        terms_small = reduce_to(terms_small, MEMBER_LOW)
+        state_rows = new_state(act_two)
+        terms_mid, terms_small, state_rows, up_rows, down_rows = tie(
+            terms_mid, terms_small, state_rows, up_rows, down_rows
+        )
+
+        piece = merge(terms_mid, terms_small, factor)
+        pieces = collect(piece, CHIPS)
+        halos = to_neighbours(up_rows, down_rows, "horiz")
+        pieces, halos = tie(pieces, halos)
+        pieces = collect(join(pieces, CHIPS), MEMBERS)
+        grad_rows = finish(field, halos)
+    else:
+        state_rows = new_state(act_two)
+        field, up_rows, down_rows = new_field(delta_one)
+        grad_rows = finish(field, to_neighbours(up_rows, down_rows, "horiz"))
+        terms_small = reduce_to([keep_small, got_small], MEMBERS)
+        pieces = collect(over_all_chips(merge(terms_mid, terms_small, 1.0), factor), MEMBERS)
+    pieces, grad_rows = tie(pieces, grad_rows)
+    own = join(pieces, MEMBERS)
+    (got,) = exchange([own], CORE)
+    block = units // 4
+    mid_half = pl.BlockSpec((units // 2, block), lambda step: (0, step))
+    small_half = pl.BlockSpec((units // 2, 2 * fields), lambda step: (0, units // (2 * fields)))
+    grad_mid, grad_in, grad_out = pl.pallas_call(
+        functools.partial(final_kernel, swapped=(4, 4) if fast else (1, 1)),
+        grid=(units // block,),
+        out_shape=[
+            jax.ShapeDtypeStruct(shape, F32)
+            for shape in ((units, units), (units, fields), (fields, units))
         ],
-        scratch=[pltpu.VMEM((tiles, fields, width), F32)] * 2,
-        smem=(0,),
-        flops=10**9,
-        moved=3 * 10**6,
-        lons=lons,
-    )(
-        tile_count,
-        moved,
-        cot_rows,
-        cols,
-        mask,
-        x_now,
-        act_two,
-        delta_one,
-        adjoint,
-        coef,
-        ratio,
-        inverse,
-        w_in,
-        w_out,
-    )
-    low_rows, high_rows = to_neighbours(up_rows, down_rows, "horiz")
-    (grad_rows,) = call(
-        last_kernel, [((fields * lons, lats), F32)], flops=10**6, moved=10**6, lons=lons
-    )(grad_field, low_rows, high_rows, low_pack, high_pack, mix_rows)
-
-    own_one, got_one, grad_rows = sum_over_all(place, *chunk_one, factor, grad_rows)
-    own_two, got_two, _ = sum_over_all(place, *chunk_two, factor)
-    grad_mid, grad_in, grad_out = call(
-        final_kernel,
-        [((units, units), F32), ((units, fields), F32), ((fields, units), F32)],
-        smem=(0,),
-        moved=8 * 10**6,
-    )(place, own_one, got_one, own_two, got_two)
+        in_specs=[mid_half, mid_half, small_half, small_half],
+        out_specs=[
+            pl.BlockSpec((units, block), lambda step: (0, step)),
+            pl.BlockSpec((units, fields), lambda step: (0, 0)),
+            pl.BlockSpec((fields, units), lambda step: (0, 0)),
+        ],
+        scratch_shapes=[pltpu.VMEM((units // 2, 2 * fields), F32)],
+        compiler_params=pltpu.CompilerParams(vmem_limit_bytes=VMEM_LIMIT),
+    )(own, got, own, got)
     return (
         state_rows.reshape(prognostic.shape),
         grad_rows.reshape(prognostic.shape),

time: 93.8 us -> 82.9 us (0.88)
  Pallas kernels: 20.5 us -> 14.3 us
  starting transfers between devices: 35 us -> 29.3 us
  waiting for transfers between devices: 27 us -> 29.8 us
  local copies, waits for them, and re-layouts: 9.27 us -> 7.61 us
    pallas_call x17 -> x16, Pallas kernels: 20.5 us -> 11.1 us  [run(): pl.pallas_call(functools.partial(kernel, **names), out_shape=[jax.ShapeDt...]
    ppermute x28 -> x19, starting transfers between devices: 30.4 us -> 21.2 us  [exchange(): lax.ppermute(array, axis, [(i, i ^ k << shift) for i in range(count)])]
    ppermute x28 -> x19, waiting for transfers between devices: 19.6 us -> 27.7 us  [exchange(): lax.ppermute(array, axis, [(i, i ^ k << shift) for i in range(count)])]
    ppermute x2, starting transfers between devices: 4.1 us -> 7.64 us  [to_neighbours(): lax.ppermute(downward, axis, backward)]
    ppermute x2, waiting for transfers between devices: 5.49 us -> 2.1 us  [to_neighbours(): lax.ppermute(upward, axis, forward)]
    pallas_call x0 -> x1, Pallas kernels: none -> 3.15 us  [per_device(): pl.pallas_call(functools.partial(final_kernel, swapped=(4, 4) if fast els...]
    ppermute x2, waiting for transfers between devices: 1.91 us -> 0.01 us  [to_neighbours(): lax.ppermute(downward, axis, backward)]
    unnamed x29 -> x17, local copies, waits for them, and re-layouts: 9.27 us -> 7.61 us
  transfers between devices with their start and end apart: 32 -> 23, of which waited for: 13 -> 9; matrix products, arithmetic and copies ran while one was open for 1% -> 1% of each run, Pallas kernels for 14% -> 9%
where the time goes in v5:
time: 82.9 us; the launch traced here: 82.5 us
  waiting for transfers between devices  29.8 us (36%)
  starting transfers between devices  29.3 us (35%)
  Pallas kernels  14.3 us (17%)
  local copies, waits for them, and re-layouts  7.61 us (9%)
  between operations  1.48 us (2%)
    ppermute x19, waiting for transfers between devices, exchange(): lax.ppermute(array, axis, [(i, i ^ k << shift) for i in range(count)])  27.7 us
    ppermute x19, starting transfers between devices, exchange(): lax.ppermute(array, axis, [(i, i ^ k << shift) for i in range(count)])  21.2 us
    pallas_call x16, Pallas kernels, run(): pl.pallas_call(functools.partial(kernel, **names), out_shape=[jax.ShapeDt...  11.1 us
    ppermute x2, starting transfers between devices, to_neighbours(): lax.ppermute(downward, axis, backward)  7.64 us
    unnamed x17, local copies, waits for them, and re-layouts  7.61 us
    pallas_call x1, Pallas kernels, per_device(): pl.pallas_call(functools.partial(final_kernel, swapped=(4, 4) if fast els...  3.15 us
    ppermute x2, waiting for transfers between devices, to_neighbours(): lax.ppermute(upward, axis, forward)  2.1 us
  transfers between devices with their start and end apart: 23, of which 9 were waited for; matrix products, arithmetic and copies ran while one was open for 1% of the time, Pallas kernels for 9%

profile of v5, /device:TPU:0, one launch (start us, length us, event | category | flops | bytes accessed | tf_op | source)
XLA Modules:
  0.0 82.5 jit_solution(3849155643799405399)
XLA Ops:
  0.6 0.9 %copy-done.5 = f32[1,128,4,128]{3,2,1,0:T(4,128)S(1)} copy-done((f32[1,128,4,128]{3,2,1,0:T(4,128)S(1)}, f32[1,128,4,128]{3,2,1,0:T(4,128)}, u32[]{:S(2)}) %copy-start.5) | copy-done | bytes 262168
  2.8 4.1 %collective-permute-start.1 = (bf16[272,128]{1,0:T(8,128)(2,1)S(1)}, bf16[272,128]{1,0:T(8,128)(2,1)S(1)}, u32[]{:S(2)}, u32[]{:S(2)}) collective-permute-start(bf16[272,128]{1,0:T(8,128)(2,1)S(1)} %get-tuple-element.84), channel_id=1, source_target_pairs={{1,0},{2,1},{3,2},{4,3},{5,4},{6,5},{7,6},{0,7},{9,8},{10,9},{11,1... | collective-permute-start | bytes 208904 | tf_op jit(solution)/shard_map/ppermute | solution.py:535
  6.9 0.7 copy_bitcast_fusion
  8.3 1.6 %copy-done = bf16[1024,1024]{1,0:T(8,128)(2,1)S(1)} copy-done((bf16[1024,1024]{1,0:T(8,128)(2,1)S(1)}, bf16[1024,1024]{1,0:T(8,128)(2,1)}, u32[]{:S(2)}) %copy-start) | copy-done | bytes 2097176
  9.9 0.9 %copy-done.1 = f32[1,128,4,128]{3,2,1,0:T(4,128)S(1)} copy-done((f32[1,128,4,128]{3,2,1,0:T(4,128)S(1)}, f32[1,128,4,128]{3,2,1,0:T(4,128)}, u32[]{:S(2)}) %copy-start.1) | copy-done | bytes 262168
  10.8 0.9 %copy-done.3 = bf16[1024,128]{1,0:T(8,128)(2,1)S(1)} copy-done((bf16[1024,128]{1,0:T(8,128)(2,1)S(1)}, bf16[1024,128]{1,0:T(8,128)(2,1)}, u32[]{:S(2)}) %copy-start.3) | copy-done | bytes 262168
  11.8 0.9 %copy-done.4 = bf16[128,1024]{1,0:T(8,128)(2,1)S(1)} copy-done((bf16[128,1024]{1,0:T(8,128)(2,1)S(1)}, bf16[128,1024]{1,0:T(8,128)(2,1)}, u32[]{:S(2)}) %copy-start.4) | copy-done | bytes 262168
  12.7 0.8 %copy-done.6 = f32[1,32,4,128]{3,2,1,0:T(4,128)S(1)} copy-done((f32[1,32,4,128]{3,2,1,0:T(4,128)S(1)}, f32[1,32,4,128]{3,2,1,0:T(4,128)}, u32[]{:S(2)}) %copy-start.6) | copy-done | bytes 65560
  13.6 0.9 %shard_map.138 = (f32[3,128,128]{2,1,0:T(8,128)S(1)}, f32[32,384]{1,0:T(8,128)S(1)}, f32[32,384]{1,0:T(8,128)S(1)}, f32[32,384]{1,0:T(8,128)S(1)}, bf16[1024,128...) custom-call(s32[1,1]{1,0:T(1,128)S(6)} %copy.19.count_ref, ...), custom_call_target="tpu_custom_call" | custom-call | bytes 30000000 | tf_op jit(solution)/shard_map/pallas_call | solution.py:27
  14.5 3.6 %shard_map.139 = (f32[4,128,128]{2,1,0:T(8,128)S(1)}, bf16[128,384]{1,0:T(8,128)(2,1)S(1)}, bf16[1024,384]{1,0:T(8,128)(2,1)}, bf16[1024,384]{1,0:T(8,128)(2,1)S...) custom-call(f32[512,128]{1,0:T(8,128)S(1)} %get-tuple-element.82.prog_ref, ...), custom_call_target="tpu_custom_call" | custom-call | bytes 15000000 | tf_op jit(solution)/shard_map/pallas_call | solution.py:27
  18.2 2.2 %shard_map.140 = (bf16[1024,384]{1,0:T(8,128)(2,1)S(1)}, bf16[512,256]{1,0:T(8,128)(2,1)S(1)}, bf16[512,256]{1,0:T(8,128)(2,1)S(1)}) custom-call(bf16[128,384]{1,0:T(8,128)(2,1)S(1)} %get-tuple-element.92.x_ref, bf16[1024,384]{1,0:T(8,128)(2,1)S(1)} %get-tuple-element.129.act_two_ref, bf16[1024,384]{1,0:T(8,128)(2,1)S(1)} %get-tuple-element.94.delta_two_ref, ...), custom_call_target="tpu_custom_call" | custom-call | bytes 4000000 | tf_op jit(solution)/shard_map/pallas_call | solution.py:27
  21.3 2.0 %collective-permute-start.3 = (bf16[128,1024]{1,0:T(8,128)(2,1)S(1)}, bf16[128,1024]{1,0:T(8,128)(2,1)S(1)}, u32[]{:S(2)}, u32[]{:S(2)}) collective-permute-start(bf16[128,1024]{1,0:T(8,128)(2,1)S(1)} %get-tuple-element.98), channel_id=1, source_target_pairs={{0,8},{8,0},{16,24},{24,16},{1,9},{9,1},{17,25},{25,17},{2,10},{10... | collective-permute-start | bytes 786440 | tf_op jit(solution)/shard_map/ppermute | solution.py:477
  23.3 1.5 %collective-permute-start.4 = (bf16[128,1024]{1,0:T(8,128)(2,1)S(1)}, bf16[128,1024]{1,0:T(8,128)(2,1)S(1)}, u32[]{:S(2)}, u32[]{:S(2)}) collective-permute-start(bf16[128,1024]{1,0:T(8,128)(2,1)S(1)} %get-tuple-element.99), channel_id=1, source_target_pairs={{0,16},{8,24},{16,0},{24,8},{1,17},{9,25},{17,1},{25,9},{2,18},{10... | collective-permute-start | bytes 786440 | tf_op jit(solution)/shard_map/ppermute | solution.py:477
  24.9 1.3 %collective-permute-start.7 = (bf16[256,256]{1,0:T(8,128)(2,1)S(1)}, bf16[256,256]{1,0:T(8,128)(2,1)S(1)}, u32[]{:S(2)}, u32[]{:S(2)}) collective-permute-start(bf16[256,256]{1,0:T(8,128)(2,1)S(1)} %get-tuple-element.104), channel_id=1, source_target_pairs={{0,4},{1,5},{2,6},{3,7},{4,0},{5,1},{6,2},{7,3},{8,12},{9,13},{10,... | collective-permute-start | bytes 393224 | tf_op jit(solution)/shard_map/ppermute | solution.py:477
  26.2 6.7 %collective-permute-done.7.refs_1_ = bf16[256,256]{1,0:T(8,128)(2,1)S(1)} collective-permute-done((bf16[256,256]{1,0:T(8,128)(2,1)S(1)}, bf16[256,256]{1,0:T(8,128)(2,1)S(1)}, u32[]{:S(2)}, u32[]{:S(2)}) %collective-permute-start.7) | collective-permute-done | bytes 131104 | tf_op jit(solution)/shard_map/ppermute | solution.py:477
  33.6 3.7 %collective-permute-done.8.refs_1_ = bf16[128,256]{1,0:T(8,128)(2,1)S(1)} collective-permute-done((bf16[128,256]{1,0:T(8,128)(2,1)S(1)}, bf16[128,256]{1,0:T(8,128)(2,1)S(1)}, u32[]{:S(2)}, u32[]{:S(2)}) %collective-permute-start.8) | collective-permute-done | bytes 65568 | tf_op jit(solution)/shard_map/ppermute | solution.py:477
  37.5 3.0 %collective-permute-start.10 = (bf16[32,1024]{1,0:T(8,128)(2,1)S(1)}, bf16[32,1024]{1,0:T(8,128)(2,1)S(1)}, u32[]{:S(2)}, u32[]{:S(2)}) collective-permute-start(bf16[32,1024]{1,0:T(8,128)(2,1)S(1)} %get-tuple-element.118), channel_id=1, source_target_pairs={{0,4},{1,5},{2,6},{3,7},{4,0},{5,1},{6,2},{7,3},{8,12},{9,13},{10,... | collective-permute-start | bytes 196616 | tf_op jit(solution)/shard_map/ppermute | solution.py:477
  40.6 1.4 %collective-permute-start.11 = (bf16[32,1024]{1,0:T(8,128)(2,1)S(1)}, bf16[32,1024]{1,0:T(8,128)(2,1)S(1)}, u32[]{:S(2)}, u32[]{:S(2)}) collective-permute-start(bf16[32,1024]{1,0:T(8,128)(2,1)S(1)} %get-tuple-element.119), channel_id=1, source_target_pairs={{0,6},{1,7},{2,4},{3,5},{4,2},{5,3},{6,0},{7,1},{8,14},{9,15},{10,... | collective-permute-start | bytes 196616 | tf_op jit(solution)/shard_map/ppermute | solution.py:477
  41.9 1.6 %collective-permute-start.12 = (bf16[64,256]{1,0:T(8,128)(2,1)S(1)}, bf16[64,256]{1,0:T(8,128)(2,1)S(1)}, u32[]{:S(2)}, u32[]{:S(2)}) collective-permute-start(bf16[64,256]{1,0:T(8,128)(2,1)S(1)} %get-tuple-element.123), channel_id=1, source_target_pairs={{0,16},{8,24},{16,0},{24,8},{1,17},{9,25},{17,1},{25,9},{2,18},{10... | collective-permute-start | bytes 98312 | tf_op jit(solution)/shard_map/ppermute | solution.py:477
  43.5 2.4 %collective-permute-done.12.refs_1_ = bf16[64,256]{1,0:T(8,128)(2,1)S(1)} collective-permute-done((bf16[64,256]{1,0:T(8,128)(2,1)S(1)}, bf16[64,256]{1,0:T(8,128)(2,1)S(1)}, u32[]{:S(2)}, u32[]{:S(2)}) %collective-permute-start.12) | collective-permute-done | bytes 32800 | tf_op jit(solution)/shard_map/ppermute | solution.py:477
  45.9 1.6 %collective-permute-start.13 = (bf16[32,256]{1,0:T(8,128)(2,1)S(1)}, bf16[32,256]{1,0:T(8,128)(2,1)S(1)}, u32[]{:S(2)}, u32[]{:S(2)}) collective-permute-start(bf16[32,256]{1,0:T(8,128)(2,1)S(1)} %get-tuple-element.127), channel_id=1, source_target_pairs={{0,8},{8,0},{16,24},{24,16},{1,9},{9,1},{17,25},{25,17},{2,10},{10... | collective-permute-start | bytes 49160 | tf_op jit(solution)/shard_map/ppermute | solution.py:477
  47.5 1.6 %shard_map.148 = f32[512,128]{1,0:T(8,128)} custom-call(s32[1,1]{1,0:T(1,128)S(6)} %copy.19.count_ref, f32[4,128,128]{2,1,0:T(8,128)S(1)} %get-tuple-element.128.moved_ref, s32[3,128]{1,0:T(4,128)S(1)} %get-tuple-element.160.cols_ref, s32[3,128]{1,0:T(4,128)S(1)} %get-tuple-element.159.mask_ref, bf16[128,384]{1,0:T(8,128)(2,1)S(1)} %get-tuple-element.92.x_ref, ...), custom_call_target="tpu_custom_call" | custom-call | tf_op jit(solution)/shard_map/pallas_call | solution.py:27
  49.8 2.5 %collective-permute-start.16 = (bf16[32,1280]{1,0:T(8,128)(2,1)S(1)}, bf16[32,1280]{1,0:T(8,128)(2,1)S(1)}, u32[]{:S(2)}, u32[]{:S(2)}) collective-permute-start(bf16[32,1280]{1,0:T(8,128)(2,1)S(1)} %shard_map.149.refs_0_), channel_id=1, source_target_pairs={{0,6},{1,7},{2,4},{3,5},{4,2},{5,3},{6,0},{7,1},{8,14},{9,15},{10,... | collective-permute-start | bytes 245768 | tf_op jit(solution)/shard_map/ppermute | solution.py:477
  52.3 1.9 %collective-permute-start.14 = (bf16[32,1280]{1,0:T(8,128)(2,1)S(1)}, bf16[32,1280]{1,0:T(8,128)(2,1)S(1)}, u32[]{:S(2)}, u32[]{:S(2)}) collective-permute-start(bf16[32,1280]{1,0:T(8,128)(2,1)S(1)} %shard_map.149.refs_0_), channel_id=1, source_target_pairs={{0,2},{1,3},{2,0},{3,1},{4,6},{5,7},{6,4},{7,5},{8,10},{9,11},{10,... | collective-permute-start | bytes 245768 | tf_op jit(solution)/shard_map/ppermute | solution.py:477
  54.3 3.5 %collective-permute-start.18 = (bf16[256,128]{1,0:T(8,128)(2,1)S(1)}, bf16[256,128]{1,0:T(8,128)(2,1)S(1)}, u32[]{:S(2)}, u32[]{:S(2)}) collective-permute-start(bf16[256,128]{1,0:T(8,128)(2,1)S(1)} %get-tuple-element.143), channel_id=1, source_target_pairs={{1,0},{2,1},{3,2},{4,3},{5,4},{6,5},{7,6},{0,7},{9,8},{10,9},{11,1... | collective-permute-start | bytes 196616 | tf_op jit(solution)/shard_map/ppermute | solution.py:535
  57.8 2.1 %collective-permute-done.17.low_ref = bf16[256,128]{1,0:T(8,128)(2,1)S(1)} collective-permute-done((bf16[256,128]{1,0:T(8,128)(2,1)S(1)}, bf16[256,128]{1,0:T(8,128)(2,1)S(1)}, u32[]{:S(2)}, u32[]{:S(2)}) %collective-permute-start.17) | collective-permute-done | bytes 65568 | tf_op jit(solution)/shard_map/ppermute | solution.py:535
  60.0 2.5 %collective-permute-start.21 = (bf16[128,1280]{1,0:T(8,128)(2,1)S(1)}, bf16[128,1280]{1,0:T(8,128)(2,1)S(1)}, u32[]{:S(2)}, u32[]{:S(2)}) collective-permute-start(bf16[128,1280]{1,0:T(8,128)(2,1)S(1)} %shard_map.150.refs_0_), channel_id=1, source_target_pairs={{0,24},{8,16},{16,8},{24,0},{1,25},{9,17},{17,9},{25,1},{2,26},{10... | collective-permute-start | bytes 983048 | tf_op jit(solution)/shard_map/ppermute | solution.py:477
  63.5 1.5 %shard_map.151 = f32[512,128]{1,0:T(8,128)} custom-call(f32[4,128,128]{2,1,0:T(8,128)S(1)} %get-tuple-element.148.field_ref, bf16[256,128]{1,0:T(8,128)(2,1)S(1)} %collective-permute-done.17.low_ref, bf16[256,128]{1,0:T(8,128)(2,1)S(1)} %collective-permute-done.18.high_ref, bf16[272,128]{1,0:T(8,128)(2,1)S(1)} %collective-permute-done.low_ref.low_mix_ref, ...), custom_call_target="tpu_custom_call" | custom-call | tf_op jit(solution)/shard_map/pallas_call | solution.py:27
  65.0 6.6 %collective-permute-done.21.refs_3_ = bf16[128,1280]{1,0:T(8,128)(2,1)S(1)} collective-permute-done((bf16[128,1280]{1,0:T(8,128)(2,1)S(1)}, bf16[128,1280]{1,0:T(8,128)(2,1)S(1)}, u32[]{:S(2)}, u32[]{:S(2)}) %collective-permute-start.21) | collective-permute-done | bytes 327712 | tf_op jit(solution)/shard_map/ppermute | solution.py:477
  71.6 4.4 %collective-permute-done.20.refs_2_ = bf16[128,1280]{1,0:T(8,128)(2,1)S(1)} collective-permute-done((bf16[128,1280]{1,0:T(8,128)(2,1)S(1)}, bf16[128,1280]{1,0:T(8,128)(2,1)S(1)}, u32[]{:S(2)}, u32[]{:S(2)}) %collective-permute-start.20) | collective-permute-done | bytes 327712 | tf_op jit(solution)/shard_map/ppermute | solution.py:477
  76.3 3.0 %collective-permute-done.22.got_mid.got_small = bf16[512,1280]{1,0:T(8,128)(2,1)S(1)} collective-permute-done((bf16[512,1280]{1,0:T(8,128)(2,1)S(1)}, bf16[512,1280]{1,0:T(8,128)(2,1)S(1)}, u32[]{:S(2)}, u32[]{:S(2)}) %collective-permute-start.22) | collective-permute-done | bytes 1310752 | tf_op jit(solution)/shard_map/ppermute | solution.py:477
  79.4 3.1 %shard_map.153 = (f32[1024,1024]{1,0:T(8,128)}, f32[1024,128]{1,0:T(8,128)}, f32[128,1024]{1,0:T(8,128)}) custom-call(bf16[512,1280]{1,0:T(8,128)(2,1)S(1)} %shard_map.152.own_mid.own_small, bf16[512,1280]{1,0:T(8,128)(2,1)S(1)} %collective-permute-done.22.got_mid.got_small, bf16[512,1280]{1,0:T(8,128)(2,1)S(1)} %shard_map.152.own_mid.own_small, ...), custom_call_target="tpu_custom_call" | custom-call | tf_op jit(solution)/shard_map/pallas_call | solution.py:650
  (48 shorter events, 5.3 us)
Async XLA Ops:
  0.6 1.0 %copy-start.5 = (f32[1,128,4,128]{3,2,1,0:T(4,128)S(1)}, f32[1,128,4,128]{3,2,1,0:T(4,128)}, u32[]{:S(2)}) copy-start(f32[1,128,4,128]{3,2,1,0:T(4,128)} %param.10) | copy-start | bytes 786436
  1.6 0.7 copy-start.7
  2.3 12.2 %collective-permute-start = (bf16[272,128]{1,0:T(8,128)(2,1)S(1)}, bf16[272,128]{1,0:T(8,128)(2,1)S(1)}, u32[]{:S(2)}, u32[]{:S(2)}) collective-permute-start(bf16[272,128]{1,0:T(8,128)(2,1)S(1)} %get-tuple-element.83), channel_id=1, source_target_pairs={{0,1},{1,2},{2,3},{3,4},{4,5},{5,6},{6,7},{7,0},{8,9},{9,10},{10,1... | collective-permute-start | bytes 208904 | tf_op jit(solution)/shard_map/ppermute | solution.py:535
  2.8 11.7 %collective-permute-start.1 = (bf16[272,128]{1,0:T(8,128)(2,1)S(1)}, bf16[272,128]{1,0:T(8,128)(2,1)S(1)}, u32[]{:S(2)}, u32[]{:S(2)}) collective-permute-start(bf16[272,128]{1,0:T(8,128)(2,1)S(1)} %get-tuple-element.84), channel_id=1, source_target_pairs={{1,0},{2,1},{3,2},{4,3},{5,4},{6,5},{7,6},{0,7},{9,8},{10,9},{11,1... | collective-permute-start | bytes 208904 | tf_op jit(solution)/shard_map/ppermute | solution.py:535
  8.3 1.6 %copy-start = (bf16[1024,1024]{1,0:T(8,128)(2,1)S(1)}, bf16[1024,1024]{1,0:T(8,128)(2,1)}, u32[]{:S(2)}) copy-start(bf16[1024,1024]{1,0:T(8,128)(2,1)} %w_mid_ref.1) | copy-start | bytes 6291460
  9.9 0.9 %copy-start.1 = (f32[1,128,4,128]{3,2,1,0:T(4,128)S(1)}, f32[1,128,4,128]{3,2,1,0:T(4,128)}, u32[]{:S(2)}) copy-start(f32[1,128,4,128]{3,2,1,0:T(4,128)} %param.13) | copy-start | bytes 786436
  10.8 0.9 %copy-start.3 = (bf16[1024,128]{1,0:T(8,128)(2,1)S(1)}, bf16[1024,128]{1,0:T(8,128)(2,1)}, u32[]{:S(2)}) copy-start(bf16[1024,128]{1,0:T(8,128)(2,1)} %w_in_ref.1) | copy-start | bytes 786436
  11.8 0.9 %copy-start.4 = (bf16[128,1024]{1,0:T(8,128)(2,1)S(1)}, bf16[128,1024]{1,0:T(8,128)(2,1)}, u32[]{:S(2)}) copy-start(bf16[128,1024]{1,0:T(8,128)(2,1)} %w_out_ref.1) | copy-start | bytes 786436
  12.7 0.8 %copy-start.6 = (f32[1,32,4,128]{3,2,1,0:T(4,128)S(1)}, f32[1,32,4,128]{3,2,1,0:T(4,128)}, u32[]{:S(2)}) copy-start(f32[1,32,4,128]{3,2,1,0:T(4,128)} %param.11) | copy-start | bytes 196612
  18.1 2.9 %collective-permute-start.2 = (bf16[512,1024]{1,0:T(8,128)(2,1)S(1)}, bf16[512,1024]{1,0:T(8,128)(2,1)S(1)}, u32[]{:S(2)}, u32[]{:S(2)}) collective-permute-start(bf16[512,1024]{1,0:T(8,128)(2,1)S(1)} %get-tuple-element.91), channel_id=1, source_target_pairs={{0,1},{1,0},{2,3},{3,2},{4,5},{5,4},{6,7},{7,6},{8,9},{9,8},{10,11... | collective-permute-start | bytes 3145736 | tf_op jit(solution)/shard_map/ppermute | solution.py:477
  20.5 12.6 %copy-start.2 = (f32[1,128,4,128]{3,2,1,0:T(4,128)S(1)}, f32[1,128,4,128]{3,2,1,0:T(4,128)}, u32[]{:S(2)}) copy-start(f32[1,128,4,128]{3,2,1,0:T(4,128)} %param.13) | copy-start | bytes 786436
  20.5 4.4 %collective-permute-start.6 = (bf16[512,256]{1,0:T(8,128)(2,1)S(1)}, bf16[512,256]{1,0:T(8,128)(2,1)S(1)}, u32[]{:S(2)}, u32[]{:S(2)}) collective-permute-start(bf16[512,256]{1,0:T(8,128)(2,1)S(1)} %get-tuple-element.102), channel_id=1, source_target_pairs={{0,1},{1,0},{2,3},{3,2},{4,5},{5,4},{6,7},{7,6},{8,9},{9,8},{10,11... | collective-permute-start | bytes 786440 | tf_op jit(solution)/shard_map/ppermute | solution.py:477
  21.3 16.0 %collective-permute-start.3 = (bf16[128,1024]{1,0:T(8,128)(2,1)S(1)}, bf16[128,1024]{1,0:T(8,128)(2,1)S(1)}, u32[]{:S(2)}, u32[]{:S(2)}) collective-permute-start(bf16[128,1024]{1,0:T(8,128)(2,1)S(1)} %get-tuple-element.98), channel_id=1, source_target_pairs={{0,8},{8,0},{16,24},{24,16},{1,9},{9,1},{17,25},{25,17},{2,10},{10... | collective-permute-start | bytes 786440 | tf_op jit(solution)/shard_map/ppermute | solution.py:477
  23.3 14.0 %collective-permute-start.4 = (bf16[128,1024]{1,0:T(8,128)(2,1)S(1)}, bf16[128,1024]{1,0:T(8,128)(2,1)S(1)}, u32[]{:S(2)}, u32[]{:S(2)}) collective-permute-start(bf16[128,1024]{1,0:T(8,128)(2,1)S(1)} %get-tuple-element.99), channel_id=1, source_target_pairs={{0,16},{8,24},{16,0},{24,8},{1,17},{9,25},{17,1},{25,9},{2,18},{10... | collective-permute-start | bytes 786440 | tf_op jit(solution)/shard_map/ppermute | solution.py:477
  24.8 12.5 %collective-permute-start.5 = (bf16[128,1024]{1,0:T(8,128)(2,1)S(1)}, bf16[128,1024]{1,0:T(8,128)(2,1)S(1)}, u32[]{:S(2)}, u32[]{:S(2)}) collective-permute-start(bf16[128,1024]{1,0:T(8,128)(2,1)S(1)} %get-tuple-element.100), channel_id=1, source_target_pairs={{0,24},{8,16},{16,8},{24,0},{1,25},{9,17},{17,9},{25,1},{2,26},{10... | collective-permute-start | bytes 786440 | tf_op jit(solution)/shard_map/ppermute | solution.py:477
  24.9 8.0 %collective-permute-start.7 = (bf16[256,256]{1,0:T(8,128)(2,1)S(1)}, bf16[256,256]{1,0:T(8,128)(2,1)S(1)}, u32[]{:S(2)}, u32[]{:S(2)}) collective-permute-start(bf16[256,256]{1,0:T(8,128)(2,1)S(1)} %get-tuple-element.104), channel_id=1, source_target_pairs={{0,4},{1,5},{2,6},{3,7},{4,0},{5,1},{6,2},{7,3},{8,12},{9,13},{10,... | collective-permute-start | bytes 393224 | tf_op jit(solution)/shard_map/ppermute | solution.py:477
  33.0 4.3 %collective-permute-start.8 = (bf16[128,256]{1,0:T(8,128)(2,1)S(1)}, bf16[128,256]{1,0:T(8,128)(2,1)S(1)}, u32[]{:S(2)}, u32[]{:S(2)}) collective-permute-start(bf16[128,256]{1,0:T(8,128)(2,1)S(1)} %get-tuple-element.109), channel_id=1, source_target_pairs={{0,2},{1,3},{2,0},{3,1},{4,6},{5,7},{6,4},{7,5},{8,10},{9,11},{10,... | collective-permute-start | bytes 196616 | tf_op jit(solution)/shard_map/ppermute | solution.py:477
  37.5 12.3 %collective-permute-start.9 = (bf16[32,1024]{1,0:T(8,128)(2,1)S(1)}, bf16[32,1024]{1,0:T(8,128)(2,1)S(1)}, u32[]{:S(2)}, u32[]{:S(2)}) collective-permute-start(bf16[32,1024]{1,0:T(8,128)(2,1)S(1)} %get-tuple-element.117), channel_id=1, source_target_pairs={{0,2},{1,3},{2,0},{3,1},{4,6},{5,7},{6,4},{7,5},{8,10},{9,11},{10,... | collective-permute-start | bytes 196616 | tf_op jit(solution)/shard_map/ppermute | solution.py:477
  37.5 12.2 %collective-permute-start.10 = (bf16[32,1024]{1,0:T(8,128)(2,1)S(1)}, bf16[32,1024]{1,0:T(8,128)(2,1)S(1)}, u32[]{:S(2)}, u32[]{:S(2)}) collective-permute-start(bf16[32,1024]{1,0:T(8,128)(2,1)S(1)} %get-tuple-element.118), channel_id=1, source_target_pairs={{0,4},{1,5},{2,6},{3,7},{4,0},{5,1},{6,2},{7,3},{8,12},{9,13},{10,... | collective-permute-start | bytes 196616 | tf_op jit(solution)/shard_map/ppermute | solution.py:477
  40.6 9.2 %collective-permute-start.11 = (bf16[32,1024]{1,0:T(8,128)(2,1)S(1)}, bf16[32,1024]{1,0:T(8,128)(2,1)S(1)}, u32[]{:S(2)}, u32[]{:S(2)}) collective-permute-start(bf16[32,1024]{1,0:T(8,128)(2,1)S(1)} %get-tuple-element.119), channel_id=1, source_target_pairs={{0,6},{1,7},{2,4},{3,5},{4,2},{5,3},{6,0},{7,1},{8,14},{9,15},{10,... | collective-permute-start | bytes 196616 | tf_op jit(solution)/shard_map/ppermute | solution.py:477
  41.9 4.0 %collective-permute-start.12 = (bf16[64,256]{1,0:T(8,128)(2,1)S(1)}, bf16[64,256]{1,0:T(8,128)(2,1)S(1)}, u32[]{:S(2)}, u32[]{:S(2)}) collective-permute-start(bf16[64,256]{1,0:T(8,128)(2,1)S(1)} %get-tuple-element.123), channel_id=1, source_target_pairs={{0,16},{8,24},{16,0},{24,8},{1,17},{9,25},{17,1},{25,9},{2,18},{10... | collective-permute-start | bytes 98312 | tf_op jit(solution)/shard_map/ppermute | solution.py:477
  45.9 3.8 %collective-permute-start.13 = (bf16[32,256]{1,0:T(8,128)(2,1)S(1)}, bf16[32,256]{1,0:T(8,128)(2,1)S(1)}, u32[]{:S(2)}, u32[]{:S(2)}) collective-permute-start(bf16[32,256]{1,0:T(8,128)(2,1)S(1)} %get-tuple-element.127), channel_id=1, source_target_pairs={{0,8},{8,0},{16,24},{24,16},{1,9},{9,1},{17,25},{25,17},{2,10},{10... | collective-permute-start | bytes 49160 | tf_op jit(solution)/shard_map/ppermute | solution.py:477
  49.8 10.1 %collective-permute-start.16 = (bf16[32,1280]{1,0:T(8,128)(2,1)S(1)}, bf16[32,1280]{1,0:T(8,128)(2,1)S(1)}, u32[]{:S(2)}, u32[]{:S(2)}) collective-permute-start(bf16[32,1280]{1,0:T(8,128)(2,1)S(1)} %shard_map.149.refs_0_), channel_id=1, source_target_pairs={{0,6},{1,7},{2,4},{3,5},{4,2},{5,3},{6,0},{7,1},{8,14},{9,15},{10,... | collective-permute-start | bytes 245768 | tf_op jit(solution)/shard_map/ppermute | solution.py:477
  52.3 7.6 %collective-permute-start.15 = (bf16[32,1280]{1,0:T(8,128)(2,1)S(1)}, bf16[32,1280]{1,0:T(8,128)(2,1)S(1)}, u32[]{:S(2)}, u32[]{:S(2)}) collective-permute-start(bf16[32,1280]{1,0:T(8,128)(2,1)S(1)} %shard_map.149.refs_0_), channel_id=1, source_target_pairs={{0,4},{1,5},{2,6},{3,7},{4,0},{5,1},{6,2},{7,3},{8,12},{9,13},{10,... | collective-permute-start | bytes 245768 | tf_op jit(solution)/shard_map/ppermute | solution.py:477
  52.3 7.6 %collective-permute-start.14 = (bf16[32,1280]{1,0:T(8,128)(2,1)S(1)}, bf16[32,1280]{1,0:T(8,128)(2,1)S(1)}, u32[]{:S(2)}, u32[]{:S(2)}) collective-permute-start(bf16[32,1280]{1,0:T(8,128)(2,1)S(1)} %shard_map.149.refs_0_), channel_id=1, source_target_pairs={{0,2},{1,3},{2,0},{3,1},{4,6},{5,7},{6,4},{7,5},{8,10},{9,11},{10,... | collective-permute-start | bytes 245768 | tf_op jit(solution)/shard_map/ppermute | solution.py:477
  54.3 5.6 %collective-permute-start.17 = (bf16[256,128]{1,0:T(8,128)(2,1)S(1)}, bf16[256,128]{1,0:T(8,128)(2,1)S(1)}, u32[]{:S(2)}, u32[]{:S(2)}) collective-permute-start(bf16[256,128]{1,0:T(8,128)(2,1)S(1)} %get-tuple-element.142), channel_id=1, source_target_pairs={{0,1},{1,2},{2,3},{3,4},{4,5},{5,6},{6,7},{7,0},{8,9},{9,10},{10,1... | collective-permute-start | bytes 196616 | tf_op jit(solution)/shard_map/ppermute | solution.py:535
  54.3 5.6 %collective-permute-start.18 = (bf16[256,128]{1,0:T(8,128)(2,1)S(1)}, bf16[256,128]{1,0:T(8,128)(2,1)S(1)}, u32[]{:S(2)}, u32[]{:S(2)}) collective-permute-start(bf16[256,128]{1,0:T(8,128)(2,1)S(1)} %get-tuple-element.143), channel_id=1, source_target_pairs={{1,0},{2,1},{3,2},{4,3},{5,4},{6,5},{7,6},{0,7},{9,8},{10,9},{11,1... | collective-permute-start | bytes 196616 | tf_op jit(solution)/shard_map/ppermute | solution.py:535
  60.0 11.7 %collective-permute-start.21 = (bf16[128,1280]{1,0:T(8,128)(2,1)S(1)}, bf16[128,1280]{1,0:T(8,128)(2,1)S(1)}, u32[]{:S(2)}, u32[]{:S(2)}) collective-permute-start(bf16[128,1280]{1,0:T(8,128)(2,1)S(1)} %shard_map.150.refs_0_), channel_id=1, source_target_pairs={{0,24},{8,16},{16,8},{24,0},{1,25},{9,17},{17,9},{25,1},{2,26},{10... | collective-permute-start | bytes 983048 | tf_op jit(solution)/shard_map/ppermute | solution.py:477
  62.5 13.6 %collective-permute-start.20 = (bf16[128,1280]{1,0:T(8,128)(2,1)S(1)}, bf16[128,1280]{1,0:T(8,128)(2,1)S(1)}, u32[]{:S(2)}, u32[]{:S(2)}) collective-permute-start(bf16[128,1280]{1,0:T(8,128)(2,1)S(1)} %shard_map.150.refs_0_), channel_id=1, source_target_pairs={{0,16},{8,24},{16,0},{24,8},{1,17},{9,25},{17,1},{25,9},{2,18},{10... | collective-permute-start | bytes 983048 | tf_op jit(solution)/shard_map/ppermute | solution.py:477
  63.0 13.2 %collective-permute-start.19 = (bf16[128,1280]{1,0:T(8,128)(2,1)S(1)}, bf16[128,1280]{1,0:T(8,128)(2,1)S(1)}, u32[]{:S(2)}, u32[]{:S(2)}) collective-permute-start(bf16[128,1280]{1,0:T(8,128)(2,1)S(1)} %shard_map.150.refs_0_), channel_id=1, source_target_pairs={{0,8},{8,0},{16,24},{24,16},{1,9},{9,1},{17,25},{25,17},{2,10},{10... | collective-permute-start | bytes 983048 | tf_op jit(solution)/shard_map/ppermute | solution.py:477
  76.3 3.1 %collective-permute-start.22 = (bf16[512,1280]{1,0:T(8,128)(2,1)S(1)}, bf16[512,1280]{1,0:T(8,128)(2,1)S(1)}, u32[]{:S(2)}, u32[]{:S(2)}) collective-permute-start(bf16[512,1280]{1,0:T(8,128)(2,1)S(1)} %shard_map.152.own_mid.own_small), channel_id=1, source_target_pairs={{0,1},{1,0},{2,3},{3,2},{4,5},{5,4},{6,7},{7,6},{8,9},{9,8},{10,11... | collective-permute-start | bytes 3932168 | tf_op jit(solution)/shard_map/ppermute | solution.py:477

commit v6 on v5

--- a/solution.py
+++ b/solution.py
@@ -59,29 +59,33 @@
     return rows
 
 
-def coefficients(mix_ref, low_mix, high_mix, lons):
-    lats = mix_ref.shape[1]
+def coefficients(base_ref, low_mix, high_mix, lons):
+    lats = base_ref.shape[1]
+    first = base_ref.shape[0] - 2 * lons
     lane = lax.broadcasted_iota(jnp.int32, (1, lats), 1)
     inside = lane < lats - 1
-    own_lon = [mix_ref[lon : lon + 1, :] for lon in range(lons)]
-    own_lat = [mix_ref[lons + lon : lons + lon + 1, :] for lon in range(lons)]
+    own_lon = [base_ref[first + lon : first + lon + 1, :] for lon in range(lons)]
+    first += lons
+    own_lat = [base_ref[first + lon : first + lon + 1, :] for lon in range(lons)]
     lon_coef = [low_mix[0:1, :], low_mix[1:2, :]] + own_lon + [high_mix[0:1, :], high_mix[1:2, :]]
     lat_coef = [low_mix[2:3, :], low_mix[3:4, :]] + own_lat + [high_mix[2:3, :], high_mix[3:4, :]]
     return lon_coef, [jnp.where(inside, coef, 0.0) for coef in lat_coef]
 
 
-def pack_kernel(prog_ref, mix_ref, up_ref, down_ref, prog_out, mix_out, *, lons):
-    fields = prog_ref.shape[0] // lons
+def pack_kernel(base_ref, up_ref, down_ref, *, lons):
+    fields = base_ref.shape[0] // lons - 2
+    mixing = fields * lons
     for out_ref, first in ((up_ref, lons - 2), (down_ref, 0)):
         for side in range(2):
-            out_ref[side * fields : (side + 1) * fields, :] = prog_ref[
+            out_ref[side * fields : (side + 1) * fields, :] = base_ref[
                 pl.ds(first + side, fields, stride=lons), :
             ].astype(BF16)
-        mix_rows = [mix_ref[first : first + 2, :], mix_ref[lons + first : lons + first + 2, :]]
-        mix_rows.append(jnp.zeros((PACK_ROWS - 4, mix_ref.shape[1]), F32))
+        mix_rows = [
+            base_ref[mixing + first : mixing + first + 2, :],
+            base_ref[mixing + lons + first : mixing + lons + first + 2, :],
+            jnp.zeros((PACK_ROWS - 4, base_ref.shape[1]), F32),
+        ]
         out_ref[2 * fields :, :] = jnp.concatenate(mix_rows, axis=0).astype(BF16)
-    prog_out[...] = prog_ref[...]
-    mix_out[...] = mix_ref[...]
 
 
 def halo_rows(pack_ref, fields):
@@ -172,34 +176,21 @@
 
 def adjoint_kernel(
     count_ref,
-    diff_ref,
-    cot_ref,
+    column_ref,
     cols_ref,
     mask_ref,
-    w_in_ref,
-    w_mid_ref,
-    w_out_ref,
     adj_ref,
     coef_ref,
     ratio_ref,
     inverse_ref,
-    w_in_out,
-    w_mid_out,
-    w_out_out,
     right_ref,
     *,
     lons,
 ):
-    w_in_out[...] = w_in_ref[...]
-    w_mid_out[...] = w_mid_ref[...]
-    w_out_out[...] = w_out_ref[...]
-    levels = diff_ref.shape[0] // lons
-    fields = cot_ref.shape[0] // lons
-    cells = lons * cot_ref.shape[1]
-    spread = one_hot(cols_ref, cells)
-    sources = jnp.concatenate(
-        [by_cell(cot_ref, fields, lons), by_cell(diff_ref, levels, lons)], axis=0
-    ).astype(BF16)
+    fields = adj_ref.shape[1]
+    levels = coef_ref.shape[0]
+    spread = one_hot(cols_ref, lons * column_ref.shape[1])
+    sources = by_cell(column_ref, fields + levels, lons).astype(BF16)
     picked = jnp.dot(sources, spread, preferred_element_type=F32)
     split_tiles(right_ref, picked[:fields] * live_row(count_ref, mask_ref))
     coef_ref[...] = picked[fields:]
@@ -226,14 +217,12 @@
 
 
 def forward_kernel(
-    prog_ref,
+    base_ref,
     low_ref,
     high_ref,
-    mix_ref,
     cols_ref,
     adj_ref,
-    w_in_ref,
-    w_mid_ref,
+    weights_ref,
     w_out_ref,
     moved_ref,
     x_ref,
@@ -245,14 +234,14 @@
     *,
     lons,
 ):
-    fields = prog_ref.shape[0] // lons
-    units = w_mid_ref.shape[0]
-    cells = lons * prog_ref.shape[1]
+    fields = x_ref.shape[0]
+    units = weights_ref.shape[0]
+    cells = lons * base_ref.shape[1]
     low_rows, high_rows = halo_rows(low_ref, fields), halo_rows(high_ref, fields)
     lon_coef, lat_coef = coefficients(
-        mix_ref, halo_mixing(low_ref, fields), halo_mixing(high_ref, fields), lons
-    )
-    rows = [prog_ref[pl.ds(lon, fields, stride=lons), :] for lon in range(lons)]
+        base_ref, halo_mixing(low_ref, fields), halo_mixing(high_ref, fields), lons
+    )
+    rows = [base_ref[pl.ds(lon, fields, stride=lons), :] for lon in range(lons)]
     rows = two_steps(low_rows + rows + high_rows, lon_coef, lat_coef)
     for lon in range(lons):
         moved_ref[lon] = rows[lon]
@@ -261,12 +250,12 @@
     x_now = jnp.dot(sources, spread, preferred_element_type=F32).astype(BF16)
     x_ref[...] = x_now
     for start in range(0, units, BLOCK):
-        pre_one = jnp.dot(w_in_ref[start : start + BLOCK, :], x_now, preferred_element_type=F32)
+        pre_one = jnp.dot(weights_ref[start : start + BLOCK, units:], x_now, preferred_element_type=F32)
         act_one_ref[start : start + BLOCK, :] = (pre_one * sigmoid(pre_one)).astype(BF16)
     adj_half = join_tiles(adj_ref).astype(BF16)
     for start in range(0, units, BLOCK):
         pre_two = jnp.dot(
-            w_mid_ref[start : start + BLOCK, :], act_one_ref[...], preferred_element_type=F32
+            weights_ref[start : start + BLOCK, :units], act_one_ref[...], preferred_element_type=F32
         )
         sigma_val = sigmoid(pre_two)
         act_two_ref[start : start + BLOCK, :] = (pre_two * sigma_val).astype(BF16)
@@ -286,23 +275,22 @@
     act_two_ref,
     delta_two_ref,
     adj_ref,
-    w_in_ref,
-    w_mid_ref,
+    weights_ref,
     delta_one_ref,
     keep_ref,
     send_ref,
 ):
     fields = x_ref.shape[0]
-    units = w_mid_ref.shape[0]
+    units = weights_ref.shape[0]
     x_now = x_ref[...]
     for start in range(0, units, BLOCK):
         back_one = lax.dot_general(
-            w_mid_ref[:, start : start + BLOCK],
+            weights_ref[:, start : start + BLOCK],
             delta_two_ref[...],
             CONTRACT_FIRST,
             preferred_element_type=F32,
         )
-        pre_one = jnp.dot(w_in_ref[start : start + BLOCK, :], x_now, preferred_element_type=F32)
+        pre_one = jnp.dot(weights_ref[start : start + BLOCK, units:], x_now, preferred_element_type=F32)
         sigma_val = sigmoid(pre_one)
         slope = sigma_val * (1.0 + pre_one * (1.0 - sigma_val))
         delta_one_ref[start : start + BLOCK, :] = (back_one * slope).astype(BF16)
@@ -357,12 +345,12 @@
 
 def grad_kernel(
     count_ref,
-    cot_ref,
+    column_ref,
     cols_ref,
     mask_ref,
     delta_one_ref,
     adj_ref,
-    w_in_ref,
+    weights_ref,
     field_ref,
     up_ref,
     down_ref,
@@ -371,13 +359,13 @@
 ):
     fields, lats = field_ref.shape[1:]
     grad_x = join_tiles(adj_ref) + lax.dot_general(
-        w_in_ref[...], delta_one_ref[...], CONTRACT_FIRST, preferred_element_type=F32
+        weights_ref[:, delta_one_ref.shape[0] :], delta_one_ref[...], CONTRACT_FIRST, preferred_element_type=F32
     )
     placed, taken = place_back(grad_x, live_row(count_ref, mask_ref), cols_ref, lons * lats)
     for lon in range(lons):
         here = slice(lon * lats, (lon + 1) * lats)
         field_now = jnp.where(
-            taken[:, here], placed[:, here], cot_ref[pl.ds(lon, fields, stride=lons), :]
+            taken[:, here], placed[:, here], column_ref[pl.ds(lon, fields, stride=lons), :]
         )
         field_ref[lon] = field_now
         if lon < 2:
@@ -387,11 +375,11 @@
             up_ref[side * fields : (side + 1) * fields, :] = field_now.astype(BF16)
 
 
-def last_kernel(field_ref, low_ref, high_ref, low_mix_ref, high_mix_ref, mix_ref, out_ref, *, lons):
+def last_kernel(field_ref, low_ref, high_ref, low_mix_ref, high_mix_ref, base_ref, out_ref, *, lons):
     fields = field_ref.shape[1]
     low_rows, high_rows = halo_rows(low_ref, fields), halo_rows(high_ref, fields)
     lon_coef, lat_coef = coefficients(
-        mix_ref, halo_mixing(low_mix_ref, fields), halo_mixing(high_mix_ref, fields), lons
+        base_ref, halo_mixing(low_mix_ref, fields), halo_mixing(high_mix_ref, fields), lons
     )
     rows = [field_ref[lon] for lon in range(lons)]
     rows = two_steps(low_rows + rows + high_rows, lon_coef, lat_coef)
@@ -424,12 +412,21 @@
         out_ref[...] = (total * factor).astype(BF16)
 
 
-def join_kernel(*refs, stage):
-    ins, out_ref = refs[:-1], refs[-1]
-    rows = ins[0].shape[0]
-    for k, ref in enumerate(ins):
+def join_kernel(*refs, stage, groups, cuts):
+    ins, out_refs = refs[:-cuts], refs[-cuts:]
+    count = len(ins) // groups
+    rows, columns = ins[0].shape
+    width = out_refs[0].shape[1]
+    for k in range(count):
         here = pl.ds(pl.multiple_of((position(stage) ^ k) * rows, rows), rows)
-        out_ref[here, :] = ref[...]
+        for group in range(groups):
+            ref = ins[group * count + k]
+            for start in range(0, columns, min(width, columns)):
+                first = group * columns + start
+                part = min(width, columns)
+                out_refs[first // width][here, first % width : first % width + part] = ref[
+                    :, start : start + part
+                ]
 
 
 def merge_kernel(*refs, terms, factor):
@@ -491,19 +488,27 @@
     )(*terms)
 
 
-def join(pieces, stage):
-    rows, columns = pieces[0].shape
-    (joined,) = call(
-        join_kernel,
-        [((rows * len(pieces), columns), BF16)],
-        stage=stage,
-    )(*pieces)
-    return joined
+def join(groups, stage, outs=1):
+    rows, columns = groups[0][0].shape
+    shape = (rows * len(groups[0]), columns * len(groups) // outs)
+    return call(
+        join_kernel, [(shape, BF16)] * outs, stage=stage, groups=len(groups), cuts=outs
+    )(*[piece for group in groups for piece in group])
 
 
 def reduce_to(terms, stage):
     parts = add(terms, stage)
     return [parts[0]] + exchange(parts[1:], stage)
+
+
+def collect_members(one, two):
+    (low_one,) = exchange([one], MEMBER_LOW)
+    (high_two,) = exchange([two], MEMBER_HIGH)
+    (high_one,) = exchange([one], MEMBER_HIGH)
+    (low_two,) = exchange([two], MEMBER_LOW)
+    (far_one,) = exchange([low_one], MEMBER_HIGH)
+    (far_two,) = exchange([high_two], MEMBER_LOW)
+    return [one, low_one, high_one, far_one], [two, low_two, high_two, far_two]
 
 
 def collect(piece, stage):
@@ -543,31 +548,24 @@
     units = w_mid.shape[0]
     tiles, width = tile_cols.shape[2:]
     slots = tiles * width
-    prog_rows = prognostic.reshape(fields * lons, lats)
-    cot_rows = cotangent.reshape(fields * lons, lats)
-    diff_rows = diffusivity.reshape(levels * lons, lats)
-    mix_rows = mixing.reshape(2 * lons, lats)
+    base = jnp.concatenate([prognostic[0], mixing], axis=0).reshape((fields + 2) * lons, lats)
+    column = jnp.concatenate([cotangent[0], diffusivity[0]], axis=0)
+    column = column.reshape((fields + levels) * lons, lats)
+    weights = jnp.concatenate([w_mid, w_in], axis=1)
     cols, mask = tile_cols[0, 0], pad_mask[0, 0]
 
     packed = ((2 * fields + PACK_ROWS, lats), BF16)
-    up_pack, down_pack, prog_rows, mix_rows = call(
-        pack_kernel,
-        [packed, packed, (prog_rows.shape, F32), (mix_rows.shape, F32)],
-        moved=20 * 10**6,
-        lons=lons,
-    )(prog_rows, mix_rows)
+    up_pack, down_pack = call(pack_kernel, [packed, packed], lons=lons)(base)
     low_pack, high_pack = to_neighbours(up_pack, down_pack, "horiz")
 
-    adjoint, coef, ratio, inverse, w_in, w_mid, w_out = call(
+    adjoint, coef, ratio, inverse = call(
         adjoint_kernel,
-        [((tiles, fields, width), F32)]
-        + [((levels, slots), F32)] * 3
-        + [(weight.shape, BF16) for weight in (w_in, w_mid, w_out)],
+        [((tiles, fields, width), F32)] + [((levels, slots), F32)] * 3,
         scratch=[pltpu.VMEM((tiles, fields, width), F32)],
         smem=(0,),
         moved=30 * 10**6,
         lons=lons,
-    )(tile_count, diff_rows, cot_rows, cols, mask, w_in, w_mid, w_out)
+    )(tile_count, column, cols, mask)
 
     hidden = ((units, slots), BF16)
     half = ((units // 2, units), BF16)
@@ -576,7 +574,7 @@
         [((lons, fields, lats), F32), ((fields, slots), BF16), hidden, hidden, hidden, half, half],
         moved=15 * 10**6,
         lons=lons,
-    )(prog_rows, low_pack, high_pack, mix_rows, cols, adjoint, w_in, w_mid, w_out)
+    )(base, low_pack, high_pack, cols, adjoint, weights, w_out)
     column_total = lax.axis_size("ens") * lax.axis_size("horiz") * lons * lats
     factor = 1.0 / math.sqrt(column_total)
     (got_mid,) = exchange([send_mid], CORE)
@@ -584,7 +582,7 @@
     half = ((units // 2, 2 * fields), BF16)
     delta_one, keep_small, send_small = call(
         backward_kernel, [hidden, half, half], moved=4 * 10**6
-    )(x_now, act_two, delta_two, adjoint, w_in, w_mid)
+    )(x_now, act_two, delta_two, adjoint, weights)
     got_mid, keep_small = tie(got_mid, keep_small)
     (got_small,) = exchange([send_small], CORE)
 
@@ -604,11 +602,11 @@
             [((lons, fields, lats), F32), packed, packed],
             smem=(0,),
             lons=lons,
-        )(tile_count, cot_rows, cols, mask, delta_one, adjoint, w_in)
+        )(tile_count, column, cols, mask, delta_one, adjoint, weights)
 
     def finish(field, halos):
         return call(last_kernel, [((fields * lons, lats), F32)], lons=lons)(
-            field, *halos, low_pack, high_pack, mix_rows
+            field, *halos, low_pack, high_pack, base
         )[0]
 
     terms_mid = reduce_to([keep_mid, got_mid], MEMBERS)
@@ -631,18 +629,17 @@
 
         piece = merge(terms_mid, terms_small, factor)
         pieces = collect(piece, CHIPS)
-        halos = to_neighbours(up_rows, down_rows, "horiz")
-        pieces, halos = tie(pieces, halos)
-        pieces = collect(join(pieces, CHIPS), MEMBERS)
-        grad_rows = finish(field, halos)
+        halves = join([pieces], CHIPS, outs=2)
+        groups = collect_members(*halves)
+        grad_rows = finish(field, to_neighbours(up_rows, down_rows, "horiz"))
     else:
         state_rows = new_state(act_two)
         field, up_rows, down_rows = new_field(delta_one)
         grad_rows = finish(field, to_neighbours(up_rows, down_rows, "horiz"))
         terms_small = reduce_to([keep_small, got_small], MEMBERS)
-        pieces = collect(over_all_chips(merge(terms_mid, terms_small, 1.0), factor), MEMBERS)
-    pieces, grad_rows = tie(pieces, grad_rows)
-    own = join(pieces, MEMBERS)
+        groups = [collect(over_all_chips(merge(terms_mid, terms_small, 1.0), factor), MEMBERS)]
+    groups, grad_rows = tie(groups, grad_rows)
+    (own,) = join(groups, MEMBERS)
     (got,) = exchange([own], CORE)
     block = units // 4
     mid_half = pl.BlockSpec((units // 2, block), lambda step: (0, step))

time: 82.9 us -> 79.3 us (0.957)
  local copies, waits for them, and re-layouts: 7.61 us -> 1.92 us
  starting transfers between devices: 29.3 us -> 30.5 us
  other arithmetic: 0 us -> 1.1 us
    unnamed x17 -> x14, local copies, waits for them, and re-layouts: 7.61 us -> 1.86 us
    ppermute x19 -> x22, waiting for transfers between devices: 27.7 us -> 22.3 us  [exchange(): lax.ppermute(array, axis, [(i, i ^ k << shift) for i in range(count)])]
    ppermute x19 -> x22, starting transfers between devices: 21.2 us -> 25.9 us  [exchange(): lax.ppermute(array, axis, [(i, i ^ k << shift) for i in range(count)])]
    ppermute x2, starting transfers between devices: 7.64 us -> 4.1 us  [to_neighbours(): lax.ppermute(downward, axis, backward)]
    ppermute x2, waiting for transfers between devices: 2.1 us -> 5.51 us  [to_neighbours(): lax.ppermute(upward, axis, forward)]
    ppermute x2, waiting for transfers between devices: 0.01 us -> 1.91 us  [to_neighbours(): lax.ppermute(downward, axis, backward)]
    concatenate x0 -> x2, other arithmetic: none -> 1.1 us  [the longest x1 1.03 us: per_device(): jnp.concatenate([prognostic[0], mixing], axis=0)]
  transfers between devices with their start and end apart: 23 -> 26, of which waited for: 9 -> 10; matrix products, arithmetic and copies ran while one was open for 1% -> 2% of each run, Pallas kernels for 9% -> 9%
where the time goes in v6:
time: 79.3 us; the launch traced here: 79.1 us
  starting transfers between devices  30.5 us (38%)
  waiting for transfers between devices  29.7 us (37%)
  Pallas kernels  14.3 us (18%)
  local copies, waits for them, and re-layouts  1.92 us (2%)
  between operations  1.55 us (2%)
  other arithmetic  1.1 us (1%)
    ppermute x22, starting transfers between devices, exchange(): lax.ppermute(array, axis, [(i, i ^ k << shift) for i in range(count)])  25.9 us
    ppermute x22, waiting for transfers between devices, exchange(): lax.ppermute(array, axis, [(i, i ^ k << shift) for i in range(count)])  22.3 us
    pallas_call x16, Pallas kernels, run(): pl.pallas_call(functools.partial(kernel, **names), out_shape=[jax.ShapeDt...  11.2 us
    ppermute x2, waiting for transfers between devices, to_neighbours(): lax.ppermute(upward, axis, forward)  5.51 us
    ppermute x2, starting transfers between devices, to_neighbours(): lax.ppermute(downward, axis, backward)  4.1 us
    pallas_call x1, Pallas kernels, per_device(): pl.pallas_call(functools.partial(final_kernel, swapped=(4, 4) if fast els...  3.15 us
    ppermute x2, waiting for transfers between devices, to_neighbours(): lax.ppermute(downward, axis, backward)  1.91 us
    unnamed x14, local copies, waits for them, and re-layouts  1.86 us
  transfers between devices with their start and end apart: 26, of which 10 were waited for; matrix products, arithmetic and copies ran while one was open for 2% of the time, Pallas kernels for 9%

profile of v6, /device:TPU:0, one launch (start us, length us, event | category | flops | bytes accessed | tf_op | source)
XLA Modules:
  0.0 79.1 jit_solution(8876136100978681424)
XLA Ops:
  0.6 1.0 %pad_maximum_fusion.1 = f32[130,4,128]{2,1,0:T(4,128)S(1)} fusion(f32[2,4,128]{2,1,0:T(4,128)} %param.12, f32[128,4,128]{2,1,0:T(4,128)} %bitcast.16), kind=kLoop, calls=%fused_computation.1 | loop fusion | flops 66560 | bytes 532480 | tf_op jit(solution)/shard_map/concatenate | solution.py:551
  2.2 4.1 %collective-permute-start.1 = (bf16[272,128]{1,0:T(8,128)(2,1)S(1)}, bf16[272,128]{1,0:T(8,128)(2,1)S(1)}, u32[]{:S(2)}, u32[]{:S(2)}) collective-permute-start(bf16[272,128]{1,0:T(8,128)(2,1)S(1)} %get-tuple-element.78), channel_id=1, source_target_pairs={{1,0},{2,1},{3,2},{4,3},{5,4},{6,5},{7,6},{0,7},{9,8},{10,9},{11,1... | collective-permute-start | bytes 208904 | tf_op jit(solution)/shard_map/ppermute | solution.py:540
  7.0 1.8 %constant_dynamic-update-slice_fusion.1 = bf16[1024,1152]{1,0:T(8,128)(2,1)S(1)} fusion(bf16[1024,1024]{1,0:T(8,128)(2,1)} %param.18), kind=kLoop, calls=%fused_computation.3 | loop fusion | bytes 4194304
  9.0 0.8 shard_map.138
  9.9 3.9 %shard_map.139 = (f32[4,128,128]{2,1,0:T(8,128)S(1)}, bf16[128,384]{1,0:T(8,128)(2,1)S(1)}, bf16[1024,384]{1,0:T(8,128)(2,1)}, bf16[1024,384]{1,0:T(8,128)(2,1)S...) custom-call(f32[520,128]{1,0:T(8,128)S(1)} %bitcast.12, ...), custom_call_target="tpu_custom_call" | custom-call | bytes 15000000 | tf_op jit(solution)/shard_map/pallas_call | solution.py:27
  13.8 2.1 %shard_map.140 = (bf16[1024,384]{1,0:T(8,128)(2,1)S(1)}, bf16[512,256]{1,0:T(8,128)(2,1)S(1)}, bf16[512,256]{1,0:T(8,128)(2,1)S(1)}) custom-call(bf16[128,384]{1,0:T(8,128)(2,1)S(1)} %get-tuple-element.82.x_ref, bf16[1024,384]{1,0:T(8,128)(2,1)S(1)} %get-tuple-element.119.act_two_ref, bf16[1024,384]{1,0:T(8,128)(2,1)S(1)} %get-tuple-element.84.delta_two_ref, ...), custom_call_target="tpu_custom_call" | custom-call | bytes 4000000 | tf_op jit(solution)/shard_map/pallas_call | solution.py:27
  16.7 2.0 %collective-permute-start.3 = (bf16[128,1024]{1,0:T(8,128)(2,1)S(1)}, bf16[128,1024]{1,0:T(8,128)(2,1)S(1)}, u32[]{:S(2)}, u32[]{:S(2)}) collective-permute-start(bf16[128,1024]{1,0:T(8,128)(2,1)S(1)} %get-tuple-element.88), channel_id=1, source_target_pairs={{0,8},{8,0},{16,24},{24,16},{1,9},{9,1},{17,25},{25,17},{2,10},{10... | collective-permute-start | bytes 786440 | tf_op jit(solution)/shard_map/ppermute | solution.py:474
  18.7 1.5 %collective-permute-start.4 = (bf16[128,1024]{1,0:T(8,128)(2,1)S(1)}, bf16[128,1024]{1,0:T(8,128)(2,1)S(1)}, u32[]{:S(2)}, u32[]{:S(2)}) collective-permute-start(bf16[128,1024]{1,0:T(8,128)(2,1)S(1)} %get-tuple-element.89), channel_id=1, source_target_pairs={{0,16},{8,24},{16,0},{24,8},{1,17},{9,25},{17,1},{25,9},{2,18},{10... | collective-permute-start | bytes 786440 | tf_op jit(solution)/shard_map/ppermute | solution.py:474
  20.3 1.3 %collective-permute-start.7 = (bf16[256,256]{1,0:T(8,128)(2,1)S(1)}, bf16[256,256]{1,0:T(8,128)(2,1)S(1)}, u32[]{:S(2)}, u32[]{:S(2)}) collective-permute-start(bf16[256,256]{1,0:T(8,128)(2,1)S(1)} %get-tuple-element.94), channel_id=1, source_target_pairs={{0,4},{1,5},{2,6},{3,7},{4,0},{5,1},{6,2},{7,3},{8,12},{9,13},{10,... | collective-permute-start | bytes 393224 | tf_op jit(solution)/shard_map/ppermute | solution.py:474
  21.6 7.1 %collective-permute-done.7.refs_1_ = bf16[256,256]{1,0:T(8,128)(2,1)S(1)} collective-permute-done((bf16[256,256]{1,0:T(8,128)(2,1)S(1)}, bf16[256,256]{1,0:T(8,128)(2,1)S(1)}, u32[]{:S(2)}, u32[]{:S(2)}) %collective-permute-start.7) | collective-permute-done | bytes 131104 | tf_op jit(solution)/shard_map/ppermute | solution.py:474
  28.8 0.6 shard_map.144
  29.4 3.7 %collective-permute-done.8.refs_1_ = bf16[128,256]{1,0:T(8,128)(2,1)S(1)} collective-permute-done((bf16[128,256]{1,0:T(8,128)(2,1)S(1)}, bf16[128,256]{1,0:T(8,128)(2,1)S(1)}, u32[]{:S(2)}, u32[]{:S(2)}) %collective-permute-start.8) | collective-permute-done | bytes 65568 | tf_op jit(solution)/shard_map/ppermute | solution.py:474
  33.4 2.8 %collective-permute-start.10 = (bf16[32,1024]{1,0:T(8,128)(2,1)S(1)}, bf16[32,1024]{1,0:T(8,128)(2,1)S(1)}, u32[]{:S(2)}, u32[]{:S(2)}) collective-permute-start(bf16[32,1024]{1,0:T(8,128)(2,1)S(1)} %get-tuple-element.108), channel_id=1, source_target_pairs={{0,4},{1,5},{2,6},{3,7},{4,0},{5,1},{6,2},{7,3},{8,12},{9,13},{10,... | collective-permute-start | bytes 196616 | tf_op jit(solution)/shard_map/ppermute | solution.py:474
  36.1 1.6 %collective-permute-start.11 = (bf16[32,1024]{1,0:T(8,128)(2,1)S(1)}, bf16[32,1024]{1,0:T(8,128)(2,1)S(1)}, u32[]{:S(2)}, u32[]{:S(2)}) collective-permute-start(bf16[32,1024]{1,0:T(8,128)(2,1)S(1)} %get-tuple-element.109), channel_id=1, source_target_pairs={{0,6},{1,7},{2,4},{3,5},{4,2},{5,3},{6,0},{7,1},{8,14},{9,15},{10,... | collective-permute-start | bytes 196616 | tf_op jit(solution)/shard_map/ppermute | solution.py:474
  37.7 1.8 %collective-permute-start.12 = (bf16[64,256]{1,0:T(8,128)(2,1)S(1)}, bf16[64,256]{1,0:T(8,128)(2,1)S(1)}, u32[]{:S(2)}, u32[]{:S(2)}) collective-permute-start(bf16[64,256]{1,0:T(8,128)(2,1)S(1)} %get-tuple-element.113), channel_id=1, source_target_pairs={{0,16},{8,24},{16,0},{24,8},{1,17},{9,25},{17,1},{25,9},{2,18},{10... | collective-permute-start | bytes 98312 | tf_op jit(solution)/shard_map/ppermute | solution.py:474
  39.5 2.2 %collective-permute-done.12.refs_1_ = bf16[64,256]{1,0:T(8,128)(2,1)S(1)} collective-permute-done((bf16[64,256]{1,0:T(8,128)(2,1)S(1)}, bf16[64,256]{1,0:T(8,128)(2,1)S(1)}, u32[]{:S(2)}, u32[]{:S(2)}) %collective-permute-start.12) | collective-permute-done | bytes 32800 | tf_op jit(solution)/shard_map/ppermute | solution.py:474
  41.7 1.7 %collective-permute-start.13 = (bf16[32,256]{1,0:T(8,128)(2,1)S(1)}, bf16[32,256]{1,0:T(8,128)(2,1)S(1)}, u32[]{:S(2)}, u32[]{:S(2)}) collective-permute-start(bf16[32,256]{1,0:T(8,128)(2,1)S(1)} %get-tuple-element.117), channel_id=1, source_target_pairs={{0,8},{8,0},{16,24},{24,16},{1,9},{9,1},{17,25},{25,17},{2,10},{10... | collective-permute-start | bytes 49160 | tf_op jit(solution)/shard_map/ppermute | solution.py:474
  43.5 1.6 %shard_map.148 = f32[512,128]{1,0:T(8,128)} custom-call(s32[1,1]{1,0:T(1,128)S(6)} %copy.20.count_ref, f32[4,128,128]{2,1,0:T(8,128)S(1)} %get-tuple-element.118.moved_ref, s32[3,128]{1,0:T(4,128)S(1)} %get-tuple-element.150.cols_ref, s32[3,128]{1,0:T(4,128)S(1)} %get-tuple-element.149.mask_ref, bf16[128,384]{1,0:T(8,128)(2,1)S(1)} %get-tuple-element.82.x_ref, ...), custom_call_target="tpu_custom_call" | custom-call | tf_op jit(solution)/shard_map/pallas_call | solution.py:27
  45.6 2.3 %collective-permute-start.16 = (bf16[32,1280]{1,0:T(8,128)(2,1)S(1)}, bf16[32,1280]{1,0:T(8,128)(2,1)S(1)}, u32[]{:S(2)}, u32[]{:S(2)}) collective-permute-start(bf16[32,1280]{1,0:T(8,128)(2,1)S(1)} %shard_map.149.refs_0_), channel_id=1, source_target_pairs={{0,6},{1,7},{2,4},{3,5},{4,2},{5,3},{6,0},{7,1},{8,14},{9,15},{10,... | collective-permute-start | bytes 245768 | tf_op jit(solution)/shard_map/ppermute | solution.py:474
  47.9 2.1 %collective-permute-start.14 = (bf16[32,1280]{1,0:T(8,128)(2,1)S(1)}, bf16[32,1280]{1,0:T(8,128)(2,1)S(1)}, u32[]{:S(2)}, u32[]{:S(2)}) collective-permute-start(bf16[32,1280]{1,0:T(8,128)(2,1)S(1)} %shard_map.149.refs_0_), channel_id=1, source_target_pairs={{0,2},{1,3},{2,0},{3,1},{4,6},{5,7},{6,4},{7,5},{8,10},{9,11},{10,... | collective-permute-start | bytes 245768 | tf_op jit(solution)/shard_map/ppermute | solution.py:474
  50.0 1.9 %collective-permute-done.16.refs_3_ = bf16[32,1280]{1,0:T(8,128)(2,1)S(1)} collective-permute-done((bf16[32,1280]{1,0:T(8,128)(2,1)S(1)}, bf16[32,1280]{1,0:T(8,128)(2,1)S(1)}, u32[]{:S(2)}, u32[]{:S(2)}) %collective-permute-start.16) | collective-permute-done | bytes 81952 | tf_op jit(solution)/shard_map/ppermute | solution.py:474
  51.9 1.7 %collective-permute-done.15.refs_2_ = bf16[32,1280]{1,0:T(8,128)(2,1)S(1)} collective-permute-done((bf16[32,1280]{1,0:T(8,128)(2,1)S(1)}, bf16[32,1280]{1,0:T(8,128)(2,1)S(1)}, u32[]{:S(2)}, u32[]{:S(2)}) %collective-permute-start.15) | collective-permute-done | bytes 81952 | tf_op jit(solution)/shard_map/ppermute | solution.py:474
  53.7 1.7 %collective-permute-start.17 = (bf16[128,640]{1,0:T(8,128)(2,1)S(1)}, bf16[128,640]{1,0:T(8,128)(2,1)S(1)}, u32[]{:S(2)}, u32[]{:S(2)}) collective-permute-start(bf16[128,640]{1,0:T(8,128)(2,1)S(1)} %get-tuple-element.138.refs_0_), channel_id=1, source_target_pairs={{0,8},{8,0},{16,24},{24,16},{1,9},{9,1},{17,25},{25,17},{2,10},{10... | collective-permute-start | bytes 491528 | tf_op jit(solution)/shard_map/ppermute | solution.py:474
  55.4 1.5 %collective-permute-start.21 = (bf16[128,640]{1,0:T(8,128)(2,1)S(1)}, bf16[128,640]{1,0:T(8,128)(2,1)S(1)}, u32[]{:S(2)}, u32[]{:S(2)}) collective-permute-start(bf16[128,640]{1,0:T(8,128)(2,1)S(1)} %get-tuple-element.142.refs_4_), channel_id=1, source_target_pairs={{0,16},{8,24},{16,0},{24,8},{1,17},{9,25},{17,1},{25,9},{2,18},{10... | collective-permute-start | bytes 491528 | tf_op jit(solution)/shard_map/ppermute | solution.py:474
  57.8 2.1 %collective-permute-done.17.refs_1_ = bf16[128,640]{1,0:T(8,128)(2,1)S(1)} collective-permute-done((bf16[128,640]{1,0:T(8,128)(2,1)S(1)}, bf16[128,640]{1,0:T(8,128)(2,1)S(1)}, u32[]{:S(2)}, u32[]{:S(2)}) %collective-permute-start.17) | collective-permute-done | bytes 163872 | tf_op jit(solution)/shard_map/ppermute | solution.py:474
  60.0 2.3 %collective-permute-start.19 = (bf16[128,640]{1,0:T(8,128)(2,1)S(1)}, bf16[128,640]{1,0:T(8,128)(2,1)S(1)}, u32[]{:S(2)}, u32[]{:S(2)}) collective-permute-start(bf16[128,640]{1,0:T(8,128)(2,1)S(1)} %collective-permute-done.17.refs_1_), channel_id=1, source_target_pairs={{0,16},{8,24},{16,0},{24,8},{1,17},{9,25},{17,1},{25,9},{2,18},{10... | collective-permute-start | bytes 491528 | tf_op jit(solution)/shard_map/ppermute | solution.py:474
  62.2 1.5 %collective-permute-start.22 = (bf16[128,640]{1,0:T(8,128)(2,1)S(1)}, bf16[128,640]{1,0:T(8,128)(2,1)S(1)}, u32[]{:S(2)}, u32[]{:S(2)}) collective-permute-start(bf16[128,640]{1,0:T(8,128)(2,1)S(1)} %collective-permute-done.21.refs_6_), channel_id=1, source_target_pairs={{0,8},{8,0},{16,24},{24,16},{1,9},{9,1},{17,25},{25,17},{2,10},{10... | collective-permute-start | bytes 491528 | tf_op jit(solution)/shard_map/ppermute | solution.py:474
  63.8 5.5 %collective-permute-done.23.low_ref = bf16[256,128]{1,0:T(8,128)(2,1)S(1)} collective-permute-done((bf16[256,128]{1,0:T(8,128)(2,1)S(1)}, bf16[256,128]{1,0:T(8,128)(2,1)S(1)}, u32[]{:S(2)}, u32[]{:S(2)}) %collective-permute-start.23) | collective-permute-done | bytes 65568 | tf_op jit(solution)/shard_map/ppermute | solution.py:540
  69.3 1.9 %collective-permute-done.24.high_ref = bf16[256,128]{1,0:T(8,128)(2,1)S(1)} collective-permute-done((bf16[256,128]{1,0:T(8,128)(2,1)S(1)}, bf16[256,128]{1,0:T(8,128)(2,1)S(1)}, u32[]{:S(2)}, u32[]{:S(2)}) %collective-permute-start.24) | collective-permute-done | bytes 65568 | tf_op jit(solution)/shard_map/ppermute | solution.py:540
  71.2 1.5 %shard_map.151 = f32[512,128]{1,0:T(8,128)} custom-call(f32[4,128,128]{2,1,0:T(8,128)S(1)} %get-tuple-element.134.field_ref, bf16[256,128]{1,0:T(8,128)(2,1)S(1)} %collective-permute-done.23.low_ref, bf16[256,128]{1,0:T(8,128)(2,1)S(1)} %collective-permute-done.24.high_ref, bf16[272,128]{1,0:T(8,128)(2,1)S(1)} %collective-permute-done.low_ref.low_mix_ref, ...), custom_call_target="tpu_custom_call" | custom-call | tf_op jit(solution)/shard_map/pallas_call | solution.py:27
  72.9 3.0 %collective-permute-done.25.got_mid.got_small = bf16[512,1280]{1,0:T(8,128)(2,1)S(1)} collective-permute-done((bf16[512,1280]{1,0:T(8,128)(2,1)S(1)}, bf16[512,1280]{1,0:T(8,128)(2,1)S(1)}, u32[]{:S(2)}, u32[]{:S(2)}) %collective-permute-start.25) | collective-permute-done | bytes 1310752 | tf_op jit(solution)/shard_map/ppermute | solution.py:474
  76.0 3.1 %shard_map.153 = (f32[1024,1024]{1,0:T(8,128)}, f32[1024,128]{1,0:T(8,128)}, f32[128,1024]{1,0:T(8,128)}) custom-call(bf16[512,1280]{1,0:T(8,128)(2,1)S(1)} %shard_map.152.own_mid.own_small, bf16[512,1280]{1,0:T(8,128)(2,1)S(1)} %collective-permute-done.25.got_mid.got_small, bf16[512,1280]{1,0:T(8,128)(2,1)S(1)} %shard_map.152.own_mid.own_small, ...), custom_call_target="tpu_custom_call" | custom-call | tf_op jit(solution)/shard_map/pallas_call | solution.py:647
  (54 shorter events, 3.7 us)
Async XLA Ops:
  1.7 7.2 %copy-start.4 = (s32[1,1,3,128]{3,1,2,0:T(1,128)S(1)}, s32[1,1,3,128]{3,1,2,0:T(1,128)}, u32[]{:S(2)}) copy-start(s32[1,1,3,128]{3,1,2,0:T(1,128)} %param.15) | copy-start | bytes 4612
  1.7 7.2 %copy-start.5 = (s32[1,1,3,128]{3,1,2,0:T(1,128)S(1)}, s32[1,1,3,128]{3,1,2,0:T(1,128)}, u32[]{:S(2)}) copy-start(s32[1,1,3,128]{3,1,2,0:T(1,128)} %param.14) | copy-start | bytes 4612
  1.7 7.2 %copy-start.1 = (f32[1,128,4,128]{3,2,1,0:T(4,128)S(1)}, f32[1,128,4,128]{3,2,1,0:T(4,128)}, u32[]{:S(2)}) copy-start(f32[1,128,4,128]{3,2,1,0:T(4,128)} %param.13) | copy-start | bytes 786436
  1.7 7.2 %copy-start.3 = (f32[1,32,4,128]{3,2,1,0:T(4,128)S(1)}, f32[1,32,4,128]{3,2,1,0:T(4,128)}, u32[]{:S(2)}) copy-start(f32[1,32,4,128]{3,2,1,0:T(4,128)} %param.11) | copy-start | bytes 196612
  1.7 8.1 %collective-permute-start = (bf16[272,128]{1,0:T(8,128)(2,1)S(1)}, bf16[272,128]{1,0:T(8,128)(2,1)S(1)}, u32[]{:S(2)}, u32[]{:S(2)}) collective-permute-start(bf16[272,128]{1,0:T(8,128)(2,1)S(1)} %get-tuple-element.77), channel_id=1, source_target_pairs={{0,1},{1,2},{2,3},{3,4},{4,5},{5,6},{6,7},{7,0},{8,9},{9,10},{10,1... | collective-permute-start | bytes 208904 | tf_op jit(solution)/shard_map/ppermute | solution.py:540
  2.2 7.6 %collective-permute-start.1 = (bf16[272,128]{1,0:T(8,128)(2,1)S(1)}, bf16[272,128]{1,0:T(8,128)(2,1)S(1)}, u32[]{:S(2)}, u32[]{:S(2)}) collective-permute-start(bf16[272,128]{1,0:T(8,128)(2,1)S(1)} %get-tuple-element.78), channel_id=1, source_target_pairs={{1,0},{2,1},{3,2},{4,3},{5,4},{6,5},{7,6},{0,7},{9,8},{10,9},{11,1... | collective-permute-start | bytes 208904 | tf_op jit(solution)/shard_map/ppermute | solution.py:540
  7.0 2.7 %copy-start.2 = (bf16[1024,128]{1,0:T(8,128)(2,1)S(1)}, bf16[1024,128]{1,0:T(8,128)(2,1)}, u32[]{:S(2)}) copy-start(bf16[1024,128]{1,0:T(8,128)(2,1)} %param.17) | copy-start | bytes 786436
  7.0 2.8 %copy-start = (bf16[128,1024]{1,0:T(8,128)(2,1)S(1)}, bf16[128,1024]{1,0:T(8,128)(2,1)}, u32[]{:S(2)}) copy-start(bf16[128,1024]{1,0:T(8,128)(2,1)} %w_out_ref.3) | copy-start | bytes 786436
  13.8 2.7 %collective-permute-start.2 = (bf16[512,1024]{1,0:T(8,128)(2,1)S(1)}, bf16[512,1024]{1,0:T(8,128)(2,1)S(1)}, u32[]{:S(2)}, u32[]{:S(2)}) collective-permute-start(bf16[512,1024]{1,0:T(8,128)(2,1)S(1)} %get-tuple-element.81), channel_id=1, source_target_pairs={{0,1},{1,0},{2,3},{3,2},{4,5},{5,4},{6,7},{7,6},{8,9},{9,8},{10,11... | collective-permute-start | bytes 3145736 | tf_op jit(solution)/shard_map/ppermute | solution.py:474
  15.9 4.4 %collective-permute-start.6 = (bf16[512,256]{1,0:T(8,128)(2,1)S(1)}, bf16[512,256]{1,0:T(8,128)(2,1)S(1)}, u32[]{:S(2)}, u32[]{:S(2)}) collective-permute-start(bf16[512,256]{1,0:T(8,128)(2,1)S(1)} %get-tuple-element.92), channel_id=1, source_target_pairs={{0,1},{1,0},{2,3},{3,2},{4,5},{5,4},{6,7},{7,6},{8,9},{9,8},{10,11... | collective-permute-start | bytes 786440 | tf_op jit(solution)/shard_map/ppermute | solution.py:474
  16.7 16.4 %collective-permute-start.3 = (bf16[128,1024]{1,0:T(8,128)(2,1)S(1)}, bf16[128,1024]{1,0:T(8,128)(2,1)S(1)}, u32[]{:S(2)}, u32[]{:S(2)}) collective-permute-start(bf16[128,1024]{1,0:T(8,128)(2,1)S(1)} %get-tuple-element.88), channel_id=1, source_target_pairs={{0,8},{8,0},{16,24},{24,16},{1,9},{9,1},{17,25},{25,17},{2,10},{10... | collective-permute-start | bytes 786440 | tf_op jit(solution)/shard_map/ppermute | solution.py:474
  18.7 14.4 %collective-permute-start.4 = (bf16[128,1024]{1,0:T(8,128)(2,1)S(1)}, bf16[128,1024]{1,0:T(8,128)(2,1)S(1)}, u32[]{:S(2)}, u32[]{:S(2)}) collective-permute-start(bf16[128,1024]{1,0:T(8,128)(2,1)S(1)} %get-tuple-element.89), channel_id=1, source_target_pairs={{0,16},{8,24},{16,0},{24,8},{1,17},{9,25},{17,1},{25,9},{2,18},{10... | collective-permute-start | bytes 786440 | tf_op jit(solution)/shard_map/ppermute | solution.py:474
  20.2 12.9 %collective-permute-start.5 = (bf16[128,1024]{1,0:T(8,128)(2,1)S(1)}, bf16[128,1024]{1,0:T(8,128)(2,1)S(1)}, u32[]{:S(2)}, u32[]{:S(2)}) collective-permute-start(bf16[128,1024]{1,0:T(8,128)(2,1)S(1)} %get-tuple-element.90), channel_id=1, source_target_pairs={{0,24},{8,16},{16,8},{24,0},{1,25},{9,17},{17,9},{25,1},{2,26},{10... | collective-permute-start | bytes 786440 | tf_op jit(solution)/shard_map/ppermute | solution.py:474
  20.3 8.4 %collective-permute-start.7 = (bf16[256,256]{1,0:T(8,128)(2,1)S(1)}, bf16[256,256]{1,0:T(8,128)(2,1)S(1)}, u32[]{:S(2)}, u32[]{:S(2)}) collective-permute-start(bf16[256,256]{1,0:T(8,128)(2,1)S(1)} %get-tuple-element.94), channel_id=1, source_target_pairs={{0,4},{1,5},{2,6},{3,7},{4,0},{5,1},{6,2},{7,3},{8,12},{9,13},{10,... | collective-permute-start | bytes 393224 | tf_op jit(solution)/shard_map/ppermute | solution.py:474
  28.8 4.3 %collective-permute-start.8 = (bf16[128,256]{1,0:T(8,128)(2,1)S(1)}, bf16[128,256]{1,0:T(8,128)(2,1)S(1)}, u32[]{:S(2)}, u32[]{:S(2)}) collective-permute-start(bf16[128,256]{1,0:T(8,128)(2,1)S(1)} %get-tuple-element.99), channel_id=1, source_target_pairs={{0,2},{1,3},{2,0},{3,1},{4,6},{5,7},{6,4},{7,5},{8,10},{9,11},{10,... | collective-permute-start | bytes 196616 | tf_op jit(solution)/shard_map/ppermute | solution.py:474
  33.3 12.3 %collective-permute-start.9 = (bf16[32,1024]{1,0:T(8,128)(2,1)S(1)}, bf16[32,1024]{1,0:T(8,128)(2,1)S(1)}, u32[]{:S(2)}, u32[]{:S(2)}) collective-permute-start(bf16[32,1024]{1,0:T(8,128)(2,1)S(1)} %get-tuple-element.107), channel_id=1, source_target_pairs={{0,2},{1,3},{2,0},{3,1},{4,6},{5,7},{6,4},{7,5},{8,10},{9,11},{10,... | collective-permute-start | bytes 196616 | tf_op jit(solution)/shard_map/ppermute | solution.py:474
  33.4 12.2 %collective-permute-start.10 = (bf16[32,1024]{1,0:T(8,128)(2,1)S(1)}, bf16[32,1024]{1,0:T(8,128)(2,1)S(1)}, u32[]{:S(2)}, u32[]{:S(2)}) collective-permute-start(bf16[32,1024]{1,0:T(8,128)(2,1)S(1)} %get-tuple-element.108), channel_id=1, source_target_pairs={{0,4},{1,5},{2,6},{3,7},{4,0},{5,1},{6,2},{7,3},{8,12},{9,13},{10,... | collective-permute-start | bytes 196616 | tf_op jit(solution)/shard_map/ppermute | solution.py:474
  36.1 9.4 %collective-permute-start.11 = (bf16[32,1024]{1,0:T(8,128)(2,1)S(1)}, bf16[32,1024]{1,0:T(8,128)(2,1)S(1)}, u32[]{:S(2)}, u32[]{:S(2)}) collective-permute-start(bf16[32,1024]{1,0:T(8,128)(2,1)S(1)} %get-tuple-element.109), channel_id=1, source_target_pairs={{0,6},{1,7},{2,4},{3,5},{4,2},{5,3},{6,0},{7,1},{8,14},{9,15},{10,... | collective-permute-start | bytes 196616 | tf_op jit(solution)/shard_map/ppermute | solution.py:474
  37.7 4.0 %collective-permute-start.12 = (bf16[64,256]{1,0:T(8,128)(2,1)S(1)}, bf16[64,256]{1,0:T(8,128)(2,1)S(1)}, u32[]{:S(2)}, u32[]{:S(2)}) collective-permute-start(bf16[64,256]{1,0:T(8,128)(2,1)S(1)} %get-tuple-element.113), channel_id=1, source_target_pairs={{0,16},{8,24},{16,0},{24,8},{1,17},{9,25},{17,1},{25,9},{2,18},{10... | collective-permute-start | bytes 98312 | tf_op jit(solution)/shard_map/ppermute | solution.py:474
  41.7 3.8 %collective-permute-start.13 = (bf16[32,256]{1,0:T(8,128)(2,1)S(1)}, bf16[32,256]{1,0:T(8,128)(2,1)S(1)}, u32[]{:S(2)}, u32[]{:S(2)}) collective-permute-start(bf16[32,256]{1,0:T(8,128)(2,1)S(1)} %get-tuple-element.117), channel_id=1, source_target_pairs={{0,8},{8,0},{16,24},{24,16},{1,9},{9,1},{17,25},{25,17},{2,10},{10... | collective-permute-start | bytes 49160 | tf_op jit(solution)/shard_map/ppermute | solution.py:474
  45.6 6.3 %collective-permute-start.16 = (bf16[32,1280]{1,0:T(8,128)(2,1)S(1)}, bf16[32,1280]{1,0:T(8,128)(2,1)S(1)}, u32[]{:S(2)}, u32[]{:S(2)}) collective-permute-start(bf16[32,1280]{1,0:T(8,128)(2,1)S(1)} %shard_map.149.refs_0_), channel_id=1, source_target_pairs={{0,6},{1,7},{2,4},{3,5},{4,2},{5,3},{6,0},{7,1},{8,14},{9,15},{10,... | collective-permute-start | bytes 245768 | tf_op jit(solution)/shard_map/ppermute | solution.py:474
  47.9 5.7 %collective-permute-start.15 = (bf16[32,1280]{1,0:T(8,128)(2,1)S(1)}, bf16[32,1280]{1,0:T(8,128)(2,1)S(1)}, u32[]{:S(2)}, u32[]{:S(2)}) collective-permute-start(bf16[32,1280]{1,0:T(8,128)(2,1)S(1)} %shard_map.149.refs_0_), channel_id=1, source_target_pairs={{0,4},{1,5},{2,6},{3,7},{4,0},{5,1},{6,2},{7,3},{8,12},{9,13},{10,... | collective-permute-start | bytes 245768 | tf_op jit(solution)/shard_map/ppermute | solution.py:474
  47.9 5.7 %collective-permute-start.14 = (bf16[32,1280]{1,0:T(8,128)(2,1)S(1)}, bf16[32,1280]{1,0:T(8,128)(2,1)S(1)}, u32[]{:S(2)}, u32[]{:S(2)}) collective-permute-start(bf16[32,1280]{1,0:T(8,128)(2,1)S(1)} %shard_map.149.refs_0_), channel_id=1, source_target_pairs={{0,2},{1,3},{2,0},{3,1},{4,6},{5,7},{6,4},{7,5},{8,10},{9,11},{10,... | collective-permute-start | bytes 245768 | tf_op jit(solution)/shard_map/ppermute | solution.py:474
  53.7 6.2 %collective-permute-start.17 = (bf16[128,640]{1,0:T(8,128)(2,1)S(1)}, bf16[128,640]{1,0:T(8,128)(2,1)S(1)}, u32[]{:S(2)}, u32[]{:S(2)}) collective-permute-start(bf16[128,640]{1,0:T(8,128)(2,1)S(1)} %get-tuple-element.138.refs_0_), channel_id=1, source_target_pairs={{0,8},{8,0},{16,24},{24,16},{1,9},{9,1},{17,25},{25,17},{2,10},{10... | collective-permute-start | bytes 491528 | tf_op jit(solution)/shard_map/ppermute | solution.py:474
  55.4 6.8 %collective-permute-start.21 = (bf16[128,640]{1,0:T(8,128)(2,1)S(1)}, bf16[128,640]{1,0:T(8,128)(2,1)S(1)}, u32[]{:S(2)}, u32[]{:S(2)}) collective-permute-start(bf16[128,640]{1,0:T(8,128)(2,1)S(1)} %get-tuple-element.142.refs_4_), channel_id=1, source_target_pairs={{0,16},{8,24},{16,0},{24,8},{1,17},{9,25},{17,1},{25,9},{2,18},{10... | collective-permute-start | bytes 491528 | tf_op jit(solution)/shard_map/ppermute | solution.py:474
  57.0 15.7 %collective-permute-start.18 = (bf16[128,640]{1,0:T(8,128)(2,1)S(1)}, bf16[128,640]{1,0:T(8,128)(2,1)S(1)}, u32[]{:S(2)}, u32[]{:S(2)}) collective-permute-start(bf16[128,640]{1,0:T(8,128)(2,1)S(1)} %get-tuple-element.138.refs_0_), channel_id=1, source_target_pairs={{0,16},{8,24},{16,0},{24,8},{1,17},{9,25},{17,1},{25,9},{2,18},{10... | collective-permute-start | bytes 491528 | tf_op jit(solution)/shard_map/ppermute | solution.py:474
  57.5 15.2 %collective-permute-start.20 = (bf16[128,640]{1,0:T(8,128)(2,1)S(1)}, bf16[128,640]{1,0:T(8,128)(2,1)S(1)}, u32[]{:S(2)}, u32[]{:S(2)}) collective-permute-start(bf16[128,640]{1,0:T(8,128)(2,1)S(1)} %get-tuple-element.142.refs_4_), channel_id=1, source_target_pairs={{0,8},{8,0},{16,24},{24,16},{1,9},{9,1},{17,25},{25,17},{2,10},{10... | collective-permute-start | bytes 491528 | tf_op jit(solution)/shard_map/ppermute | solution.py:474
  60.0 12.8 %collective-permute-start.19 = (bf16[128,640]{1,0:T(8,128)(2,1)S(1)}, bf16[128,640]{1,0:T(8,128)(2,1)S(1)}, u32[]{:S(2)}, u32[]{:S(2)}) collective-permute-start(bf16[128,640]{1,0:T(8,128)(2,1)S(1)} %collective-permute-done.17.refs_1_), channel_id=1, source_target_pairs={{0,16},{8,24},{16,0},{24,8},{1,17},{9,25},{17,1},{25,9},{2,18},{10... | collective-permute-start | bytes 491528 | tf_op jit(solution)/shard_map/ppermute | solution.py:474
  62.2 10.5 %collective-permute-start.22 = (bf16[128,640]{1,0:T(8,128)(2,1)S(1)}, bf16[128,640]{1,0:T(8,128)(2,1)S(1)}, u32[]{:S(2)}, u32[]{:S(2)}) collective-permute-start(bf16[128,640]{1,0:T(8,128)(2,1)S(1)} %collective-permute-done.21.refs_6_), channel_id=1, source_target_pairs={{0,8},{8,0},{16,24},{24,16},{1,9},{9,1},{17,25},{25,17},{2,10},{10... | collective-permute-start | bytes 491528 | tf_op jit(solution)/shard_map/ppermute | solution.py:474
  63.8 5.5 %collective-permute-start.23 = (bf16[256,128]{1,0:T(8,128)(2,1)S(1)}, bf16[256,128]{1,0:T(8,128)(2,1)S(1)}, u32[]{:S(2)}, u32[]{:S(2)}) collective-permute-start(bf16[256,128]{1,0:T(8,128)(2,1)S(1)} %get-tuple-element.135), channel_id=1, source_target_pairs={{0,1},{1,2},{2,3},{3,4},{4,5},{5,6},{6,7},{7,0},{8,9},{9,10},{10,1... | collective-permute-start | bytes 196616 | tf_op jit(solution)/shard_map/ppermute | solution.py:540
  69.3 1.9 %collective-permute-start.24 = (bf16[256,128]{1,0:T(8,128)(2,1)S(1)}, bf16[256,128]{1,0:T(8,128)(2,1)S(1)}, u32[]{:S(2)}, u32[]{:S(2)}) collective-permute-start(bf16[256,128]{1,0:T(8,128)(2,1)S(1)} %get-tuple-element.136), channel_id=1, source_target_pairs={{1,0},{2,1},{3,2},{4,3},{5,4},{6,5},{7,6},{0,7},{9,8},{10,9},{11,1... | collective-permute-start | bytes 196616 | tf_op jit(solution)/shard_map/ppermute | solution.py:540
  72.9 3.1 %collective-permute-start.25 = (bf16[512,1280]{1,0:T(8,128)(2,1)S(1)}, bf16[512,1280]{1,0:T(8,128)(2,1)S(1)}, u32[]{:S(2)}, u32[]{:S(2)}) collective-permute-start(bf16[512,1280]{1,0:T(8,128)(2,1)S(1)} %shard_map.152.own_mid.own_small), channel_id=1, source_target_pairs={{0,1},{1,0},{2,3},{3,2},{4,5},{5,4},{6,7},{7,6},{8,9},{9,8},{10,11... | collective-permute-start | bytes 3932168 | tf_op jit(solution)/shard_map/ppermute | solution.py:474

commit v7 on v6

--- a/solution.py
+++ b/solution.py
@@ -442,13 +442,12 @@
 
 
 def final_kernel(
-    own_mid, got_mid, own_small, got_small, mid_ref, in_ref, out_ref, sorted_ref, *, swapped
+    own_mid, got_mid, own_small, got_small, mid_ref, in_ref, out_ref, sorted_ref, *, order
 ):
     rows = own_mid.shape[0]
     fields = in_ref.shape[1]
     core = lax.axis_index("horiz") % 2
-    outer, inner = swapped
-    block = rows // (outer * inner)
+    block = rows // len(order)
     for mid_half, small_half, half in (
         (own_mid, own_small, core),
         (got_mid, got_small, 1 - core),
@@ -458,9 +457,8 @@
 
         @pl.when(pl.program_id(0) == 0)
         def _():
-            for place in range(outer * inner):
-                target = (place % inner * outer + place // inner) * block
-                sorted_ref[target : target + block, :] = small_half[
+            for place, target in enumerate(order):
+                sorted_ref[target * block : (target + 1) * block, :] = small_half[
                     place * block : (place + 1) * block, :
                 ].astype(F32)
             in_ref[here, :] = sorted_ref[:, :fields]
@@ -612,26 +610,25 @@
     terms_mid = reduce_to([keep_mid, got_mid], MEMBERS)
     fast = lax.axis_size("ens") == 4 and lax.axis_size("horiz") == 8
     if fast:
-        terms_small = reduce_to([keep_small, got_small], FAR)
+        terms_small = reduce_to([keep_small, got_small], NEAR)
         terms_small, delta_one = tie(terms_small, delta_one)
-        terms_small = reduce_to(terms_small, NEAR)
         field, up_rows, down_rows = new_field(delta_one)
-        terms_mid, terms_small, field = tie(terms_mid, terms_small, field)
+        halos = to_neighbours(up_rows, down_rows, "horiz")
+        terms_small = reduce_to(terms_small, FAR)
+        terms_mid, terms_small, field, halos = tie(terms_mid, terms_small, field, halos)
 
         terms_mid = reduce_to(terms_mid, CHIPS)
         terms_small = reduce_to(terms_small, MEMBER_HIGH)
         terms_small, act_two = tie(terms_small, act_two)
         terms_small = reduce_to(terms_small, MEMBER_LOW)
         state_rows = new_state(act_two)
-        terms_mid, terms_small, state_rows, up_rows, down_rows = tie(
-            terms_mid, terms_small, state_rows, up_rows, down_rows
-        )
+        terms_mid, terms_small, state_rows = tie(terms_mid, terms_small, state_rows)
 
         piece = merge(terms_mid, terms_small, factor)
         pieces = collect(piece, CHIPS)
         halves = join([pieces], CHIPS, outs=2)
         groups = collect_members(*halves)
-        grad_rows = finish(field, to_neighbours(up_rows, down_rows, "horiz"))
+        grad_rows = finish(field, halos)
     else:
         state_rows = new_state(act_two)
         field, up_rows, down_rows = new_field(delta_one)
@@ -641,11 +638,16 @@
     groups, grad_rows = tie(groups, grad_rows)
     (own,) = join(groups, MEMBERS)
     (got,) = exchange([own], CORE)
+    order = [0]
+    if fast:
+        order = [
+            (chip % 2 * 2 + chip // 2) * 4 + member for member in range(4) for chip in range(4)
+        ]
     block = units // 4
     mid_half = pl.BlockSpec((units // 2, block), lambda step: (0, step))
     small_half = pl.BlockSpec((units // 2, 2 * fields), lambda step: (0, units // (2 * fields)))
     grad_mid, grad_in, grad_out = pl.pallas_call(
-        functools.partial(final_kernel, swapped=(4, 4) if fast else (1, 1)),
+        functools.partial(final_kernel, order=order),
         grid=(units // block,),
         out_shape=[
             jax.ShapeDtypeStruct(shape, F32)

time: 79.3 us -> 74.8 us (0.943)
  waiting for transfers between devices: 29.7 us -> 26.8 us
  starting transfers between devices: 30.5 us -> 29 us
    ppermute x2, waiting for transfers between devices: 5.51 us -> 1.35 us  [to_neighbours(): lax.ppermute(upward, axis, forward)]
    ppermute x22, waiting for transfers between devices: 22.3 us -> 24.9 us  [exchange(): lax.ppermute(array, axis, [(i, i ^ k << shift) for i in range(count)])]
    ppermute x22, starting transfers between devices: 25.9 us -> 24 us  [exchange(): lax.ppermute(array, axis, [(i, i ^ k << shift) for i in range(count)])]
    ppermute x2, waiting for transfers between devices: 1.91 us -> 0.56 us  [to_neighbours(): lax.ppermute(downward, axis, backward)]
  transfers between devices with their start and end apart: 26 -> 26, of which waited for: 10 -> 14; matrix products, arithmetic and copies ran while one was open for 2% -> 3% of each run, Pallas kernels for 9% -> 9%
where the time goes in v7:
time: 74.8 us; the launch traced here: 74.6 us
  starting transfers between devices  29 us (39%)
  waiting for transfers between devices  26.8 us (36%)
  Pallas kernels  14.3 us (19%)
  local copies, waits for them, and re-layouts  1.92 us (3%)
  between operations  1.53 us (2%)
  other arithmetic  1.1 us (1%)
    ppermute x22, waiting for transfers between devices, exchange(): lax.ppermute(array, axis, [(i, i ^ k << shift) for i in range(count)])  24.9 us
    ppermute x22, starting transfers between devices, exchange(): lax.ppermute(array, axis, [(i, i ^ k << shift) for i in range(count)])  24 us
    pallas_call x16, Pallas kernels, run(): pl.pallas_call(functools.partial(kernel, **names), out_shape=[jax.ShapeDt...  11.1 us
    ppermute x2, starting transfers between devices, to_neighbours(): lax.ppermute(downward, axis, backward)  4.47 us
    pallas_call x1, Pallas kernels, per_device(): pl.pallas_call(functools.partial(final_kernel, order=order), grid=(units...  3.15 us
    unnamed x14, local copies, waits for them, and re-layouts  1.86 us
  transfers between devices with their start and end apart: 26, of which 14 were waited for; matrix products, arithmetic and copies ran while one was open for 3% of the time, Pallas kernels for 9%

profile of v7, /device:TPU:0, one launch (start us, length us, event | category | flops | bytes accessed | tf_op | source)
XLA Modules:
  0.0 74.6 jit_solution(1698428310763563240)
XLA Ops:
  0.6 1.0 %pad_maximum_fusion.1 = f32[130,4,128]{2,1,0:T(4,128)S(1)} fusion(f32[2,4,128]{2,1,0:T(4,128)} %param.12, f32[128,4,128]{2,1,0:T(4,128)} %bitcast.16), kind=kLoop, calls=%fused_computation.1 | loop fusion | flops 66560 | bytes 532480 | tf_op jit(solution)/shard_map/concatenate | solution.py:549
  2.2 4.1 %collective-permute-start.1 = (bf16[272,128]{1,0:T(8,128)(2,1)S(1)}, bf16[272,128]{1,0:T(8,128)(2,1)S(1)}, u32[]{:S(2)}, u32[]{:S(2)}) collective-permute-start(bf16[272,128]{1,0:T(8,128)(2,1)S(1)} %get-tuple-element.78), channel_id=1, source_target_pairs={{1,0},{2,1},{3,2},{4,3},{5,4},{6,5},{7,6},{0,7},{9,8},{10,9},{11,1... | collective-permute-start | bytes 208904 | tf_op jit(solution)/shard_map/ppermute | solution.py:538
  7.0 1.8 %constant_dynamic-update-slice_fusion.1 = bf16[1024,1152]{1,0:T(8,128)(2,1)S(1)} fusion(bf16[1024,1024]{1,0:T(8,128)(2,1)} %param.18), kind=kLoop, calls=%fused_computation.3 | loop fusion | bytes 4194304
  9.9 3.9 %shard_map.139 = (f32[4,128,128]{2,1,0:T(8,128)S(1)}, bf16[128,384]{1,0:T(8,128)(2,1)S(1)}, bf16[1024,384]{1,0:T(8,128)(2,1)}, bf16[1024,384]{1,0:T(8,128)(2,1)S...) custom-call(f32[520,128]{1,0:T(8,128)S(1)} %bitcast.12, ...), custom_call_target="tpu_custom_call" | custom-call | bytes 15000000 | tf_op jit(solution)/shard_map/pallas_call | solution.py:27
  13.8 2.1 %shard_map.140 = (bf16[1024,384]{1,0:T(8,128)(2,1)S(1)}, bf16[512,256]{1,0:T(8,128)(2,1)S(1)}, bf16[512,256]{1,0:T(8,128)(2,1)S(1)}) custom-call(bf16[128,384]{1,0:T(8,128)(2,1)S(1)} %get-tuple-element.82.x_ref, bf16[1024,384]{1,0:T(8,128)(2,1)S(1)} %get-tuple-element.121.act_two_ref, bf16[1024,384]{1,0:T(8,128)(2,1)S(1)} %get-tuple-element.84.delta_two_ref, ...), custom_call_target="tpu_custom_call" | custom-call | bytes 4000000 | tf_op jit(solution)/shard_map/pallas_call | solution.py:27
  16.5 1.1 %collective-permute-done.6.refs_1_ = bf16[512,256]{1,0:T(8,128)(2,1)S(1)} collective-permute-done((bf16[512,256]{1,0:T(8,128)(2,1)S(1)}, bf16[512,256]{1,0:T(8,128)(2,1)S(1)}, u32[]{:S(2)}, u32[]{:S(2)}) %collective-permute-start.6) | collective-permute-done | bytes 262176 | tf_op jit(solution)/shard_map/ppermute | solution.py:472
  18.2 1.8 %collective-permute-start.3 = (bf16[128,1024]{1,0:T(8,128)(2,1)S(1)}, bf16[128,1024]{1,0:T(8,128)(2,1)S(1)}, u32[]{:S(2)}, u32[]{:S(2)}) collective-permute-start(bf16[128,1024]{1,0:T(8,128)(2,1)S(1)} %get-tuple-element.88), channel_id=1, source_target_pairs={{0,8},{8,0},{16,24},{24,16},{1,9},{9,1},{17,25},{25,17},{2,10},{10... | collective-permute-start | bytes 786440 | tf_op jit(solution)/shard_map/ppermute | solution.py:472
  20.0 1.5 %collective-permute-start.4 = (bf16[128,1024]{1,0:T(8,128)(2,1)S(1)}, bf16[128,1024]{1,0:T(8,128)(2,1)S(1)}, u32[]{:S(2)}, u32[]{:S(2)}) collective-permute-start(bf16[128,1024]{1,0:T(8,128)(2,1)S(1)} %get-tuple-element.89), channel_id=1, source_target_pairs={{0,16},{8,24},{16,0},{24,8},{1,17},{9,25},{17,1},{25,9},{2,18},{10... | collective-permute-start | bytes 786440 | tf_op jit(solution)/shard_map/ppermute | solution.py:472
  21.8 1.7 %collective-permute-done.7.refs_1_ = bf16[256,256]{1,0:T(8,128)(2,1)S(1)} collective-permute-done((bf16[256,256]{1,0:T(8,128)(2,1)S(1)}, bf16[256,256]{1,0:T(8,128)(2,1)S(1)}, u32[]{:S(2)}, u32[]{:S(2)}) %collective-permute-start.7) | collective-permute-done | bytes 131104 | tf_op jit(solution)/shard_map/ppermute | solution.py:472
  23.5 1.3 %collective-permute-start.8 = (bf16[128,256]{1,0:T(8,128)(2,1)S(1)}, bf16[128,256]{1,0:T(8,128)(2,1)S(1)}, u32[]{:S(2)}, u32[]{:S(2)}) collective-permute-start(bf16[128,256]{1,0:T(8,128)(2,1)S(1)} %get-tuple-element.99), channel_id=1, source_target_pairs={{0,4},{1,5},{2,6},{3,7},{4,0},{5,1},{6,2},{7,3},{8,12},{9,13},{10,... | collective-permute-start | bytes 196616 | tf_op jit(solution)/shard_map/ppermute | solution.py:472
  25.5 3.8 %collective-permute-done.8.refs_1_ = bf16[128,256]{1,0:T(8,128)(2,1)S(1)} collective-permute-done((bf16[128,256]{1,0:T(8,128)(2,1)S(1)}, bf16[128,256]{1,0:T(8,128)(2,1)S(1)}, u32[]{:S(2)}, u32[]{:S(2)}) %collective-permute-start.8) | collective-permute-done | bytes 65568 | tf_op jit(solution)/shard_map/ppermute | solution.py:472
  29.6 1.3 %collective-permute-done.9.low_ref = bf16[256,128]{1,0:T(8,128)(2,1)S(1)} collective-permute-done((bf16[256,128]{1,0:T(8,128)(2,1)S(1)}, bf16[256,128]{1,0:T(8,128)(2,1)S(1)}, u32[]{:S(2)}, u32[]{:S(2)}) %collective-permute-start.9) | collective-permute-done | bytes 65568 | tf_op jit(solution)/shard_map/ppermute | solution.py:538
  31.5 2.4 %collective-permute-done.4.refs_2_ = bf16[128,1024]{1,0:T(8,128)(2,1)S(1)} collective-permute-done((bf16[128,1024]{1,0:T(8,128)(2,1)S(1)}, bf16[128,1024]{1,0:T(8,128)(2,1)S(1)}, u32[]{:S(2)}, u32[]{:S(2)}) %collective-permute-start.4) | collective-permute-done | bytes 262176 | tf_op jit(solution)/shard_map/ppermute | solution.py:472
  34.1 1.8 %collective-permute-start.11 = (bf16[32,1024]{1,0:T(8,128)(2,1)S(1)}, bf16[32,1024]{1,0:T(8,128)(2,1)S(1)}, u32[]{:S(2)}, u32[]{:S(2)}) collective-permute-start(bf16[32,1024]{1,0:T(8,128)(2,1)S(1)} %get-tuple-element.109), channel_id=1, source_target_pairs={{0,2},{1,3},{2,0},{3,1},{4,6},{5,7},{6,4},{7,5},{8,10},{9,11},{10,... | collective-permute-start | bytes 196616 | tf_op jit(solution)/shard_map/ppermute | solution.py:472
  36.8 1.8 %collective-permute-start.13 = (bf16[32,1024]{1,0:T(8,128)(2,1)S(1)}, bf16[32,1024]{1,0:T(8,128)(2,1)S(1)}, u32[]{:S(2)}, u32[]{:S(2)}) collective-permute-start(bf16[32,1024]{1,0:T(8,128)(2,1)S(1)} %get-tuple-element.111), channel_id=1, source_target_pairs={{0,6},{1,7},{2,4},{3,5},{4,2},{5,3},{6,0},{7,1},{8,14},{9,15},{10,... | collective-permute-start | bytes 196616 | tf_op jit(solution)/shard_map/ppermute | solution.py:472
  38.5 1.6 %collective-permute-start.14 = (bf16[64,256]{1,0:T(8,128)(2,1)S(1)}, bf16[64,256]{1,0:T(8,128)(2,1)S(1)}, u32[]{:S(2)}, u32[]{:S(2)}) collective-permute-start(bf16[64,256]{1,0:T(8,128)(2,1)S(1)} %get-tuple-element.115), channel_id=1, source_target_pairs={{0,16},{8,24},{16,0},{24,8},{1,17},{9,25},{17,1},{25,9},{2,18},{10... | collective-permute-start | bytes 98312 | tf_op jit(solution)/shard_map/ppermute | solution.py:472
  40.1 2.4 %collective-permute-done.14.refs_1_ = bf16[64,256]{1,0:T(8,128)(2,1)S(1)} collective-permute-done((bf16[64,256]{1,0:T(8,128)(2,1)S(1)}, bf16[64,256]{1,0:T(8,128)(2,1)S(1)}, u32[]{:S(2)}, u32[]{:S(2)}) %collective-permute-start.14) | collective-permute-done | bytes 32800 | tf_op jit(solution)/shard_map/ppermute | solution.py:472
  42.5 1.3 %collective-permute-start.15 = (bf16[32,256]{1,0:T(8,128)(2,1)S(1)}, bf16[32,256]{1,0:T(8,128)(2,1)S(1)}, u32[]{:S(2)}, u32[]{:S(2)}) collective-permute-start(bf16[32,256]{1,0:T(8,128)(2,1)S(1)} %get-tuple-element.119), channel_id=1, source_target_pairs={{0,8},{8,0},{16,24},{24,16},{1,9},{9,1},{17,25},{25,17},{2,10},{10... | collective-permute-start | bytes 49160 | tf_op jit(solution)/shard_map/ppermute | solution.py:472
  43.8 1.6 %shard_map.148 = f32[512,128]{1,0:T(8,128)} custom-call(s32[1,1]{1,0:T(1,128)S(6)} %copy.20.count_ref, f32[4,128,128]{2,1,0:T(8,128)S(1)} %get-tuple-element.120.moved_ref, s32[3,128]{1,0:T(4,128)S(1)} %get-tuple-element.150.cols_ref, s32[3,128]{1,0:T(4,128)S(1)} %get-tuple-element.149.mask_ref, bf16[128,384]{1,0:T(8,128)(2,1)S(1)} %get-tuple-element.82.x_ref, ...), custom_call_target="tpu_custom_call" | custom-call | tf_op jit(solution)/shard_map/pallas_call | solution.py:27
  46.4 2.1 %collective-permute-start.18 = (bf16[32,1280]{1,0:T(8,128)(2,1)S(1)}, bf16[32,1280]{1,0:T(8,128)(2,1)S(1)}, u32[]{:S(2)}, u32[]{:S(2)}) collective-permute-start(bf16[32,1280]{1,0:T(8,128)(2,1)S(1)} %shard_map.149.refs_0_), channel_id=1, source_target_pairs={{0,6},{1,7},{2,4},{3,5},{4,2},{5,3},{6,0},{7,1},{8,14},{9,15},{10,... | collective-permute-start | bytes 245768 | tf_op jit(solution)/shard_map/ppermute | solution.py:472
  48.7 2.1 %collective-permute-start.16 = (bf16[32,1280]{1,0:T(8,128)(2,1)S(1)}, bf16[32,1280]{1,0:T(8,128)(2,1)S(1)}, u32[]{:S(2)}, u32[]{:S(2)}) collective-permute-start(bf16[32,1280]{1,0:T(8,128)(2,1)S(1)} %shard_map.149.refs_0_), channel_id=1, source_target_pairs={{0,2},{1,3},{2,0},{3,1},{4,6},{5,7},{6,4},{7,5},{8,10},{9,11},{10,... | collective-permute-start | bytes 245768 | tf_op jit(solution)/shard_map/ppermute | solution.py:472
  50.9 1.9 %collective-permute-done.18.refs_3_ = bf16[32,1280]{1,0:T(8,128)(2,1)S(1)} collective-permute-done((bf16[32,1280]{1,0:T(8,128)(2,1)S(1)}, bf16[32,1280]{1,0:T(8,128)(2,1)S(1)}, u32[]{:S(2)}, u32[]{:S(2)}) %collective-permute-start.18) | collective-permute-done | bytes 81952 | tf_op jit(solution)/shard_map/ppermute | solution.py:472
  52.7 1.7 %collective-permute-done.17.refs_2_ = bf16[32,1280]{1,0:T(8,128)(2,1)S(1)} collective-permute-done((bf16[32,1280]{1,0:T(8,128)(2,1)S(1)}, bf16[32,1280]{1,0:T(8,128)(2,1)S(1)}, u32[]{:S(2)}, u32[]{:S(2)}) %collective-permute-start.17) | collective-permute-done | bytes 81952 | tf_op jit(solution)/shard_map/ppermute | solution.py:472
  54.5 1.3 %collective-permute-start.19 = (bf16[128,640]{1,0:T(8,128)(2,1)S(1)}, bf16[128,640]{1,0:T(8,128)(2,1)S(1)}, u32[]{:S(2)}, u32[]{:S(2)}) collective-permute-start(bf16[128,640]{1,0:T(8,128)(2,1)S(1)} %get-tuple-element.138.refs_0_), channel_id=1, source_target_pairs={{0,8},{8,0},{16,24},{24,16},{1,9},{9,1},{17,25},{25,17},{2,10},{10... | collective-permute-start | bytes 491528 | tf_op jit(solution)/shard_map/ppermute | solution.py:472
  56.6 1.2 %collective-permute-start.20 = (bf16[128,640]{1,0:T(8,128)(2,1)S(1)}, bf16[128,640]{1,0:T(8,128)(2,1)S(1)}, u32[]{:S(2)}, u32[]{:S(2)}) collective-permute-start(bf16[128,640]{1,0:T(8,128)(2,1)S(1)} %get-tuple-element.138.refs_0_), channel_id=1, source_target_pairs={{0,16},{8,24},{16,0},{24,8},{1,17},{9,25},{17,1},{25,9},{2,18},{10... | collective-permute-start | bytes 491528 | tf_op jit(solution)/shard_map/ppermute | solution.py:472
  58.6 2.7 %collective-permute-done.19.refs_1_ = bf16[128,640]{1,0:T(8,128)(2,1)S(1)} collective-permute-done((bf16[128,640]{1,0:T(8,128)(2,1)S(1)}, bf16[128,640]{1,0:T(8,128)(2,1)S(1)}, u32[]{:S(2)}, u32[]{:S(2)}) %collective-permute-start.19) | collective-permute-done | bytes 163872 | tf_op jit(solution)/shard_map/ppermute | solution.py:472
  61.4 1.5 %collective-permute-start.21 = (bf16[128,640]{1,0:T(8,128)(2,1)S(1)}, bf16[128,640]{1,0:T(8,128)(2,1)S(1)}, u32[]{:S(2)}, u32[]{:S(2)}) collective-permute-start(bf16[128,640]{1,0:T(8,128)(2,1)S(1)} %collective-permute-done.19.refs_1_), channel_id=1, source_target_pairs={{0,16},{8,24},{16,0},{24,8},{1,17},{9,25},{17,1},{25,9},{2,18},{10... | collective-permute-start | bytes 491528 | tf_op jit(solution)/shard_map/ppermute | solution.py:472
  63.6 1.5 %shard_map.151 = f32[512,128]{1,0:T(8,128)} custom-call(f32[4,128,128]{2,1,0:T(8,128)S(1)} %get-tuple-element.134.field_ref, bf16[256,128]{1,0:T(8,128)(2,1)S(1)} %collective-permute-done.9.low_ref, bf16[256,128]{1,0:T(8,128)(2,1)S(1)} %collective-permute-done.10.high_ref, bf16[272,128]{1,0:T(8,128)(2,1)S(1)} %collective-permute-done.low_ref.low_mix_ref, ...), custom_call_target="tpu_custom_call" | custom-call | tf_op jit(solution)/shard_map/pallas_call | solution.py:27
  65.1 1.6 %collective-permute-done.21.refs_3_ = bf16[128,640]{1,0:T(8,128)(2,1)S(1)} collective-permute-done((bf16[128,640]{1,0:T(8,128)(2,1)S(1)}, bf16[128,640]{1,0:T(8,128)(2,1)S(1)}, u32[]{:S(2)}, u32[]{:S(2)}) %collective-permute-start.21) | collective-permute-done | bytes 163872 | tf_op jit(solution)/shard_map/ppermute | solution.py:472
  66.7 1.5 %collective-permute-done.24.refs_7_ = bf16[128,640]{1,0:T(8,128)(2,1)S(1)} collective-permute-done((bf16[128,640]{1,0:T(8,128)(2,1)S(1)}, bf16[128,640]{1,0:T(8,128)(2,1)S(1)}, u32[]{:S(2)}, u32[]{:S(2)}) %collective-permute-start.24) | collective-permute-done | bytes 163872 | tf_op jit(solution)/shard_map/ppermute | solution.py:472
  68.5 3.0 %collective-permute-done.25.got_mid.got_small = bf16[512,1280]{1,0:T(8,128)(2,1)S(1)} collective-permute-done((bf16[512,1280]{1,0:T(8,128)(2,1)S(1)}, bf16[512,1280]{1,0:T(8,128)(2,1)S(1)}, u32[]{:S(2)}, u32[]{:S(2)}) %collective-permute-start.25) | collective-permute-done | bytes 1310752 | tf_op jit(solution)/shard_map/ppermute | solution.py:472
  71.5 3.1 %shard_map.153 = (f32[1024,1024]{1,0:T(8,128)}, f32[1024,128]{1,0:T(8,128)}, f32[128,1024]{1,0:T(8,128)}) custom-call(bf16[512,1280]{1,0:T(8,128)(2,1)S(1)} %shard_map.152.own_mid.own_small, bf16[512,1280]{1,0:T(8,128)(2,1)S(1)} %collective-permute-done.25.got_mid.got_small, bf16[512,1280]{1,0:T(8,128)(2,1)S(1)} %shard_map.152.own_mid.own_small, ...), custom_call_target="tpu_custom_call" | custom-call | tf_op jit(solution)/shard_map/pallas_call | solution.py:649
  (54 shorter events, 9.4 us)
Async XLA Ops:
  1.7 7.2 %copy-start.4 = (s32[1,1,3,128]{3,1,2,0:T(1,128)S(1)}, s32[1,1,3,128]{3,1,2,0:T(1,128)}, u32[]{:S(2)}) copy-start(s32[1,1,3,128]{3,1,2,0:T(1,128)} %param.15) | copy-start | bytes 4612
  1.7 7.2 %copy-start.5 = (s32[1,1,3,128]{3,1,2,0:T(1,128)S(1)}, s32[1,1,3,128]{3,1,2,0:T(1,128)}, u32[]{:S(2)}) copy-start(s32[1,1,3,128]{3,1,2,0:T(1,128)} %param.14) | copy-start | bytes 4612
  1.7 7.2 %copy-start.1 = (f32[1,128,4,128]{3,2,1,0:T(4,128)S(1)}, f32[1,128,4,128]{3,2,1,0:T(4,128)}, u32[]{:S(2)}) copy-start(f32[1,128,4,128]{3,2,1,0:T(4,128)} %param.13) | copy-start | bytes 786436
  1.7 7.2 %copy-start.3 = (f32[1,32,4,128]{3,2,1,0:T(4,128)S(1)}, f32[1,32,4,128]{3,2,1,0:T(4,128)}, u32[]{:S(2)}) copy-start(f32[1,32,4,128]{3,2,1,0:T(4,128)} %param.11) | copy-start | bytes 196612
  1.7 8.1 %collective-permute-start = (bf16[272,128]{1,0:T(8,128)(2,1)S(1)}, bf16[272,128]{1,0:T(8,128)(2,1)S(1)}, u32[]{:S(2)}, u32[]{:S(2)}) collective-permute-start(bf16[272,128]{1,0:T(8,128)(2,1)S(1)} %get-tuple-element.77), channel_id=1, source_target_pairs={{0,1},{1,2},{2,3},{3,4},{4,5},{5,6},{6,7},{7,0},{8,9},{9,10},{10,1... | collective-permute-start | bytes 208904 | tf_op jit(solution)/shard_map/ppermute | solution.py:538
  2.2 7.6 %collective-permute-start.1 = (bf16[272,128]{1,0:T(8,128)(2,1)S(1)}, bf16[272,128]{1,0:T(8,128)(2,1)S(1)}, u32[]{:S(2)}, u32[]{:S(2)}) collective-permute-start(bf16[272,128]{1,0:T(8,128)(2,1)S(1)} %get-tuple-element.78), channel_id=1, source_target_pairs={{1,0},{2,1},{3,2},{4,3},{5,4},{6,5},{7,6},{0,7},{9,8},{10,9},{11,1... | collective-permute-start | bytes 208904 | tf_op jit(solution)/shard_map/ppermute | solution.py:538
  7.0 2.7 %copy-start.2 = (bf16[1024,128]{1,0:T(8,128)(2,1)S(1)}, bf16[1024,128]{1,0:T(8,128)(2,1)}, u32[]{:S(2)}) copy-start(bf16[1024,128]{1,0:T(8,128)(2,1)} %param.17) | copy-start | bytes 786436
  7.0 2.8 %copy-start = (bf16[128,1024]{1,0:T(8,128)(2,1)S(1)}, bf16[128,1024]{1,0:T(8,128)(2,1)}, u32[]{:S(2)}) copy-start(bf16[128,1024]{1,0:T(8,128)(2,1)} %w_out_ref.3) | copy-start | bytes 786436
  13.8 2.7 %collective-permute-start.2 = (bf16[512,1024]{1,0:T(8,128)(2,1)S(1)}, bf16[512,1024]{1,0:T(8,128)(2,1)S(1)}, u32[]{:S(2)}, u32[]{:S(2)}) collective-permute-start(bf16[512,1024]{1,0:T(8,128)(2,1)S(1)} %get-tuple-element.81), channel_id=1, source_target_pairs={{0,1},{1,0},{2,3},{3,2},{4,5},{5,4},{6,7},{7,6},{8,9},{9,8},{10,11... | collective-permute-start | bytes 3145736 | tf_op jit(solution)/shard_map/ppermute | solution.py:472
  15.9 1.7 %collective-permute-start.6 = (bf16[512,256]{1,0:T(8,128)(2,1)S(1)}, bf16[512,256]{1,0:T(8,128)(2,1)S(1)}, u32[]{:S(2)}, u32[]{:S(2)}) collective-permute-start(bf16[512,256]{1,0:T(8,128)(2,1)S(1)} %get-tuple-element.92), channel_id=1, source_target_pairs={{0,1},{1,0},{2,3},{3,2},{4,5},{5,4},{6,7},{7,6},{8,9},{9,8},{10,11... | collective-permute-start | bytes 786440 | tf_op jit(solution)/shard_map/ppermute | solution.py:472
  17.7 5.8 %collective-permute-start.7 = (bf16[256,256]{1,0:T(8,128)(2,1)S(1)}, bf16[256,256]{1,0:T(8,128)(2,1)S(1)}, u32[]{:S(2)}, u32[]{:S(2)}) collective-permute-start(bf16[256,256]{1,0:T(8,128)(2,1)S(1)} %get-tuple-element.94), channel_id=1, source_target_pairs={{0,2},{1,3},{2,0},{3,1},{4,6},{5,7},{6,4},{7,5},{8,10},{9,11},{10,... | collective-permute-start | bytes 393224 | tf_op jit(solution)/shard_map/ppermute | solution.py:472
  18.2 13.3 %collective-permute-start.3 = (bf16[128,1024]{1,0:T(8,128)(2,1)S(1)}, bf16[128,1024]{1,0:T(8,128)(2,1)S(1)}, u32[]{:S(2)}, u32[]{:S(2)}) collective-permute-start(bf16[128,1024]{1,0:T(8,128)(2,1)S(1)} %get-tuple-element.88), channel_id=1, source_target_pairs={{0,8},{8,0},{16,24},{24,16},{1,9},{9,1},{17,25},{25,17},{2,10},{10... | collective-permute-start | bytes 786440 | tf_op jit(solution)/shard_map/ppermute | solution.py:472
  20.0 13.9 %collective-permute-start.4 = (bf16[128,1024]{1,0:T(8,128)(2,1)S(1)}, bf16[128,1024]{1,0:T(8,128)(2,1)S(1)}, u32[]{:S(2)}, u32[]{:S(2)}) collective-permute-start(bf16[128,1024]{1,0:T(8,128)(2,1)S(1)} %get-tuple-element.89), channel_id=1, source_target_pairs={{0,16},{8,24},{16,0},{24,8},{1,17},{9,25},{17,1},{25,9},{2,18},{10... | collective-permute-start | bytes 786440 | tf_op jit(solution)/shard_map/ppermute | solution.py:472
  21.5 12.4 %collective-permute-start.5 = (bf16[128,1024]{1,0:T(8,128)(2,1)S(1)}, bf16[128,1024]{1,0:T(8,128)(2,1)S(1)}, u32[]{:S(2)}, u32[]{:S(2)}) collective-permute-start(bf16[128,1024]{1,0:T(8,128)(2,1)S(1)} %get-tuple-element.90), channel_id=1, source_target_pairs={{0,24},{8,16},{16,8},{24,0},{1,25},{9,17},{17,9},{25,1},{2,26},{10... | collective-permute-start | bytes 786440 | tf_op jit(solution)/shard_map/ppermute | solution.py:472
  23.5 5.7 %collective-permute-start.8 = (bf16[128,256]{1,0:T(8,128)(2,1)S(1)}, bf16[128,256]{1,0:T(8,128)(2,1)S(1)}, u32[]{:S(2)}, u32[]{:S(2)}) collective-permute-start(bf16[128,256]{1,0:T(8,128)(2,1)S(1)} %get-tuple-element.99), channel_id=1, source_target_pairs={{0,4},{1,5},{2,6},{3,7},{4,0},{5,1},{6,2},{7,3},{8,12},{9,13},{10,... | collective-permute-start | bytes 196616 | tf_op jit(solution)/shard_map/ppermute | solution.py:472
  25.4 5.5 %collective-permute-start.9 = (bf16[256,128]{1,0:T(8,128)(2,1)S(1)}, bf16[256,128]{1,0:T(8,128)(2,1)S(1)}, u32[]{:S(2)}, u32[]{:S(2)}) collective-permute-start(bf16[256,128]{1,0:T(8,128)(2,1)S(1)} %get-tuple-element.102), channel_id=1, source_target_pairs={{0,1},{1,2},{2,3},{3,4},{4,5},{5,6},{6,7},{7,0},{8,9},{9,10},{10,1... | collective-permute-start | bytes 196616 | tf_op jit(solution)/shard_map/ppermute | solution.py:538
  29.2 2.3 %collective-permute-start.10 = (bf16[256,128]{1,0:T(8,128)(2,1)S(1)}, bf16[256,128]{1,0:T(8,128)(2,1)S(1)}, u32[]{:S(2)}, u32[]{:S(2)}) collective-permute-start(bf16[256,128]{1,0:T(8,128)(2,1)S(1)} %get-tuple-element.103), channel_id=1, source_target_pairs={{1,0},{2,1},{3,2},{4,3},{5,4},{6,5},{7,6},{0,7},{9,8},{10,9},{11,1... | collective-permute-start | bytes 196616 | tf_op jit(solution)/shard_map/ppermute | solution.py:538
  34.1 12.3 %collective-permute-start.11 = (bf16[32,1024]{1,0:T(8,128)(2,1)S(1)}, bf16[32,1024]{1,0:T(8,128)(2,1)S(1)}, u32[]{:S(2)}, u32[]{:S(2)}) collective-permute-start(bf16[32,1024]{1,0:T(8,128)(2,1)S(1)} %get-tuple-element.109), channel_id=1, source_target_pairs={{0,2},{1,3},{2,0},{3,1},{4,6},{5,7},{6,4},{7,5},{8,10},{9,11},{10,... | collective-permute-start | bytes 196616 | tf_op jit(solution)/shard_map/ppermute | solution.py:472
  35.8 10.5 %collective-permute-start.12 = (bf16[32,1024]{1,0:T(8,128)(2,1)S(1)}, bf16[32,1024]{1,0:T(8,128)(2,1)S(1)}, u32[]{:S(2)}, u32[]{:S(2)}) collective-permute-start(bf16[32,1024]{1,0:T(8,128)(2,1)S(1)} %get-tuple-element.110), channel_id=1, source_target_pairs={{0,4},{1,5},{2,6},{3,7},{4,0},{5,1},{6,2},{7,3},{8,12},{9,13},{10,... | collective-permute-start | bytes 196616 | tf_op jit(solution)/shard_map/ppermute | solution.py:472
  36.8 9.6 %collective-permute-start.13 = (bf16[32,1024]{1,0:T(8,128)(2,1)S(1)}, bf16[32,1024]{1,0:T(8,128)(2,1)S(1)}, u32[]{:S(2)}, u32[]{:S(2)}) collective-permute-start(bf16[32,1024]{1,0:T(8,128)(2,1)S(1)} %get-tuple-element.111), channel_id=1, source_target_pairs={{0,6},{1,7},{2,4},{3,5},{4,2},{5,3},{6,0},{7,1},{8,14},{9,15},{10,... | collective-permute-start | bytes 196616 | tf_op jit(solution)/shard_map/ppermute | solution.py:472
  38.5 4.0 %collective-permute-start.14 = (bf16[64,256]{1,0:T(8,128)(2,1)S(1)}, bf16[64,256]{1,0:T(8,128)(2,1)S(1)}, u32[]{:S(2)}, u32[]{:S(2)}) collective-permute-start(bf16[64,256]{1,0:T(8,128)(2,1)S(1)} %get-tuple-element.115), channel_id=1, source_target_pairs={{0,16},{8,24},{16,0},{24,8},{1,17},{9,25},{17,1},{25,9},{2,18},{10... | collective-permute-start | bytes 98312 | tf_op jit(solution)/shard_map/ppermute | solution.py:472
  42.5 3.8 %collective-permute-start.15 = (bf16[32,256]{1,0:T(8,128)(2,1)S(1)}, bf16[32,256]{1,0:T(8,128)(2,1)S(1)}, u32[]{:S(2)}, u32[]{:S(2)}) collective-permute-start(bf16[32,256]{1,0:T(8,128)(2,1)S(1)} %get-tuple-element.119), channel_id=1, source_target_pairs={{0,8},{8,0},{16,24},{24,16},{1,9},{9,1},{17,25},{25,17},{2,10},{10... | collective-permute-start | bytes 49160 | tf_op jit(solution)/shard_map/ppermute | solution.py:472
  46.4 6.3 %collective-permute-start.18 = (bf16[32,1280]{1,0:T(8,128)(2,1)S(1)}, bf16[32,1280]{1,0:T(8,128)(2,1)S(1)}, u32[]{:S(2)}, u32[]{:S(2)}) collective-permute-start(bf16[32,1280]{1,0:T(8,128)(2,1)S(1)} %shard_map.149.refs_0_), channel_id=1, source_target_pairs={{0,6},{1,7},{2,4},{3,5},{4,2},{5,3},{6,0},{7,1},{8,14},{9,15},{10,... | collective-permute-start | bytes 245768 | tf_op jit(solution)/shard_map/ppermute | solution.py:472
  48.5 5.9 %collective-permute-start.17 = (bf16[32,1280]{1,0:T(8,128)(2,1)S(1)}, bf16[32,1280]{1,0:T(8,128)(2,1)S(1)}, u32[]{:S(2)}, u32[]{:S(2)}) collective-permute-start(bf16[32,1280]{1,0:T(8,128)(2,1)S(1)} %shard_map.149.refs_0_), channel_id=1, source_target_pairs={{0,4},{1,5},{2,6},{3,7},{4,0},{5,1},{6,2},{7,3},{8,12},{9,13},{10,... | collective-permute-start | bytes 245768 | tf_op jit(solution)/shard_map/ppermute | solution.py:472
  48.7 5.7 %collective-permute-start.16 = (bf16[32,1280]{1,0:T(8,128)(2,1)S(1)}, bf16[32,1280]{1,0:T(8,128)(2,1)S(1)}, u32[]{:S(2)}, u32[]{:S(2)}) collective-permute-start(bf16[32,1280]{1,0:T(8,128)(2,1)S(1)} %shard_map.149.refs_0_), channel_id=1, source_target_pairs={{0,2},{1,3},{2,0},{3,1},{4,6},{5,7},{6,4},{7,5},{8,10},{9,11},{10,... | collective-permute-start | bytes 245768 | tf_op jit(solution)/shard_map/ppermute | solution.py:472
  54.5 6.9 %collective-permute-start.19 = (bf16[128,640]{1,0:T(8,128)(2,1)S(1)}, bf16[128,640]{1,0:T(8,128)(2,1)S(1)}, u32[]{:S(2)}, u32[]{:S(2)}) collective-permute-start(bf16[128,640]{1,0:T(8,128)(2,1)S(1)} %get-tuple-element.138.refs_0_), channel_id=1, source_target_pairs={{0,8},{8,0},{16,24},{24,16},{1,9},{9,1},{17,25},{25,17},{2,10},{10... | collective-permute-start | bytes 491528 | tf_op jit(solution)/shard_map/ppermute | solution.py:472
  55.8 7.1 %collective-permute-start.23 = (bf16[128,640]{1,0:T(8,128)(2,1)S(1)}, bf16[128,640]{1,0:T(8,128)(2,1)S(1)}, u32[]{:S(2)}, u32[]{:S(2)}) collective-permute-start(bf16[128,640]{1,0:T(8,128)(2,1)S(1)} %get-tuple-element.142.refs_4_), channel_id=1, source_target_pairs={{0,16},{8,24},{16,0},{24,8},{1,17},{9,25},{17,1},{25,9},{2,18},{10... | collective-permute-start | bytes 491528 | tf_op jit(solution)/shard_map/ppermute | solution.py:472
  56.6 8.5 %collective-permute-start.20 = (bf16[128,640]{1,0:T(8,128)(2,1)S(1)}, bf16[128,640]{1,0:T(8,128)(2,1)S(1)}, u32[]{:S(2)}, u32[]{:S(2)}) collective-permute-start(bf16[128,640]{1,0:T(8,128)(2,1)S(1)} %get-tuple-element.138.refs_0_), channel_id=1, source_target_pairs={{0,16},{8,24},{16,0},{24,8},{1,17},{9,25},{17,1},{25,9},{2,18},{10... | collective-permute-start | bytes 491528 | tf_op jit(solution)/shard_map/ppermute | solution.py:472
  57.8 7.3 %collective-permute-start.22 = (bf16[128,640]{1,0:T(8,128)(2,1)S(1)}, bf16[128,640]{1,0:T(8,128)(2,1)S(1)}, u32[]{:S(2)}, u32[]{:S(2)}) collective-permute-start(bf16[128,640]{1,0:T(8,128)(2,1)S(1)} %get-tuple-element.142.refs_4_), channel_id=1, source_target_pairs={{0,8},{8,0},{16,24},{24,16},{1,9},{9,1},{17,25},{25,17},{2,10},{10... | collective-permute-start | bytes 491528 | tf_op jit(solution)/shard_map/ppermute | solution.py:472
  61.4 5.3 %collective-permute-start.21 = (bf16[128,640]{1,0:T(8,128)(2,1)S(1)}, bf16[128,640]{1,0:T(8,128)(2,1)S(1)}, u32[]{:S(2)}, u32[]{:S(2)}) collective-permute-start(bf16[128,640]{1,0:T(8,128)(2,1)S(1)} %collective-permute-done.19.refs_1_), channel_id=1, source_target_pairs={{0,16},{8,24},{16,0},{24,8},{1,17},{9,25},{17,1},{25,9},{2,18},{10... | collective-permute-start | bytes 491528 | tf_op jit(solution)/shard_map/ppermute | solution.py:472
  62.9 5.3 %collective-permute-start.24 = (bf16[128,640]{1,0:T(8,128)(2,1)S(1)}, bf16[128,640]{1,0:T(8,128)(2,1)S(1)}, u32[]{:S(2)}, u32[]{:S(2)}) collective-permute-start(bf16[128,640]{1,0:T(8,128)(2,1)S(1)} %collective-permute-done.23.refs_6_), channel_id=1, source_target_pairs={{0,8},{8,0},{16,24},{24,16},{1,9},{9,1},{17,25},{25,17},{2,10},{10... | collective-permute-start | bytes 491528 | tf_op jit(solution)/shard_map/ppermute | solution.py:472
  68.4 3.1 %collective-permute-start.25 = (bf16[512,1280]{1,0:T(8,128)(2,1)S(1)}, bf16[512,1280]{1,0:T(8,128)(2,1)S(1)}, u32[]{:S(2)}, u32[]{:S(2)}) collective-permute-start(bf16[512,1280]{1,0:T(8,128)(2,1)S(1)} %shard_map.152.own_mid.own_small), channel_id=1, source_target_pairs={{0,1},{1,0},{2,3},{3,2},{4,5},{5,4},{6,7},{7,6},{8,9},{9,8},{10,11... | collective-permute-start | bytes 3932168 | tf_op jit(solution)/shard_map/ppermute | solution.py:472

commit v8 on v7

--- a/solution.py
+++ b/solution.py
@@ -582,7 +582,10 @@
         backward_kernel, [hidden, half, half], moved=4 * 10**6
     )(x_now, act_two, delta_two, adjoint, weights)
     got_mid, keep_small = tie(got_mid, keep_small)
+    parts_mid = add([keep_mid, got_mid], MEMBERS)
+    terms_mid = [parts_mid[0]] + exchange(parts_mid[1:], MEMBERS)
     (got_small,) = exchange([send_small], CORE)
+    keep_small, delta_one = tie(keep_small, delta_one, parts_mid)[:2]
 
     def new_state(act_two):
         return call(
@@ -607,11 +610,9 @@
             field, *halos, low_pack, high_pack, base
         )[0]
 
-    terms_mid = reduce_to([keep_mid, got_mid], MEMBERS)
     fast = lax.axis_size("ens") == 4 and lax.axis_size("horiz") == 8
     if fast:
         terms_small = reduce_to([keep_small, got_small], NEAR)
-        terms_small, delta_one = tie(terms_small, delta_one)
         field, up_rows, down_rows = new_field(delta_one)
         halos = to_neighbours(up_rows, down_rows, "horiz")
         terms_small = reduce_to(terms_small, FAR)
@@ -619,23 +620,22 @@
 
         terms_mid = reduce_to(terms_mid, CHIPS)
         terms_small = reduce_to(terms_small, MEMBER_HIGH)
-        terms_small, act_two = tie(terms_small, act_two)
         terms_small = reduce_to(terms_small, MEMBER_LOW)
-        state_rows = new_state(act_two)
-        terms_mid, terms_small, state_rows = tie(terms_mid, terms_small, state_rows)
+        terms_mid, terms_small = tie(terms_mid, terms_small)
 
         piece = merge(terms_mid, terms_small, factor)
         pieces = collect(piece, CHIPS)
-        halves = join([pieces], CHIPS, outs=2)
+        halves, act_two = tie(join([pieces], CHIPS, outs=2), act_two)
         groups = collect_members(*halves)
         grad_rows = finish(field, halos)
+        state_rows = new_state(act_two)
     else:
         state_rows = new_state(act_two)
         field, up_rows, down_rows = new_field(delta_one)
         grad_rows = finish(field, to_neighbours(up_rows, down_rows, "horiz"))
         terms_small = reduce_to([keep_small, got_small], MEMBERS)
         groups = [collect(over_all_chips(merge(terms_mid, terms_small, 1.0), factor), MEMBERS)]
-    groups, grad_rows = tie(groups, grad_rows)
+    groups, grad_rows, state_rows = tie(groups, grad_rows, state_rows)
     (own,) = join(groups, MEMBERS)
     (got,) = exchange([own], CORE)
     order = [0]

time: 74.8 us -> 73.8 us (0.987)
  waiting for transfers between devices: 26.8 us -> 24.7 us
  starting transfers between devices: 29 us -> 30.1 us
    ppermute x22, waiting for transfers between devices: 24.9 us -> 23.3 us  [exchange(): lax.ppermute(array, axis, [(i, i ^ k << shift) for i in range(count)])]
    ppermute x22, starting transfers between devices: 24 us -> 24.8 us  [exchange(): lax.ppermute(array, axis, [(i, i ^ k << shift) for i in range(count)])]
  transfers between devices with their start and end apart: 26 -> 26, of which waited for: 14 -> 11; matrix products, arithmetic and copies ran while one was open for 3% -> 3% of each run, Pallas kernels for 9% -> 9%
where the time goes in v8:
time: 73.8 us; the launch traced here: 73.6 us
  starting transfers between devices  30.1 us (41%)
  waiting for transfers between devices  24.7 us (33%)
  Pallas kernels  14.3 us (19%)
  local copies, waits for them, and re-layouts  1.92 us (3%)
  between operations  1.55 us (2%)
  other arithmetic  1.1 us (1%)
    ppermute x22, starting transfers between devices, exchange(): lax.ppermute(array, axis, [(i, i ^ k << shift) for i in range(count)])  24.8 us
    ppermute x22, waiting for transfers between devices, exchange(): lax.ppermute(array, axis, [(i, i ^ k << shift) for i in range(count)])  23.3 us
    pallas_call x16, Pallas kernels, run(): pl.pallas_call(functools.partial(kernel, **names), out_shape=[jax.ShapeDt...  11.2 us
    ppermute x2, starting transfers between devices, to_neighbours(): lax.ppermute(downward, axis, backward)  4.7 us
    pallas_call x1, Pallas kernels, per_device(): pl.pallas_call(functools.partial(final_kernel, order=order), grid=(units...  3.15 us
    unnamed x14, local copies, waits for them, and re-layouts  1.86 us
  transfers between devices with their start and end apart: 26, of which 11 were waited for; matrix products, arithmetic and copies ran while one was open for 3% of the time, Pallas kernels for 9%

profile of v8, /device:TPU:0, one launch (start us, length us, event | category | flops | bytes accessed | tf_op | source)
XLA Modules:
  0.0 73.6 jit_solution(346776273814719164)
XLA Ops:
  0.6 1.0 %pad_maximum_fusion.1 = f32[130,4,128]{2,1,0:T(4,128)S(1)} fusion(f32[2,4,128]{2,1,0:T(4,128)} %param.12, f32[128,4,128]{2,1,0:T(4,128)} %bitcast.16), kind=kLoop, calls=%fused_computation.1 | loop fusion | flops 66560 | bytes 532480 | tf_op jit(solution)/shard_map/concatenate | solution.py:549
  2.2 4.1 %collective-permute-start.1 = (bf16[272,128]{1,0:T(8,128)(2,1)S(1)}, bf16[272,128]{1,0:T(8,128)(2,1)S(1)}, u32[]{:S(2)}, u32[]{:S(2)}) collective-permute-start(bf16[272,128]{1,0:T(8,128)(2,1)S(1)} %get-tuple-element.77), channel_id=1, source_target_pairs={{1,0},{2,1},{3,2},{4,3},{5,4},{6,5},{7,6},{0,7},{9,8},{10,9},{11,1... | collective-permute-start | bytes 208904 | tf_op jit(solution)/shard_map/ppermute | solution.py:538
  7.0 1.8 %constant_dynamic-update-slice_fusion.1 = bf16[1024,1152]{1,0:T(8,128)(2,1)S(1)} fusion(bf16[1024,1024]{1,0:T(8,128)(2,1)} %param.18), kind=kLoop, calls=%fused_computation.3 | loop fusion | bytes 4194304
  9.0 0.8 %shard_map.138 = (f32[3,128,128]{2,1,0:T(8,128)S(1)}, f32[32,384]{1,0:T(8,128)S(1)}, f32[32,384]{1,0:T(8,128)S(1)}, f32[32,384]{1,0:T(8,128)S(1)}) custom-call(s32[1,1]{1,0:T(1,128)S(6)} %copy.20.count_ref, f32[640,128]{1,0:T(8,128)S(1)} %bitcast.14, s32[3,128]{1,0:T(4,128)S(1)} %get-tuple-element.148.cols_ref, s32[3,128]{1,0:T(4,128)S(1)} %get-tuple-element.147.mask_ref), custom_call_target="tpu_custom_call" | custom-call | bytes 30000000 | tf_op jit(solution)/shard_map/pallas_call | solution.py:27
  9.9 3.9 %shard_map.139 = (f32[4,128,128]{2,1,0:T(8,128)S(1)}, bf16[128,384]{1,0:T(8,128)(2,1)S(1)}, bf16[1024,384]{1,0:T(8,128)(2,1)}, bf16[1024,384]{1,0:T(8,128)(2,1)S...) custom-call(f32[520,128]{1,0:T(8,128)S(1)} %bitcast.12, ...), custom_call_target="tpu_custom_call" | custom-call | bytes 15000000 | tf_op jit(solution)/shard_map/pallas_call | solution.py:27
  13.8 2.1 %shard_map.140 = (bf16[1024,384]{1,0:T(8,128)(2,1)S(1)}, bf16[512,256]{1,0:T(8,128)(2,1)S(1)}, bf16[512,256]{1,0:T(8,128)(2,1)S(1)}) custom-call(bf16[128,384]{1,0:T(8,128)(2,1)S(1)} %get-tuple-element.81.x_ref, bf16[1024,384]{1,0:T(8,128)(2,1)S(1)} %get-tuple-element.130.act_two_ref, bf16[1024,384]{1,0:T(8,128)(2,1)S(1)} %get-tuple-element.83.delta_two_ref, ...), custom_call_target="tpu_custom_call" | custom-call | bytes 4000000 | tf_op jit(solution)/shard_map/pallas_call | solution.py:27
  16.7 2.0 %collective-permute-start.3 = (bf16[128,1024]{1,0:T(8,128)(2,1)S(1)}, bf16[128,1024]{1,0:T(8,128)(2,1)S(1)}, u32[]{:S(2)}, u32[]{:S(2)}) collective-permute-start(bf16[128,1024]{1,0:T(8,128)(2,1)S(1)} %get-tuple-element.87), channel_id=1, source_target_pairs={{0,8},{8,0},{16,24},{24,16},{1,9},{9,1},{17,25},{25,17},{2,10},{10... | collective-permute-start | bytes 786440 | tf_op jit(solution)/shard_map/ppermute | solution.py:472
  18.7 1.5 %collective-permute-start.4 = (bf16[128,1024]{1,0:T(8,128)(2,1)S(1)}, bf16[128,1024]{1,0:T(8,128)(2,1)S(1)}, u32[]{:S(2)}, u32[]{:S(2)}) collective-permute-start(bf16[128,1024]{1,0:T(8,128)(2,1)S(1)} %get-tuple-element.88), channel_id=1, source_target_pairs={{0,16},{8,24},{16,0},{24,8},{1,17},{9,25},{17,1},{25,9},{2,18},{10... | collective-permute-start | bytes 786440 | tf_op jit(solution)/shard_map/ppermute | solution.py:472
  21.3 4.1 %collective-permute-done.7.refs_1_ = bf16[256,256]{1,0:T(8,128)(2,1)S(1)} collective-permute-done((bf16[256,256]{1,0:T(8,128)(2,1)S(1)}, bf16[256,256]{1,0:T(8,128)(2,1)S(1)}, u32[]{:S(2)}, u32[]{:S(2)}) %collective-permute-start.7) | collective-permute-done | bytes 131104 | tf_op jit(solution)/shard_map/ppermute | solution.py:472
  26.0 0.7 collective-permute-done.9.low_ref
  26.7 0.8 %collective-permute-start.8 = (bf16[128,256]{1,0:T(8,128)(2,1)S(1)}, bf16[128,256]{1,0:T(8,128)(2,1)S(1)}, u32[]{:S(2)}, u32[]{:S(2)}) collective-permute-start(bf16[128,256]{1,0:T(8,128)(2,1)S(1)} %get-tuple-element.97), channel_id=1, source_target_pairs={{0,4},{1,5},{2,6},{3,7},{4,0},{5,1},{6,2},{7,3},{8,12},{9,13},{10,... | collective-permute-start | bytes 196616 | tf_op jit(solution)/shard_map/ppermute | solution.py:472
  28.2 4.4 %collective-permute-done.8.refs_1_ = bf16[128,256]{1,0:T(8,128)(2,1)S(1)} collective-permute-done((bf16[128,256]{1,0:T(8,128)(2,1)S(1)}, bf16[128,256]{1,0:T(8,128)(2,1)S(1)}, u32[]{:S(2)}, u32[]{:S(2)}) %collective-permute-start.8) | collective-permute-done | bytes 65568 | tf_op jit(solution)/shard_map/ppermute | solution.py:472
  32.9 2.8 %collective-permute-start.12 = (bf16[32,1024]{1,0:T(8,128)(2,1)S(1)}, bf16[32,1024]{1,0:T(8,128)(2,1)S(1)}, u32[]{:S(2)}, u32[]{:S(2)}) collective-permute-start(bf16[32,1024]{1,0:T(8,128)(2,1)S(1)} %get-tuple-element.108), channel_id=1, source_target_pairs={{0,4},{1,5},{2,6},{3,7},{4,0},{5,1},{6,2},{7,3},{8,12},{9,13},{10,... | collective-permute-start | bytes 196616 | tf_op jit(solution)/shard_map/ppermute | solution.py:472
  35.6 1.6 %collective-permute-start.13 = (bf16[32,1024]{1,0:T(8,128)(2,1)S(1)}, bf16[32,1024]{1,0:T(8,128)(2,1)S(1)}, u32[]{:S(2)}, u32[]{:S(2)}) collective-permute-start(bf16[32,1024]{1,0:T(8,128)(2,1)S(1)} %get-tuple-element.109), channel_id=1, source_target_pairs={{0,6},{1,7},{2,4},{3,5},{4,2},{5,3},{6,0},{7,1},{8,14},{9,15},{10,... | collective-permute-start | bytes 196616 | tf_op jit(solution)/shard_map/ppermute | solution.py:472
  37.2 1.8 %collective-permute-start.14 = (bf16[64,256]{1,0:T(8,128)(2,1)S(1)}, bf16[64,256]{1,0:T(8,128)(2,1)S(1)}, u32[]{:S(2)}, u32[]{:S(2)}) collective-permute-start(bf16[64,256]{1,0:T(8,128)(2,1)S(1)} %get-tuple-element.113), channel_id=1, source_target_pairs={{0,16},{8,24},{16,0},{24,8},{1,17},{9,25},{17,1},{25,9},{2,18},{10... | collective-permute-start | bytes 98312 | tf_op jit(solution)/shard_map/ppermute | solution.py:472
  39.1 2.2 %collective-permute-done.14.refs_1_ = bf16[64,256]{1,0:T(8,128)(2,1)S(1)} collective-permute-done((bf16[64,256]{1,0:T(8,128)(2,1)S(1)}, bf16[64,256]{1,0:T(8,128)(2,1)S(1)}, u32[]{:S(2)}, u32[]{:S(2)}) %collective-permute-start.14) | collective-permute-done | bytes 32800 | tf_op jit(solution)/shard_map/ppermute | solution.py:472
  41.2 1.8 %collective-permute-start.15 = (bf16[32,256]{1,0:T(8,128)(2,1)S(1)}, bf16[32,256]{1,0:T(8,128)(2,1)S(1)}, u32[]{:S(2)}, u32[]{:S(2)}) collective-permute-start(bf16[32,256]{1,0:T(8,128)(2,1)S(1)} %get-tuple-element.115), channel_id=1, source_target_pairs={{0,8},{8,0},{16,24},{24,16},{1,9},{9,1},{17,25},{25,17},{2,10},{10... | collective-permute-start | bytes 49160 | tf_op jit(solution)/shard_map/ppermute | solution.py:472
  43.0 2.0 %collective-permute-done.15.refs_5_ = bf16[32,256]{1,0:T(8,128)(2,1)S(1)} collective-permute-done((bf16[32,256]{1,0:T(8,128)(2,1)S(1)}, bf16[32,256]{1,0:T(8,128)(2,1)S(1)}, u32[]{:S(2)}, u32[]{:S(2)}) %collective-permute-start.15) | collective-permute-done | bytes 16416 | tf_op jit(solution)/shard_map/ppermute | solution.py:472
  45.1 2.3 %collective-permute-start.18 = (bf16[32,1280]{1,0:T(8,128)(2,1)S(1)}, bf16[32,1280]{1,0:T(8,128)(2,1)S(1)}, u32[]{:S(2)}, u32[]{:S(2)}) collective-permute-start(bf16[32,1280]{1,0:T(8,128)(2,1)S(1)} %shard_map.148.refs_0_), channel_id=1, source_target_pairs={{0,6},{1,7},{2,4},{3,5},{4,2},{5,3},{6,0},{7,1},{8,14},{9,15},{10,... | collective-permute-start | bytes 245768 | tf_op jit(solution)/shard_map/ppermute | solution.py:472
  47.4 2.1 %collective-permute-start.16 = (bf16[32,1280]{1,0:T(8,128)(2,1)S(1)}, bf16[32,1280]{1,0:T(8,128)(2,1)S(1)}, u32[]{:S(2)}, u32[]{:S(2)}) collective-permute-start(bf16[32,1280]{1,0:T(8,128)(2,1)S(1)} %shard_map.148.refs_0_), channel_id=1, source_target_pairs={{0,2},{1,3},{2,0},{3,1},{4,6},{5,7},{6,4},{7,5},{8,10},{9,11},{10,... | collective-permute-start | bytes 245768 | tf_op jit(solution)/shard_map/ppermute | solution.py:472
  49.6 1.9 %collective-permute-done.18.refs_3_ = bf16[32,1280]{1,0:T(8,128)(2,1)S(1)} collective-permute-done((bf16[32,1280]{1,0:T(8,128)(2,1)S(1)}, bf16[32,1280]{1,0:T(8,128)(2,1)S(1)}, u32[]{:S(2)}, u32[]{:S(2)}) %collective-permute-start.18) | collective-permute-done | bytes 81952 | tf_op jit(solution)/shard_map/ppermute | solution.py:472
  51.5 1.7 %collective-permute-done.17.refs_2_ = bf16[32,1280]{1,0:T(8,128)(2,1)S(1)} collective-permute-done((bf16[32,1280]{1,0:T(8,128)(2,1)S(1)}, bf16[32,1280]{1,0:T(8,128)(2,1)S(1)}, u32[]{:S(2)}, u32[]{:S(2)}) %collective-permute-start.17) | collective-permute-done | bytes 81952 | tf_op jit(solution)/shard_map/ppermute | solution.py:472
  53.2 1.8 %collective-permute-start.19 = (bf16[128,640]{1,0:T(8,128)(2,1)S(1)}, bf16[128,640]{1,0:T(8,128)(2,1)S(1)}, u32[]{:S(2)}, u32[]{:S(2)}) collective-permute-start(bf16[128,640]{1,0:T(8,128)(2,1)S(1)} %get-tuple-element.136.refs_0_), channel_id=1, source_target_pairs={{0,8},{8,0},{16,24},{24,16},{1,9},{9,1},{17,25},{25,17},{2,10},{10... | collective-permute-start | bytes 491528 | tf_op jit(solution)/shard_map/ppermute | solution.py:472
  55.0 1.5 %collective-permute-start.23 = (bf16[128,640]{1,0:T(8,128)(2,1)S(1)}, bf16[128,640]{1,0:T(8,128)(2,1)S(1)}, u32[]{:S(2)}, u32[]{:S(2)}) collective-permute-start(bf16[128,640]{1,0:T(8,128)(2,1)S(1)} %get-tuple-element.140.refs_4_), channel_id=1, source_target_pairs={{0,16},{8,24},{16,0},{24,8},{1,17},{9,25},{17,1},{25,9},{2,18},{10... | collective-permute-start | bytes 491528 | tf_op jit(solution)/shard_map/ppermute | solution.py:472
  57.3 2.6 %collective-permute-done.19.refs_1_ = bf16[128,640]{1,0:T(8,128)(2,1)S(1)} collective-permute-done((bf16[128,640]{1,0:T(8,128)(2,1)S(1)}, bf16[128,640]{1,0:T(8,128)(2,1)S(1)}, u32[]{:S(2)}, u32[]{:S(2)}) %collective-permute-start.19) | collective-permute-done | bytes 163872 | tf_op jit(solution)/shard_map/ppermute | solution.py:472
  59.9 2.0 %collective-permute-start.21 = (bf16[128,640]{1,0:T(8,128)(2,1)S(1)}, bf16[128,640]{1,0:T(8,128)(2,1)S(1)}, u32[]{:S(2)}, u32[]{:S(2)}) collective-permute-start(bf16[128,640]{1,0:T(8,128)(2,1)S(1)} %collective-permute-done.19.refs_1_), channel_id=1, source_target_pairs={{0,16},{8,24},{16,0},{24,8},{1,17},{9,25},{17,1},{25,9},{2,18},{10... | collective-permute-start | bytes 491528 | tf_op jit(solution)/shard_map/ppermute | solution.py:472
  61.9 0.9 %collective-permute-start.24 = (bf16[128,640]{1,0:T(8,128)(2,1)S(1)}, bf16[128,640]{1,0:T(8,128)(2,1)S(1)}, u32[]{:S(2)}, u32[]{:S(2)}) collective-permute-start(bf16[128,640]{1,0:T(8,128)(2,1)S(1)} %collective-permute-done.23.refs_6_), channel_id=1, source_target_pairs={{0,8},{8,0},{16,24},{24,16},{1,9},{9,1},{17,25},{25,17},{2,10},{10... | collective-permute-start | bytes 491528 | tf_op jit(solution)/shard_map/ppermute | solution.py:472
  62.9 1.5 %shard_map.150 = f32[512,128]{1,0:T(8,128)} custom-call(f32[4,128,128]{2,1,0:T(8,128)S(1)} %get-tuple-element.126.field_ref, bf16[256,128]{1,0:T(8,128)(2,1)S(1)} %collective-permute-done.9.low_ref, bf16[256,128]{1,0:T(8,128)(2,1)S(1)} %collective-permute-done.10.high_ref, bf16[272,128]{1,0:T(8,128)(2,1)S(1)} %collective-permute-done.low_ref.low_mix_ref, ...), custom_call_target="tpu_custom_call" | custom-call | tf_op jit(solution)/shard_map/pallas_call | solution.py:27
  64.4 1.6 %shard_map.151 = f32[512,128]{1,0:T(8,128)} custom-call(s32[1,1]{1,0:T(1,128)S(6)} %copy.20.count_ref, f32[4,128,128]{2,1,0:T(8,128)S(1)} %get-tuple-element.129.moved_ref, s32[3,128]{1,0:T(4,128)S(1)} %get-tuple-element.148.cols_ref, s32[3,128]{1,0:T(4,128)S(1)} %get-tuple-element.147.mask_ref, bf16[128,384]{1,0:T(8,128)(2,1)S(1)} %get-tuple-element.81.x_ref, ...), custom_call_target="tpu_custom_call" | custom-call | tf_op jit(solution)/shard_map/pallas_call | solution.py:27
  65.9 1.3 %collective-permute-done.24.refs_7_ = bf16[128,640]{1,0:T(8,128)(2,1)S(1)} collective-permute-done((bf16[128,640]{1,0:T(8,128)(2,1)S(1)}, bf16[128,640]{1,0:T(8,128)(2,1)S(1)}, u32[]{:S(2)}, u32[]{:S(2)}) %collective-permute-start.24) | collective-permute-done | bytes 163872 | tf_op jit(solution)/shard_map/ppermute | solution.py:472
  67.5 3.0 %collective-permute-done.25.got_mid.got_small = bf16[512,1280]{1,0:T(8,128)(2,1)S(1)} collective-permute-done((bf16[512,1280]{1,0:T(8,128)(2,1)S(1)}, bf16[512,1280]{1,0:T(8,128)(2,1)S(1)}, u32[]{:S(2)}, u32[]{:S(2)}) %collective-permute-start.25) | collective-permute-done | bytes 1310752 | tf_op jit(solution)/shard_map/ppermute | solution.py:472
  70.5 3.1 %shard_map.153 = (f32[1024,1024]{1,0:T(8,128)}, f32[1024,128]{1,0:T(8,128)}, f32[128,1024]{1,0:T(8,128)}) custom-call(bf16[512,1280]{1,0:T(8,128)(2,1)S(1)} %shard_map.152.own_mid.own_small, bf16[512,1280]{1,0:T(8,128)(2,1)S(1)} %collective-permute-done.25.got_mid.got_small, bf16[512,1280]{1,0:T(8,128)(2,1)S(1)} %shard_map.152.own_mid.own_small, ...), custom_call_target="tpu_custom_call" | custom-call | tf_op jit(solution)/shard_map/pallas_call | solution.py:649
  (54 shorter events, 5.2 us)
Async XLA Ops:
  1.7 7.2 %copy-start.4 = (s32[1,1,3,128]{3,1,2,0:T(1,128)S(1)}, s32[1,1,3,128]{3,1,2,0:T(1,128)}, u32[]{:S(2)}) copy-start(s32[1,1,3,128]{3,1,2,0:T(1,128)} %param.15) | copy-start | bytes 4612
  1.7 7.2 %copy-start.5 = (s32[1,1,3,128]{3,1,2,0:T(1,128)S(1)}, s32[1,1,3,128]{3,1,2,0:T(1,128)}, u32[]{:S(2)}) copy-start(s32[1,1,3,128]{3,1,2,0:T(1,128)} %param.14) | copy-start | bytes 4612
  1.7 7.2 %copy-start.1 = (f32[1,128,4,128]{3,2,1,0:T(4,128)S(1)}, f32[1,128,4,128]{3,2,1,0:T(4,128)}, u32[]{:S(2)}) copy-start(f32[1,128,4,128]{3,2,1,0:T(4,128)} %param.13) | copy-start | bytes 786436
  1.7 7.2 %copy-start.3 = (f32[1,32,4,128]{3,2,1,0:T(4,128)S(1)}, f32[1,32,4,128]{3,2,1,0:T(4,128)}, u32[]{:S(2)}) copy-start(f32[1,32,4,128]{3,2,1,0:T(4,128)} %param.11) | copy-start | bytes 196612
  1.7 8.1 %collective-permute-start = (bf16[272,128]{1,0:T(8,128)(2,1)S(1)}, bf16[272,128]{1,0:T(8,128)(2,1)S(1)}, u32[]{:S(2)}, u32[]{:S(2)}) collective-permute-start(bf16[272,128]{1,0:T(8,128)(2,1)S(1)} %get-tuple-element.76), channel_id=1, source_target_pairs={{0,1},{1,2},{2,3},{3,4},{4,5},{5,6},{6,7},{7,0},{8,9},{9,10},{10,1... | collective-permute-start | bytes 208904 | tf_op jit(solution)/shard_map/ppermute | solution.py:538
  2.2 7.6 %collective-permute-start.1 = (bf16[272,128]{1,0:T(8,128)(2,1)S(1)}, bf16[272,128]{1,0:T(8,128)(2,1)S(1)}, u32[]{:S(2)}, u32[]{:S(2)}) collective-permute-start(bf16[272,128]{1,0:T(8,128)(2,1)S(1)} %get-tuple-element.77), channel_id=1, source_target_pairs={{1,0},{2,1},{3,2},{4,3},{5,4},{6,5},{7,6},{0,7},{9,8},{10,9},{11,1... | collective-permute-start | bytes 208904 | tf_op jit(solution)/shard_map/ppermute | solution.py:538
  7.0 2.7 %copy-start.2 = (bf16[1024,128]{1,0:T(8,128)(2,1)S(1)}, bf16[1024,128]{1,0:T(8,128)(2,1)}, u32[]{:S(2)}) copy-start(bf16[1024,128]{1,0:T(8,128)(2,1)} %param.17) | copy-start | bytes 786436
  7.0 2.8 %copy-start = (bf16[128,1024]{1,0:T(8,128)(2,1)S(1)}, bf16[128,1024]{1,0:T(8,128)(2,1)}, u32[]{:S(2)}) copy-start(bf16[128,1024]{1,0:T(8,128)(2,1)} %w_out_ref.3) | copy-start | bytes 786436
  13.8 2.7 %collective-permute-start.2 = (bf16[512,1024]{1,0:T(8,128)(2,1)S(1)}, bf16[512,1024]{1,0:T(8,128)(2,1)S(1)}, u32[]{:S(2)}, u32[]{:S(2)}) collective-permute-start(bf16[512,1024]{1,0:T(8,128)(2,1)S(1)} %get-tuple-element.80), channel_id=1, source_target_pairs={{0,1},{1,0},{2,3},{3,2},{4,5},{5,4},{6,7},{7,6},{8,9},{9,8},{10,11... | collective-permute-start | bytes 3145736 | tf_op jit(solution)/shard_map/ppermute | solution.py:472
  15.9 4.4 %collective-permute-start.6 = (bf16[512,256]{1,0:T(8,128)(2,1)S(1)}, bf16[512,256]{1,0:T(8,128)(2,1)S(1)}, u32[]{:S(2)}, u32[]{:S(2)}) collective-permute-start(bf16[512,256]{1,0:T(8,128)(2,1)S(1)} %get-tuple-element.93), channel_id=1, source_target_pairs={{0,1},{1,0},{2,3},{3,2},{4,5},{5,4},{6,7},{7,6},{8,9},{9,8},{10,11... | collective-permute-start | bytes 786440 | tf_op jit(solution)/shard_map/ppermute | solution.py:472
  16.7 15.9 %collective-permute-start.3 = (bf16[128,1024]{1,0:T(8,128)(2,1)S(1)}, bf16[128,1024]{1,0:T(8,128)(2,1)S(1)}, u32[]{:S(2)}, u32[]{:S(2)}) collective-permute-start(bf16[128,1024]{1,0:T(8,128)(2,1)S(1)} %get-tuple-element.87), channel_id=1, source_target_pairs={{0,8},{8,0},{16,24},{24,16},{1,9},{9,1},{17,25},{25,17},{2,10},{10... | collective-permute-start | bytes 786440 | tf_op jit(solution)/shard_map/ppermute | solution.py:472
  18.7 13.9 %collective-permute-start.4 = (bf16[128,1024]{1,0:T(8,128)(2,1)S(1)}, bf16[128,1024]{1,0:T(8,128)(2,1)S(1)}, u32[]{:S(2)}, u32[]{:S(2)}) collective-permute-start(bf16[128,1024]{1,0:T(8,128)(2,1)S(1)} %get-tuple-element.88), channel_id=1, source_target_pairs={{0,16},{8,24},{16,0},{24,8},{1,17},{9,25},{17,1},{25,9},{2,18},{10... | collective-permute-start | bytes 786440 | tf_op jit(solution)/shard_map/ppermute | solution.py:472
  20.2 12.4 %collective-permute-start.5 = (bf16[128,1024]{1,0:T(8,128)(2,1)S(1)}, bf16[128,1024]{1,0:T(8,128)(2,1)S(1)}, u32[]{:S(2)}, u32[]{:S(2)}) collective-permute-start(bf16[128,1024]{1,0:T(8,128)(2,1)S(1)} %get-tuple-element.89), channel_id=1, source_target_pairs={{0,24},{8,16},{16,8},{24,0},{1,25},{9,17},{17,9},{25,1},{2,26},{10... | collective-permute-start | bytes 786440 | tf_op jit(solution)/shard_map/ppermute | solution.py:472
  20.3 5.0 %collective-permute-start.7 = (bf16[256,256]{1,0:T(8,128)(2,1)S(1)}, bf16[256,256]{1,0:T(8,128)(2,1)S(1)}, u32[]{:S(2)}, u32[]{:S(2)}) collective-permute-start(bf16[256,256]{1,0:T(8,128)(2,1)S(1)} %get-tuple-element.95), channel_id=1, source_target_pairs={{0,2},{1,3},{2,0},{3,1},{4,6},{5,7},{6,4},{7,5},{8,10},{9,11},{10,... | collective-permute-start | bytes 393224 | tf_op jit(solution)/shard_map/ppermute | solution.py:472
  21.2 5.5 %collective-permute-start.9 = (bf16[256,128]{1,0:T(8,128)(2,1)S(1)}, bf16[256,128]{1,0:T(8,128)(2,1)S(1)}, u32[]{:S(2)}, u32[]{:S(2)}) collective-permute-start(bf16[256,128]{1,0:T(8,128)(2,1)S(1)} %get-tuple-element.100), channel_id=1, source_target_pairs={{0,1},{1,2},{2,3},{3,4},{4,5},{5,6},{6,7},{7,0},{8,9},{9,10},{10,1... | collective-permute-start | bytes 196616 | tf_op jit(solution)/shard_map/ppermute | solution.py:538
  25.4 2.8 %collective-permute-start.10 = (bf16[256,128]{1,0:T(8,128)(2,1)S(1)}, bf16[256,128]{1,0:T(8,128)(2,1)S(1)}, u32[]{:S(2)}, u32[]{:S(2)}) collective-permute-start(bf16[256,128]{1,0:T(8,128)(2,1)S(1)} %get-tuple-element.101), channel_id=1, source_target_pairs={{1,0},{2,1},{3,2},{4,3},{5,4},{6,5},{7,6},{0,7},{9,8},{10,9},{11,1... | collective-permute-start | bytes 196616 | tf_op jit(solution)/shard_map/ppermute | solution.py:538
  26.7 5.9 %collective-permute-start.8 = (bf16[128,256]{1,0:T(8,128)(2,1)S(1)}, bf16[128,256]{1,0:T(8,128)(2,1)S(1)}, u32[]{:S(2)}, u32[]{:S(2)}) collective-permute-start(bf16[128,256]{1,0:T(8,128)(2,1)S(1)} %get-tuple-element.97), channel_id=1, source_target_pairs={{0,4},{1,5},{2,6},{3,7},{4,0},{5,1},{6,2},{7,3},{8,12},{9,13},{10,... | collective-permute-start | bytes 196616 | tf_op jit(solution)/shard_map/ppermute | solution.py:472
  32.8 12.3 %collective-permute-start.11 = (bf16[32,1024]{1,0:T(8,128)(2,1)S(1)}, bf16[32,1024]{1,0:T(8,128)(2,1)S(1)}, u32[]{:S(2)}, u32[]{:S(2)}) collective-permute-start(bf16[32,1024]{1,0:T(8,128)(2,1)S(1)} %get-tuple-element.107), channel_id=1, source_target_pairs={{0,2},{1,3},{2,0},{3,1},{4,6},{5,7},{6,4},{7,5},{8,10},{9,11},{10,... | collective-permute-start | bytes 196616 | tf_op jit(solution)/shard_map/ppermute | solution.py:472
  32.9 12.2 %collective-permute-start.12 = (bf16[32,1024]{1,0:T(8,128)(2,1)S(1)}, bf16[32,1024]{1,0:T(8,128)(2,1)S(1)}, u32[]{:S(2)}, u32[]{:S(2)}) collective-permute-start(bf16[32,1024]{1,0:T(8,128)(2,1)S(1)} %get-tuple-element.108), channel_id=1, source_target_pairs={{0,4},{1,5},{2,6},{3,7},{4,0},{5,1},{6,2},{7,3},{8,12},{9,13},{10,... | collective-permute-start | bytes 196616 | tf_op jit(solution)/shard_map/ppermute | solution.py:472
  35.6 9.4 %collective-permute-start.13 = (bf16[32,1024]{1,0:T(8,128)(2,1)S(1)}, bf16[32,1024]{1,0:T(8,128)(2,1)S(1)}, u32[]{:S(2)}, u32[]{:S(2)}) collective-permute-start(bf16[32,1024]{1,0:T(8,128)(2,1)S(1)} %get-tuple-element.109), channel_id=1, source_target_pairs={{0,6},{1,7},{2,4},{3,5},{4,2},{5,3},{6,0},{7,1},{8,14},{9,15},{10,... | collective-permute-start | bytes 196616 | tf_op jit(solution)/shard_map/ppermute | solution.py:472
  37.2 4.0 %collective-permute-start.14 = (bf16[64,256]{1,0:T(8,128)(2,1)S(1)}, bf16[64,256]{1,0:T(8,128)(2,1)S(1)}, u32[]{:S(2)}, u32[]{:S(2)}) collective-permute-start(bf16[64,256]{1,0:T(8,128)(2,1)S(1)} %get-tuple-element.113), channel_id=1, source_target_pairs={{0,16},{8,24},{16,0},{24,8},{1,17},{9,25},{17,1},{25,9},{2,18},{10... | collective-permute-start | bytes 98312 | tf_op jit(solution)/shard_map/ppermute | solution.py:472
  41.2 3.8 %collective-permute-start.15 = (bf16[32,256]{1,0:T(8,128)(2,1)S(1)}, bf16[32,256]{1,0:T(8,128)(2,1)S(1)}, u32[]{:S(2)}, u32[]{:S(2)}) collective-permute-start(bf16[32,256]{1,0:T(8,128)(2,1)S(1)} %get-tuple-element.115), channel_id=1, source_target_pairs={{0,8},{8,0},{16,24},{24,16},{1,9},{9,1},{17,25},{25,17},{2,10},{10... | collective-permute-start | bytes 49160 | tf_op jit(solution)/shard_map/ppermute | solution.py:472
  45.1 6.3 %collective-permute-start.18 = (bf16[32,1280]{1,0:T(8,128)(2,1)S(1)}, bf16[32,1280]{1,0:T(8,128)(2,1)S(1)}, u32[]{:S(2)}, u32[]{:S(2)}) collective-permute-start(bf16[32,1280]{1,0:T(8,128)(2,1)S(1)} %shard_map.148.refs_0_), channel_id=1, source_target_pairs={{0,6},{1,7},{2,4},{3,5},{4,2},{5,3},{6,0},{7,1},{8,14},{9,15},{10,... | collective-permute-start | bytes 245768 | tf_op jit(solution)/shard_map/ppermute | solution.py:472
  47.4 5.8 %collective-permute-start.17 = (bf16[32,1280]{1,0:T(8,128)(2,1)S(1)}, bf16[32,1280]{1,0:T(8,128)(2,1)S(1)}, u32[]{:S(2)}, u32[]{:S(2)}) collective-permute-start(bf16[32,1280]{1,0:T(8,128)(2,1)S(1)} %shard_map.148.refs_0_), channel_id=1, source_target_pairs={{0,4},{1,5},{2,6},{3,7},{4,0},{5,1},{6,2},{7,3},{8,12},{9,13},{10,... | collective-permute-start | bytes 245768 | tf_op jit(solution)/shard_map/ppermute | solution.py:472
  47.4 5.8 %collective-permute-start.16 = (bf16[32,1280]{1,0:T(8,128)(2,1)S(1)}, bf16[32,1280]{1,0:T(8,128)(2,1)S(1)}, u32[]{:S(2)}, u32[]{:S(2)}) collective-permute-start(bf16[32,1280]{1,0:T(8,128)(2,1)S(1)} %shard_map.148.refs_0_), channel_id=1, source_target_pairs={{0,2},{1,3},{2,0},{3,1},{4,6},{5,7},{6,4},{7,5},{8,10},{9,11},{10,... | collective-permute-start | bytes 245768 | tf_op jit(solution)/shard_map/ppermute | solution.py:472
  53.2 6.7 %collective-permute-start.19 = (bf16[128,640]{1,0:T(8,128)(2,1)S(1)}, bf16[128,640]{1,0:T(8,128)(2,1)S(1)}, u32[]{:S(2)}, u32[]{:S(2)}) collective-permute-start(bf16[128,640]{1,0:T(8,128)(2,1)S(1)} %get-tuple-element.136.refs_0_), channel_id=1, source_target_pairs={{0,8},{8,0},{16,24},{24,16},{1,9},{9,1},{17,25},{25,17},{2,10},{10... | collective-permute-start | bytes 491528 | tf_op jit(solution)/shard_map/ppermute | solution.py:472
  55.0 6.9 %collective-permute-start.23 = (bf16[128,640]{1,0:T(8,128)(2,1)S(1)}, bf16[128,640]{1,0:T(8,128)(2,1)S(1)}, u32[]{:S(2)}, u32[]{:S(2)}) collective-permute-start(bf16[128,640]{1,0:T(8,128)(2,1)S(1)} %get-tuple-element.140.refs_4_), channel_id=1, source_target_pairs={{0,16},{8,24},{16,0},{24,8},{1,17},{9,25},{17,1},{25,9},{2,18},{10... | collective-permute-start | bytes 491528 | tf_op jit(solution)/shard_map/ppermute | solution.py:472
  56.5 9.4 %collective-permute-start.20 = (bf16[128,640]{1,0:T(8,128)(2,1)S(1)}, bf16[128,640]{1,0:T(8,128)(2,1)S(1)}, u32[]{:S(2)}, u32[]{:S(2)}) collective-permute-start(bf16[128,640]{1,0:T(8,128)(2,1)S(1)} %get-tuple-element.136.refs_0_), channel_id=1, source_target_pairs={{0,16},{8,24},{16,0},{24,8},{1,17},{9,25},{17,1},{25,9},{2,18},{10... | collective-permute-start | bytes 491528 | tf_op jit(solution)/shard_map/ppermute | solution.py:472
  57.0 8.9 %collective-permute-start.22 = (bf16[128,640]{1,0:T(8,128)(2,1)S(1)}, bf16[128,640]{1,0:T(8,128)(2,1)S(1)}, u32[]{:S(2)}, u32[]{:S(2)}) collective-permute-start(bf16[128,640]{1,0:T(8,128)(2,1)S(1)} %get-tuple-element.140.refs_4_), channel_id=1, source_target_pairs={{0,8},{8,0},{16,24},{24,16},{1,9},{9,1},{17,25},{25,17},{2,10},{10... | collective-permute-start | bytes 491528 | tf_op jit(solution)/shard_map/ppermute | solution.py:472
  59.9 6.0 %collective-permute-start.21 = (bf16[128,640]{1,0:T(8,128)(2,1)S(1)}, bf16[128,640]{1,0:T(8,128)(2,1)S(1)}, u32[]{:S(2)}, u32[]{:S(2)}) collective-permute-start(bf16[128,640]{1,0:T(8,128)(2,1)S(1)} %collective-permute-done.19.refs_1_), channel_id=1, source_target_pairs={{0,16},{8,24},{16,0},{24,8},{1,17},{9,25},{17,1},{25,9},{2,18},{10... | collective-permute-start | bytes 491528 | tf_op jit(solution)/shard_map/ppermute | solution.py:472
  61.9 5.3 %collective-permute-start.24 = (bf16[128,640]{1,0:T(8,128)(2,1)S(1)}, bf16[128,640]{1,0:T(8,128)(2,1)S(1)}, u32[]{:S(2)}, u32[]{:S(2)}) collective-permute-start(bf16[128,640]{1,0:T(8,128)(2,1)S(1)} %collective-permute-done.23.refs_6_), channel_id=1, source_target_pairs={{0,8},{8,0},{16,24},{24,16},{1,9},{9,1},{17,25},{25,17},{2,10},{10... | collective-permute-start | bytes 491528 | tf_op jit(solution)/shard_map/ppermute | solution.py:472
  67.4 3.1 %collective-permute-start.25 = (bf16[512,1280]{1,0:T(8,128)(2,1)S(1)}, bf16[512,1280]{1,0:T(8,128)(2,1)S(1)}, u32[]{:S(2)}, u32[]{:S(2)}) collective-permute-start(bf16[512,1280]{1,0:T(8,128)(2,1)S(1)} %shard_map.152.own_mid.own_small), channel_id=1, source_target_pairs={{0,1},{1,0},{2,3},{3,2},{4,5},{5,4},{6,7},{7,6},{8,9},{9,8},{10,11... | collective-permute-start | bytes 3932168 | tf_op jit(solution)/shard_map/ppermute | solution.py:472

commit v9 on v6

--- a/solution.py
+++ b/solution.py
@@ -429,42 +429,59 @@
                 ]
 
 
-def merge_kernel(*refs, terms, factor):
-    out_ref = refs[-1]
-    first = 0
-    for group in (refs[:terms], refs[terms:-1]):
-        total = group[0][...].astype(F32)
-        for ref in group[1:]:
-            total = total + ref[...].astype(F32)
-        columns = total.shape[1]
-        out_ref[:, first : first + columns] = (total * factor).astype(BF16)
-        first += columns
-
-
-def final_kernel(
-    own_mid, got_mid, own_small, got_small, mid_ref, in_ref, out_ref, sorted_ref, *, swapped
-):
-    rows = own_mid.shape[0]
+def core_sum_kernel(keep_mid, got_mid, keep_small, got_small, *outs, stage):
+    rows = outs[0].shape[0]
+    for k, out_ref in enumerate(outs):
+        here = pl.ds(pl.multiple_of((position(stage) ^ k) * rows, rows), rows)
+        first = 0
+        for keep_ref, got_ref in ((keep_mid, got_mid), (keep_small, got_small)):
+            columns = keep_ref.shape[1]
+            out_ref[:, first : first + columns] = (
+                keep_ref[here, :].astype(F32) + got_ref[here, :].astype(F32)
+            ).astype(BF16)
+            first += columns
+
+
+def final_kernel(mid_half, small_half, *refs):
+    mid_ref, in_ref, out_ref = refs[-3:]
     fields = in_ref.shape[1]
-    core = lax.axis_index("horiz") % 2
-    outer, inner = swapped
-    block = rows // (outer * inner)
-    for mid_half, small_half, half in (
-        (own_mid, own_small, core),
-        (got_mid, got_small, 1 - core),
-    ):
-        here = pl.ds(pl.multiple_of(half * rows, rows), rows)
-        mid_ref[here, :] = mid_half[...].astype(F32)
-
-        @pl.when(pl.program_id(0) == 0)
-        def _():
-            for place in range(outer * inner):
-                target = (place % inner * outer + place // inner) * block
-                sorted_ref[target : target + block, :] = small_half[
-                    place * block : (place + 1) * block, :
-                ].astype(F32)
-            in_ref[here, :] = sorted_ref[:, :fields]
-            out_ref[:, here] = sorted_ref[:, fields:].T
+    mid_ref[...] = mid_half[...].astype(F32)
+
+    @pl.when(pl.program_id(0) == 0)
+    def _():
+        in_ref[...] = small_half[:, :fields].astype(F32)
+        out_ref[...] = small_half[:, fields:].astype(F32).T
+
+
+def final(rows, other, before, fields):
+    half, columns = rows.shape
+    units = 2 * half
+    block = units // 4
+
+    def place():
+        core = lax.axis_index("horiz") % 2
+        return 1 - core if other else core
+
+    return pl.pallas_call(
+        final_kernel,
+        grid=(units // block,),
+        out_shape=[
+            jax.ShapeDtypeStruct(shape, F32)
+            for shape in ((units, units), (units, fields), (fields, units))
+        ],
+        in_specs=[
+            pl.BlockSpec((half, block), lambda step: (0, step)),
+            pl.BlockSpec((half, 2 * fields), lambda step: (0, units // (2 * fields))),
+        ]
+        + [pl.BlockSpec(memory_space=pl.ANY)] * len(before),
+        out_specs=[
+            pl.BlockSpec((half, block), lambda step: (place(), step)),
+            pl.BlockSpec((half, fields), lambda step: (place(), 0)),
+            pl.BlockSpec((fields, half), lambda step: (0, place())),
+        ],
+        input_output_aliases={2 + index: index for index in range(len(before))},
+        compiler_params=pltpu.CompilerParams(vmem_limit_bytes=VMEM_LIMIT),
+    )(rows, rows, *before)
 
 
 def exchange(arrays, stage):
@@ -513,14 +530,6 @@
 
 def collect(piece, stage):
     return [piece] + exchange([piece] * (stage[2] - 1), stage)
-
-
-def merge(terms_mid, terms_small, factor):
-    rows = terms_mid[0].shape[0]
-    columns = terms_mid[0].shape[1] + terms_small[0].shape[1]
-    return call(
-        merge_kernel, [((rows, columns), BF16)], terms=len(terms_mid), factor=factor
-    )(*terms_mid, *terms_small)[0]
 
 
 def tie(*values):
@@ -583,83 +592,47 @@
     delta_one, keep_small, send_small = call(
         backward_kernel, [hidden, half, half], moved=4 * 10**6
     )(x_now, act_two, delta_two, adjoint, weights)
-    got_mid, keep_small = tie(got_mid, keep_small)
     (got_small,) = exchange([send_small], CORE)
 
-    def new_state(act_two):
-        return call(
-            state_kernel,
-            [((fields * lons, lats), F32)],
-            scratch=[pltpu.VMEM((tiles, fields, width), F32)] * 2,
-            smem=(0,),
-            lons=lons,
-        )(tile_count, moved, cols, mask, x_now, act_two, coef, ratio, inverse, w_out)[0]
-
-    def new_field(delta_one):
-        packed = ((2 * fields, lats), BF16)
-        return call(
-            grad_kernel,
-            [((lons, fields, lats), F32), packed, packed],
-            smem=(0,),
-            lons=lons,
-        )(tile_count, column, cols, mask, delta_one, adjoint, weights)
-
-    def finish(field, halos):
-        return call(last_kernel, [((fields * lons, lats), F32)], lons=lons)(
-            field, *halos, low_pack, high_pack, base
-        )[0]
-
-    terms_mid = reduce_to([keep_mid, got_mid], MEMBERS)
-    fast = lax.axis_size("ens") == 4 and lax.axis_size("horiz") == 8
-    if fast:
-        terms_small = reduce_to([keep_small, got_small], FAR)
-        terms_small, delta_one = tie(terms_small, delta_one)
-        terms_small = reduce_to(terms_small, NEAR)
-        field, up_rows, down_rows = new_field(delta_one)
-        terms_mid, terms_small, field = tie(terms_mid, terms_small, field)
-
-        terms_mid = reduce_to(terms_mid, CHIPS)
-        terms_small = reduce_to(terms_small, MEMBER_HIGH)
-        terms_small, act_two = tie(terms_small, act_two)
-        terms_small = reduce_to(terms_small, MEMBER_LOW)
-        state_rows = new_state(act_two)
-        terms_mid, terms_small, state_rows, up_rows, down_rows = tie(
-            terms_mid, terms_small, state_rows, up_rows, down_rows
-        )
-
-        piece = merge(terms_mid, terms_small, factor)
-        pieces = collect(piece, CHIPS)
-        halves = join([pieces], CHIPS, outs=2)
-        groups = collect_members(*halves)
-        grad_rows = finish(field, to_neighbours(up_rows, down_rows, "horiz"))
+    packed = ((2 * fields, lats), BF16)
+    field, up_rows, down_rows = call(
+        grad_kernel,
+        [((lons, fields, lats), F32), packed, packed],
+        smem=(0,),
+        lons=lons,
+    )(tile_count, column, cols, mask, delta_one, adjoint, weights)
+    got_small, field = tie(got_small, field)
+
+    parts = call(
+        core_sum_kernel,
+        [((units // 2 // MEMBERS[2], units + 2 * fields), BF16)] * MEMBERS[2],
+        stage=MEMBERS,
+    )(keep_mid, got_mid, keep_small, got_small)
+    terms = [parts[0]] + exchange(parts[1:], MEMBERS)
+    act_two, up_rows, down_rows = tie(act_two, up_rows, down_rows, parts)[:3]
+    halos = to_neighbours(up_rows, down_rows, "horiz")
+    (state_rows,) = call(
+        state_kernel,
+        [((fields * lons, lats), F32)],
+        scratch=[pltpu.VMEM((tiles, fields, width), F32)] * 2,
+        smem=(0,),
+        lons=lons,
+    )(tile_count, moved, cols, mask, x_now, act_two, coef, ratio, inverse, w_out)
+    (grad_rows,) = call(last_kernel, [((fields * lons, lats), F32)], lons=lons)(
+        field, *halos, low_pack, high_pack, base
+    )
+    terms, state_rows, grad_rows = tie(terms, state_rows, grad_rows)
+
+    if lax.axis_size("horiz") == 8:
+        terms = reduce_to(terms, CHIPS)
+        pieces = collect(add(terms, None, factor)[0], CHIPS)
+        groups = collect_members(*join([pieces], CHIPS, outs=2))
     else:
-        state_rows = new_state(act_two)
-        field, up_rows, down_rows = new_field(delta_one)
-        grad_rows = finish(field, to_neighbours(up_rows, down_rows, "horiz"))
-        terms_small = reduce_to([keep_small, got_small], MEMBERS)
-        groups = [collect(over_all_chips(merge(terms_mid, terms_small, 1.0), factor), MEMBERS)]
-    groups, grad_rows = tie(groups, grad_rows)
+        groups = [collect(over_all_chips(add(terms, None)[0], factor), MEMBERS)]
     (own,) = join(groups, MEMBERS)
     (got,) = exchange([own], CORE)
-    block = units // 4
-    mid_half = pl.BlockSpec((units // 2, block), lambda step: (0, step))
-    small_half = pl.BlockSpec((units // 2, 2 * fields), lambda step: (0, units // (2 * fields)))
-    grad_mid, grad_in, grad_out = pl.pallas_call(
-        functools.partial(final_kernel, swapped=(4, 4) if fast else (1, 1)),
-        grid=(units // block,),
-        out_shape=[
-            jax.ShapeDtypeStruct(shape, F32)
-            for shape in ((units, units), (units, fields), (fields, units))
-        ],
-        in_specs=[mid_half, mid_half, small_half, small_half],
-        out_specs=[
-            pl.BlockSpec((units, block), lambda step: (0, step)),
-            pl.BlockSpec((units, fields), lambda step: (0, 0)),
-            pl.BlockSpec((fields, units), lambda step: (0, 0)),
-        ],
-        scratch_shapes=[pltpu.VMEM((units // 2, 2 * fields), F32)],
-        compiler_params=pltpu.CompilerParams(vmem_limit_bytes=VMEM_LIMIT),
-    )(own, got, own, got)
+    half_done = final(own, False, [], fields)
+    grad_mid, grad_in, grad_out = final(got, True, half_done, fields)
     return (
         state_rows.reshape(prognostic.shape),
         grad_rows.reshape(prognostic.shape),

time: 79.3 us -> 73.7 us (0.929)
  waiting for transfers between devices: 29.7 us -> 25.8 us
  starting transfers between devices: 30.5 us -> 27.6 us
  Pallas kernels: 14.3 us -> 15.6 us
    ppermute x22 -> x18, starting transfers between devices: 25.9 us -> 19.5 us  [exchange(): lax.ppermute(array, axis, [(i, i ^ k << shift) for i in range(count)])]
    ppermute x2, waiting for transfers between devices: 5.51 us -> 0.47 us  [to_neighbours(): lax.ppermute(upward, axis, forward)]
    ppermute x2, starting transfers between devices: 4.1 us -> 7.64 us  [to_neighbours(): lax.ppermute(downward, axis, backward)]
    ppermute x22 -> x18, waiting for transfers between devices: 22.3 us -> 25.3 us  [exchange(): lax.ppermute(array, axis, [(i, i ^ k << shift) for i in range(count)])]
    ppermute x2, waiting for transfers between devices: 1.91 us -> 0.01 us  [to_neighbours(): lax.ppermute(downward, axis, backward)]
    pallas_call x1 -> x2, Pallas kernels: 3.15 us -> 4.47 us  [final(): pl.pallas_call(final_kernel, grid=(units // block,), out_shape=[jax.Shape...]
    pallas_call x16 -> x12, Pallas kernels: 11.2 us -> 11.1 us  [run(): pl.pallas_call(functools.partial(kernel, **names), out_shape=[jax.ShapeDt...]
  transfers between devices with their start and end apart: 26 -> 22, of which waited for: 10 -> 12; matrix products, arithmetic and copies ran while one was open for 2% -> 3% of each run, Pallas kernels for 9% -> 12%
where the time goes in v9:
time: 73.7 us; the launch traced here: 73.5 us
  starting transfers between devices  27.6 us (37%)
  waiting for transfers between devices  25.8 us (35%)
  Pallas kernels  15.6 us (21%)
  local copies, waits for them, and re-layouts  1.92 us (3%)
  between operations  1.51 us (2%)
  other arithmetic  1.1 us (1%)
    ppermute x18, waiting for transfers between devices, exchange(): lax.ppermute(array, axis, [(i, i ^ k << shift) for i in range(count)])  25.3 us
    ppermute x18, starting transfers between devices, exchange(): lax.ppermute(array, axis, [(i, i ^ k << shift) for i in range(count)])  19.5 us
    pallas_call x12, Pallas kernels, run(): pl.pallas_call(functools.partial(kernel, **names), out_shape=[jax.ShapeDt...  11.1 us
    ppermute x2, starting transfers between devices, to_neighbours(): lax.ppermute(downward, axis, backward)  7.64 us
    pallas_call x2, Pallas kernels, final(): pl.pallas_call(final_kernel, grid=(units // block,), out_shape=[jax.Shape...  4.47 us
    unnamed x14, local copies, waits for them, and re-layouts  1.86 us
  transfers between devices with their start and end apart: 22, of which 12 were waited for; matrix products, arithmetic and copies ran while one was open for 3% of the time, Pallas kernels for 12%

profile of v9, /device:TPU:0, one launch (start us, length us, event | category | flops | bytes accessed | tf_op | source)
XLA Modules:
  0.0 73.5 jit_solution(2543166445804187915)
XLA Ops:
  0.6 1.0 %pad_maximum_fusion.1 = f32[130,4,128]{2,1,0:T(4,128)S(1)} fusion(f32[2,4,128]{2,1,0:T(4,128)} %param.12, f32[128,4,128]{2,1,0:T(4,128)} %bitcast.16), kind=kLoop, calls=%fused_computation.1 | loop fusion | flops 66560 | bytes 532480 | tf_op jit(solution)/shard_map/concatenate | solution.py:560
  2.2 4.1 %collective-permute-start.1 = (bf16[272,128]{1,0:T(8,128)(2,1)S(1)}, bf16[272,128]{1,0:T(8,128)(2,1)S(1)}, u32[]{:S(2)}, u32[]{:S(2)}) collective-permute-start(bf16[272,128]{1,0:T(8,128)(2,1)S(1)} %get-tuple-element.51), channel_id=1, source_target_pairs={{1,0},{2,1},{3,2},{4,3},{5,4},{6,5},{7,6},{0,7},{9,8},{10,9},{11,1... | collective-permute-start | bytes 208904 | tf_op jit(solution)/shard_map/ppermute | solution.py:549
  7.0 1.8 %constant_dynamic-update-slice_fusion.1 = bf16[1024,1152]{1,0:T(8,128)(2,1)S(1)} fusion(bf16[1024,1024]{1,0:T(8,128)(2,1)} %param.18), kind=kLoop, calls=%fused_computation.3 | loop fusion | bytes 4194304
  9.0 0.8 %shard_map.138 = (f32[3,128,128]{2,1,0:T(8,128)S(1)}, f32[32,384]{1,0:T(8,128)S(1)}, f32[32,384]{1,0:T(8,128)S(1)}, f32[32,384]{1,0:T(8,128)S(1)}) custom-call(s32[1,1]{1,0:T(1,128)S(6)} %copy.26.count_ref, f32[640,128]{1,0:T(8,128)S(1)} %bitcast.14, s32[3,128]{1,0:T(4,128)S(1)} %get-tuple-element.96.cols_ref, s32[3,128]{1,0:T(4,128)S(1)} %get-tuple-element.95.mask_ref), custom_call_target="tpu_custom_call" | custom-call | bytes 30000000 | tf_op jit(solution)/shard_map/pallas_call | solution.py:27
  9.9 4.0 %shard_map.139 = (f32[4,128,128]{2,1,0:T(8,128)S(1)}, bf16[128,384]{1,0:T(8,128)(2,1)S(1)}, bf16[1024,384]{1,0:T(8,128)(2,1)}, bf16[1024,384]{1,0:T(8,128)(2,1)S...) custom-call(f32[520,128]{1,0:T(8,128)S(1)} %bitcast.12, ...), custom_call_target="tpu_custom_call" | custom-call | bytes 15000000 | tf_op jit(solution)/shard_map/pallas_call | solution.py:27
  13.8 2.1 %shard_map.140 = (bf16[1024,384]{1,0:T(8,128)(2,1)S(1)}, bf16[512,256]{1,0:T(8,128)(2,1)S(1)}, bf16[512,256]{1,0:T(8,128)(2,1)S(1)}) custom-call(bf16[128,384]{1,0:T(8,128)(2,1)S(1)} %get-tuple-element.55.x_ref, bf16[1024,384]{1,0:T(8,128)(2,1)S(1)} %get-tuple-element.70.act_two_ref, bf16[1024,384]{1,0:T(8,128)(2,1)S(1)} %get-tuple-element.57.delta_two_ref, ...), custom_call_target="tpu_custom_call" | custom-call | bytes 4000000 | tf_op jit(solution)/shard_map/pallas_call | solution.py:27
  17.0 0.6 collective-permute-done.3.got_small
  17.9 2.0 %collective-permute-start.4 = (bf16[128,1280]{1,0:T(8,128)(2,1)S(1)}, bf16[128,1280]{1,0:T(8,128)(2,1)S(1)}, u32[]{:S(2)}, u32[]{:S(2)}) collective-permute-start(bf16[128,1280]{1,0:T(8,128)(2,1)S(1)} %get-tuple-element.64), channel_id=1, source_target_pairs={{0,8},{8,0},{16,24},{24,16},{1,9},{9,1},{17,25},{25,17},{2,10},{10... | collective-permute-start | bytes 983048 | tf_op jit(solution)/shard_map/ppermute | solution.py:491
  19.9 1.5 %collective-permute-start.5 = (bf16[128,1280]{1,0:T(8,128)(2,1)S(1)}, bf16[128,1280]{1,0:T(8,128)(2,1)S(1)}, u32[]{:S(2)}, u32[]{:S(2)}) collective-permute-start(bf16[128,1280]{1,0:T(8,128)(2,1)S(1)} %get-tuple-element.65), channel_id=1, source_target_pairs={{0,16},{8,24},{16,0},{24,8},{1,17},{9,25},{17,1},{25,9},{2,18},{10... | collective-permute-start | bytes 983048 | tf_op jit(solution)/shard_map/ppermute | solution.py:491
  21.5 3.5 %collective-permute-start.8 = (bf16[256,128]{1,0:T(8,128)(2,1)S(1)}, bf16[256,128]{1,0:T(8,128)(2,1)S(1)}, u32[]{:S(2)}, u32[]{:S(2)}) collective-permute-start(bf16[256,128]{1,0:T(8,128)(2,1)S(1)} %get-tuple-element.76), channel_id=1, source_target_pairs={{1,0},{2,1},{3,2},{4,3},{5,4},{6,5},{7,6},{0,7},{9,8},{10,9},{11,1... | collective-permute-start | bytes 196616 | tf_op jit(solution)/shard_map/ppermute | solution.py:549
  25.0 1.6 %shard_map.143 = f32[512,128]{1,0:T(8,128)} custom-call(s32[1,1]{1,0:T(1,128)S(6)} %copy.26.count_ref, f32[4,128,128]{2,1,0:T(8,128)S(1)} %get-tuple-element.67.moved_ref, s32[3,128]{1,0:T(4,128)S(1)} %get-tuple-element.96.cols_ref, s32[3,128]{1,0:T(4,128)S(1)} %get-tuple-element.95.mask_ref, bf16[128,384]{1,0:T(8,128)(2,1)S(1)} %get-tuple-element.55.x_ref, ...), custom_call_target="tpu_custom_call" | custom-call | tf_op jit(solution)/shard_map/pallas_call | solution.py:27
  27.1 1.5 %shard_map.144 = f32[512,128]{1,0:T(8,128)} custom-call(f32[4,128,128]{2,1,0:T(8,128)S(1)} %get-tuple-element.74.field_ref, bf16[256,128]{1,0:T(8,128)(2,1)S(1)} %collective-permute-done.7.low_ref, bf16[256,128]{1,0:T(8,128)(2,1)S(1)} %collective-permute-done.8.high_ref, bf16[272,128]{1,0:T(8,128)(2,1)S(1)} %collective-permute-done.low_ref.low_mix_ref, ...), custom_call_target="tpu_custom_call" | custom-call | tf_op jit(solution)/shard_map/pallas_call | solution.py:27
  28.6 8.1 %collective-permute-done.5.refs_2_ = bf16[128,1280]{1,0:T(8,128)(2,1)S(1)} collective-permute-done((bf16[128,1280]{1,0:T(8,128)(2,1)S(1)}, bf16[128,1280]{1,0:T(8,128)(2,1)S(1)}, u32[]{:S(2)}, u32[]{:S(2)}) %collective-permute-start.5) | collective-permute-done | bytes 327712 | tf_op jit(solution)/shard_map/ppermute | solution.py:491
  36.9 2.6 %collective-permute-start.10 = (bf16[32,1280]{1,0:T(8,128)(2,1)S(1)}, bf16[32,1280]{1,0:T(8,128)(2,1)S(1)}, u32[]{:S(2)}, u32[]{:S(2)}) collective-permute-start(bf16[32,1280]{1,0:T(8,128)(2,1)S(1)} %get-tuple-element.85), channel_id=1, source_target_pairs={{0,4},{1,5},{2,6},{3,7},{4,0},{5,1},{6,2},{7,3},{8,12},{9,13},{10,... | collective-permute-start | bytes 245768 | tf_op jit(solution)/shard_map/ppermute | solution.py:491
  39.5 1.8 %collective-permute-start.11 = (bf16[32,1280]{1,0:T(8,128)(2,1)S(1)}, bf16[32,1280]{1,0:T(8,128)(2,1)S(1)}, u32[]{:S(2)}, u32[]{:S(2)}) collective-permute-start(bf16[32,1280]{1,0:T(8,128)(2,1)S(1)} %get-tuple-element.86), channel_id=1, source_target_pairs={{0,6},{1,7},{2,4},{3,5},{4,2},{5,3},{6,0},{7,1},{8,14},{9,15},{10,... | collective-permute-start | bytes 245768 | tf_op jit(solution)/shard_map/ppermute | solution.py:491
  41.5 4.4 %collective-permute-done.10.refs_2_ = bf16[32,1280]{1,0:T(8,128)(2,1)S(1)} collective-permute-done((bf16[32,1280]{1,0:T(8,128)(2,1)S(1)}, bf16[32,1280]{1,0:T(8,128)(2,1)S(1)}, u32[]{:S(2)}, u32[]{:S(2)}) %collective-permute-start.10) | collective-permute-done | bytes 81952 | tf_op jit(solution)/shard_map/ppermute | solution.py:491
  46.0 1.9 %collective-permute-start.14 = (bf16[32,1280]{1,0:T(8,128)(2,1)S(1)}, bf16[32,1280]{1,0:T(8,128)(2,1)S(1)}, u32[]{:S(2)}, u32[]{:S(2)}) collective-permute-start(bf16[32,1280]{1,0:T(8,128)(2,1)S(1)} %shard_map.146.refs_0_), channel_id=1, source_target_pairs={{0,6},{1,7},{2,4},{3,5},{4,2},{5,3},{6,0},{7,1},{8,14},{9,15},{10,... | collective-permute-start | bytes 245768 | tf_op jit(solution)/shard_map/ppermute | solution.py:491
  47.9 1.0 %collective-permute-start.13 = (bf16[32,1280]{1,0:T(8,128)(2,1)S(1)}, bf16[32,1280]{1,0:T(8,128)(2,1)S(1)}, u32[]{:S(2)}, u32[]{:S(2)}) collective-permute-start(bf16[32,1280]{1,0:T(8,128)(2,1)S(1)} %shard_map.146.refs_0_), channel_id=1, source_target_pairs={{0,4},{1,5},{2,6},{3,7},{4,0},{5,1},{6,2},{7,3},{8,12},{9,13},{10,... | collective-permute-start | bytes 245768 | tf_op jit(solution)/shard_map/ppermute | solution.py:491
  49.0 1.5 %collective-permute-start.12 = (bf16[32,1280]{1,0:T(8,128)(2,1)S(1)}, bf16[32,1280]{1,0:T(8,128)(2,1)S(1)}, u32[]{:S(2)}, u32[]{:S(2)}) collective-permute-start(bf16[32,1280]{1,0:T(8,128)(2,1)S(1)} %shard_map.146.refs_0_), channel_id=1, source_target_pairs={{0,2},{1,3},{2,0},{3,1},{4,6},{5,7},{6,4},{7,5},{8,10},{9,11},{10,... | collective-permute-start | bytes 245768 | tf_op jit(solution)/shard_map/ppermute | solution.py:491
  50.4 2.0 %collective-permute-done.14.refs_3_ = bf16[32,1280]{1,0:T(8,128)(2,1)S(1)} collective-permute-done((bf16[32,1280]{1,0:T(8,128)(2,1)S(1)}, bf16[32,1280]{1,0:T(8,128)(2,1)S(1)}, u32[]{:S(2)}, u32[]{:S(2)}) %collective-permute-start.14) | collective-permute-done | bytes 81952 | tf_op jit(solution)/shard_map/ppermute | solution.py:491
  52.4 2.1 %collective-permute-done.13.refs_2_ = bf16[32,1280]{1,0:T(8,128)(2,1)S(1)} collective-permute-done((bf16[32,1280]{1,0:T(8,128)(2,1)S(1)}, bf16[32,1280]{1,0:T(8,128)(2,1)S(1)}, u32[]{:S(2)}, u32[]{:S(2)}) %collective-permute-start.13) | collective-permute-done | bytes 81952 | tf_op jit(solution)/shard_map/ppermute | solution.py:491
  54.5 1.5 %collective-permute-start.15 = (bf16[128,640]{1,0:T(8,128)(2,1)S(1)}, bf16[128,640]{1,0:T(8,128)(2,1)S(1)}, u32[]{:S(2)}, u32[]{:S(2)}) collective-permute-start(bf16[128,640]{1,0:T(8,128)(2,1)S(1)} %get-tuple-element.87.refs_0_), channel_id=1, source_target_pairs={{0,8},{8,0},{16,24},{24,16},{1,9},{9,1},{17,25},{25,17},{2,10},{10... | collective-permute-start | bytes 491528 | tf_op jit(solution)/shard_map/ppermute | solution.py:491
  56.5 1.6 %collective-permute-start.16 = (bf16[128,640]{1,0:T(8,128)(2,1)S(1)}, bf16[128,640]{1,0:T(8,128)(2,1)S(1)}, u32[]{:S(2)}, u32[]{:S(2)}) collective-permute-start(bf16[128,640]{1,0:T(8,128)(2,1)S(1)} %get-tuple-element.87.refs_0_), channel_id=1, source_target_pairs={{0,16},{8,24},{16,0},{24,8},{1,17},{9,25},{17,1},{25,9},{2,18},{10... | collective-permute-start | bytes 491528 | tf_op jit(solution)/shard_map/ppermute | solution.py:491
  58.6 2.5 %collective-permute-done.15.refs_1_ = bf16[128,640]{1,0:T(8,128)(2,1)S(1)} collective-permute-done((bf16[128,640]{1,0:T(8,128)(2,1)S(1)}, bf16[128,640]{1,0:T(8,128)(2,1)S(1)}, u32[]{:S(2)}, u32[]{:S(2)}) %collective-permute-start.15) | collective-permute-done | bytes 163872 | tf_op jit(solution)/shard_map/ppermute | solution.py:491
  61.2 1.6 %collective-permute-start.17 = (bf16[128,640]{1,0:T(8,128)(2,1)S(1)}, bf16[128,640]{1,0:T(8,128)(2,1)S(1)}, u32[]{:S(2)}, u32[]{:S(2)}) collective-permute-start(bf16[128,640]{1,0:T(8,128)(2,1)S(1)} %collective-permute-done.15.refs_1_), channel_id=1, source_target_pairs={{0,16},{8,24},{16,0},{24,8},{1,17},{9,25},{17,1},{25,9},{2,18},{10... | collective-permute-start | bytes 491528 | tf_op jit(solution)/shard_map/ppermute | solution.py:491
  62.7 0.7 collective-permute-start.20
  63.4 0.8 %collective-permute-done.16.refs_2_ = bf16[128,640]{1,0:T(8,128)(2,1)S(1)} collective-permute-done((bf16[128,640]{1,0:T(8,128)(2,1)S(1)}, bf16[128,640]{1,0:T(8,128)(2,1)S(1)}, u32[]{:S(2)}, u32[]{:S(2)}) %collective-permute-start.16) | collective-permute-done | bytes 163872 | tf_op jit(solution)/shard_map/ppermute | solution.py:491
  64.2 2.3 %collective-permute-done.17.refs_3_ = bf16[128,640]{1,0:T(8,128)(2,1)S(1)} collective-permute-done((bf16[128,640]{1,0:T(8,128)(2,1)S(1)}, bf16[128,640]{1,0:T(8,128)(2,1)S(1)}, u32[]{:S(2)}, u32[]{:S(2)}) %collective-permute-start.17) | collective-permute-done | bytes 163872 | tf_op jit(solution)/shard_map/ppermute | solution.py:491
  66.5 1.6 %collective-permute-done.20.refs_7_ = bf16[128,640]{1,0:T(8,128)(2,1)S(1)} collective-permute-done((bf16[128,640]{1,0:T(8,128)(2,1)S(1)}, bf16[128,640]{1,0:T(8,128)(2,1)S(1)}, u32[]{:S(2)}, u32[]{:S(2)}) %collective-permute-start.20) | collective-permute-done | bytes 163872 | tf_op jit(solution)/shard_map/ppermute | solution.py:491
  68.3 2.2 %shard_map.149 = (f32[1024,1024]{1,0:T(8,128)}, f32[1024,128]{1,0:T(8,128)}, f32[128,1024]{1,0:T(8,128)}) custom-call(bf16[512,1280]{1,0:T(8,128)(2,1)S(1)} %shard_map.148.mid_half.small_half, bf16[512,1280]{1,0:T(8,128)(2,1)S(1)} %shard_map.148.mid_half.small_half), custom_call_target="tpu_custom_call" | custom-call | tf_op jit(solution)/shard_map/pallas_call | solution.py:465
  70.5 0.8 %collective-permute-done.21.mid_half.small_half = bf16[512,1280]{1,0:T(8,128)(2,1)S(1)} collective-permute-done((bf16[512,1280]{1,0:T(8,128)(2,1)S(1)}, bf16[512,1280]{1,0:T(8,128)(2,1)S(1)}, u32[]{:S(2)}, u32[]{:S(2)}) %collective-permute-start.21) | collective-permute-done | bytes 1310752 | tf_op jit(solution)/shard_map/ppermute | solution.py:491
  71.3 2.2 %shard_map.150 = (f32[1024,1024]{1,0:T(8,128)}, f32[1024,128]{1,0:T(8,128)}, f32[128,1024]{1,0:T(8,128)}) custom-call(bf16[512,1280]{1,0:T(8,128)(2,1)S(1)} %collective-permute-done.21.mid_half.small_half, bf16[512,1280]{1,0:T(8,128)(2,1)S(1)} %collective-permute-done.21.mid_half.small_half, ...), custom_call_target="tpu_custom_call", output_to_operand_aliasing={{0}: (2, {}), {1}: (3, {}), {2}: (4, {})} | custom-call | tf_op jit(solution)/shard_map/pallas_call | solution.py:465
  (43 shorter events, 4.4 us)
Async XLA Ops:
  1.7 7.2 %copy-start.4 = (s32[1,1,3,128]{3,1,2,0:T(1,128)S(1)}, s32[1,1,3,128]{3,1,2,0:T(1,128)}, u32[]{:S(2)}) copy-start(s32[1,1,3,128]{3,1,2,0:T(1,128)} %param.15) | copy-start | bytes 4612
  1.7 7.2 %copy-start.5 = (s32[1,1,3,128]{3,1,2,0:T(1,128)S(1)}, s32[1,1,3,128]{3,1,2,0:T(1,128)}, u32[]{:S(2)}) copy-start(s32[1,1,3,128]{3,1,2,0:T(1,128)} %param.14) | copy-start | bytes 4612
  1.7 7.2 %copy-start.1 = (f32[1,128,4,128]{3,2,1,0:T(4,128)S(1)}, f32[1,128,4,128]{3,2,1,0:T(4,128)}, u32[]{:S(2)}) copy-start(f32[1,128,4,128]{3,2,1,0:T(4,128)} %param.13) | copy-start | bytes 786436
  1.7 7.2 %copy-start.3 = (f32[1,32,4,128]{3,2,1,0:T(4,128)S(1)}, f32[1,32,4,128]{3,2,1,0:T(4,128)}, u32[]{:S(2)}) copy-start(f32[1,32,4,128]{3,2,1,0:T(4,128)} %param.11) | copy-start | bytes 196612
  1.7 8.1 %collective-permute-start = (bf16[272,128]{1,0:T(8,128)(2,1)S(1)}, bf16[272,128]{1,0:T(8,128)(2,1)S(1)}, u32[]{:S(2)}, u32[]{:S(2)}) collective-permute-start(bf16[272,128]{1,0:T(8,128)(2,1)S(1)} %get-tuple-element.50), channel_id=1, source_target_pairs={{0,1},{1,2},{2,3},{3,4},{4,5},{5,6},{6,7},{7,0},{8,9},{9,10},{10,1... | collective-permute-start | bytes 208904 | tf_op jit(solution)/shard_map/ppermute | solution.py:549
  2.2 7.6 %collective-permute-start.1 = (bf16[272,128]{1,0:T(8,128)(2,1)S(1)}, bf16[272,128]{1,0:T(8,128)(2,1)S(1)}, u32[]{:S(2)}, u32[]{:S(2)}) collective-permute-start(bf16[272,128]{1,0:T(8,128)(2,1)S(1)} %get-tuple-element.51), channel_id=1, source_target_pairs={{1,0},{2,1},{3,2},{4,3},{5,4},{6,5},{7,6},{0,7},{9,8},{10,9},{11,1... | collective-permute-start | bytes 208904 | tf_op jit(solution)/shard_map/ppermute | solution.py:549
  7.0 2.7 %copy-start.2 = (bf16[1024,128]{1,0:T(8,128)(2,1)S(1)}, bf16[1024,128]{1,0:T(8,128)(2,1)}, u32[]{:S(2)}) copy-start(bf16[1024,128]{1,0:T(8,128)(2,1)} %param.17) | copy-start | bytes 786436
  7.0 2.8 %copy-start = (bf16[128,1024]{1,0:T(8,128)(2,1)S(1)}, bf16[128,1024]{1,0:T(8,128)(2,1)}, u32[]{:S(2)}) copy-start(bf16[128,1024]{1,0:T(8,128)(2,1)} %w_out_ref.3) | copy-start | bytes 786436
  13.8 3.8 %collective-permute-start.2 = (bf16[512,1024]{1,0:T(8,128)(2,1)S(1)}, bf16[512,1024]{1,0:T(8,128)(2,1)S(1)}, u32[]{:S(2)}, u32[]{:S(2)}) collective-permute-start(bf16[512,1024]{1,0:T(8,128)(2,1)S(1)} %get-tuple-element.54), channel_id=1, source_target_pairs={{0,1},{1,0},{2,3},{3,2},{4,5},{5,4},{6,7},{7,6},{8,9},{9,8},{10,11... | collective-permute-start | bytes 3145736 | tf_op jit(solution)/shard_map/ppermute | solution.py:491
  15.9 1.7 %collective-permute-start.3 = (bf16[512,256]{1,0:T(8,128)(2,1)S(1)}, bf16[512,256]{1,0:T(8,128)(2,1)S(1)}, u32[]{:S(2)}, u32[]{:S(2)}) collective-permute-start(bf16[512,256]{1,0:T(8,128)(2,1)S(1)} %get-tuple-element.59), channel_id=1, source_target_pairs={{0,1},{1,0},{2,3},{3,2},{4,5},{5,4},{6,7},{7,6},{8,9},{9,8},{10,11... | collective-permute-start | bytes 786440 | tf_op jit(solution)/shard_map/ppermute | solution.py:491
  17.9 10.7 %collective-permute-start.4 = (bf16[128,1280]{1,0:T(8,128)(2,1)S(1)}, bf16[128,1280]{1,0:T(8,128)(2,1)S(1)}, u32[]{:S(2)}, u32[]{:S(2)}) collective-permute-start(bf16[128,1280]{1,0:T(8,128)(2,1)S(1)} %get-tuple-element.64), channel_id=1, source_target_pairs={{0,8},{8,0},{16,24},{24,16},{1,9},{9,1},{17,25},{25,17},{2,10},{10... | collective-permute-start | bytes 983048 | tf_op jit(solution)/shard_map/ppermute | solution.py:491
  19.9 16.7 %collective-permute-start.5 = (bf16[128,1280]{1,0:T(8,128)(2,1)S(1)}, bf16[128,1280]{1,0:T(8,128)(2,1)S(1)}, u32[]{:S(2)}, u32[]{:S(2)}) collective-permute-start(bf16[128,1280]{1,0:T(8,128)(2,1)S(1)} %get-tuple-element.65), channel_id=1, source_target_pairs={{0,16},{8,24},{16,0},{24,8},{1,17},{9,25},{17,1},{25,9},{2,18},{10... | collective-permute-start | bytes 983048 | tf_op jit(solution)/shard_map/ppermute | solution.py:491
  21.4 15.2 %collective-permute-start.6 = (bf16[128,1280]{1,0:T(8,128)(2,1)S(1)}, bf16[128,1280]{1,0:T(8,128)(2,1)S(1)}, u32[]{:S(2)}, u32[]{:S(2)}) collective-permute-start(bf16[128,1280]{1,0:T(8,128)(2,1)S(1)} %get-tuple-element.66), channel_id=1, source_target_pairs={{0,24},{8,16},{16,8},{24,0},{1,25},{9,17},{17,9},{25,1},{2,26},{10... | collective-permute-start | bytes 983048 | tf_op jit(solution)/shard_map/ppermute | solution.py:491
  21.5 5.6 %collective-permute-start.7 = (bf16[256,128]{1,0:T(8,128)(2,1)S(1)}, bf16[256,128]{1,0:T(8,128)(2,1)S(1)}, u32[]{:S(2)}, u32[]{:S(2)}) collective-permute-start(bf16[256,128]{1,0:T(8,128)(2,1)S(1)} %get-tuple-element.75), channel_id=1, source_target_pairs={{0,1},{1,2},{2,3},{3,4},{4,5},{5,6},{6,7},{7,0},{8,9},{9,10},{10,1... | collective-permute-start | bytes 196616 | tf_op jit(solution)/shard_map/ppermute | solution.py:549
  21.5 5.6 %collective-permute-start.8 = (bf16[256,128]{1,0:T(8,128)(2,1)S(1)}, bf16[256,128]{1,0:T(8,128)(2,1)S(1)}, u32[]{:S(2)}, u32[]{:S(2)}) collective-permute-start(bf16[256,128]{1,0:T(8,128)(2,1)S(1)} %get-tuple-element.76), channel_id=1, source_target_pairs={{1,0},{2,1},{3,2},{4,3},{5,4},{6,5},{7,6},{0,7},{9,8},{10,9},{11,1... | collective-permute-start | bytes 196616 | tf_op jit(solution)/shard_map/ppermute | solution.py:549
  36.8 4.7 %collective-permute-start.9 = (bf16[32,1280]{1,0:T(8,128)(2,1)S(1)}, bf16[32,1280]{1,0:T(8,128)(2,1)S(1)}, u32[]{:S(2)}, u32[]{:S(2)}) collective-permute-start(bf16[32,1280]{1,0:T(8,128)(2,1)S(1)} %get-tuple-element.84), channel_id=1, source_target_pairs={{0,2},{1,3},{2,0},{3,1},{4,6},{5,7},{6,4},{7,5},{8,10},{9,11},{10,... | collective-permute-start | bytes 245768 | tf_op jit(solution)/shard_map/ppermute | solution.py:491
  36.9 9.0 %collective-permute-start.10 = (bf16[32,1280]{1,0:T(8,128)(2,1)S(1)}, bf16[32,1280]{1,0:T(8,128)(2,1)S(1)}, u32[]{:S(2)}, u32[]{:S(2)}) collective-permute-start(bf16[32,1280]{1,0:T(8,128)(2,1)S(1)} %get-tuple-element.85), channel_id=1, source_target_pairs={{0,4},{1,5},{2,6},{3,7},{4,0},{5,1},{6,2},{7,3},{8,12},{9,13},{10,... | collective-permute-start | bytes 245768 | tf_op jit(solution)/shard_map/ppermute | solution.py:491
  39.5 6.4 %collective-permute-start.11 = (bf16[32,1280]{1,0:T(8,128)(2,1)S(1)}, bf16[32,1280]{1,0:T(8,128)(2,1)S(1)}, u32[]{:S(2)}, u32[]{:S(2)}) collective-permute-start(bf16[32,1280]{1,0:T(8,128)(2,1)S(1)} %get-tuple-element.86), channel_id=1, source_target_pairs={{0,6},{1,7},{2,4},{3,5},{4,2},{5,3},{6,0},{7,1},{8,14},{9,15},{10,... | collective-permute-start | bytes 245768 | tf_op jit(solution)/shard_map/ppermute | solution.py:491
  46.0 6.4 %collective-permute-start.14 = (bf16[32,1280]{1,0:T(8,128)(2,1)S(1)}, bf16[32,1280]{1,0:T(8,128)(2,1)S(1)}, u32[]{:S(2)}, u32[]{:S(2)}) collective-permute-start(bf16[32,1280]{1,0:T(8,128)(2,1)S(1)} %shard_map.146.refs_0_), channel_id=1, source_target_pairs={{0,6},{1,7},{2,4},{3,5},{4,2},{5,3},{6,0},{7,1},{8,14},{9,15},{10,... | collective-permute-start | bytes 245768 | tf_op jit(solution)/shard_map/ppermute | solution.py:491
  47.9 6.5 %collective-permute-start.13 = (bf16[32,1280]{1,0:T(8,128)(2,1)S(1)}, bf16[32,1280]{1,0:T(8,128)(2,1)S(1)}, u32[]{:S(2)}, u32[]{:S(2)}) collective-permute-start(bf16[32,1280]{1,0:T(8,128)(2,1)S(1)} %shard_map.146.refs_0_), channel_id=1, source_target_pairs={{0,4},{1,5},{2,6},{3,7},{4,0},{5,1},{6,2},{7,3},{8,12},{9,13},{10,... | collective-permute-start | bytes 245768 | tf_op jit(solution)/shard_map/ppermute | solution.py:491
  49.0 5.5 %collective-permute-start.12 = (bf16[32,1280]{1,0:T(8,128)(2,1)S(1)}, bf16[32,1280]{1,0:T(8,128)(2,1)S(1)}, u32[]{:S(2)}, u32[]{:S(2)}) collective-permute-start(bf16[32,1280]{1,0:T(8,128)(2,1)S(1)} %shard_map.146.refs_0_), channel_id=1, source_target_pairs={{0,2},{1,3},{2,0},{3,1},{4,6},{5,7},{6,4},{7,5},{8,10},{9,11},{10,... | collective-permute-start | bytes 245768 | tf_op jit(solution)/shard_map/ppermute | solution.py:491
  54.5 6.6 %collective-permute-start.15 = (bf16[128,640]{1,0:T(8,128)(2,1)S(1)}, bf16[128,640]{1,0:T(8,128)(2,1)S(1)}, u32[]{:S(2)}, u32[]{:S(2)}) collective-permute-start(bf16[128,640]{1,0:T(8,128)(2,1)S(1)} %get-tuple-element.87.refs_0_), channel_id=1, source_target_pairs={{0,8},{8,0},{16,24},{24,16},{1,9},{9,1},{17,25},{25,17},{2,10},{10... | collective-permute-start | bytes 491528 | tf_op jit(solution)/shard_map/ppermute | solution.py:491
  56.1 6.7 %collective-permute-start.19 = (bf16[128,640]{1,0:T(8,128)(2,1)S(1)}, bf16[128,640]{1,0:T(8,128)(2,1)S(1)}, u32[]{:S(2)}, u32[]{:S(2)}) collective-permute-start(bf16[128,640]{1,0:T(8,128)(2,1)S(1)} %get-tuple-element.88.refs_4_), channel_id=1, source_target_pairs={{0,16},{8,24},{16,0},{24,8},{1,17},{9,25},{17,1},{25,9},{2,18},{10... | collective-permute-start | bytes 491528 | tf_op jit(solution)/shard_map/ppermute | solution.py:491
  56.5 7.7 %collective-permute-start.16 = (bf16[128,640]{1,0:T(8,128)(2,1)S(1)}, bf16[128,640]{1,0:T(8,128)(2,1)S(1)}, u32[]{:S(2)}, u32[]{:S(2)}) collective-permute-start(bf16[128,640]{1,0:T(8,128)(2,1)S(1)} %get-tuple-element.87.refs_0_), channel_id=1, source_target_pairs={{0,16},{8,24},{16,0},{24,8},{1,17},{9,25},{17,1},{25,9},{2,18},{10... | collective-permute-start | bytes 491528 | tf_op jit(solution)/shard_map/ppermute | solution.py:491
  58.1 6.1 %collective-permute-start.18 = (bf16[128,640]{1,0:T(8,128)(2,1)S(1)}, bf16[128,640]{1,0:T(8,128)(2,1)S(1)}, u32[]{:S(2)}, u32[]{:S(2)}) collective-permute-start(bf16[128,640]{1,0:T(8,128)(2,1)S(1)} %get-tuple-element.88.refs_4_), channel_id=1, source_target_pairs={{0,8},{8,0},{16,24},{24,16},{1,9},{9,1},{17,25},{25,17},{2,10},{10... | collective-permute-start | bytes 491528 | tf_op jit(solution)/shard_map/ppermute | solution.py:491
  61.2 5.3 %collective-permute-start.17 = (bf16[128,640]{1,0:T(8,128)(2,1)S(1)}, bf16[128,640]{1,0:T(8,128)(2,1)S(1)}, u32[]{:S(2)}, u32[]{:S(2)}) collective-permute-start(bf16[128,640]{1,0:T(8,128)(2,1)S(1)} %collective-permute-done.15.refs_1_), channel_id=1, source_target_pairs={{0,16},{8,24},{16,0},{24,8},{1,17},{9,25},{17,1},{25,9},{2,18},{10... | collective-permute-start | bytes 491528 | tf_op jit(solution)/shard_map/ppermute | solution.py:491
  62.7 5.3 %collective-permute-start.20 = (bf16[128,640]{1,0:T(8,128)(2,1)S(1)}, bf16[128,640]{1,0:T(8,128)(2,1)S(1)}, u32[]{:S(2)}, u32[]{:S(2)}) collective-permute-start(bf16[128,640]{1,0:T(8,128)(2,1)S(1)} %collective-permute-done.19.refs_6_), channel_id=1, source_target_pairs={{0,8},{8,0},{16,24},{24,16},{1,9},{9,1},{17,25},{25,17},{2,10},{10... | collective-permute-start | bytes 491528 | tf_op jit(solution)/shard_map/ppermute | solution.py:491
  68.2 3.1 %collective-permute-start.21 = (bf16[512,1280]{1,0:T(8,128)(2,1)S(1)}, bf16[512,1280]{1,0:T(8,128)(2,1)S(1)}, u32[]{:S(2)}, u32[]{:S(2)}) collective-permute-start(bf16[512,1280]{1,0:T(8,128)(2,1)S(1)} %shard_map.148.mid_half.small_half), channel_id=1, source_target_pairs={{0,1},{1,0},{2,3},{3,2},{4,5},{5,4},{6,7},{7,6},{8,9},{9,8},{10,11... | collective-permute-start | bytes 3932168 | tf_op jit(solution)/shard_map/ppermute | solution.py:491

commit v10 on v9

--- a/solution.py
+++ b/solution.py
@@ -388,7 +388,6 @@
 
 
 CORE = ("horiz", 0, 2)
-NEAR, FAR = ("horiz", 1, 2), ("horiz", 2, 2)
 CHIPS = ("horiz", 1, 4)
 MEMBER_LOW, MEMBER_HIGH = ("ens", 0, 2), ("ens", 1, 2)
 MEMBERS = ("ens", 0, 4)
@@ -399,17 +398,22 @@
     return lax.axis_index(axis) // (1 << shift) % parts
 
 
-def sum_kernel(*refs, terms, stage, factor):
-    ins, outs = refs[:terms], refs[terms:]
+def sum_kernel(*refs, counts, stage, factor):
+    ins, outs = refs[: sum(counts)], refs[sum(counts) :]
     rows = outs[0].shape[0]
-    for k, out_ref in enumerate(outs):
+    for index, out_ref in enumerate(outs):
+        k = -index % len(outs)
         here = pl.ds(0, rows)
         if stage is not None:
             here = pl.ds(pl.multiple_of((position(stage) ^ k) * rows, rows), rows)
-        total = ins[0][here, :].astype(F32)
-        for ref in ins[1:]:
-            total = total + ref[here, :].astype(F32)
-        out_ref[...] = (total * factor).astype(BF16)
+        first, taken = 0, 0
+        for count in counts:
+            total = ins[taken][here, :].astype(F32)
+            for ref in ins[taken + 1 : taken + count]:
+                total = total + ref[here, :].astype(F32)
+            columns = total.shape[1]
+            out_ref[:, first : first + columns] = (total * factor).astype(BF16)
+            first, taken = first + columns, taken + count
 
 
 def join_kernel(*refs, stage, groups, cuts):
@@ -429,17 +433,22 @@
                 ]
 
 
-def core_sum_kernel(keep_mid, got_mid, keep_small, got_small, *outs, stage):
-    rows = outs[0].shape[0]
+def core_sum_kernel(*refs, spans, stage, members):
+    outs = refs[2 * len(spans) :]
+    rows = refs[0].shape[0] // members
+    low = stage == MEMBER_LOW
     for k, out_ref in enumerate(outs):
-        here = pl.ds(pl.multiple_of((position(stage) ^ k) * rows, rows), rows)
-        first = 0
-        for keep_ref, got_ref in ((keep_mid, got_mid), (keep_small, got_small)):
-            columns = keep_ref.shape[1]
-            out_ref[:, first : first + columns] = (
-                keep_ref[here, :].astype(F32) + got_ref[here, :].astype(F32)
-            ).astype(BF16)
-            first += columns
+        mine = position(stage) ^ k
+        for other in range(members // 2):
+            member = 2 * other + mine if low else 2 * mine + other
+            here = pl.ds(pl.multiple_of(member * rows, rows), rows)
+            first = 0
+            for group, (start, stop) in enumerate(spans):
+                keep_ref, got_ref = refs[2 * group : 2 * group + 2]
+                out_ref[other * rows : (other + 1) * rows, first : first + stop - start] = (
+                    keep_ref[here, start:stop].astype(F32) + got_ref[here, start:stop].astype(F32)
+                ).astype(BF16)
+                first += stop - start
 
 
 def final_kernel(mid_half, small_half, *refs):
@@ -487,22 +496,24 @@
 def exchange(arrays, stage):
     axis, shift, _ = stage
     count = lax.axis_size(axis)
-    return [
-        lax.ppermute(array, axis, [(i, i ^ (k << shift)) for i in range(count)])
-        for k, array in enumerate(arrays, 1)
-    ]
-
-
-def add(terms, stage, factor=1.0):
-    rows, columns = terms[0].shape
+    sent = {}
+    for k in range(len(arrays), 0, -1):
+        route = [(i, i ^ (k << shift)) for i in range(count)]
+        sent[k] = lax.ppermute(arrays[k - 1], axis, route)
+    return [sent[k] for k in range(1, len(arrays) + 1)]
+
+
+def add(groups, stage, factor=1.0):
+    rows = groups[0][0].shape[0]
+    columns = sum(terms[0].shape[1] for terms in groups)
     parts = 1 if stage is None else stage[2]
     return call(
         sum_kernel,
         [((rows // parts, columns), BF16)] * parts,
-        terms=len(terms),
+        counts=tuple(len(terms) for terms in groups),
         stage=stage,
         factor=factor,
-    )(*terms)
+    )(*[term for terms in groups for term in terms])
 
 
 def join(groups, stage, outs=1):
@@ -513,9 +524,9 @@
     )(*[piece for group in groups for piece in group])
 
 
-def reduce_to(terms, stage):
-    parts = add(terms, stage)
-    return [parts[0]] + exchange(parts[1:], stage)
+def reduce_to(groups, stage):
+    parts = add(groups, stage)
+    return [parts[0]] + exchange(parts[:0:-1], stage)[::-1]
 
 
 def collect_members(one, two):
@@ -593,7 +604,23 @@
         backward_kernel, [hidden, half, half], moved=4 * 10**6
     )(x_now, act_two, delta_two, adjoint, weights)
     (got_small,) = exchange([send_small], CORE)
-
+    got_mid, delta_one = tie(got_mid, delta_one)
+
+    def both_cores(operands, spans, stage):
+        columns = sum(stop - start for start, stop in spans)
+        members = lax.axis_size("ens")
+        parts = call(
+            core_sum_kernel,
+            [((units // 2 // 2, columns), BF16)] * 2,
+            spans=spans,
+            stage=stage,
+            members=members,
+        )(*operands)
+        return parts, [parts[0]] + exchange(parts[1:], stage)
+
+    split = (units + 2 * fields) // 2
+    parts_one, terms_one = both_cores([keep_mid, got_mid], [(0, split)], MEMBER_LOW)
+    delta_one, keep_small = tie(delta_one, keep_small, parts_one)[:2]
     packed = ((2 * fields, lats), BF16)
     field, up_rows, down_rows = call(
         grad_kernel,
@@ -601,15 +628,10 @@
         smem=(0,),
         lons=lons,
     )(tile_count, column, cols, mask, delta_one, adjoint, weights)
-    got_small, field = tie(got_small, field)
-
-    parts = call(
-        core_sum_kernel,
-        [((units // 2 // MEMBERS[2], units + 2 * fields), BF16)] * MEMBERS[2],
-        stage=MEMBERS,
-    )(keep_mid, got_mid, keep_small, got_small)
-    terms = [parts[0]] + exchange(parts[1:], MEMBERS)
-    act_two, up_rows, down_rows = tie(act_two, up_rows, down_rows, parts)[:3]
+    parts_two, terms_two = both_cores(
+        [keep_mid, got_mid, keep_small, got_small], [(split, units), (0, 2 * fields)], MEMBER_HIGH
+    )
+    act_two, up_rows, down_rows = tie(act_two, up_rows, down_rows, parts_two)[:3]
     halos = to_neighbours(up_rows, down_rows, "horiz")
     (state_rows,) = call(
         state_kernel,
@@ -618,17 +640,21 @@
         smem=(0,),
         lons=lons,
     )(tile_count, moved, cols, mask, x_now, act_two, coef, ratio, inverse, w_out)
+    terms_one, terms_two, state_rows, halos = tie(terms_one, terms_two, state_rows, halos)
+    terms_one = reduce_to([terms_one], MEMBER_HIGH)
+    terms_two = reduce_to([terms_two], MEMBER_LOW)
     (grad_rows,) = call(last_kernel, [((fields * lons, lats), F32)], lons=lons)(
         field, *halos, low_pack, high_pack, base
     )
-    terms, state_rows, grad_rows = tie(terms, state_rows, grad_rows)
+    terms_one, terms_two, grad_rows = tie(terms_one, terms_two, grad_rows)
+    groups = [terms_one, terms_two]
 
     if lax.axis_size("horiz") == 8:
-        terms = reduce_to(terms, CHIPS)
-        pieces = collect(add(terms, None, factor)[0], CHIPS)
+        terms = reduce_to(groups, CHIPS)
+        pieces = collect(add([terms], None, factor)[0], CHIPS)
         groups = collect_members(*join([pieces], CHIPS, outs=2))
     else:
-        groups = [collect(over_all_chips(add(terms, None)[0], factor), MEMBERS)]
+        groups = [collect(over_all_chips(add(groups, None)[0], factor), MEMBERS)]
     (own,) = join(groups, MEMBERS)
     (got,) = exchange([own], CORE)
     half_done = final(own, False, [], fields)

time: 73.7 us -> 73.8 us (level)
  starting transfers between devices: 27.6 us -> 29.5 us
  waiting for transfers between devices: 25.8 us -> 24 us
    ppermute x18 -> x19, starting transfers between devices: 19.5 us -> 21.3 us  [exchange(): sent[k] = lax.ppermute(arrays[k - 1], axis, route)]
    ppermute x18 -> x19, waiting for transfers between devices: 25.3 us -> 23.6 us  [exchange(): sent[k] = lax.ppermute(arrays[k - 1], axis, route)]
    pallas_call x12 -> x15, Pallas kernels: 11.1 us -> 11.2 us  [run(): pl.pallas_call(functools.partial(kernel, **names), out_shape=[jax.ShapeDt...]
  transfers between devices with their start and end apart: 22 -> 23, of which waited for: 12 -> 15; matrix products, arithmetic and copies ran while one was open for 3% -> 3% of each run, Pallas kernels for 12% -> 12%
where the time goes in v10:
time: 73.8 us; the launch traced here: 73.7 us
  starting transfers between devices  29.5 us (40%)
  waiting for transfers between devices  24 us (33%)
  Pallas kernels  15.7 us (21%)
  local copies, waits for them, and re-layouts  1.92 us (3%)
  between operations  1.52 us (2%)
  other arithmetic  1.1 us (1%)
    ppermute x19, waiting for transfers between devices, exchange(): sent[k] = lax.ppermute(arrays[k - 1], axis, route)  23.6 us
    ppermute x19, starting transfers between devices, exchange(): sent[k] = lax.ppermute(arrays[k - 1], axis, route)  21.3 us
    pallas_call x15, Pallas kernels, run(): pl.pallas_call(functools.partial(kernel, **names), out_shape=[jax.ShapeDt...  11.2 us
    ppermute x2, starting transfers between devices, to_neighbours(): lax.ppermute(downward, axis, backward)  7.63 us
    pallas_call x2, Pallas kernels, final(): pl.pallas_call(final_kernel, grid=(units // block,), out_shape=[jax.Shape...  4.47 us
    unnamed x14, local copies, waits for them, and re-layouts  1.86 us
  transfers between devices with their start and end apart: 23, of which 15 were waited for; matrix products, arithmetic and copies ran while one was open for 3% of the time, Pallas kernels for 12%

profile of v10, /device:TPU:0, one launch (start us, length us, event | category | flops | bytes accessed | tf_op | source)
XLA Modules:
  0.0 73.7 jit_solution(4827375261301523237)
XLA Ops:
  0.6 1.0 %pad_maximum_fusion.1 = f32[130,4,128]{2,1,0:T(4,128)S(1)} fusion(f32[2,4,128]{2,1,0:T(4,128)} %param.12, f32[128,4,128]{2,1,0:T(4,128)} %bitcast.16), kind=kLoop, calls=%fused_computation.1 | loop fusion | flops 66560 | bytes 532480 | tf_op jit(solution)/shard_map/concatenate | solution.py:571
  2.2 4.1 %collective-permute-start.1 = (bf16[272,128]{1,0:T(8,128)(2,1)S(1)}, bf16[272,128]{1,0:T(8,128)(2,1)S(1)}, u32[]{:S(2)}, u32[]{:S(2)}) collective-permute-start(bf16[272,128]{1,0:T(8,128)(2,1)S(1)} %get-tuple-element.63), channel_id=1, source_target_pairs={{1,0},{2,1},{3,2},{4,3},{5,4},{6,5},{7,6},{0,7},{9,8},{10,9},{11,1... | collective-permute-start | bytes 208904 | tf_op jit(solution)/shard_map/ppermute | solution.py:560
  7.0 1.8 %constant_dynamic-update-slice_fusion.1 = bf16[1024,1152]{1,0:T(8,128)(2,1)S(1)} fusion(bf16[1024,1024]{1,0:T(8,128)(2,1)} %param.18), kind=kLoop, calls=%fused_computation.3 | loop fusion | bytes 4194304
  9.9 3.9 %shard_map.139 = (f32[4,128,128]{2,1,0:T(8,128)S(1)}, bf16[128,384]{1,0:T(8,128)(2,1)S(1)}, bf16[1024,384]{1,0:T(8,128)(2,1)}, bf16[1024,384]{1,0:T(8,128)(2,1)S...) custom-call(f32[520,128]{1,0:T(8,128)S(1)} %bitcast.12, ...), custom_call_target="tpu_custom_call" | custom-call | bytes 15000000 | tf_op jit(solution)/shard_map/pallas_call | solution.py:27
  13.8 2.1 %shard_map.140 = (bf16[1024,384]{1,0:T(8,128)(2,1)S(1)}, bf16[512,256]{1,0:T(8,128)(2,1)S(1)}, bf16[512,256]{1,0:T(8,128)(2,1)S(1)}) custom-call(bf16[128,384]{1,0:T(8,128)(2,1)S(1)} %get-tuple-element.67.x_ref, bf16[1024,384]{1,0:T(8,128)(2,1)S(1)} %get-tuple-element.84.act_two_ref, bf16[1024,384]{1,0:T(8,128)(2,1)S(1)} %get-tuple-element.69.delta_two_ref, ...), custom_call_target="tpu_custom_call" | custom-call | bytes 4000000 | tf_op jit(solution)/shard_map/pallas_call | solution.py:27
  16.6 1.0 %collective-permute-done.4.refs_3_ = bf16[512,256]{1,0:T(8,128)(2,1)S(1)} collective-permute-done((bf16[512,256]{1,0:T(8,128)(2,1)S(1)}, bf16[512,256]{1,0:T(8,128)(2,1)S(1)}, u32[]{:S(2)}, u32[]{:S(2)}) %collective-permute-start.4) | collective-permute-done | bytes 262176 | tf_op jit(solution)/shard_map/ppermute | solution.py:502
  17.8 2.0 %collective-permute-start.5 = (bf16[256,640]{1,0:T(8,128)(2,1)S(1)}, bf16[256,640]{1,0:T(8,128)(2,1)S(1)}, u32[]{:S(2)}, u32[]{:S(2)}) collective-permute-start(bf16[256,640]{1,0:T(8,128)(2,1)S(1)} %get-tuple-element.79), channel_id=1, source_target_pairs={{0,16},{8,24},{16,0},{24,8},{1,17},{9,25},{17,1},{25,9},{2,18},{10... | collective-permute-start | bytes 983048 | tf_op jit(solution)/shard_map/ppermute | solution.py:502
  19.8 1.5 %collective-permute-start.3 = (bf16[256,640]{1,0:T(8,128)(2,1)S(1)}, bf16[256,640]{1,0:T(8,128)(2,1)S(1)}, u32[]{:S(2)}, u32[]{:S(2)}) collective-permute-start(bf16[256,640]{1,0:T(8,128)(2,1)S(1)} %get-tuple-element.73), channel_id=1, source_target_pairs={{0,8},{8,0},{16,24},{24,16},{1,9},{9,1},{17,25},{25,17},{2,10},{10... | collective-permute-start | bytes 983048 | tf_op jit(solution)/shard_map/ppermute | solution.py:502
  21.9 3.5 %collective-permute-start.7 = (bf16[256,128]{1,0:T(8,128)(2,1)S(1)}, bf16[256,128]{1,0:T(8,128)(2,1)S(1)}, u32[]{:S(2)}, u32[]{:S(2)}) collective-permute-start(bf16[256,128]{1,0:T(8,128)(2,1)S(1)} %get-tuple-element.89), channel_id=1, source_target_pairs={{1,0},{2,1},{3,2},{4,3},{5,4},{6,5},{7,6},{0,7},{9,8},{10,9},{11,1... | collective-permute-start | bytes 196616 | tf_op jit(solution)/shard_map/ppermute | solution.py:560
  25.5 1.6 %shard_map.144 = f32[512,128]{1,0:T(8,128)} custom-call(s32[1,1]{1,0:T(1,128)S(6)} %copy.26.count_ref, f32[4,128,128]{2,1,0:T(8,128)S(1)} %get-tuple-element.80.moved_ref, s32[3,128]{1,0:T(4,128)S(1)} %get-tuple-element.120.cols_ref, s32[3,128]{1,0:T(4,128)S(1)} %get-tuple-element.119.mask_ref, bf16[128,384]{1,0:T(8,128)(2,1)S(1)} %get-tuple-element.67.x_ref, ...), custom_call_target="tpu_custom_call" | custom-call | tf_op jit(solution)/shard_map/pallas_call | solution.py:27
  28.0 1.5 %collective-permute-done.3.refs_1_ = bf16[256,640]{1,0:T(8,128)(2,1)S(1)} collective-permute-done((bf16[256,640]{1,0:T(8,128)(2,1)S(1)}, bf16[256,640]{1,0:T(8,128)(2,1)S(1)}, u32[]{:S(2)}, u32[]{:S(2)}) %collective-permute-start.3) | collective-permute-done | bytes 327712 | tf_op jit(solution)/shard_map/ppermute | solution.py:502
  30.1 1.7 %collective-permute-start.9 = (bf16[128,640]{1,0:T(8,128)(2,1)S(1)}, bf16[128,640]{1,0:T(8,128)(2,1)S(1)}, u32[]{:S(2)}, u32[]{:S(2)}) collective-permute-start(bf16[128,640]{1,0:T(8,128)(2,1)S(1)} %get-tuple-element.98), channel_id=1, source_target_pairs={{0,8},{8,0},{16,24},{24,16},{1,9},{9,1},{17,25},{25,17},{2,10},{10... | collective-permute-start | bytes 491528 | tf_op jit(solution)/shard_map/ppermute | solution.py:502
  31.8 1.5 %shard_map.147 = f32[512,128]{1,0:T(8,128)} custom-call(f32[4,128,128]{2,1,0:T(8,128)S(1)} %get-tuple-element.99.field_ref, bf16[256,128]{1,0:T(8,128)(2,1)S(1)} %collective-permute-done.6.low_ref, bf16[256,128]{1,0:T(8,128)(2,1)S(1)} %collective-permute-done.7.high_ref, bf16[272,128]{1,0:T(8,128)(2,1)S(1)} %collective-permute-done.low_ref.low_mix_ref, ...), custom_call_target="tpu_custom_call" | custom-call | tf_op jit(solution)/shard_map/pallas_call | solution.py:27
  33.3 1.7 %collective-permute-done.8.refs_1_ = bf16[128,640]{1,0:T(8,128)(2,1)S(1)} collective-permute-done((bf16[128,640]{1,0:T(8,128)(2,1)S(1)}, bf16[128,640]{1,0:T(8,128)(2,1)S(1)}, u32[]{:S(2)}, u32[]{:S(2)}) %collective-permute-start.8) | collective-permute-done | bytes 163872 | tf_op jit(solution)/shard_map/ppermute | solution.py:502
  35.6 2.5 %collective-permute-start.10 = (bf16[32,1280]{1,0:T(8,128)(2,1)S(1)}, bf16[32,1280]{1,0:T(8,128)(2,1)S(1)}, u32[]{:S(2)}, u32[]{:S(2)}) collective-permute-start(bf16[32,1280]{1,0:T(8,128)(2,1)S(1)} %get-tuple-element.108), channel_id=1, source_target_pairs={{0,6},{1,7},{2,4},{3,5},{4,2},{5,3},{6,0},{7,1},{8,14},{9,15},{10,... | collective-permute-start | bytes 245768 | tf_op jit(solution)/shard_map/ppermute | solution.py:502
  38.1 1.9 %collective-permute-start.12 = (bf16[32,1280]{1,0:T(8,128)(2,1)S(1)}, bf16[32,1280]{1,0:T(8,128)(2,1)S(1)}, u32[]{:S(2)}, u32[]{:S(2)}) collective-permute-start(bf16[32,1280]{1,0:T(8,128)(2,1)S(1)} %get-tuple-element.110), channel_id=1, source_target_pairs={{0,2},{1,3},{2,0},{3,1},{4,6},{5,7},{6,4},{7,5},{8,10},{9,11},{10,... | collective-permute-start | bytes 245768 | tf_op jit(solution)/shard_map/ppermute | solution.py:502
  40.1 2.5 %collective-permute-done.10.refs_1_ = bf16[32,1280]{1,0:T(8,128)(2,1)S(1)} collective-permute-done((bf16[32,1280]{1,0:T(8,128)(2,1)S(1)}, bf16[32,1280]{1,0:T(8,128)(2,1)S(1)}, u32[]{:S(2)}, u32[]{:S(2)}) %collective-permute-start.10) | collective-permute-done | bytes 81952 | tf_op jit(solution)/shard_map/ppermute | solution.py:502
  42.5 2.0 %collective-permute-done.11.refs_2_ = bf16[32,1280]{1,0:T(8,128)(2,1)S(1)} collective-permute-done((bf16[32,1280]{1,0:T(8,128)(2,1)S(1)}, bf16[32,1280]{1,0:T(8,128)(2,1)S(1)}, u32[]{:S(2)}, u32[]{:S(2)}) %collective-permute-start.11) | collective-permute-done | bytes 81952 | tf_op jit(solution)/shard_map/ppermute | solution.py:502
  44.6 2.7 %collective-permute-start.15 = (bf16[32,1280]{1,0:T(8,128)(2,1)S(1)}, bf16[32,1280]{1,0:T(8,128)(2,1)S(1)}, u32[]{:S(2)}, u32[]{:S(2)}) collective-permute-start(bf16[32,1280]{1,0:T(8,128)(2,1)S(1)} %shard_map.149.refs_0_), channel_id=1, source_target_pairs={{0,6},{1,7},{2,4},{3,5},{4,2},{5,3},{6,0},{7,1},{8,14},{9,15},{10,... | collective-permute-start | bytes 245768 | tf_op jit(solution)/shard_map/ppermute | solution.py:502
  47.3 1.8 %collective-permute-start.13 = (bf16[32,1280]{1,0:T(8,128)(2,1)S(1)}, bf16[32,1280]{1,0:T(8,128)(2,1)S(1)}, u32[]{:S(2)}, u32[]{:S(2)}) collective-permute-start(bf16[32,1280]{1,0:T(8,128)(2,1)S(1)} %shard_map.149.refs_0_), channel_id=1, source_target_pairs={{0,2},{1,3},{2,0},{3,1},{4,6},{5,7},{6,4},{7,5},{8,10},{9,11},{10,... | collective-permute-start | bytes 245768 | tf_op jit(solution)/shard_map/ppermute | solution.py:502
  49.1 2.2 %collective-permute-done.15.refs_3_ = bf16[32,1280]{1,0:T(8,128)(2,1)S(1)} collective-permute-done((bf16[32,1280]{1,0:T(8,128)(2,1)S(1)}, bf16[32,1280]{1,0:T(8,128)(2,1)S(1)}, u32[]{:S(2)}, u32[]{:S(2)}) %collective-permute-start.15) | collective-permute-done | bytes 81952 | tf_op jit(solution)/shard_map/ppermute | solution.py:502
  51.2 2.8 %collective-permute-done.14.refs_2_ = bf16[32,1280]{1,0:T(8,128)(2,1)S(1)} collective-permute-done((bf16[32,1280]{1,0:T(8,128)(2,1)S(1)}, bf16[32,1280]{1,0:T(8,128)(2,1)S(1)}, u32[]{:S(2)}, u32[]{:S(2)}) %collective-permute-start.14) | collective-permute-done | bytes 81952 | tf_op jit(solution)/shard_map/ppermute | solution.py:502
  54.1 1.4 %collective-permute-start.16 = (bf16[128,640]{1,0:T(8,128)(2,1)S(1)}, bf16[128,640]{1,0:T(8,128)(2,1)S(1)}, u32[]{:S(2)}, u32[]{:S(2)}) collective-permute-start(bf16[128,640]{1,0:T(8,128)(2,1)S(1)} %get-tuple-element.111.refs_0_), channel_id=1, source_target_pairs={{0,8},{8,0},{16,24},{24,16},{1,9},{9,1},{17,25},{25,17},{2,10},{10... | collective-permute-start | bytes 491528 | tf_op jit(solution)/shard_map/ppermute | solution.py:502
  55.5 1.5 %collective-permute-start.20 = (bf16[128,640]{1,0:T(8,128)(2,1)S(1)}, bf16[128,640]{1,0:T(8,128)(2,1)S(1)}, u32[]{:S(2)}, u32[]{:S(2)}) collective-permute-start(bf16[128,640]{1,0:T(8,128)(2,1)S(1)} %get-tuple-element.112.refs_4_), channel_id=1, source_target_pairs={{0,16},{8,24},{16,0},{24,8},{1,17},{9,25},{17,1},{25,9},{2,18},{10... | collective-permute-start | bytes 491528 | tf_op jit(solution)/shard_map/ppermute | solution.py:502
  58.2 2.9 %collective-permute-done.16.refs_1_ = bf16[128,640]{1,0:T(8,128)(2,1)S(1)} collective-permute-done((bf16[128,640]{1,0:T(8,128)(2,1)S(1)}, bf16[128,640]{1,0:T(8,128)(2,1)S(1)}, u32[]{:S(2)}, u32[]{:S(2)}) %collective-permute-start.16) | collective-permute-done | bytes 163872 | tf_op jit(solution)/shard_map/ppermute | solution.py:502
  61.6 1.0 %collective-permute-done.20.refs_6_ = bf16[128,640]{1,0:T(8,128)(2,1)S(1)} collective-permute-done((bf16[128,640]{1,0:T(8,128)(2,1)S(1)}, bf16[128,640]{1,0:T(8,128)(2,1)S(1)}, u32[]{:S(2)}, u32[]{:S(2)}) %collective-permute-start.20) | collective-permute-done | bytes 163872 | tf_op jit(solution)/shard_map/ppermute | solution.py:502
  62.6 1.5 %collective-permute-start.21 = (bf16[128,640]{1,0:T(8,128)(2,1)S(1)}, bf16[128,640]{1,0:T(8,128)(2,1)S(1)}, u32[]{:S(2)}, u32[]{:S(2)}) collective-permute-start(bf16[128,640]{1,0:T(8,128)(2,1)S(1)} %collective-permute-done.20.refs_6_), channel_id=1, source_target_pairs={{0,8},{8,0},{16,24},{24,16},{1,9},{9,1},{17,25},{25,17},{2,10},{10... | collective-permute-start | bytes 491528 | tf_op jit(solution)/shard_map/ppermute | solution.py:502
  64.1 2.0 %collective-permute-done.17.refs_2_ = bf16[128,640]{1,0:T(8,128)(2,1)S(1)} collective-permute-done((bf16[128,640]{1,0:T(8,128)(2,1)S(1)}, bf16[128,640]{1,0:T(8,128)(2,1)S(1)}, u32[]{:S(2)}, u32[]{:S(2)}) %collective-permute-start.17) | collective-permute-done | bytes 163872 | tf_op jit(solution)/shard_map/ppermute | solution.py:502
  66.1 2.1 %collective-permute-done.18.refs_3_ = bf16[128,640]{1,0:T(8,128)(2,1)S(1)} collective-permute-done((bf16[128,640]{1,0:T(8,128)(2,1)S(1)}, bf16[128,640]{1,0:T(8,128)(2,1)S(1)}, u32[]{:S(2)}, u32[]{:S(2)}) %collective-permute-start.18) | collective-permute-done | bytes 163872 | tf_op jit(solution)/shard_map/ppermute | solution.py:502
  68.4 2.2 %shard_map.152 = (f32[1024,1024]{1,0:T(8,128)}, f32[1024,128]{1,0:T(8,128)}, f32[128,1024]{1,0:T(8,128)}) custom-call(bf16[512,1280]{1,0:T(8,128)(2,1)S(1)} %shard_map.151.mid_half.small_half, bf16[512,1280]{1,0:T(8,128)(2,1)S(1)} %shard_map.151.mid_half.small_half), custom_call_target="tpu_custom_call" | custom-call | tf_op jit(solution)/shard_map/pallas_call | solution.py:474
  70.7 0.8 %collective-permute-done.22.mid_half.small_half = bf16[512,1280]{1,0:T(8,128)(2,1)S(1)} collective-permute-done((bf16[512,1280]{1,0:T(8,128)(2,1)S(1)}, bf16[512,1280]{1,0:T(8,128)(2,1)S(1)}, u32[]{:S(2)}, u32[]{:S(2)}) %collective-permute-start.22) | collective-permute-done | bytes 1310752 | tf_op jit(solution)/shard_map/ppermute | solution.py:502
  71.4 2.2 %shard_map.153 = (f32[1024,1024]{1,0:T(8,128)}, f32[1024,128]{1,0:T(8,128)}, f32[128,1024]{1,0:T(8,128)}) custom-call(bf16[512,1280]{1,0:T(8,128)(2,1)S(1)} %collective-permute-done.22.mid_half.small_half, bf16[512,1280]{1,0:T(8,128)(2,1)S(1)} %collective-permute-done.22.mid_half.small_half, ...), custom_call_target="tpu_custom_call", output_to_operand_aliasing={{0}: (2, {}), {1}: (3, {}), {2}: (4, {})} | custom-call | tf_op jit(solution)/shard_map/pallas_call | solution.py:474
  (48 shorter events, 7.2 us)
Async XLA Ops:
  1.7 7.2 %copy-start.4 = (s32[1,1,3,128]{3,1,2,0:T(1,128)S(1)}, s32[1,1,3,128]{3,1,2,0:T(1,128)}, u32[]{:S(2)}) copy-start(s32[1,1,3,128]{3,1,2,0:T(1,128)} %param.15) | copy-start | bytes 4612
  1.7 7.2 %copy-start.5 = (s32[1,1,3,128]{3,1,2,0:T(1,128)S(1)}, s32[1,1,3,128]{3,1,2,0:T(1,128)}, u32[]{:S(2)}) copy-start(s32[1,1,3,128]{3,1,2,0:T(1,128)} %param.14) | copy-start | bytes 4612
  1.7 7.2 %copy-start.1 = (f32[1,128,4,128]{3,2,1,0:T(4,128)S(1)}, f32[1,128,4,128]{3,2,1,0:T(4,128)}, u32[]{:S(2)}) copy-start(f32[1,128,4,128]{3,2,1,0:T(4,128)} %param.13) | copy-start | bytes 786436
  1.7 7.2 %copy-start.3 = (f32[1,32,4,128]{3,2,1,0:T(4,128)S(1)}, f32[1,32,4,128]{3,2,1,0:T(4,128)}, u32[]{:S(2)}) copy-start(f32[1,32,4,128]{3,2,1,0:T(4,128)} %param.11) | copy-start | bytes 196612
  1.7 8.1 %collective-permute-start = (bf16[272,128]{1,0:T(8,128)(2,1)S(1)}, bf16[272,128]{1,0:T(8,128)(2,1)S(1)}, u32[]{:S(2)}, u32[]{:S(2)}) collective-permute-start(bf16[272,128]{1,0:T(8,128)(2,1)S(1)} %get-tuple-element.62), channel_id=1, source_target_pairs={{0,1},{1,2},{2,3},{3,4},{4,5},{5,6},{6,7},{7,0},{8,9},{9,10},{10,1... | collective-permute-start | bytes 208904 | tf_op jit(solution)/shard_map/ppermute | solution.py:560
  2.2 7.6 %collective-permute-start.1 = (bf16[272,128]{1,0:T(8,128)(2,1)S(1)}, bf16[272,128]{1,0:T(8,128)(2,1)S(1)}, u32[]{:S(2)}, u32[]{:S(2)}) collective-permute-start(bf16[272,128]{1,0:T(8,128)(2,1)S(1)} %get-tuple-element.63), channel_id=1, source_target_pairs={{1,0},{2,1},{3,2},{4,3},{5,4},{6,5},{7,6},{0,7},{9,8},{10,9},{11,1... | collective-permute-start | bytes 208904 | tf_op jit(solution)/shard_map/ppermute | solution.py:560
  7.0 2.7 %copy-start.2 = (bf16[1024,128]{1,0:T(8,128)(2,1)S(1)}, bf16[1024,128]{1,0:T(8,128)(2,1)}, u32[]{:S(2)}) copy-start(bf16[1024,128]{1,0:T(8,128)(2,1)} %param.17) | copy-start | bytes 786436
  7.0 2.8 %copy-start = (bf16[128,1024]{1,0:T(8,128)(2,1)S(1)}, bf16[128,1024]{1,0:T(8,128)(2,1)}, u32[]{:S(2)}) copy-start(bf16[128,1024]{1,0:T(8,128)(2,1)} %w_out_ref.3) | copy-start | bytes 786436
  13.8 2.7 %collective-permute-start.2 = (bf16[512,1024]{1,0:T(8,128)(2,1)S(1)}, bf16[512,1024]{1,0:T(8,128)(2,1)S(1)}, u32[]{:S(2)}, u32[]{:S(2)}) collective-permute-start(bf16[512,1024]{1,0:T(8,128)(2,1)S(1)} %get-tuple-element.66), channel_id=1, source_target_pairs={{0,1},{1,0},{2,3},{3,2},{4,5},{5,4},{6,7},{7,6},{8,9},{9,8},{10,11... | collective-permute-start | bytes 3145736 | tf_op jit(solution)/shard_map/ppermute | solution.py:502
  15.9 1.7 %collective-permute-start.4 = (bf16[512,256]{1,0:T(8,128)(2,1)S(1)}, bf16[512,256]{1,0:T(8,128)(2,1)S(1)}, u32[]{:S(2)}, u32[]{:S(2)}) collective-permute-start(bf16[512,256]{1,0:T(8,128)(2,1)S(1)} %get-tuple-element.77), channel_id=1, source_target_pairs={{0,1},{1,0},{2,3},{3,2},{4,5},{5,4},{6,7},{7,6},{8,9},{9,8},{10,11... | collective-permute-start | bytes 786440 | tf_op jit(solution)/shard_map/ppermute | solution.py:502
  17.8 10.3 %collective-permute-start.5 = (bf16[256,640]{1,0:T(8,128)(2,1)S(1)}, bf16[256,640]{1,0:T(8,128)(2,1)S(1)}, u32[]{:S(2)}, u32[]{:S(2)}) collective-permute-start(bf16[256,640]{1,0:T(8,128)(2,1)S(1)} %get-tuple-element.79), channel_id=1, source_target_pairs={{0,16},{8,24},{16,0},{24,8},{1,17},{9,25},{17,1},{25,9},{2,18},{10... | collective-permute-start | bytes 983048 | tf_op jit(solution)/shard_map/ppermute | solution.py:502
  19.8 9.7 %collective-permute-start.3 = (bf16[256,640]{1,0:T(8,128)(2,1)S(1)}, bf16[256,640]{1,0:T(8,128)(2,1)S(1)}, u32[]{:S(2)}, u32[]{:S(2)}) collective-permute-start(bf16[256,640]{1,0:T(8,128)(2,1)S(1)} %get-tuple-element.73), channel_id=1, source_target_pairs={{0,8},{8,0},{16,24},{24,16},{1,9},{9,1},{17,25},{25,17},{2,10},{10... | collective-permute-start | bytes 983048 | tf_op jit(solution)/shard_map/ppermute | solution.py:502
  21.9 5.6 %collective-permute-start.6 = (bf16[256,128]{1,0:T(8,128)(2,1)S(1)}, bf16[256,128]{1,0:T(8,128)(2,1)S(1)}, u32[]{:S(2)}, u32[]{:S(2)}) collective-permute-start(bf16[256,128]{1,0:T(8,128)(2,1)S(1)} %get-tuple-element.88), channel_id=1, source_target_pairs={{0,1},{1,2},{2,3},{3,4},{4,5},{5,6},{6,7},{7,0},{8,9},{9,10},{10,1... | collective-permute-start | bytes 196616 | tf_op jit(solution)/shard_map/ppermute | solution.py:560
  21.9 5.5 %collective-permute-start.7 = (bf16[256,128]{1,0:T(8,128)(2,1)S(1)}, bf16[256,128]{1,0:T(8,128)(2,1)S(1)}, u32[]{:S(2)}, u32[]{:S(2)}) collective-permute-start(bf16[256,128]{1,0:T(8,128)(2,1)S(1)} %get-tuple-element.89), channel_id=1, source_target_pairs={{1,0},{2,1},{3,2},{4,3},{5,4},{6,5},{7,6},{0,7},{9,8},{10,9},{11,1... | collective-permute-start | bytes 196616 | tf_op jit(solution)/shard_map/ppermute | solution.py:560
  29.6 5.4 %collective-permute-start.8 = (bf16[128,640]{1,0:T(8,128)(2,1)S(1)}, bf16[128,640]{1,0:T(8,128)(2,1)S(1)}, u32[]{:S(2)}, u32[]{:S(2)}) collective-permute-start(bf16[128,640]{1,0:T(8,128)(2,1)S(1)} %get-tuple-element.94), channel_id=1, source_target_pairs={{0,16},{8,24},{16,0},{24,8},{1,17},{9,25},{17,1},{25,9},{2,18},{10... | collective-permute-start | bytes 491528 | tf_op jit(solution)/shard_map/ppermute | solution.py:502
  30.1 5.4 %collective-permute-start.9 = (bf16[128,640]{1,0:T(8,128)(2,1)S(1)}, bf16[128,640]{1,0:T(8,128)(2,1)S(1)}, u32[]{:S(2)}, u32[]{:S(2)}) collective-permute-start(bf16[128,640]{1,0:T(8,128)(2,1)S(1)} %get-tuple-element.98), channel_id=1, source_target_pairs={{0,8},{8,0},{16,24},{24,16},{1,9},{9,1},{17,25},{25,17},{2,10},{10... | collective-permute-start | bytes 491528 | tf_op jit(solution)/shard_map/ppermute | solution.py:502
  35.6 6.9 %collective-permute-start.10 = (bf16[32,1280]{1,0:T(8,128)(2,1)S(1)}, bf16[32,1280]{1,0:T(8,128)(2,1)S(1)}, u32[]{:S(2)}, u32[]{:S(2)}) collective-permute-start(bf16[32,1280]{1,0:T(8,128)(2,1)S(1)} %get-tuple-element.108), channel_id=1, source_target_pairs={{0,6},{1,7},{2,4},{3,5},{4,2},{5,3},{6,0},{7,1},{8,14},{9,15},{10,... | collective-permute-start | bytes 245768 | tf_op jit(solution)/shard_map/ppermute | solution.py:502
  38.1 6.4 %collective-permute-start.11 = (bf16[32,1280]{1,0:T(8,128)(2,1)S(1)}, bf16[32,1280]{1,0:T(8,128)(2,1)S(1)}, u32[]{:S(2)}, u32[]{:S(2)}) collective-permute-start(bf16[32,1280]{1,0:T(8,128)(2,1)S(1)} %get-tuple-element.109), channel_id=1, source_target_pairs={{0,4},{1,5},{2,6},{3,7},{4,0},{5,1},{6,2},{7,3},{8,12},{9,13},{10,... | collective-permute-start | bytes 245768 | tf_op jit(solution)/shard_map/ppermute | solution.py:502
  38.1 6.4 %collective-permute-start.12 = (bf16[32,1280]{1,0:T(8,128)(2,1)S(1)}, bf16[32,1280]{1,0:T(8,128)(2,1)S(1)}, u32[]{:S(2)}, u32[]{:S(2)}) collective-permute-start(bf16[32,1280]{1,0:T(8,128)(2,1)S(1)} %get-tuple-element.110), channel_id=1, source_target_pairs={{0,2},{1,3},{2,0},{3,1},{4,6},{5,7},{6,4},{7,5},{8,10},{9,11},{10,... | collective-permute-start | bytes 245768 | tf_op jit(solution)/shard_map/ppermute | solution.py:502
  44.6 6.6 %collective-permute-start.15 = (bf16[32,1280]{1,0:T(8,128)(2,1)S(1)}, bf16[32,1280]{1,0:T(8,128)(2,1)S(1)}, u32[]{:S(2)}, u32[]{:S(2)}) collective-permute-start(bf16[32,1280]{1,0:T(8,128)(2,1)S(1)} %shard_map.149.refs_0_), channel_id=1, source_target_pairs={{0,6},{1,7},{2,4},{3,5},{4,2},{5,3},{6,0},{7,1},{8,14},{9,15},{10,... | collective-permute-start | bytes 245768 | tf_op jit(solution)/shard_map/ppermute | solution.py:502
  47.3 6.8 %collective-permute-start.14 = (bf16[32,1280]{1,0:T(8,128)(2,1)S(1)}, bf16[32,1280]{1,0:T(8,128)(2,1)S(1)}, u32[]{:S(2)}, u32[]{:S(2)}) collective-permute-start(bf16[32,1280]{1,0:T(8,128)(2,1)S(1)} %shard_map.149.refs_0_), channel_id=1, source_target_pairs={{0,4},{1,5},{2,6},{3,7},{4,0},{5,1},{6,2},{7,3},{8,12},{9,13},{10,... | collective-permute-start | bytes 245768 | tf_op jit(solution)/shard_map/ppermute | solution.py:502
  47.3 6.8 %collective-permute-start.13 = (bf16[32,1280]{1,0:T(8,128)(2,1)S(1)}, bf16[32,1280]{1,0:T(8,128)(2,1)S(1)}, u32[]{:S(2)}, u32[]{:S(2)}) collective-permute-start(bf16[32,1280]{1,0:T(8,128)(2,1)S(1)} %shard_map.149.refs_0_), channel_id=1, source_target_pairs={{0,2},{1,3},{2,0},{3,1},{4,6},{5,7},{6,4},{7,5},{8,10},{9,11},{10,... | collective-permute-start | bytes 245768 | tf_op jit(solution)/shard_map/ppermute | solution.py:502
  54.1 7.1 %collective-permute-start.16 = (bf16[128,640]{1,0:T(8,128)(2,1)S(1)}, bf16[128,640]{1,0:T(8,128)(2,1)S(1)}, u32[]{:S(2)}, u32[]{:S(2)}) collective-permute-start(bf16[128,640]{1,0:T(8,128)(2,1)S(1)} %get-tuple-element.111.refs_0_), channel_id=1, source_target_pairs={{0,8},{8,0},{16,24},{24,16},{1,9},{9,1},{17,25},{25,17},{2,10},{10... | collective-permute-start | bytes 491528 | tf_op jit(solution)/shard_map/ppermute | solution.py:502
  55.5 7.1 %collective-permute-start.20 = (bf16[128,640]{1,0:T(8,128)(2,1)S(1)}, bf16[128,640]{1,0:T(8,128)(2,1)S(1)}, u32[]{:S(2)}, u32[]{:S(2)}) collective-permute-start(bf16[128,640]{1,0:T(8,128)(2,1)S(1)} %get-tuple-element.112.refs_4_), channel_id=1, source_target_pairs={{0,16},{8,24},{16,0},{24,8},{1,17},{9,25},{17,1},{25,9},{2,18},{10... | collective-permute-start | bytes 491528 | tf_op jit(solution)/shard_map/ppermute | solution.py:502
  57.0 9.1 %collective-permute-start.17 = (bf16[128,640]{1,0:T(8,128)(2,1)S(1)}, bf16[128,640]{1,0:T(8,128)(2,1)S(1)}, u32[]{:S(2)}, u32[]{:S(2)}) collective-permute-start(bf16[128,640]{1,0:T(8,128)(2,1)S(1)} %get-tuple-element.111.refs_0_), channel_id=1, source_target_pairs={{0,16},{8,24},{16,0},{24,8},{1,17},{9,25},{17,1},{25,9},{2,18},{10... | collective-permute-start | bytes 491528 | tf_op jit(solution)/shard_map/ppermute | solution.py:502
  57.5 8.6 %collective-permute-start.19 = (bf16[128,640]{1,0:T(8,128)(2,1)S(1)}, bf16[128,640]{1,0:T(8,128)(2,1)S(1)}, u32[]{:S(2)}, u32[]{:S(2)}) collective-permute-start(bf16[128,640]{1,0:T(8,128)(2,1)S(1)} %get-tuple-element.112.refs_4_), channel_id=1, source_target_pairs={{0,8},{8,0},{16,24},{24,16},{1,9},{9,1},{17,25},{25,17},{2,10},{10... | collective-permute-start | bytes 491528 | tf_op jit(solution)/shard_map/ppermute | solution.py:502
  61.2 7.0 %collective-permute-start.18 = (bf16[128,640]{1,0:T(8,128)(2,1)S(1)}, bf16[128,640]{1,0:T(8,128)(2,1)S(1)}, u32[]{:S(2)}, u32[]{:S(2)}) collective-permute-start(bf16[128,640]{1,0:T(8,128)(2,1)S(1)} %collective-permute-done.16.refs_1_), channel_id=1, source_target_pairs={{0,16},{8,24},{16,0},{24,8},{1,17},{9,25},{17,1},{25,9},{2,18},{10... | collective-permute-start | bytes 491528 | tf_op jit(solution)/shard_map/ppermute | solution.py:502
  62.6 5.6 %collective-permute-start.21 = (bf16[128,640]{1,0:T(8,128)(2,1)S(1)}, bf16[128,640]{1,0:T(8,128)(2,1)S(1)}, u32[]{:S(2)}, u32[]{:S(2)}) collective-permute-start(bf16[128,640]{1,0:T(8,128)(2,1)S(1)} %collective-permute-done.20.refs_6_), channel_id=1, source_target_pairs={{0,8},{8,0},{16,24},{24,16},{1,9},{9,1},{17,25},{25,17},{2,10},{10... | collective-permute-start | bytes 491528 | tf_op jit(solution)/shard_map/ppermute | solution.py:502
  68.3 3.1 %collective-permute-start.22 = (bf16[512,1280]{1,0:T(8,128)(2,1)S(1)}, bf16[512,1280]{1,0:T(8,128)(2,1)S(1)}, u32[]{:S(2)}, u32[]{:S(2)}) collective-permute-start(bf16[512,1280]{1,0:T(8,128)(2,1)S(1)} %shard_map.151.mid_half.small_half), channel_id=1, source_target_pairs={{0,1},{1,0},{2,3},{3,2},{4,5},{5,4},{6,7},{7,6},{8,9},{9,8},{10,11... | collective-permute-start | bytes 3932168 | tf_op jit(solution)/shard_map/ppermute | solution.py:502

commit v11 on v9

--- a/solution.py
+++ b/solution.py
@@ -388,10 +388,7 @@
 
 
 CORE = ("horiz", 0, 2)
-NEAR, FAR = ("horiz", 1, 2), ("horiz", 2, 2)
 CHIPS = ("horiz", 1, 4)
-MEMBER_LOW, MEMBER_HIGH = ("ens", 0, 2), ("ens", 1, 2)
-MEMBERS = ("ens", 0, 4)
 
 
 def position(stage):
@@ -402,37 +399,37 @@
 def sum_kernel(*refs, terms, stage, factor):
     ins, outs = refs[:terms], refs[terms:]
     rows = outs[0].shape[0]
-    for k, out_ref in enumerate(outs):
+    for index, out_ref in enumerate(outs):
         here = pl.ds(0, rows)
         if stage is not None:
-            here = pl.ds(pl.multiple_of((position(stage) ^ k) * rows, rows), rows)
+            start = (position(stage) ^ (-index % len(outs))) * rows
+            here = pl.ds(pl.multiple_of(start, rows), rows)
         total = ins[0][here, :].astype(F32)
         for ref in ins[1:]:
             total = total + ref[here, :].astype(F32)
         out_ref[...] = (total * factor).astype(BF16)
 
 
-def join_kernel(*refs, stage, groups, cuts):
-    ins, out_refs = refs[:-cuts], refs[-cuts:]
-    count = len(ins) // groups
-    rows, columns = ins[0].shape
-    width = out_refs[0].shape[1]
-    for k in range(count):
-        here = pl.ds(pl.multiple_of((position(stage) ^ k) * rows, rows), rows)
-        for group in range(groups):
-            ref = ins[group * count + k]
-            for start in range(0, columns, min(width, columns)):
-                first = group * columns + start
-                part = min(width, columns)
-                out_refs[first // width][here, first % width : first % width + part] = ref[
-                    :, start : start + part
-                ]
-
-
-def core_sum_kernel(keep_mid, got_mid, keep_small, got_small, *outs, stage):
+def join_kernel(*refs, stage):
+    ins, out_ref = refs[:-1], refs[-1]
+    rows = ins[0].shape[0]
+    if stage is None:
+        places = member_order()
+    else:
+        places = [position(stage) ^ k for k in range(len(ins))]
+    for place, ref in zip(places, ins):
+        out_ref[pl.ds(pl.multiple_of(place * rows, rows), rows), :] = ref[...]
+
+
+def member_order():
+    member, core = lax.axis_index("ens"), lax.axis_index("horiz") % 2
+    return [member, member ^ (1 + core), member ^ (2 - core), member ^ 3]
+
+
+def core_sum_kernel(keep_mid, got_mid, keep_small, got_small, *outs):
     rows = outs[0].shape[0]
-    for k, out_ref in enumerate(outs):
-        here = pl.ds(pl.multiple_of((position(stage) ^ k) * rows, rows), rows)
+    for member, out_ref in zip(member_order(), outs):
+        here = pl.ds(pl.multiple_of(member * rows, rows), rows)
         first = 0
         for keep_ref, got_ref in ((keep_mid, got_mid), (keep_small, got_small)):
             columns = keep_ref.shape[1]
@@ -487,10 +484,27 @@
 def exchange(arrays, stage):
     axis, shift, _ = stage
     count = lax.axis_size(axis)
-    return [
-        lax.ppermute(array, axis, [(i, i ^ (k << shift)) for i in range(count)])
-        for k, array in enumerate(arrays, 1)
-    ]
+    sent = {}
+    for k in range(len(arrays), 0, -1):
+        route = [(i, i ^ (k << shift)) for i in range(count)]
+        sent[k] = lax.ppermute(arrays[k - 1], axis, route)
+    return [sent[k] for k in range(1, len(arrays) + 1)]
+
+
+def to_member(array, second):
+    members, count = lax.axis_size("ens"), lax.axis_size("horiz")
+    route = []
+    for member in range(members):
+        for place in range(count):
+            neighbour = member ^ (1 << (place % 2 ^ second))
+            route.append((member * count + place, neighbour * count + place))
+    return lax.ppermute(array, ("ens", "horiz"), route)
+
+
+def collect_members(piece):
+    got_first = to_member(piece, 0)
+    got_second = to_member(piece, 1)
+    return [piece, got_first, got_second, to_member(got_first, 1)]
 
 
 def add(terms, stage, factor=1.0):
@@ -505,27 +519,14 @@
     )(*terms)
 
 
-def join(groups, stage, outs=1):
-    rows, columns = groups[0][0].shape
-    shape = (rows * len(groups[0]), columns * len(groups) // outs)
-    return call(
-        join_kernel, [(shape, BF16)] * outs, stage=stage, groups=len(groups), cuts=outs
-    )(*[piece for group in groups for piece in group])
+def join(pieces, stage):
+    rows, columns = pieces[0].shape
+    return call(join_kernel, [((rows * len(pieces), columns), BF16)], stage=stage)(*pieces)[0]
 
 
 def reduce_to(terms, stage):
     parts = add(terms, stage)
-    return [parts[0]] + exchange(parts[1:], stage)
-
-
-def collect_members(one, two):
-    (low_one,) = exchange([one], MEMBER_LOW)
-    (high_two,) = exchange([two], MEMBER_HIGH)
-    (high_one,) = exchange([one], MEMBER_HIGH)
-    (low_two,) = exchange([two], MEMBER_LOW)
-    (far_one,) = exchange([low_one], MEMBER_HIGH)
-    (far_two,) = exchange([high_two], MEMBER_LOW)
-    return [one, low_one, high_one, far_one], [two, low_two, high_two, far_two]
+    return [parts[0]] + exchange(parts[:0:-1], stage)[::-1]
 
 
 def collect(piece, stage):
@@ -603,12 +604,14 @@
     )(tile_count, column, cols, mask, delta_one, adjoint, weights)
     got_small, field = tie(got_small, field)
 
-    parts = call(
-        core_sum_kernel,
-        [((units // 2 // MEMBERS[2], units + 2 * fields), BF16)] * MEMBERS[2],
-        stage=MEMBERS,
-    )(keep_mid, got_mid, keep_small, got_small)
-    terms = [parts[0]] + exchange(parts[1:], MEMBERS)
+    members = lax.axis_size("ens")
+    parts = call(core_sum_kernel, [((units // 2 // members, units + 2 * fields), BF16)] * members)(
+        keep_mid, got_mid, keep_small, got_small
+    )
+    own, first, second, far = parts
+    got_far = to_member(far, 0)
+    got_first = to_member(first, 0)
+
     act_two, up_rows, down_rows = tie(act_two, up_rows, down_rows, parts)[:3]
     halos = to_neighbours(up_rows, down_rows, "horiz")
     (state_rows,) = call(
@@ -618,18 +621,19 @@
         smem=(0,),
         lons=lons,
     )(tile_count, moved, cols, mask, x_now, act_two, coef, ratio, inverse, w_out)
+    got_far, state_rows, halos = tie(got_far, state_rows, halos)
+    terms = [own, got_first, to_member(add([second, got_far], None)[0], 1)]
     (grad_rows,) = call(last_kernel, [((fields * lons, lats), F32)], lons=lons)(
         field, *halos, low_pack, high_pack, base
     )
-    terms, state_rows, grad_rows = tie(terms, state_rows, grad_rows)
+    terms, grad_rows = tie(terms, grad_rows)
 
     if lax.axis_size("horiz") == 8:
         terms = reduce_to(terms, CHIPS)
-        pieces = collect(add(terms, None, factor)[0], CHIPS)
-        groups = collect_members(*join([pieces], CHIPS, outs=2))
+        own = join(collect(add(terms, None, factor)[0], CHIPS), CHIPS)
     else:
-        groups = [collect(over_all_chips(add(terms, None)[0], factor), MEMBERS)]
-    (own,) = join(groups, MEMBERS)
+        own = over_all_chips(add(terms, None)[0], factor)
+    own = join(collect_members(own), None)
     (got,) = exchange([own], CORE)
     half_done = final(own, False, [], fields)
     grad_mid, grad_in, grad_out = final(got, True, half_done, fields)

time: 73.7 us -> 76.7 us (1.041)
  waiting for transfers between devices: 25.8 us -> 31.8 us
  starting transfers between devices: 27.6 us -> 24.6 us
    ppermute x18 -> x15, waiting for transfers between devices: 25.3 us -> 31.5 us  [the longest x6 19.2 us: to_member(): return lax.ppermute(array, ('ens', 'horiz'), route)]
    ppermute x18 -> x15, starting transfers between devices: 19.5 us -> 16.5 us  [the longest x9 9.54 us: exchange(): sent[k] = lax.ppermute(arrays[k - 1], axis, route)]
    pallas_call x12 -> x13, Pallas kernels: 11.1 us -> 11.1 us  [run(): pl.pallas_call(functools.partial(kernel, **names), out_shape=[jax.ShapeDt...]
  transfers between devices with their start and end apart: 22 -> 19, of which waited for: 12 -> 10; matrix products, arithmetic and copies ran while one was open for 3% -> 3% of each run, Pallas kernels for 12% -> 11%
where the time goes in v11:
time: 76.7 us; the launch traced here: 76.5 us
  waiting for transfers between devices  31.8 us (41%)
  starting transfers between devices  24.6 us (32%)
  Pallas kernels  15.6 us (20%)
  local copies, waits for them, and re-layouts  1.92 us (3%)
  between operations  1.51 us (2%)
  other arithmetic  1.1 us (1%)
    ppermute x6, waiting for transfers between devices, to_member(): return lax.ppermute(array, ('ens', 'horiz'), route)  19.2 us
    ppermute x9, waiting for transfers between devices, exchange(): sent[k] = lax.ppermute(arrays[k - 1], axis, route)  12.3 us
    pallas_call x13, Pallas kernels, run(): pl.pallas_call(functools.partial(kernel, **names), out_shape=[jax.ShapeDt...  11.1 us
    ppermute x9, starting transfers between devices, exchange(): sent[k] = lax.ppermute(arrays[k - 1], axis, route)  9.54 us
    ppermute x2, starting transfers between devices, to_neighbours(): lax.ppermute(downward, axis, backward)  7.52 us
    ppermute x6, starting transfers between devices, to_member(): return lax.ppermute(array, ('ens', 'horiz'), route)  6.92 us
    pallas_call x2, Pallas kernels, final(): pl.pallas_call(final_kernel, grid=(units // block,), out_shape=[jax.Shape...  4.47 us
    unnamed x14, local copies, waits for them, and re-layouts  1.86 us
  transfers between devices with their start and end apart: 19, of which 10 were waited for; matrix products, arithmetic and copies ran while one was open for 3% of the time, Pallas kernels for 11%

profile of v11, /device:TPU:0, one launch (start us, length us, event | category | flops | bytes accessed | tf_op | source)
XLA Modules:
  0.0 76.5 jit_solution(671716881998540951)
XLA Ops:
  0.6 1.0 %pad_maximum_fusion.1 = f32[130,4,128]{2,1,0:T(4,128)S(1)} fusion(f32[2,4,128]{2,1,0:T(4,128)} %param.12, f32[128,4,128]{2,1,0:T(4,128)} %bitcast.16), kind=kLoop, calls=%fused_computation.1 | loop fusion | flops 66560 | bytes 532480 | tf_op jit(solution)/shard_map/concatenate | solution.py:561
  1.7 0.5 collective-permute-start
  2.2 4.1 %collective-permute-start.1 = (bf16[272,128]{1,0:T(8,128)(2,1)S(1)}, bf16[272,128]{1,0:T(8,128)(2,1)S(1)}, u32[]{:S(2)}, u32[]{:S(2)}) collective-permute-start(bf16[272,128]{1,0:T(8,128)(2,1)S(1)} %get-tuple-element.51), channel_id=1, source_target_pairs={{1,0},{2,1},{3,2},{4,3},{5,4},{6,5},{7,6},{0,7},{9,8},{10,9},{11,1... | collective-permute-start | bytes 208904 | tf_op jit(solution)/shard_map/ppermute | solution.py:550
  7.0 1.8 %constant_dynamic-update-slice_fusion.1 = bf16[1024,1152]{1,0:T(8,128)(2,1)S(1)} fusion(bf16[1024,1024]{1,0:T(8,128)(2,1)} %param.18), kind=kLoop, calls=%fused_computation.3 | loop fusion | bytes 4194304
  9.0 0.8 shard_map.138
  9.9 4.0 %shard_map.139 = (f32[4,128,128]{2,1,0:T(8,128)S(1)}, bf16[128,384]{1,0:T(8,128)(2,1)S(1)}, bf16[1024,384]{1,0:T(8,128)(2,1)}, bf16[1024,384]{1,0:T(8,128)(2,1)S...) custom-call(f32[520,128]{1,0:T(8,128)S(1)} %bitcast.12, ...), custom_call_target="tpu_custom_call" | custom-call | bytes 15000000 | tf_op jit(solution)/shard_map/pallas_call | solution.py:27
  13.8 2.1 %shard_map.140 = (bf16[1024,384]{1,0:T(8,128)(2,1)S(1)}, bf16[512,256]{1,0:T(8,128)(2,1)S(1)}, bf16[512,256]{1,0:T(8,128)(2,1)S(1)}) custom-call(bf16[128,384]{1,0:T(8,128)(2,1)S(1)} %get-tuple-element.55.x_ref, bf16[1024,384]{1,0:T(8,128)(2,1)S(1)} %get-tuple-element.70.act_two_ref, bf16[1024,384]{1,0:T(8,128)(2,1)S(1)} %get-tuple-element.57.delta_two_ref, ...), custom_call_target="tpu_custom_call" | custom-call | bytes 4000000 | tf_op jit(solution)/shard_map/pallas_call | solution.py:27
  15.9 0.6 collective-permute-start.3
  16.4 0.6 shard_map.141
  17.0 0.6 collective-permute-done.3.got_small
  17.9 2.0 %collective-permute-start.4 = (bf16[128,1280]{1,0:T(8,128)(2,1)S(1)}, bf16[128,1280]{1,0:T(8,128)(2,1)S(1)}, u32[]{:S(2)}, u32[]{:S(2)}) collective-permute-start(bf16[128,1280]{1,0:T(8,128)(2,1)S(1)} %get-tuple-element.63), channel_id=1, source_target_pairs={{0,8},{1,17},{2,10},{3,19},{4,12},{5,21},{6,14},{7,23},{8,0},{9,25... | collective-permute-start | bytes 983048 | tf_op jit(solution)/shard_map/ppermute | solution.py:501
  20.0 3.4 %collective-permute-start.6 = (bf16[256,128]{1,0:T(8,128)(2,1)S(1)}, bf16[256,128]{1,0:T(8,128)(2,1)S(1)}, u32[]{:S(2)}, u32[]{:S(2)}) collective-permute-start(bf16[256,128]{1,0:T(8,128)(2,1)S(1)} %get-tuple-element.75), channel_id=1, source_target_pairs={{1,0},{2,1},{3,2},{4,3},{5,4},{6,5},{7,6},{0,7},{9,8},{10,9},{11,1... | collective-permute-start | bytes 196616 | tf_op jit(solution)/shard_map/ppermute | solution.py:550
  23.6 1.6 %shard_map.143 = f32[512,128]{1,0:T(8,128)} custom-call(s32[1,1]{1,0:T(1,128)S(6)} %copy.26.count_ref, f32[4,128,128]{2,1,0:T(8,128)S(1)} %get-tuple-element.64.moved_ref, s32[3,128]{1,0:T(4,128)S(1)} %get-tuple-element.96.cols_ref, s32[3,128]{1,0:T(4,128)S(1)} %get-tuple-element.95.mask_ref, bf16[128,384]{1,0:T(8,128)(2,1)S(1)} %get-tuple-element.55.x_ref, ...), custom_call_target="tpu_custom_call" | custom-call | tf_op jit(solution)/shard_map/pallas_call | solution.py:27
  25.5 1.7 %collective-permute-start.8 = (bf16[128,1280]{1,0:T(8,128)(2,1)S(1)}, bf16[128,1280]{1,0:T(8,128)(2,1)S(1)}, u32[]{:S(2)}, u32[]{:S(2)}) collective-permute-start(bf16[128,1280]{1,0:T(8,128)(2,1)S(1)} %shard_map.144), channel_id=1, source_target_pairs={{0,16},{1,9},{2,18},{3,11},{4,20},{5,13},{6,22},{7,15},{8,24},{9,1... | collective-permute-start | bytes 983048 | tf_op jit(solution)/shard_map/ppermute | solution.py:501
  27.3 1.5 %shard_map.145 = f32[512,128]{1,0:T(8,128)} custom-call(f32[4,128,128]{2,1,0:T(8,128)S(1)} %get-tuple-element.78.field_ref, bf16[256,128]{1,0:T(8,128)(2,1)S(1)} %collective-permute-done.5.low_ref, bf16[256,128]{1,0:T(8,128)(2,1)S(1)} %collective-permute-done.6.high_ref, bf16[272,128]{1,0:T(8,128)(2,1)S(1)} %collective-permute-done.low_ref.low_mix_ref, ...), custom_call_target="tpu_custom_call" | custom-call | tf_op jit(solution)/shard_map/pallas_call | solution.py:27
  28.7 4.9 %collective-permute-done.7.refs_1_ = bf16[128,1280]{1,0:T(8,128)(2,1)S(1)} collective-permute-done((bf16[128,1280]{1,0:T(8,128)(2,1)S(1)}, bf16[128,1280]{1,0:T(8,128)(2,1)S(1)}, u32[]{:S(2)}, u32[]{:S(2)}) %collective-permute-start.7) | collective-permute-done | bytes 327712 | tf_op jit(solution)/shard_map/ppermute | solution.py:501
  33.7 1.0 %collective-permute-start.9 = (bf16[32,1280]{1,0:T(8,128)(2,1)S(1)}, bf16[32,1280]{1,0:T(8,128)(2,1)S(1)}, u32[]{:S(2)}, u32[]{:S(2)}) collective-permute-start(bf16[32,1280]{1,0:T(8,128)(2,1)S(1)} %get-tuple-element.86), channel_id=1, source_target_pairs={{0,6},{1,7},{2,4},{3,5},{4,2},{5,3},{6,0},{7,1},{8,14},{9,15},{10,... | collective-permute-start | bytes 245768 | tf_op jit(solution)/shard_map/ppermute | solution.py:490
  34.8 3.4 %collective-permute-start.11 = (bf16[32,1280]{1,0:T(8,128)(2,1)S(1)}, bf16[32,1280]{1,0:T(8,128)(2,1)S(1)}, u32[]{:S(2)}, u32[]{:S(2)}) collective-permute-start(bf16[32,1280]{1,0:T(8,128)(2,1)S(1)} %get-tuple-element.88), channel_id=1, source_target_pairs={{0,2},{1,3},{2,0},{3,1},{4,6},{5,7},{6,4},{7,5},{8,10},{9,11},{10,... | collective-permute-start | bytes 245768 | tf_op jit(solution)/shard_map/ppermute | solution.py:490
  38.2 2.8 %collective-permute-done.9.refs_1_ = bf16[32,1280]{1,0:T(8,128)(2,1)S(1)} collective-permute-done((bf16[32,1280]{1,0:T(8,128)(2,1)S(1)}, bf16[32,1280]{1,0:T(8,128)(2,1)S(1)}, u32[]{:S(2)}, u32[]{:S(2)}) %collective-permute-start.9) | collective-permute-done | bytes 81952 | tf_op jit(solution)/shard_map/ppermute | solution.py:490
  41.0 2.7 %collective-permute-done.10.refs_2_ = bf16[32,1280]{1,0:T(8,128)(2,1)S(1)} collective-permute-done((bf16[32,1280]{1,0:T(8,128)(2,1)S(1)}, bf16[32,1280]{1,0:T(8,128)(2,1)S(1)}, u32[]{:S(2)}, u32[]{:S(2)}) %collective-permute-start.10) | collective-permute-done | bytes 81952 | tf_op jit(solution)/shard_map/ppermute | solution.py:490
  43.8 1.6 %collective-permute-start.14 = (bf16[32,1280]{1,0:T(8,128)(2,1)S(1)}, bf16[32,1280]{1,0:T(8,128)(2,1)S(1)}, u32[]{:S(2)}, u32[]{:S(2)}) collective-permute-start(bf16[32,1280]{1,0:T(8,128)(2,1)S(1)} %shard_map.147.refs_0_), channel_id=1, source_target_pairs={{0,6},{1,7},{2,4},{3,5},{4,2},{5,3},{6,0},{7,1},{8,14},{9,15},{10,... | collective-permute-start | bytes 245768 | tf_op jit(solution)/shard_map/ppermute | solution.py:490
  45.4 2.8 %collective-permute-start.12 = (bf16[32,1280]{1,0:T(8,128)(2,1)S(1)}, bf16[32,1280]{1,0:T(8,128)(2,1)S(1)}, u32[]{:S(2)}, u32[]{:S(2)}) collective-permute-start(bf16[32,1280]{1,0:T(8,128)(2,1)S(1)} %shard_map.147.refs_0_), channel_id=1, source_target_pairs={{0,2},{1,3},{2,0},{3,1},{4,6},{5,7},{6,4},{7,5},{8,10},{9,11},{10,... | collective-permute-start | bytes 245768 | tf_op jit(solution)/shard_map/ppermute | solution.py:490
  48.2 2.8 %collective-permute-done.14.refs_3_ = bf16[32,1280]{1,0:T(8,128)(2,1)S(1)} collective-permute-done((bf16[32,1280]{1,0:T(8,128)(2,1)S(1)}, bf16[32,1280]{1,0:T(8,128)(2,1)S(1)}, u32[]{:S(2)}, u32[]{:S(2)}) %collective-permute-start.14) | collective-permute-done | bytes 81952 | tf_op jit(solution)/shard_map/ppermute | solution.py:490
  51.0 2.5 %collective-permute-done.13.refs_2_ = bf16[32,1280]{1,0:T(8,128)(2,1)S(1)} collective-permute-done((bf16[32,1280]{1,0:T(8,128)(2,1)S(1)}, bf16[32,1280]{1,0:T(8,128)(2,1)S(1)}, u32[]{:S(2)}, u32[]{:S(2)}) %collective-permute-start.13) | collective-permute-done | bytes 81952 | tf_op jit(solution)/shard_map/ppermute | solution.py:490
  53.6 0.4 collective-permute-start.15
  54.0 1.7 %collective-permute-start.16 = (bf16[128,1280]{1,0:T(8,128)(2,1)S(1)}, bf16[128,1280]{1,0:T(8,128)(2,1)S(1)}, u32[]{:S(2)}, u32[]{:S(2)}) collective-permute-start(bf16[128,1280]{1,0:T(8,128)(2,1)S(1)} %shard_map.148.refs_0_), channel_id=1, source_target_pairs={{0,16},{1,9},{2,18},{3,11},{4,20},{5,13},{6,22},{7,15},{8,24},{9,1... | collective-permute-start | bytes 983048 | tf_op jit(solution)/shard_map/ppermute | solution.py:501
  55.7 8.3 %collective-permute-done.15.refs_1_ = bf16[128,1280]{1,0:T(8,128)(2,1)S(1)} collective-permute-done((bf16[128,1280]{1,0:T(8,128)(2,1)S(1)}, bf16[128,1280]{1,0:T(8,128)(2,1)S(1)}, u32[]{:S(2)}, u32[]{:S(2)}) %collective-permute-start.15) | collective-permute-done | bytes 327712 | tf_op jit(solution)/shard_map/ppermute | solution.py:501
  64.0 1.0 %collective-permute-start.17 = (bf16[128,1280]{1,0:T(8,128)(2,1)S(1)}, bf16[128,1280]{1,0:T(8,128)(2,1)S(1)}, u32[]{:S(2)}, u32[]{:S(2)}) collective-permute-start(bf16[128,1280]{1,0:T(8,128)(2,1)S(1)} %collective-permute-done.15.refs_1_), channel_id=1, source_target_pairs={{0,16},{1,9},{2,18},{3,11},{4,20},{5,13},{6,22},{7,15},{8,24},{9,1... | collective-permute-start | bytes 983048 | tf_op jit(solution)/shard_map/ppermute | solution.py:501
  65.1 6.0 %collective-permute-done.17.refs_3_ = bf16[128,1280]{1,0:T(8,128)(2,1)S(1)} collective-permute-done((bf16[128,1280]{1,0:T(8,128)(2,1)S(1)}, bf16[128,1280]{1,0:T(8,128)(2,1)S(1)}, u32[]{:S(2)}, u32[]{:S(2)}) %collective-permute-start.17) | collective-permute-done | bytes 327712 | tf_op jit(solution)/shard_map/ppermute | solution.py:501
  71.3 2.2 %shard_map.150 = (f32[1024,1024]{1,0:T(8,128)}, f32[1024,128]{1,0:T(8,128)}, f32[128,1024]{1,0:T(8,128)}) custom-call(bf16[512,1280]{1,0:T(8,128)(2,1)S(1)} %shard_map.149.mid_half.small_half, bf16[512,1280]{1,0:T(8,128)(2,1)S(1)} %shard_map.149.mid_half.small_half), custom_call_target="tpu_custom_call" | custom-call | tf_op jit(solution)/shard_map/pallas_call | solution.py:462
  73.5 0.8 %collective-permute-done.18.mid_half.small_half = bf16[512,1280]{1,0:T(8,128)(2,1)S(1)} collective-permute-done((bf16[512,1280]{1,0:T(8,128)(2,1)S(1)}, bf16[512,1280]{1,0:T(8,128)(2,1)S(1)}, u32[]{:S(2)}, u32[]{:S(2)}) %collective-permute-start.18) | collective-permute-done | bytes 1310752 | tf_op jit(solution)/shard_map/ppermute | solution.py:490
  74.3 2.2 %shard_map.151 = (f32[1024,1024]{1,0:T(8,128)}, f32[1024,128]{1,0:T(8,128)}, f32[128,1024]{1,0:T(8,128)}) custom-call(bf16[512,1280]{1,0:T(8,128)(2,1)S(1)} %collective-permute-done.18.mid_half.small_half, bf16[512,1280]{1,0:T(8,128)(2,1)S(1)} %collective-permute-done.18.mid_half.small_half, ...), custom_call_target="tpu_custom_call", output_to_operand_aliasing={{0}: (2, {}), {1}: (3, {}), {2}: (4, {})} | custom-call | tf_op jit(solution)/shard_map/pallas_call | solution.py:462
  (38 shorter events, 1.5 us)
Async XLA Ops:
  1.7 7.2 %copy-start.4 = (s32[1,1,3,128]{3,1,2,0:T(1,128)S(1)}, s32[1,1,3,128]{3,1,2,0:T(1,128)}, u32[]{:S(2)}) copy-start(s32[1,1,3,128]{3,1,2,0:T(1,128)} %param.15) | copy-start | bytes 4612
  1.7 7.2 %copy-start.5 = (s32[1,1,3,128]{3,1,2,0:T(1,128)S(1)}, s32[1,1,3,128]{3,1,2,0:T(1,128)}, u32[]{:S(2)}) copy-start(s32[1,1,3,128]{3,1,2,0:T(1,128)} %param.14) | copy-start | bytes 4612
  1.7 7.2 %copy-start.1 = (f32[1,128,4,128]{3,2,1,0:T(4,128)S(1)}, f32[1,128,4,128]{3,2,1,0:T(4,128)}, u32[]{:S(2)}) copy-start(f32[1,128,4,128]{3,2,1,0:T(4,128)} %param.13) | copy-start | bytes 786436
  1.7 7.2 %copy-start.3 = (f32[1,32,4,128]{3,2,1,0:T(4,128)S(1)}, f32[1,32,4,128]{3,2,1,0:T(4,128)}, u32[]{:S(2)}) copy-start(f32[1,32,4,128]{3,2,1,0:T(4,128)} %param.11) | copy-start | bytes 196612
  1.7 8.1 %collective-permute-start = (bf16[272,128]{1,0:T(8,128)(2,1)S(1)}, bf16[272,128]{1,0:T(8,128)(2,1)S(1)}, u32[]{:S(2)}, u32[]{:S(2)}) collective-permute-start(bf16[272,128]{1,0:T(8,128)(2,1)S(1)} %get-tuple-element.50), channel_id=1, source_target_pairs={{0,1},{1,2},{2,3},{3,4},{4,5},{5,6},{6,7},{7,0},{8,9},{9,10},{10,1... | collective-permute-start | bytes 208904 | tf_op jit(solution)/shard_map/ppermute | solution.py:550
  2.2 7.6 %collective-permute-start.1 = (bf16[272,128]{1,0:T(8,128)(2,1)S(1)}, bf16[272,128]{1,0:T(8,128)(2,1)S(1)}, u32[]{:S(2)}, u32[]{:S(2)}) collective-permute-start(bf16[272,128]{1,0:T(8,128)(2,1)S(1)} %get-tuple-element.51), channel_id=1, source_target_pairs={{1,0},{2,1},{3,2},{4,3},{5,4},{6,5},{7,6},{0,7},{9,8},{10,9},{11,1... | collective-permute-start | bytes 208904 | tf_op jit(solution)/shard_map/ppermute | solution.py:550
  7.0 2.7 %copy-start.2 = (bf16[1024,128]{1,0:T(8,128)(2,1)S(1)}, bf16[1024,128]{1,0:T(8,128)(2,1)}, u32[]{:S(2)}) copy-start(bf16[1024,128]{1,0:T(8,128)(2,1)} %param.17) | copy-start | bytes 786436
  7.0 2.8 %copy-start = (bf16[128,1024]{1,0:T(8,128)(2,1)S(1)}, bf16[128,1024]{1,0:T(8,128)(2,1)}, u32[]{:S(2)}) copy-start(bf16[128,1024]{1,0:T(8,128)(2,1)} %w_out_ref.3) | copy-start | bytes 786436
  13.8 3.8 %collective-permute-start.2 = (bf16[512,1024]{1,0:T(8,128)(2,1)S(1)}, bf16[512,1024]{1,0:T(8,128)(2,1)S(1)}, u32[]{:S(2)}, u32[]{:S(2)}) collective-permute-start(bf16[512,1024]{1,0:T(8,128)(2,1)S(1)} %get-tuple-element.54), channel_id=1, source_target_pairs={{0,1},{1,0},{2,3},{3,2},{4,5},{5,4},{6,7},{7,6},{8,9},{9,8},{10,11... | collective-permute-start | bytes 3145736 | tf_op jit(solution)/shard_map/ppermute | solution.py:490
  15.9 1.7 %collective-permute-start.3 = (bf16[512,256]{1,0:T(8,128)(2,1)S(1)}, bf16[512,256]{1,0:T(8,128)(2,1)S(1)}, u32[]{:S(2)}, u32[]{:S(2)}) collective-permute-start(bf16[512,256]{1,0:T(8,128)(2,1)S(1)} %get-tuple-element.59), channel_id=1, source_target_pairs={{0,1},{1,0},{2,3},{3,2},{4,5},{5,4},{6,7},{7,6},{8,9},{9,8},{10,11... | collective-permute-start | bytes 786440 | tf_op jit(solution)/shard_map/ppermute | solution.py:490
  17.9 7.5 %collective-permute-start.4 = (bf16[128,1280]{1,0:T(8,128)(2,1)S(1)}, bf16[128,1280]{1,0:T(8,128)(2,1)S(1)}, u32[]{:S(2)}, u32[]{:S(2)}) collective-permute-start(bf16[128,1280]{1,0:T(8,128)(2,1)S(1)} %get-tuple-element.63), channel_id=1, source_target_pairs={{0,8},{1,17},{2,10},{3,19},{4,12},{5,21},{6,14},{7,23},{8,0},{9,25... | collective-permute-start | bytes 983048 | tf_op jit(solution)/shard_map/ppermute | solution.py:501
  19.9 5.5 %collective-permute-start.5 = (bf16[256,128]{1,0:T(8,128)(2,1)S(1)}, bf16[256,128]{1,0:T(8,128)(2,1)S(1)}, u32[]{:S(2)}, u32[]{:S(2)}) collective-permute-start(bf16[256,128]{1,0:T(8,128)(2,1)S(1)} %get-tuple-element.74), channel_id=1, source_target_pairs={{0,1},{1,2},{2,3},{3,4},{4,5},{5,6},{6,7},{7,0},{8,9},{9,10},{10,1... | collective-permute-start | bytes 196616 | tf_op jit(solution)/shard_map/ppermute | solution.py:550
  20.0 5.4 %collective-permute-start.6 = (bf16[256,128]{1,0:T(8,128)(2,1)S(1)}, bf16[256,128]{1,0:T(8,128)(2,1)S(1)}, u32[]{:S(2)}, u32[]{:S(2)}) collective-permute-start(bf16[256,128]{1,0:T(8,128)(2,1)S(1)} %get-tuple-element.75), channel_id=1, source_target_pairs={{1,0},{2,1},{3,2},{4,3},{5,4},{6,5},{7,6},{0,7},{9,8},{10,9},{11,1... | collective-permute-start | bytes 196616 | tf_op jit(solution)/shard_map/ppermute | solution.py:550
  23.5 10.1 %collective-permute-start.7 = (bf16[128,1280]{1,0:T(8,128)(2,1)S(1)}, bf16[128,1280]{1,0:T(8,128)(2,1)S(1)}, u32[]{:S(2)}, u32[]{:S(2)}) collective-permute-start(bf16[128,1280]{1,0:T(8,128)(2,1)S(1)} %get-tuple-element.68), channel_id=1, source_target_pairs={{0,8},{1,17},{2,10},{3,19},{4,12},{5,21},{6,14},{7,23},{8,0},{9,25... | collective-permute-start | bytes 983048 | tf_op jit(solution)/shard_map/ppermute | solution.py:501
  25.5 8.1 %collective-permute-start.8 = (bf16[128,1280]{1,0:T(8,128)(2,1)S(1)}, bf16[128,1280]{1,0:T(8,128)(2,1)S(1)}, u32[]{:S(2)}, u32[]{:S(2)}) collective-permute-start(bf16[128,1280]{1,0:T(8,128)(2,1)S(1)} %shard_map.144), channel_id=1, source_target_pairs={{0,16},{1,9},{2,18},{3,11},{4,20},{5,13},{6,22},{7,15},{8,24},{9,1... | collective-permute-start | bytes 983048 | tf_op jit(solution)/shard_map/ppermute | solution.py:501
  33.7 7.2 %collective-permute-start.9 = (bf16[32,1280]{1,0:T(8,128)(2,1)S(1)}, bf16[32,1280]{1,0:T(8,128)(2,1)S(1)}, u32[]{:S(2)}, u32[]{:S(2)}) collective-permute-start(bf16[32,1280]{1,0:T(8,128)(2,1)S(1)} %get-tuple-element.86), channel_id=1, source_target_pairs={{0,6},{1,7},{2,4},{3,5},{4,2},{5,3},{6,0},{7,1},{8,14},{9,15},{10,... | collective-permute-start | bytes 245768 | tf_op jit(solution)/shard_map/ppermute | solution.py:490
  34.8 8.9 %collective-permute-start.10 = (bf16[32,1280]{1,0:T(8,128)(2,1)S(1)}, bf16[32,1280]{1,0:T(8,128)(2,1)S(1)}, u32[]{:S(2)}, u32[]{:S(2)}) collective-permute-start(bf16[32,1280]{1,0:T(8,128)(2,1)S(1)} %get-tuple-element.87), channel_id=1, source_target_pairs={{0,4},{1,5},{2,6},{3,7},{4,0},{5,1},{6,2},{7,3},{8,12},{9,13},{10,... | collective-permute-start | bytes 245768 | tf_op jit(solution)/shard_map/ppermute | solution.py:490
  34.8 8.9 %collective-permute-start.11 = (bf16[32,1280]{1,0:T(8,128)(2,1)S(1)}, bf16[32,1280]{1,0:T(8,128)(2,1)S(1)}, u32[]{:S(2)}, u32[]{:S(2)}) collective-permute-start(bf16[32,1280]{1,0:T(8,128)(2,1)S(1)} %get-tuple-element.88), channel_id=1, source_target_pairs={{0,2},{1,3},{2,0},{3,1},{4,6},{5,7},{6,4},{7,5},{8,10},{9,11},{10,... | collective-permute-start | bytes 245768 | tf_op jit(solution)/shard_map/ppermute | solution.py:490
  43.8 7.3 %collective-permute-start.14 = (bf16[32,1280]{1,0:T(8,128)(2,1)S(1)}, bf16[32,1280]{1,0:T(8,128)(2,1)S(1)}, u32[]{:S(2)}, u32[]{:S(2)}) collective-permute-start(bf16[32,1280]{1,0:T(8,128)(2,1)S(1)} %shard_map.147.refs_0_), channel_id=1, source_target_pairs={{0,6},{1,7},{2,4},{3,5},{4,2},{5,3},{6,0},{7,1},{8,14},{9,15},{10,... | collective-permute-start | bytes 245768 | tf_op jit(solution)/shard_map/ppermute | solution.py:490
  45.4 8.2 %collective-permute-start.13 = (bf16[32,1280]{1,0:T(8,128)(2,1)S(1)}, bf16[32,1280]{1,0:T(8,128)(2,1)S(1)}, u32[]{:S(2)}, u32[]{:S(2)}) collective-permute-start(bf16[32,1280]{1,0:T(8,128)(2,1)S(1)} %shard_map.147.refs_0_), channel_id=1, source_target_pairs={{0,4},{1,5},{2,6},{3,7},{4,0},{5,1},{6,2},{7,3},{8,12},{9,13},{10,... | collective-permute-start | bytes 245768 | tf_op jit(solution)/shard_map/ppermute | solution.py:490
  45.4 8.2 %collective-permute-start.12 = (bf16[32,1280]{1,0:T(8,128)(2,1)S(1)}, bf16[32,1280]{1,0:T(8,128)(2,1)S(1)}, u32[]{:S(2)}, u32[]{:S(2)}) collective-permute-start(bf16[32,1280]{1,0:T(8,128)(2,1)S(1)} %shard_map.147.refs_0_), channel_id=1, source_target_pairs={{0,2},{1,3},{2,0},{3,1},{4,6},{5,7},{6,4},{7,5},{8,10},{9,11},{10,... | collective-permute-start | bytes 245768 | tf_op jit(solution)/shard_map/ppermute | solution.py:490
  53.6 10.4 %collective-permute-start.15 = (bf16[128,1280]{1,0:T(8,128)(2,1)S(1)}, bf16[128,1280]{1,0:T(8,128)(2,1)S(1)}, u32[]{:S(2)}, u32[]{:S(2)}) collective-permute-start(bf16[128,1280]{1,0:T(8,128)(2,1)S(1)} %shard_map.148.refs_0_), channel_id=1, source_target_pairs={{0,8},{1,17},{2,10},{3,19},{4,12},{5,21},{6,14},{7,23},{8,0},{9,25... | collective-permute-start | bytes 983048 | tf_op jit(solution)/shard_map/ppermute | solution.py:501
  54.0 11.0 %collective-permute-start.16 = (bf16[128,1280]{1,0:T(8,128)(2,1)S(1)}, bf16[128,1280]{1,0:T(8,128)(2,1)S(1)}, u32[]{:S(2)}, u32[]{:S(2)}) collective-permute-start(bf16[128,1280]{1,0:T(8,128)(2,1)S(1)} %shard_map.148.refs_0_), channel_id=1, source_target_pairs={{0,16},{1,9},{2,18},{3,11},{4,20},{5,13},{6,22},{7,15},{8,24},{9,1... | collective-permute-start | bytes 983048 | tf_op jit(solution)/shard_map/ppermute | solution.py:501
  64.0 7.1 %collective-permute-start.17 = (bf16[128,1280]{1,0:T(8,128)(2,1)S(1)}, bf16[128,1280]{1,0:T(8,128)(2,1)S(1)}, u32[]{:S(2)}, u32[]{:S(2)}) collective-permute-start(bf16[128,1280]{1,0:T(8,128)(2,1)S(1)} %collective-permute-done.15.refs_1_), channel_id=1, source_target_pairs={{0,16},{1,9},{2,18},{3,11},{4,20},{5,13},{6,22},{7,15},{8,24},{9,1... | collective-permute-start | bytes 983048 | tf_op jit(solution)/shard_map/ppermute | solution.py:501
  71.2 3.1 %collective-permute-start.18 = (bf16[512,1280]{1,0:T(8,128)(2,1)S(1)}, bf16[512,1280]{1,0:T(8,128)(2,1)S(1)}, u32[]{:S(2)}, u32[]{:S(2)}) collective-permute-start(bf16[512,1280]{1,0:T(8,128)(2,1)S(1)} %shard_map.149.mid_half.small_half), channel_id=1, source_target_pairs={{0,1},{1,0},{2,3},{3,2},{4,5},{5,4},{6,7},{7,6},{8,9},{9,8},{10,11... | collective-permute-start | bytes 3932168 | tf_op jit(solution)/shard_map/ppermute | solution.py:490

commit v12 on v11

--- a/solution.py
+++ b/solution.py
@@ -389,6 +389,8 @@
 
 CORE = ("horiz", 0, 2)
 CHIPS = ("horiz", 1, 4)
+MEMBERS = ("ens", 0, 4)
+MEMBER_LOW, MEMBER_HIGH = ("ens", 0, 2), ("ens", 1, 2)
 
 
 def position(stage):
@@ -410,15 +412,20 @@
         out_ref[...] = (total * factor).astype(BF16)
 
 
-def join_kernel(*refs, stage):
-    ins, out_ref = refs[:-1], refs[-1]
-    rows = ins[0].shape[0]
-    if stage is None:
-        places = member_order()
-    else:
-        places = [position(stage) ^ k for k in range(len(ins))]
-    for place, ref in zip(places, ins):
-        out_ref[pl.ds(pl.multiple_of(place * rows, rows), rows), :] = ref[...]
+def join_kernel(*refs, stage, groups, cuts):
+    ins, outs = refs[:-cuts], refs[-cuts:]
+    count = len(ins) // groups
+    rows, columns = ins[0].shape
+    width = outs[0].shape[1]
+    part = min(width, columns)
+    for k in range(count):
+        here = pl.ds(pl.multiple_of((position(stage) ^ k) * rows, rows), rows)
+        for group in range(groups):
+            for start in range(0, columns, part):
+                first = group * columns + start
+                outs[first // width][here, first % width : first % width + part] = ins[
+                    group * count + k
+                ][:, start : start + part]
 
 
 def member_order():
@@ -501,10 +508,14 @@
     return lax.ppermute(array, ("ens", "horiz"), route)
 
 
-def collect_members(piece):
-    got_first = to_member(piece, 0)
-    got_second = to_member(piece, 1)
-    return [piece, got_first, got_second, to_member(got_first, 1)]
+def collect_members(one, two):
+    (low_one,) = exchange([one], MEMBER_LOW)
+    (high_two,) = exchange([two], MEMBER_HIGH)
+    (high_one,) = exchange([one], MEMBER_HIGH)
+    (low_two,) = exchange([two], MEMBER_LOW)
+    (far_one,) = exchange([low_one], MEMBER_HIGH)
+    (far_two,) = exchange([high_two], MEMBER_LOW)
+    return [one, low_one, high_one, far_one], [two, low_two, high_two, far_two]
 
 
 def add(terms, stage, factor=1.0):
@@ -519,9 +530,12 @@
     )(*terms)
 
 
-def join(pieces, stage):
-    rows, columns = pieces[0].shape
-    return call(join_kernel, [((rows * len(pieces), columns), BF16)], stage=stage)(*pieces)[0]
+def join(groups, stage, cuts=1):
+    rows, columns = groups[0][0].shape
+    shape = (rows * len(groups[0]), columns * len(groups) // cuts)
+    return call(
+        join_kernel, [(shape, BF16)] * cuts, stage=stage, groups=len(groups), cuts=cuts
+    )(*[piece for group in groups for piece in group])
 
 
 def reduce_to(terms, stage):
@@ -630,10 +644,10 @@
 
     if lax.axis_size("horiz") == 8:
         terms = reduce_to(terms, CHIPS)
-        own = join(collect(add(terms, None, factor)[0], CHIPS), CHIPS)
+        halves = join([collect(add(terms, None, factor)[0], CHIPS)], CHIPS, cuts=2)
     else:
-        own = over_all_chips(add(terms, None)[0], factor)
-    own = join(collect_members(own), None)
+        halves = jnp.split(over_all_chips(add(terms, None)[0], factor), 2, axis=1)
+    (own,) = join(collect_members(*halves), MEMBERS)
     (got,) = exchange([own], CORE)
     half_done = final(own, False, [], fields)
     grad_mid, grad_in, grad_out = final(got, True, half_done, fields)

time: 76.7 us -> 73.2 us (0.954)
  waiting for transfers between devices: 31.8 us -> 25.2 us
  starting transfers between devices: 24.6 us -> 27.7 us
    ppermute x6 -> x3, waiting for transfers between devices: 19.2 us -> 4.86 us  [to_member(): return lax.ppermute(array, ('ens', 'horiz'), route)]
    ppermute x9 -> x15, waiting for transfers between devices: 12.3 us -> 20 us  [exchange(): sent[k] = lax.ppermute(arrays[k - 1], axis, route)]
    ppermute x9 -> x15, starting transfers between devices: 9.54 us -> 15.7 us  [exchange(): sent[k] = lax.ppermute(arrays[k - 1], axis, route)]
    ppermute x6 -> x3, starting transfers between devices: 6.92 us -> 3.8 us  [to_member(): return lax.ppermute(array, ('ens', 'horiz'), route)]
  transfers between devices with their start and end apart: 19 -> 22, of which waited for: 10 -> 12; matrix products, arithmetic and copies ran while one was open for 3% -> 3% of each run, Pallas kernels for 11% -> 12%
where the time goes in v12:
time: 73.2 us; the launch traced here: 73 us
  starting transfers between devices  27.7 us (38%)
  waiting for transfers between devices  25.2 us (34%)
  Pallas kernels  15.6 us (21%)
  local copies, waits for them, and re-layouts  1.92 us (3%)
  between operations  1.51 us (2%)
  other arithmetic  1.1 us (2%)
    ppermute x15, waiting for transfers between devices, exchange(): sent[k] = lax.ppermute(arrays[k - 1], axis, route)  20 us
    ppermute x15, starting transfers between devices, exchange(): sent[k] = lax.ppermute(arrays[k - 1], axis, route)  15.7 us
    pallas_call x13, Pallas kernels, run(): pl.pallas_call(functools.partial(kernel, **names), out_shape=[jax.ShapeDt...  11.1 us
    ppermute x2, starting transfers between devices, to_neighbours(): lax.ppermute(downward, axis, backward)  7.52 us
    ppermute x3, waiting for transfers between devices, to_member(): return lax.ppermute(array, ('ens', 'horiz'), route)  4.86 us
    pallas_call x2, Pallas kernels, final(): pl.pallas_call(final_kernel, grid=(units // block,), out_shape=[jax.Shape...  4.47 us
    ppermute x3, starting transfers between devices, to_member(): return lax.ppermute(array, ('ens', 'horiz'), route)  3.8 us
    unnamed x14, local copies, waits for them, and re-layouts  1.86 us
  transfers between devices with their start and end apart: 22, of which 12 were waited for; matrix products, arithmetic and copies ran while one was open for 3% of the time, Pallas kernels for 12%

profile of v12, /device:TPU:0, one launch (start us, length us, event | category | flops | bytes accessed | tf_op | source)
XLA Modules:
  0.0 73.0 jit_solution(13035630401310397493)
XLA Ops:
  0.6 1.0 %pad_maximum_fusion.1 = f32[130,4,128]{2,1,0:T(4,128)S(1)} fusion(f32[2,4,128]{2,1,0:T(4,128)} %param.12, f32[128,4,128]{2,1,0:T(4,128)} %bitcast.16), kind=kLoop, calls=%fused_computation.1 | loop fusion | flops 66560 | bytes 532480 | tf_op jit(solution)/shard_map/concatenate | solution.py:575
  2.2 4.1 %collective-permute-start.1 = (bf16[272,128]{1,0:T(8,128)(2,1)S(1)}, bf16[272,128]{1,0:T(8,128)(2,1)S(1)}, u32[]{:S(2)}, u32[]{:S(2)}) collective-permute-start(bf16[272,128]{1,0:T(8,128)(2,1)S(1)} %get-tuple-element.53), channel_id=1, source_target_pairs={{1,0},{2,1},{3,2},{4,3},{5,4},{6,5},{7,6},{0,7},{9,8},{10,9},{11,1... | collective-permute-start | bytes 208904 | tf_op jit(solution)/shard_map/ppermute | solution.py:564
  7.0 1.8 %constant_dynamic-update-slice_fusion.1 = bf16[1024,1152]{1,0:T(8,128)(2,1)S(1)} fusion(bf16[1024,1024]{1,0:T(8,128)(2,1)} %param.18), kind=kLoop, calls=%fused_computation.3 | loop fusion | bytes 4194304
  9.0 0.8 %shard_map.138 = (f32[3,128,128]{2,1,0:T(8,128)S(1)}, f32[32,384]{1,0:T(8,128)S(1)}, f32[32,384]{1,0:T(8,128)S(1)}, f32[32,384]{1,0:T(8,128)S(1)}) custom-call(s32[1,1]{1,0:T(1,128)S(6)} %copy.26.count_ref, f32[640,128]{1,0:T(8,128)S(1)} %bitcast.14, s32[3,128]{1,0:T(4,128)S(1)} %get-tuple-element.100.cols_ref, s32[3,128]{1,0:T(4,128)S(1)} %get-tuple-element.99.mask_ref), custom_call_target="tpu_custom_call" | custom-call | bytes 30000000 | tf_op jit(solution)/shard_map/pallas_call | solution.py:27
  9.9 4.0 %shard_map.139 = (f32[4,128,128]{2,1,0:T(8,128)S(1)}, bf16[128,384]{1,0:T(8,128)(2,1)S(1)}, bf16[1024,384]{1,0:T(8,128)(2,1)}, bf16[1024,384]{1,0:T(8,128)(2,1)S...) custom-call(f32[520,128]{1,0:T(8,128)S(1)} %bitcast.12, ...), custom_call_target="tpu_custom_call" | custom-call | bytes 15000000 | tf_op jit(solution)/shard_map/pallas_call | solution.py:27
  13.8 2.1 %shard_map.140 = (bf16[1024,384]{1,0:T(8,128)(2,1)S(1)}, bf16[512,256]{1,0:T(8,128)(2,1)S(1)}, bf16[512,256]{1,0:T(8,128)(2,1)S(1)}) custom-call(bf16[128,384]{1,0:T(8,128)(2,1)S(1)} %get-tuple-element.57.x_ref, bf16[1024,384]{1,0:T(8,128)(2,1)S(1)} %get-tuple-element.72.act_two_ref, bf16[1024,384]{1,0:T(8,128)(2,1)S(1)} %get-tuple-element.59.delta_two_ref, ...), custom_call_target="tpu_custom_call" | custom-call | bytes 4000000 | tf_op jit(solution)/shard_map/pallas_call | solution.py:27
  17.0 0.6 collective-permute-done.3.got_small
  17.9 2.0 %collective-permute-start.4 = (bf16[128,1280]{1,0:T(8,128)(2,1)S(1)}, bf16[128,1280]{1,0:T(8,128)(2,1)S(1)}, u32[]{:S(2)}, u32[]{:S(2)}) collective-permute-start(bf16[128,1280]{1,0:T(8,128)(2,1)S(1)} %get-tuple-element.65), channel_id=1, source_target_pairs={{0,8},{1,17},{2,10},{3,19},{4,12},{5,21},{6,14},{7,23},{8,0},{9,25... | collective-permute-start | bytes 983048 | tf_op jit(solution)/shard_map/ppermute | solution.py:508
  20.0 3.4 %collective-permute-start.6 = (bf16[256,128]{1,0:T(8,128)(2,1)S(1)}, bf16[256,128]{1,0:T(8,128)(2,1)S(1)}, u32[]{:S(2)}, u32[]{:S(2)}) collective-permute-start(bf16[256,128]{1,0:T(8,128)(2,1)S(1)} %get-tuple-element.77), channel_id=1, source_target_pairs={{1,0},{2,1},{3,2},{4,3},{5,4},{6,5},{7,6},{0,7},{9,8},{10,9},{11,1... | collective-permute-start | bytes 196616 | tf_op jit(solution)/shard_map/ppermute | solution.py:564
  23.6 1.6 %shard_map.143 = f32[512,128]{1,0:T(8,128)} custom-call(s32[1,1]{1,0:T(1,128)S(6)} %copy.26.count_ref, f32[4,128,128]{2,1,0:T(8,128)S(1)} %get-tuple-element.66.moved_ref, s32[3,128]{1,0:T(4,128)S(1)} %get-tuple-element.100.cols_ref, s32[3,128]{1,0:T(4,128)S(1)} %get-tuple-element.99.mask_ref, bf16[128,384]{1,0:T(8,128)(2,1)S(1)} %get-tuple-element.57.x_ref, ...), custom_call_target="tpu_custom_call" | custom-call | tf_op jit(solution)/shard_map/pallas_call | solution.py:27
  25.5 1.7 %collective-permute-start.8 = (bf16[128,1280]{1,0:T(8,128)(2,1)S(1)}, bf16[128,1280]{1,0:T(8,128)(2,1)S(1)}, u32[]{:S(2)}, u32[]{:S(2)}) collective-permute-start(bf16[128,1280]{1,0:T(8,128)(2,1)S(1)} %shard_map.144), channel_id=1, source_target_pairs={{0,16},{1,9},{2,18},{3,11},{4,20},{5,13},{6,22},{7,15},{8,24},{9,1... | collective-permute-start | bytes 983048 | tf_op jit(solution)/shard_map/ppermute | solution.py:508
  27.3 1.5 %shard_map.145 = f32[512,128]{1,0:T(8,128)} custom-call(f32[4,128,128]{2,1,0:T(8,128)S(1)} %get-tuple-element.80.field_ref, bf16[256,128]{1,0:T(8,128)(2,1)S(1)} %collective-permute-done.5.low_ref, bf16[256,128]{1,0:T(8,128)(2,1)S(1)} %collective-permute-done.6.high_ref, bf16[272,128]{1,0:T(8,128)(2,1)S(1)} %collective-permute-done.low_ref.low_mix_ref, ...), custom_call_target="tpu_custom_call" | custom-call | tf_op jit(solution)/shard_map/pallas_call | solution.py:27
  28.7 4.9 %collective-permute-done.7.refs_1_ = bf16[128,1280]{1,0:T(8,128)(2,1)S(1)} collective-permute-done((bf16[128,1280]{1,0:T(8,128)(2,1)S(1)}, bf16[128,1280]{1,0:T(8,128)(2,1)S(1)}, u32[]{:S(2)}, u32[]{:S(2)}) %collective-permute-start.7) | collective-permute-done | bytes 327712 | tf_op jit(solution)/shard_map/ppermute | solution.py:508
  33.7 1.0 %collective-permute-start.9 = (bf16[32,1280]{1,0:T(8,128)(2,1)S(1)}, bf16[32,1280]{1,0:T(8,128)(2,1)S(1)}, u32[]{:S(2)}, u32[]{:S(2)}) collective-permute-start(bf16[32,1280]{1,0:T(8,128)(2,1)S(1)} %get-tuple-element.88), channel_id=1, source_target_pairs={{0,6},{1,7},{2,4},{3,5},{4,2},{5,3},{6,0},{7,1},{8,14},{9,15},{10,... | collective-permute-start | bytes 245768 | tf_op jit(solution)/shard_map/ppermute | solution.py:497
  34.8 3.4 %collective-permute-start.11 = (bf16[32,1280]{1,0:T(8,128)(2,1)S(1)}, bf16[32,1280]{1,0:T(8,128)(2,1)S(1)}, u32[]{:S(2)}, u32[]{:S(2)}) collective-permute-start(bf16[32,1280]{1,0:T(8,128)(2,1)S(1)} %get-tuple-element.90), channel_id=1, source_target_pairs={{0,2},{1,3},{2,0},{3,1},{4,6},{5,7},{6,4},{7,5},{8,10},{9,11},{10,... | collective-permute-start | bytes 245768 | tf_op jit(solution)/shard_map/ppermute | solution.py:497
  38.2 2.8 %collective-permute-done.9.refs_1_ = bf16[32,1280]{1,0:T(8,128)(2,1)S(1)} collective-permute-done((bf16[32,1280]{1,0:T(8,128)(2,1)S(1)}, bf16[32,1280]{1,0:T(8,128)(2,1)S(1)}, u32[]{:S(2)}, u32[]{:S(2)}) %collective-permute-start.9) | collective-permute-done | bytes 81952 | tf_op jit(solution)/shard_map/ppermute | solution.py:497
  41.0 2.7 %collective-permute-done.10.refs_2_ = bf16[32,1280]{1,0:T(8,128)(2,1)S(1)} collective-permute-done((bf16[32,1280]{1,0:T(8,128)(2,1)S(1)}, bf16[32,1280]{1,0:T(8,128)(2,1)S(1)}, u32[]{:S(2)}, u32[]{:S(2)}) %collective-permute-start.10) | collective-permute-done | bytes 81952 | tf_op jit(solution)/shard_map/ppermute | solution.py:497
  43.8 1.6 %collective-permute-start.14 = (bf16[32,1280]{1,0:T(8,128)(2,1)S(1)}, bf16[32,1280]{1,0:T(8,128)(2,1)S(1)}, u32[]{:S(2)}, u32[]{:S(2)}) collective-permute-start(bf16[32,1280]{1,0:T(8,128)(2,1)S(1)} %shard_map.147.refs_0_), channel_id=1, source_target_pairs={{0,6},{1,7},{2,4},{3,5},{4,2},{5,3},{6,0},{7,1},{8,14},{9,15},{10,... | collective-permute-start | bytes 245768 | tf_op jit(solution)/shard_map/ppermute | solution.py:497
  45.4 2.8 %collective-permute-start.12 = (bf16[32,1280]{1,0:T(8,128)(2,1)S(1)}, bf16[32,1280]{1,0:T(8,128)(2,1)S(1)}, u32[]{:S(2)}, u32[]{:S(2)}) collective-permute-start(bf16[32,1280]{1,0:T(8,128)(2,1)S(1)} %shard_map.147.refs_0_), channel_id=1, source_target_pairs={{0,2},{1,3},{2,0},{3,1},{4,6},{5,7},{6,4},{7,5},{8,10},{9,11},{10,... | collective-permute-start | bytes 245768 | tf_op jit(solution)/shard_map/ppermute | solution.py:497
  48.2 2.8 %collective-permute-done.14.refs_3_ = bf16[32,1280]{1,0:T(8,128)(2,1)S(1)} collective-permute-done((bf16[32,1280]{1,0:T(8,128)(2,1)S(1)}, bf16[32,1280]{1,0:T(8,128)(2,1)S(1)}, u32[]{:S(2)}, u32[]{:S(2)}) %collective-permute-start.14) | collective-permute-done | bytes 81952 | tf_op jit(solution)/shard_map/ppermute | solution.py:497
  51.0 2.5 %collective-permute-done.13.refs_2_ = bf16[32,1280]{1,0:T(8,128)(2,1)S(1)} collective-permute-done((bf16[32,1280]{1,0:T(8,128)(2,1)S(1)}, bf16[32,1280]{1,0:T(8,128)(2,1)S(1)}, u32[]{:S(2)}, u32[]{:S(2)}) %collective-permute-start.13) | collective-permute-done | bytes 81952 | tf_op jit(solution)/shard_map/ppermute | solution.py:497
  54.0 1.7 %collective-permute-start.19 = (bf16[128,640]{1,0:T(8,128)(2,1)S(1)}, bf16[128,640]{1,0:T(8,128)(2,1)S(1)}, u32[]{:S(2)}, u32[]{:S(2)}) collective-permute-start(bf16[128,640]{1,0:T(8,128)(2,1)S(1)} %get-tuple-element.92.refs_4_), channel_id=1, source_target_pairs={{0,16},{8,24},{16,0},{24,8},{1,17},{9,25},{17,1},{25,9},{2,18},{10... | collective-permute-start | bytes 491528 | tf_op jit(solution)/shard_map/ppermute | solution.py:497
  56.0 1.7 %collective-permute-start.18 = (bf16[128,640]{1,0:T(8,128)(2,1)S(1)}, bf16[128,640]{1,0:T(8,128)(2,1)S(1)}, u32[]{:S(2)}, u32[]{:S(2)}) collective-permute-start(bf16[128,640]{1,0:T(8,128)(2,1)S(1)} %get-tuple-element.92.refs_4_), channel_id=1, source_target_pairs={{0,8},{8,0},{16,24},{24,16},{1,9},{9,1},{17,25},{25,17},{2,10},{10... | collective-permute-start | bytes 491528 | tf_op jit(solution)/shard_map/ppermute | solution.py:497
  57.7 3.0 %collective-permute-done.15.refs_1_ = bf16[128,640]{1,0:T(8,128)(2,1)S(1)} collective-permute-done((bf16[128,640]{1,0:T(8,128)(2,1)S(1)}, bf16[128,640]{1,0:T(8,128)(2,1)S(1)}, u32[]{:S(2)}, u32[]{:S(2)}) %collective-permute-start.15) | collective-permute-done | bytes 163872 | tf_op jit(solution)/shard_map/ppermute | solution.py:497
  60.7 1.5 %collective-permute-start.17 = (bf16[128,640]{1,0:T(8,128)(2,1)S(1)}, bf16[128,640]{1,0:T(8,128)(2,1)S(1)}, u32[]{:S(2)}, u32[]{:S(2)}) collective-permute-start(bf16[128,640]{1,0:T(8,128)(2,1)S(1)} %collective-permute-done.15.refs_1_), channel_id=1, source_target_pairs={{0,16},{8,24},{16,0},{24,8},{1,17},{9,25},{17,1},{25,9},{2,18},{10... | collective-permute-start | bytes 491528 | tf_op jit(solution)/shard_map/ppermute | solution.py:497
  62.2 0.6 collective-permute-start.20
  62.8 1.8 %collective-permute-done.16.refs_2_ = bf16[128,640]{1,0:T(8,128)(2,1)S(1)} collective-permute-done((bf16[128,640]{1,0:T(8,128)(2,1)S(1)}, bf16[128,640]{1,0:T(8,128)(2,1)S(1)}, u32[]{:S(2)}, u32[]{:S(2)}) %collective-permute-start.16) | collective-permute-done | bytes 163872 | tf_op jit(solution)/shard_map/ppermute | solution.py:497
  64.6 2.3 %collective-permute-done.17.refs_3_ = bf16[128,640]{1,0:T(8,128)(2,1)S(1)} collective-permute-done((bf16[128,640]{1,0:T(8,128)(2,1)S(1)}, bf16[128,640]{1,0:T(8,128)(2,1)S(1)}, u32[]{:S(2)}, u32[]{:S(2)}) %collective-permute-start.17) | collective-permute-done | bytes 163872 | tf_op jit(solution)/shard_map/ppermute | solution.py:497
  66.9 0.6 collective-permute-done.20.refs_7_
  67.8 2.2 %shard_map.150 = (f32[1024,1024]{1,0:T(8,128)}, f32[1024,128]{1,0:T(8,128)}, f32[128,1024]{1,0:T(8,128)}) custom-call(bf16[512,1280]{1,0:T(8,128)(2,1)S(1)} %shard_map.149.mid_half.small_half, bf16[512,1280]{1,0:T(8,128)(2,1)S(1)} %shard_map.149.mid_half.small_half), custom_call_target="tpu_custom_call" | custom-call | tf_op jit(solution)/shard_map/pallas_call | solution.py:469
  70.0 0.8 %collective-permute-done.21.mid_half.small_half = bf16[512,1280]{1,0:T(8,128)(2,1)S(1)} collective-permute-done((bf16[512,1280]{1,0:T(8,128)(2,1)S(1)}, bf16[512,1280]{1,0:T(8,128)(2,1)S(1)}, u32[]{:S(2)}, u32[]{:S(2)}) %collective-permute-start.21) | collective-permute-done | bytes 1310752 | tf_op jit(solution)/shard_map/ppermute | solution.py:497
  70.8 2.2 %shard_map.151 = (f32[1024,1024]{1,0:T(8,128)}, f32[1024,128]{1,0:T(8,128)}, f32[128,1024]{1,0:T(8,128)}) custom-call(bf16[512,1280]{1,0:T(8,128)(2,1)S(1)} %collective-permute-done.21.mid_half.small_half, bf16[512,1280]{1,0:T(8,128)(2,1)S(1)} %collective-permute-done.21.mid_half.small_half, ...), custom_call_target="tpu_custom_call", output_to_operand_aliasing={{0}: (2, {}), {1}: (3, {}), {2}: (4, {})} | custom-call | tf_op jit(solution)/shard_map/pallas_call | solution.py:469
  (44 shorter events, 3.9 us)
Async XLA Ops:
  1.7 7.2 %copy-start.4 = (s32[1,1,3,128]{3,1,2,0:T(1,128)S(1)}, s32[1,1,3,128]{3,1,2,0:T(1,128)}, u32[]{:S(2)}) copy-start(s32[1,1,3,128]{3,1,2,0:T(1,128)} %param.15) | copy-start | bytes 4612
  1.7 7.2 %copy-start.5 = (s32[1,1,3,128]{3,1,2,0:T(1,128)S(1)}, s32[1,1,3,128]{3,1,2,0:T(1,128)}, u32[]{:S(2)}) copy-start(s32[1,1,3,128]{3,1,2,0:T(1,128)} %param.14) | copy-start | bytes 4612
  1.7 7.2 %copy-start.1 = (f32[1,128,4,128]{3,2,1,0:T(4,128)S(1)}, f32[1,128,4,128]{3,2,1,0:T(4,128)}, u32[]{:S(2)}) copy-start(f32[1,128,4,128]{3,2,1,0:T(4,128)} %param.13) | copy-start | bytes 786436
  1.7 7.2 %copy-start.3 = (f32[1,32,4,128]{3,2,1,0:T(4,128)S(1)}, f32[1,32,4,128]{3,2,1,0:T(4,128)}, u32[]{:S(2)}) copy-start(f32[1,32,4,128]{3,2,1,0:T(4,128)} %param.11) | copy-start | bytes 196612
  1.7 8.1 %collective-permute-start = (bf16[272,128]{1,0:T(8,128)(2,1)S(1)}, bf16[272,128]{1,0:T(8,128)(2,1)S(1)}, u32[]{:S(2)}, u32[]{:S(2)}) collective-permute-start(bf16[272,128]{1,0:T(8,128)(2,1)S(1)} %get-tuple-element.52), channel_id=1, source_target_pairs={{0,1},{1,2},{2,3},{3,4},{4,5},{5,6},{6,7},{7,0},{8,9},{9,10},{10,1... | collective-permute-start | bytes 208904 | tf_op jit(solution)/shard_map/ppermute | solution.py:564
  2.2 7.6 %collective-permute-start.1 = (bf16[272,128]{1,0:T(8,128)(2,1)S(1)}, bf16[272,128]{1,0:T(8,128)(2,1)S(1)}, u32[]{:S(2)}, u32[]{:S(2)}) collective-permute-start(bf16[272,128]{1,0:T(8,128)(2,1)S(1)} %get-tuple-element.53), channel_id=1, source_target_pairs={{1,0},{2,1},{3,2},{4,3},{5,4},{6,5},{7,6},{0,7},{9,8},{10,9},{11,1... | collective-permute-start | bytes 208904 | tf_op jit(solution)/shard_map/ppermute | solution.py:564
  7.0 2.7 %copy-start.2 = (bf16[1024,128]{1,0:T(8,128)(2,1)S(1)}, bf16[1024,128]{1,0:T(8,128)(2,1)}, u32[]{:S(2)}) copy-start(bf16[1024,128]{1,0:T(8,128)(2,1)} %param.17) | copy-start | bytes 786436
  7.0 2.8 %copy-start = (bf16[128,1024]{1,0:T(8,128)(2,1)S(1)}, bf16[128,1024]{1,0:T(8,128)(2,1)}, u32[]{:S(2)}) copy-start(bf16[128,1024]{1,0:T(8,128)(2,1)} %w_out_ref.3) | copy-start | bytes 786436
  13.8 3.8 %collective-permute-start.2 = (bf16[512,1024]{1,0:T(8,128)(2,1)S(1)}, bf16[512,1024]{1,0:T(8,128)(2,1)S(1)}, u32[]{:S(2)}, u32[]{:S(2)}) collective-permute-start(bf16[512,1024]{1,0:T(8,128)(2,1)S(1)} %get-tuple-element.56), channel_id=1, source_target_pairs={{0,1},{1,0},{2,3},{3,2},{4,5},{5,4},{6,7},{7,6},{8,9},{9,8},{10,11... | collective-permute-start | bytes 3145736 | tf_op jit(solution)/shard_map/ppermute | solution.py:497
  15.9 1.7 %collective-permute-start.3 = (bf16[512,256]{1,0:T(8,128)(2,1)S(1)}, bf16[512,256]{1,0:T(8,128)(2,1)S(1)}, u32[]{:S(2)}, u32[]{:S(2)}) collective-permute-start(bf16[512,256]{1,0:T(8,128)(2,1)S(1)} %get-tuple-element.61), channel_id=1, source_target_pairs={{0,1},{1,0},{2,3},{3,2},{4,5},{5,4},{6,7},{7,6},{8,9},{9,8},{10,11... | collective-permute-start | bytes 786440 | tf_op jit(solution)/shard_map/ppermute | solution.py:497
  17.9 7.5 %collective-permute-start.4 = (bf16[128,1280]{1,0:T(8,128)(2,1)S(1)}, bf16[128,1280]{1,0:T(8,128)(2,1)S(1)}, u32[]{:S(2)}, u32[]{:S(2)}) collective-permute-start(bf16[128,1280]{1,0:T(8,128)(2,1)S(1)} %get-tuple-element.65), channel_id=1, source_target_pairs={{0,8},{1,17},{2,10},{3,19},{4,12},{5,21},{6,14},{7,23},{8,0},{9,25... | collective-permute-start | bytes 983048 | tf_op jit(solution)/shard_map/ppermute | solution.py:508
  19.9 5.5 %collective-permute-start.5 = (bf16[256,128]{1,0:T(8,128)(2,1)S(1)}, bf16[256,128]{1,0:T(8,128)(2,1)S(1)}, u32[]{:S(2)}, u32[]{:S(2)}) collective-permute-start(bf16[256,128]{1,0:T(8,128)(2,1)S(1)} %get-tuple-element.76), channel_id=1, source_target_pairs={{0,1},{1,2},{2,3},{3,4},{4,5},{5,6},{6,7},{7,0},{8,9},{9,10},{10,1... | collective-permute-start | bytes 196616 | tf_op jit(solution)/shard_map/ppermute | solution.py:564
  20.0 5.4 %collective-permute-start.6 = (bf16[256,128]{1,0:T(8,128)(2,1)S(1)}, bf16[256,128]{1,0:T(8,128)(2,1)S(1)}, u32[]{:S(2)}, u32[]{:S(2)}) collective-permute-start(bf16[256,128]{1,0:T(8,128)(2,1)S(1)} %get-tuple-element.77), channel_id=1, source_target_pairs={{1,0},{2,1},{3,2},{4,3},{5,4},{6,5},{7,6},{0,7},{9,8},{10,9},{11,1... | collective-permute-start | bytes 196616 | tf_op jit(solution)/shard_map/ppermute | solution.py:564
  23.5 10.1 %collective-permute-start.7 = (bf16[128,1280]{1,0:T(8,128)(2,1)S(1)}, bf16[128,1280]{1,0:T(8,128)(2,1)S(1)}, u32[]{:S(2)}, u32[]{:S(2)}) collective-permute-start(bf16[128,1280]{1,0:T(8,128)(2,1)S(1)} %get-tuple-element.70), channel_id=1, source_target_pairs={{0,8},{1,17},{2,10},{3,19},{4,12},{5,21},{6,14},{7,23},{8,0},{9,25... | collective-permute-start | bytes 983048 | tf_op jit(solution)/shard_map/ppermute | solution.py:508
  25.5 8.1 %collective-permute-start.8 = (bf16[128,1280]{1,0:T(8,128)(2,1)S(1)}, bf16[128,1280]{1,0:T(8,128)(2,1)S(1)}, u32[]{:S(2)}, u32[]{:S(2)}) collective-permute-start(bf16[128,1280]{1,0:T(8,128)(2,1)S(1)} %shard_map.144), channel_id=1, source_target_pairs={{0,16},{1,9},{2,18},{3,11},{4,20},{5,13},{6,22},{7,15},{8,24},{9,1... | collective-permute-start | bytes 983048 | tf_op jit(solution)/shard_map/ppermute | solution.py:508
  33.7 7.2 %collective-permute-start.9 = (bf16[32,1280]{1,0:T(8,128)(2,1)S(1)}, bf16[32,1280]{1,0:T(8,128)(2,1)S(1)}, u32[]{:S(2)}, u32[]{:S(2)}) collective-permute-start(bf16[32,1280]{1,0:T(8,128)(2,1)S(1)} %get-tuple-element.88), channel_id=1, source_target_pairs={{0,6},{1,7},{2,4},{3,5},{4,2},{5,3},{6,0},{7,1},{8,14},{9,15},{10,... | collective-permute-start | bytes 245768 | tf_op jit(solution)/shard_map/ppermute | solution.py:497
  34.8 8.9 %collective-permute-start.10 = (bf16[32,1280]{1,0:T(8,128)(2,1)S(1)}, bf16[32,1280]{1,0:T(8,128)(2,1)S(1)}, u32[]{:S(2)}, u32[]{:S(2)}) collective-permute-start(bf16[32,1280]{1,0:T(8,128)(2,1)S(1)} %get-tuple-element.89), channel_id=1, source_target_pairs={{0,4},{1,5},{2,6},{3,7},{4,0},{5,1},{6,2},{7,3},{8,12},{9,13},{10,... | collective-permute-start | bytes 245768 | tf_op jit(solution)/shard_map/ppermute | solution.py:497
  34.8 8.9 %collective-permute-start.11 = (bf16[32,1280]{1,0:T(8,128)(2,1)S(1)}, bf16[32,1280]{1,0:T(8,128)(2,1)S(1)}, u32[]{:S(2)}, u32[]{:S(2)}) collective-permute-start(bf16[32,1280]{1,0:T(8,128)(2,1)S(1)} %get-tuple-element.90), channel_id=1, source_target_pairs={{0,2},{1,3},{2,0},{3,1},{4,6},{5,7},{6,4},{7,5},{8,10},{9,11},{10,... | collective-permute-start | bytes 245768 | tf_op jit(solution)/shard_map/ppermute | solution.py:497
  43.8 7.3 %collective-permute-start.14 = (bf16[32,1280]{1,0:T(8,128)(2,1)S(1)}, bf16[32,1280]{1,0:T(8,128)(2,1)S(1)}, u32[]{:S(2)}, u32[]{:S(2)}) collective-permute-start(bf16[32,1280]{1,0:T(8,128)(2,1)S(1)} %shard_map.147.refs_0_), channel_id=1, source_target_pairs={{0,6},{1,7},{2,4},{3,5},{4,2},{5,3},{6,0},{7,1},{8,14},{9,15},{10,... | collective-permute-start | bytes 245768 | tf_op jit(solution)/shard_map/ppermute | solution.py:497
  45.4 8.2 %collective-permute-start.13 = (bf16[32,1280]{1,0:T(8,128)(2,1)S(1)}, bf16[32,1280]{1,0:T(8,128)(2,1)S(1)}, u32[]{:S(2)}, u32[]{:S(2)}) collective-permute-start(bf16[32,1280]{1,0:T(8,128)(2,1)S(1)} %shard_map.147.refs_0_), channel_id=1, source_target_pairs={{0,4},{1,5},{2,6},{3,7},{4,0},{5,1},{6,2},{7,3},{8,12},{9,13},{10,... | collective-permute-start | bytes 245768 | tf_op jit(solution)/shard_map/ppermute | solution.py:497
  45.4 8.2 %collective-permute-start.12 = (bf16[32,1280]{1,0:T(8,128)(2,1)S(1)}, bf16[32,1280]{1,0:T(8,128)(2,1)S(1)}, u32[]{:S(2)}, u32[]{:S(2)}) collective-permute-start(bf16[32,1280]{1,0:T(8,128)(2,1)S(1)} %shard_map.147.refs_0_), channel_id=1, source_target_pairs={{0,2},{1,3},{2,0},{3,1},{4,6},{5,7},{6,4},{7,5},{8,10},{9,11},{10,... | collective-permute-start | bytes 245768 | tf_op jit(solution)/shard_map/ppermute | solution.py:497
  53.6 7.1 %collective-permute-start.15 = (bf16[128,640]{1,0:T(8,128)(2,1)S(1)}, bf16[128,640]{1,0:T(8,128)(2,1)S(1)}, u32[]{:S(2)}, u32[]{:S(2)}) collective-permute-start(bf16[128,640]{1,0:T(8,128)(2,1)S(1)} %get-tuple-element.91.refs_0_), channel_id=1, source_target_pairs={{0,8},{8,0},{16,24},{24,16},{1,9},{9,1},{17,25},{25,17},{2,10},{10... | collective-permute-start | bytes 491528 | tf_op jit(solution)/shard_map/ppermute | solution.py:497
  54.0 8.2 %collective-permute-start.19 = (bf16[128,640]{1,0:T(8,128)(2,1)S(1)}, bf16[128,640]{1,0:T(8,128)(2,1)S(1)}, u32[]{:S(2)}, u32[]{:S(2)}) collective-permute-start(bf16[128,640]{1,0:T(8,128)(2,1)S(1)} %get-tuple-element.92.refs_4_), channel_id=1, source_target_pairs={{0,16},{8,24},{16,0},{24,8},{1,17},{9,25},{17,1},{25,9},{2,18},{10... | collective-permute-start | bytes 491528 | tf_op jit(solution)/shard_map/ppermute | solution.py:497
  55.7 8.9 %collective-permute-start.16 = (bf16[128,640]{1,0:T(8,128)(2,1)S(1)}, bf16[128,640]{1,0:T(8,128)(2,1)S(1)}, u32[]{:S(2)}, u32[]{:S(2)}) collective-permute-start(bf16[128,640]{1,0:T(8,128)(2,1)S(1)} %get-tuple-element.91.refs_0_), channel_id=1, source_target_pairs={{0,16},{8,24},{16,0},{24,8},{1,17},{9,25},{17,1},{25,9},{2,18},{10... | collective-permute-start | bytes 491528 | tf_op jit(solution)/shard_map/ppermute | solution.py:497
  56.0 8.6 %collective-permute-start.18 = (bf16[128,640]{1,0:T(8,128)(2,1)S(1)}, bf16[128,640]{1,0:T(8,128)(2,1)S(1)}, u32[]{:S(2)}, u32[]{:S(2)}) collective-permute-start(bf16[128,640]{1,0:T(8,128)(2,1)S(1)} %get-tuple-element.92.refs_4_), channel_id=1, source_target_pairs={{0,8},{8,0},{16,24},{24,16},{1,9},{9,1},{17,25},{25,17},{2,10},{10... | collective-permute-start | bytes 491528 | tf_op jit(solution)/shard_map/ppermute | solution.py:497
  60.7 6.2 %collective-permute-start.17 = (bf16[128,640]{1,0:T(8,128)(2,1)S(1)}, bf16[128,640]{1,0:T(8,128)(2,1)S(1)}, u32[]{:S(2)}, u32[]{:S(2)}) collective-permute-start(bf16[128,640]{1,0:T(8,128)(2,1)S(1)} %collective-permute-done.15.refs_1_), channel_id=1, source_target_pairs={{0,16},{8,24},{16,0},{24,8},{1,17},{9,25},{17,1},{25,9},{2,18},{10... | collective-permute-start | bytes 491528 | tf_op jit(solution)/shard_map/ppermute | solution.py:497
  62.2 5.3 %collective-permute-start.20 = (bf16[128,640]{1,0:T(8,128)(2,1)S(1)}, bf16[128,640]{1,0:T(8,128)(2,1)S(1)}, u32[]{:S(2)}, u32[]{:S(2)}) collective-permute-start(bf16[128,640]{1,0:T(8,128)(2,1)S(1)} %collective-permute-done.19.refs_6_), channel_id=1, source_target_pairs={{0,8},{8,0},{16,24},{24,16},{1,9},{9,1},{17,25},{25,17},{2,10},{10... | collective-permute-start | bytes 491528 | tf_op jit(solution)/shard_map/ppermute | solution.py:497
  67.7 3.1 %collective-permute-start.21 = (bf16[512,1280]{1,0:T(8,128)(2,1)S(1)}, bf16[512,1280]{1,0:T(8,128)(2,1)S(1)}, u32[]{:S(2)}, u32[]{:S(2)}) collective-permute-start(bf16[512,1280]{1,0:T(8,128)(2,1)S(1)} %shard_map.149.mid_half.small_half), channel_id=1, source_target_pairs={{0,1},{1,0},{2,3},{3,2},{4,5},{5,4},{6,7},{7,6},{8,9},{9,8},{10,11... | collective-permute-start | bytes 3932168 | tf_op jit(solution)/shard_map/ppermute | solution.py:497

commit v13 on v12

--- a/solution.py
+++ b/solution.py
@@ -9,7 +9,8 @@
 from jax.sharding import PartitionSpec as P
 
 DYN_STEPS = 2
-BLOCK = 256
+BLOCK = 512
+COLUMN_BLOCK = 256
 PACK_ROWS = 16
 VMEM_LIMIT = 32 * 1024 * 1024
 F32 = jnp.float32
@@ -204,16 +205,17 @@
 
 def weight_product(left_ref, right, keep_ref, send_ref, first):
     half = left_ref.shape[0] // 2
-    block = min(BLOCK, half)
     core = lax.axis_index("horiz") % 2
-    for out_ref, side in ((send_ref, 1 - core), (keep_ref, core)):
-        for start in range(0, half, block):
-            out_ref[start : start + block, first : first + right.shape[0]] = lax.dot_general(
-                left_ref[pl.ds(pl.multiple_of(side * half + start, block), block), :],
-                right,
-                CONTRACT_LAST,
-                preferred_element_type=F32,
-            ).astype(BF16)
+    sides = [left_ref[pl.ds(pl.multiple_of(side * half, half), half), :] for side in (1 - core, core)]
+    left = jnp.concatenate(sides, axis=0)
+    block = min(COLUMN_BLOCK, right.shape[0])
+    for start in range(0, right.shape[0], block):
+        product = lax.dot_general(
+            left, right[start : start + block, :], CONTRACT_LAST, preferred_element_type=F32
+        ).astype(BF16)
+        here = slice(first + start, first + start + block)
+        send_ref[:, here] = product[:half]
+        keep_ref[:, here] = product[half:]
 
 
 def forward_kernel(
@@ -460,7 +462,7 @@
 def final(rows, other, before, fields):
     half, columns = rows.shape
     units = 2 * half
-    block = units // 4
+    block = units // 2
 
     def place():
         core = lax.axis_index("horiz") % 2

time: 73.2 us -> 73.1 us (level)
    pallas_call x2, Pallas kernels: 4.47 us -> 3.64 us  [final(): pl.pallas_call(final_kernel, grid=(units // block,), out_shape=[jax.Shape...]
where the time goes in v13:
time: 73.1 us; the launch traced here: 72.9 us
  starting transfers between devices  27.7 us (38%)
  waiting for transfers between devices  25.6 us (35%)
  Pallas kernels  15.1 us (21%)
  local copies, waits for them, and re-layouts  1.92 us (3%)
  between operations  1.51 us (2%)
  other arithmetic  1.1 us (2%)
    ppermute x15, waiting for transfers between devices, exchange(): sent[k] = lax.ppermute(arrays[k - 1], axis, route)  20.4 us
    ppermute x15, starting transfers between devices, exchange(): sent[k] = lax.ppermute(arrays[k - 1], axis, route)  15.7 us
    pallas_call x13, Pallas kernels, run(): pl.pallas_call(functools.partial(kernel, **names), out_shape=[jax.ShapeDt...  11.5 us
    ppermute x2, starting transfers between devices, to_neighbours(): lax.ppermute(downward, axis, backward)  7.52 us
    ppermute x3, waiting for transfers between devices, to_member(): return lax.ppermute(array, ('ens', 'horiz'), route)  4.86 us
    ppermute x3, starting transfers between devices, to_member(): return lax.ppermute(array, ('ens', 'horiz'), route)  3.82 us
    pallas_call x2, Pallas kernels, final(): pl.pallas_call(final_kernel, grid=(units // block,), out_shape=[jax.Shape...  3.64 us
    unnamed x14, local copies, waits for them, and re-layouts  1.86 us
  transfers between devices with their start and end apart: 22, of which 12 were waited for; matrix products, arithmetic and copies ran while one was open for 3% of the time, Pallas kernels for 12%

profile of v13, /device:TPU:0, one launch (start us, length us, event | category | flops | bytes accessed | tf_op | source)
XLA Modules:
  0.0 72.9 jit_solution(14947434049718803144)
XLA Ops:
  0.6 1.0 %pad_maximum_fusion.1 = f32[130,4,128]{2,1,0:T(4,128)S(1)} fusion(f32[2,4,128]{2,1,0:T(4,128)} %param.12, f32[128,4,128]{2,1,0:T(4,128)} %bitcast.16), kind=kLoop, calls=%fused_computation.1 | loop fusion | flops 66560 | bytes 532480 | tf_op jit(solution)/shard_map/concatenate | solution.py:577
  2.2 4.1 %collective-permute-start.1 = (bf16[272,128]{1,0:T(8,128)(2,1)S(1)}, bf16[272,128]{1,0:T(8,128)(2,1)S(1)}, u32[]{:S(2)}, u32[]{:S(2)}) collective-permute-start(bf16[272,128]{1,0:T(8,128)(2,1)S(1)} %get-tuple-element.53), channel_id=1, source_target_pairs={{1,0},{2,1},{3,2},{4,3},{5,4},{6,5},{7,6},{0,7},{9,8},{10,9},{11,1... | collective-permute-start | bytes 208904 | tf_op jit(solution)/shard_map/ppermute | solution.py:566
  7.0 1.8 %constant_dynamic-update-slice_fusion.1 = bf16[1024,1152]{1,0:T(8,128)(2,1)S(1)} fusion(bf16[1024,1024]{1,0:T(8,128)(2,1)} %param.18), kind=kLoop, calls=%fused_computation.3 | loop fusion | bytes 4194304
  9.0 0.8 %shard_map.138 = (f32[3,128,128]{2,1,0:T(8,128)S(1)}, f32[32,384]{1,0:T(8,128)S(1)}, f32[32,384]{1,0:T(8,128)S(1)}, f32[32,384]{1,0:T(8,128)S(1)}) custom-call(s32[1,1]{1,0:T(1,128)S(6)} %copy.26.count_ref, f32[640,128]{1,0:T(8,128)S(1)} %bitcast.14, s32[3,128]{1,0:T(4,128)S(1)} %get-tuple-element.100.cols_ref, s32[3,128]{1,0:T(4,128)S(1)} %get-tuple-element.99.mask_ref), custom_call_target="tpu_custom_call" | custom-call | bytes 30000000 | tf_op jit(solution)/shard_map/pallas_call | solution.py:28
  9.9 4.2 %shard_map.139 = (f32[4,128,128]{2,1,0:T(8,128)S(1)}, bf16[128,384]{1,0:T(8,128)(2,1)S(1)}, bf16[1024,384]{1,0:T(8,128)(2,1)}, bf16[1024,384]{1,0:T(8,128)(2,1)S...) custom-call(f32[520,128]{1,0:T(8,128)S(1)} %bitcast.12, ...), custom_call_target="tpu_custom_call" | custom-call | bytes 15000000 | tf_op jit(solution)/shard_map/pallas_call | solution.py:28
  14.0 2.2 %shard_map.140 = (bf16[1024,384]{1,0:T(8,128)(2,1)S(1)}, bf16[512,256]{1,0:T(8,128)(2,1)S(1)}, bf16[512,256]{1,0:T(8,128)(2,1)S(1)}) custom-call(bf16[128,384]{1,0:T(8,128)(2,1)S(1)} %get-tuple-element.57.x_ref, bf16[1024,384]{1,0:T(8,128)(2,1)S(1)} %get-tuple-element.72.act_two_ref, bf16[1024,384]{1,0:T(8,128)(2,1)S(1)} %get-tuple-element.59.delta_two_ref, ...), custom_call_target="tpu_custom_call" | custom-call | bytes 4000000 | tf_op jit(solution)/shard_map/pallas_call | solution.py:28
  17.4 0.6 collective-permute-done.3.got_small
  18.3 2.0 %collective-permute-start.4 = (bf16[128,1280]{1,0:T(8,128)(2,1)S(1)}, bf16[128,1280]{1,0:T(8,128)(2,1)S(1)}, u32[]{:S(2)}, u32[]{:S(2)}) collective-permute-start(bf16[128,1280]{1,0:T(8,128)(2,1)S(1)} %get-tuple-element.65), channel_id=1, source_target_pairs={{0,8},{1,17},{2,10},{3,19},{4,12},{5,21},{6,14},{7,23},{8,0},{9,25... | collective-permute-start | bytes 983048 | tf_op jit(solution)/shard_map/ppermute | solution.py:510
  20.4 3.4 %collective-permute-start.6 = (bf16[256,128]{1,0:T(8,128)(2,1)S(1)}, bf16[256,128]{1,0:T(8,128)(2,1)S(1)}, u32[]{:S(2)}, u32[]{:S(2)}) collective-permute-start(bf16[256,128]{1,0:T(8,128)(2,1)S(1)} %get-tuple-element.77), channel_id=1, source_target_pairs={{1,0},{2,1},{3,2},{4,3},{5,4},{6,5},{7,6},{0,7},{9,8},{10,9},{11,1... | collective-permute-start | bytes 196616 | tf_op jit(solution)/shard_map/ppermute | solution.py:566
  23.9 1.6 %shard_map.143 = f32[512,128]{1,0:T(8,128)} custom-call(s32[1,1]{1,0:T(1,128)S(6)} %copy.26.count_ref, f32[4,128,128]{2,1,0:T(8,128)S(1)} %get-tuple-element.66.moved_ref, s32[3,128]{1,0:T(4,128)S(1)} %get-tuple-element.100.cols_ref, s32[3,128]{1,0:T(4,128)S(1)} %get-tuple-element.99.mask_ref, bf16[128,384]{1,0:T(8,128)(2,1)S(1)} %get-tuple-element.57.x_ref, ...), custom_call_target="tpu_custom_call" | custom-call | tf_op jit(solution)/shard_map/pallas_call | solution.py:28
  25.9 1.7 %collective-permute-start.8 = (bf16[128,1280]{1,0:T(8,128)(2,1)S(1)}, bf16[128,1280]{1,0:T(8,128)(2,1)S(1)}, u32[]{:S(2)}, u32[]{:S(2)}) collective-permute-start(bf16[128,1280]{1,0:T(8,128)(2,1)S(1)} %shard_map.144), channel_id=1, source_target_pairs={{0,16},{1,9},{2,18},{3,11},{4,20},{5,13},{6,22},{7,15},{8,24},{9,1... | collective-permute-start | bytes 983048 | tf_op jit(solution)/shard_map/ppermute | solution.py:510
  27.6 1.5 %shard_map.145 = f32[512,128]{1,0:T(8,128)} custom-call(f32[4,128,128]{2,1,0:T(8,128)S(1)} %get-tuple-element.80.field_ref, bf16[256,128]{1,0:T(8,128)(2,1)S(1)} %collective-permute-done.5.low_ref, bf16[256,128]{1,0:T(8,128)(2,1)S(1)} %collective-permute-done.6.high_ref, bf16[272,128]{1,0:T(8,128)(2,1)S(1)} %collective-permute-done.low_ref.low_mix_ref, ...), custom_call_target="tpu_custom_call" | custom-call | tf_op jit(solution)/shard_map/pallas_call | solution.py:28
  29.1 4.9 %collective-permute-done.7.refs_1_ = bf16[128,1280]{1,0:T(8,128)(2,1)S(1)} collective-permute-done((bf16[128,1280]{1,0:T(8,128)(2,1)S(1)}, bf16[128,1280]{1,0:T(8,128)(2,1)S(1)}, u32[]{:S(2)}, u32[]{:S(2)}) %collective-permute-start.7) | collective-permute-done | bytes 327712 | tf_op jit(solution)/shard_map/ppermute | solution.py:510
  34.1 1.0 %collective-permute-start.9 = (bf16[32,1280]{1,0:T(8,128)(2,1)S(1)}, bf16[32,1280]{1,0:T(8,128)(2,1)S(1)}, u32[]{:S(2)}, u32[]{:S(2)}) collective-permute-start(bf16[32,1280]{1,0:T(8,128)(2,1)S(1)} %get-tuple-element.88), channel_id=1, source_target_pairs={{0,6},{1,7},{2,4},{3,5},{4,2},{5,3},{6,0},{7,1},{8,14},{9,15},{10,... | collective-permute-start | bytes 245768 | tf_op jit(solution)/shard_map/ppermute | solution.py:499
  35.1 3.4 %collective-permute-start.11 = (bf16[32,1280]{1,0:T(8,128)(2,1)S(1)}, bf16[32,1280]{1,0:T(8,128)(2,1)S(1)}, u32[]{:S(2)}, u32[]{:S(2)}) collective-permute-start(bf16[32,1280]{1,0:T(8,128)(2,1)S(1)} %get-tuple-element.90), channel_id=1, source_target_pairs={{0,2},{1,3},{2,0},{3,1},{4,6},{5,7},{6,4},{7,5},{8,10},{9,11},{10,... | collective-permute-start | bytes 245768 | tf_op jit(solution)/shard_map/ppermute | solution.py:499
  38.5 2.8 %collective-permute-done.9.refs_1_ = bf16[32,1280]{1,0:T(8,128)(2,1)S(1)} collective-permute-done((bf16[32,1280]{1,0:T(8,128)(2,1)S(1)}, bf16[32,1280]{1,0:T(8,128)(2,1)S(1)}, u32[]{:S(2)}, u32[]{:S(2)}) %collective-permute-start.9) | collective-permute-done | bytes 81952 | tf_op jit(solution)/shard_map/ppermute | solution.py:499
  41.3 2.7 %collective-permute-done.10.refs_2_ = bf16[32,1280]{1,0:T(8,128)(2,1)S(1)} collective-permute-done((bf16[32,1280]{1,0:T(8,128)(2,1)S(1)}, bf16[32,1280]{1,0:T(8,128)(2,1)S(1)}, u32[]{:S(2)}, u32[]{:S(2)}) %collective-permute-start.10) | collective-permute-done | bytes 81952 | tf_op jit(solution)/shard_map/ppermute | solution.py:499
  44.1 1.6 %collective-permute-start.14 = (bf16[32,1280]{1,0:T(8,128)(2,1)S(1)}, bf16[32,1280]{1,0:T(8,128)(2,1)S(1)}, u32[]{:S(2)}, u32[]{:S(2)}) collective-permute-start(bf16[32,1280]{1,0:T(8,128)(2,1)S(1)} %shard_map.147.refs_0_), channel_id=1, source_target_pairs={{0,6},{1,7},{2,4},{3,5},{4,2},{5,3},{6,0},{7,1},{8,14},{9,15},{10,... | collective-permute-start | bytes 245768 | tf_op jit(solution)/shard_map/ppermute | solution.py:499
  45.7 2.8 %collective-permute-start.12 = (bf16[32,1280]{1,0:T(8,128)(2,1)S(1)}, bf16[32,1280]{1,0:T(8,128)(2,1)S(1)}, u32[]{:S(2)}, u32[]{:S(2)}) collective-permute-start(bf16[32,1280]{1,0:T(8,128)(2,1)S(1)} %shard_map.147.refs_0_), channel_id=1, source_target_pairs={{0,2},{1,3},{2,0},{3,1},{4,6},{5,7},{6,4},{7,5},{8,10},{9,11},{10,... | collective-permute-start | bytes 245768 | tf_op jit(solution)/shard_map/ppermute | solution.py:499
  48.6 2.8 %collective-permute-done.14.refs_3_ = bf16[32,1280]{1,0:T(8,128)(2,1)S(1)} collective-permute-done((bf16[32,1280]{1,0:T(8,128)(2,1)S(1)}, bf16[32,1280]{1,0:T(8,128)(2,1)S(1)}, u32[]{:S(2)}, u32[]{:S(2)}) %collective-permute-start.14) | collective-permute-done | bytes 81952 | tf_op jit(solution)/shard_map/ppermute | solution.py:499
  51.4 2.5 %collective-permute-done.13.refs_2_ = bf16[32,1280]{1,0:T(8,128)(2,1)S(1)} collective-permute-done((bf16[32,1280]{1,0:T(8,128)(2,1)S(1)}, bf16[32,1280]{1,0:T(8,128)(2,1)S(1)}, u32[]{:S(2)}, u32[]{:S(2)}) %collective-permute-start.13) | collective-permute-done | bytes 81952 | tf_op jit(solution)/shard_map/ppermute | solution.py:499
  54.4 1.7 %collective-permute-start.19 = (bf16[128,640]{1,0:T(8,128)(2,1)S(1)}, bf16[128,640]{1,0:T(8,128)(2,1)S(1)}, u32[]{:S(2)}, u32[]{:S(2)}) collective-permute-start(bf16[128,640]{1,0:T(8,128)(2,1)S(1)} %get-tuple-element.92.refs_4_), channel_id=1, source_target_pairs={{0,16},{8,24},{16,0},{24,8},{1,17},{9,25},{17,1},{25,9},{2,18},{10... | collective-permute-start | bytes 491528 | tf_op jit(solution)/shard_map/ppermute | solution.py:499
  56.4 1.7 %collective-permute-start.18 = (bf16[128,640]{1,0:T(8,128)(2,1)S(1)}, bf16[128,640]{1,0:T(8,128)(2,1)S(1)}, u32[]{:S(2)}, u32[]{:S(2)}) collective-permute-start(bf16[128,640]{1,0:T(8,128)(2,1)S(1)} %get-tuple-element.92.refs_4_), channel_id=1, source_target_pairs={{0,8},{8,0},{16,24},{24,16},{1,9},{9,1},{17,25},{25,17},{2,10},{10... | collective-permute-start | bytes 491528 | tf_op jit(solution)/shard_map/ppermute | solution.py:499
  58.1 3.0 %collective-permute-done.15.refs_1_ = bf16[128,640]{1,0:T(8,128)(2,1)S(1)} collective-permute-done((bf16[128,640]{1,0:T(8,128)(2,1)S(1)}, bf16[128,640]{1,0:T(8,128)(2,1)S(1)}, u32[]{:S(2)}, u32[]{:S(2)}) %collective-permute-start.15) | collective-permute-done | bytes 163872 | tf_op jit(solution)/shard_map/ppermute | solution.py:499
  61.1 1.5 %collective-permute-start.17 = (bf16[128,640]{1,0:T(8,128)(2,1)S(1)}, bf16[128,640]{1,0:T(8,128)(2,1)S(1)}, u32[]{:S(2)}, u32[]{:S(2)}) collective-permute-start(bf16[128,640]{1,0:T(8,128)(2,1)S(1)} %collective-permute-done.15.refs_1_), channel_id=1, source_target_pairs={{0,16},{8,24},{16,0},{24,8},{1,17},{9,25},{17,1},{25,9},{2,18},{10... | collective-permute-start | bytes 491528 | tf_op jit(solution)/shard_map/ppermute | solution.py:499
  62.6 0.6 collective-permute-start.20
  63.2 1.8 %collective-permute-done.16.refs_2_ = bf16[128,640]{1,0:T(8,128)(2,1)S(1)} collective-permute-done((bf16[128,640]{1,0:T(8,128)(2,1)S(1)}, bf16[128,640]{1,0:T(8,128)(2,1)S(1)}, u32[]{:S(2)}, u32[]{:S(2)}) %collective-permute-start.16) | collective-permute-done | bytes 163872 | tf_op jit(solution)/shard_map/ppermute | solution.py:499
  65.0 2.3 %collective-permute-done.17.refs_3_ = bf16[128,640]{1,0:T(8,128)(2,1)S(1)} collective-permute-done((bf16[128,640]{1,0:T(8,128)(2,1)S(1)}, bf16[128,640]{1,0:T(8,128)(2,1)S(1)}, u32[]{:S(2)}, u32[]{:S(2)}) %collective-permute-start.17) | collective-permute-done | bytes 163872 | tf_op jit(solution)/shard_map/ppermute | solution.py:499
  67.3 0.6 collective-permute-done.20.refs_7_
  68.1 1.8 %shard_map.150 = (f32[1024,1024]{1,0:T(8,128)}, f32[1024,128]{1,0:T(8,128)}, f32[128,1024]{1,0:T(8,128)}) custom-call(bf16[512,1280]{1,0:T(8,128)(2,1)S(1)} %shard_map.149.mid_half.small_half, bf16[512,1280]{1,0:T(8,128)(2,1)S(1)} %shard_map.149.mid_half.small_half), custom_call_target="tpu_custom_call" | custom-call | tf_op jit(solution)/shard_map/pallas_call | solution.py:471
  69.9 1.2 %collective-permute-done.21.mid_half.small_half = bf16[512,1280]{1,0:T(8,128)(2,1)S(1)} collective-permute-done((bf16[512,1280]{1,0:T(8,128)(2,1)S(1)}, bf16[512,1280]{1,0:T(8,128)(2,1)S(1)}, u32[]{:S(2)}, u32[]{:S(2)}) %collective-permute-start.21) | collective-permute-done | bytes 1310752 | tf_op jit(solution)/shard_map/ppermute | solution.py:499
  71.1 1.8 %shard_map.151 = (f32[1024,1024]{1,0:T(8,128)}, f32[1024,128]{1,0:T(8,128)}, f32[128,1024]{1,0:T(8,128)}) custom-call(bf16[512,1280]{1,0:T(8,128)(2,1)S(1)} %collective-permute-done.21.mid_half.small_half, bf16[512,1280]{1,0:T(8,128)(2,1)S(1)} %collective-permute-done.21.mid_half.small_half, ...), custom_call_target="tpu_custom_call", output_to_operand_aliasing={{0}: (2, {}), {1}: (3, {}), {2}: (4, {})} | custom-call | tf_op jit(solution)/shard_map/pallas_call | solution.py:471
  (44 shorter events, 3.9 us)
Async XLA Ops:
  1.7 7.2 %copy-start.4 = (s32[1,1,3,128]{3,1,2,0:T(1,128)S(1)}, s32[1,1,3,128]{3,1,2,0:T(1,128)}, u32[]{:S(2)}) copy-start(s32[1,1,3,128]{3,1,2,0:T(1,128)} %param.15) | copy-start | bytes 4612
  1.7 7.2 %copy-start.5 = (s32[1,1,3,128]{3,1,2,0:T(1,128)S(1)}, s32[1,1,3,128]{3,1,2,0:T(1,128)}, u32[]{:S(2)}) copy-start(s32[1,1,3,128]{3,1,2,0:T(1,128)} %param.14) | copy-start | bytes 4612
  1.7 7.2 %copy-start.1 = (f32[1,128,4,128]{3,2,1,0:T(4,128)S(1)}, f32[1,128,4,128]{3,2,1,0:T(4,128)}, u32[]{:S(2)}) copy-start(f32[1,128,4,128]{3,2,1,0:T(4,128)} %param.13) | copy-start | bytes 786436
  1.7 7.2 %copy-start.3 = (f32[1,32,4,128]{3,2,1,0:T(4,128)S(1)}, f32[1,32,4,128]{3,2,1,0:T(4,128)}, u32[]{:S(2)}) copy-start(f32[1,32,4,128]{3,2,1,0:T(4,128)} %param.11) | copy-start | bytes 196612
  1.7 8.1 %collective-permute-start = (bf16[272,128]{1,0:T(8,128)(2,1)S(1)}, bf16[272,128]{1,0:T(8,128)(2,1)S(1)}, u32[]{:S(2)}, u32[]{:S(2)}) collective-permute-start(bf16[272,128]{1,0:T(8,128)(2,1)S(1)} %get-tuple-element.52), channel_id=1, source_target_pairs={{0,1},{1,2},{2,3},{3,4},{4,5},{5,6},{6,7},{7,0},{8,9},{9,10},{10,1... | collective-permute-start | bytes 208904 | tf_op jit(solution)/shard_map/ppermute | solution.py:566
  2.2 7.6 %collective-permute-start.1 = (bf16[272,128]{1,0:T(8,128)(2,1)S(1)}, bf16[272,128]{1,0:T(8,128)(2,1)S(1)}, u32[]{:S(2)}, u32[]{:S(2)}) collective-permute-start(bf16[272,128]{1,0:T(8,128)(2,1)S(1)} %get-tuple-element.53), channel_id=1, source_target_pairs={{1,0},{2,1},{3,2},{4,3},{5,4},{6,5},{7,6},{0,7},{9,8},{10,9},{11,1... | collective-permute-start | bytes 208904 | tf_op jit(solution)/shard_map/ppermute | solution.py:566
  7.0 2.7 %copy-start.2 = (bf16[1024,128]{1,0:T(8,128)(2,1)S(1)}, bf16[1024,128]{1,0:T(8,128)(2,1)}, u32[]{:S(2)}) copy-start(bf16[1024,128]{1,0:T(8,128)(2,1)} %param.17) | copy-start | bytes 786436
  7.0 2.8 %copy-start = (bf16[128,1024]{1,0:T(8,128)(2,1)S(1)}, bf16[128,1024]{1,0:T(8,128)(2,1)}, u32[]{:S(2)}) copy-start(bf16[128,1024]{1,0:T(8,128)(2,1)} %w_out_ref.3) | copy-start | bytes 786436
  14.0 3.9 %collective-permute-start.2 = (bf16[512,1024]{1,0:T(8,128)(2,1)S(1)}, bf16[512,1024]{1,0:T(8,128)(2,1)S(1)}, u32[]{:S(2)}, u32[]{:S(2)}) collective-permute-start(bf16[512,1024]{1,0:T(8,128)(2,1)S(1)} %get-tuple-element.56), channel_id=1, source_target_pairs={{0,1},{1,0},{2,3},{3,2},{4,5},{5,4},{6,7},{7,6},{8,9},{9,8},{10,11... | collective-permute-start | bytes 3145736 | tf_op jit(solution)/shard_map/ppermute | solution.py:499
  16.2 1.7 %collective-permute-start.3 = (bf16[512,256]{1,0:T(8,128)(2,1)S(1)}, bf16[512,256]{1,0:T(8,128)(2,1)S(1)}, u32[]{:S(2)}, u32[]{:S(2)}) collective-permute-start(bf16[512,256]{1,0:T(8,128)(2,1)S(1)} %get-tuple-element.61), channel_id=1, source_target_pairs={{0,1},{1,0},{2,3},{3,2},{4,5},{5,4},{6,7},{7,6},{8,9},{9,8},{10,11... | collective-permute-start | bytes 786440 | tf_op jit(solution)/shard_map/ppermute | solution.py:499
  18.3 7.5 %collective-permute-start.4 = (bf16[128,1280]{1,0:T(8,128)(2,1)S(1)}, bf16[128,1280]{1,0:T(8,128)(2,1)S(1)}, u32[]{:S(2)}, u32[]{:S(2)}) collective-permute-start(bf16[128,1280]{1,0:T(8,128)(2,1)S(1)} %get-tuple-element.65), channel_id=1, source_target_pairs={{0,8},{1,17},{2,10},{3,19},{4,12},{5,21},{6,14},{7,23},{8,0},{9,25... | collective-permute-start | bytes 983048 | tf_op jit(solution)/shard_map/ppermute | solution.py:510
  20.3 5.5 %collective-permute-start.5 = (bf16[256,128]{1,0:T(8,128)(2,1)S(1)}, bf16[256,128]{1,0:T(8,128)(2,1)S(1)}, u32[]{:S(2)}, u32[]{:S(2)}) collective-permute-start(bf16[256,128]{1,0:T(8,128)(2,1)S(1)} %get-tuple-element.76), channel_id=1, source_target_pairs={{0,1},{1,2},{2,3},{3,4},{4,5},{5,6},{6,7},{7,0},{8,9},{9,10},{10,1... | collective-permute-start | bytes 196616 | tf_op jit(solution)/shard_map/ppermute | solution.py:566
  20.4 5.4 %collective-permute-start.6 = (bf16[256,128]{1,0:T(8,128)(2,1)S(1)}, bf16[256,128]{1,0:T(8,128)(2,1)S(1)}, u32[]{:S(2)}, u32[]{:S(2)}) collective-permute-start(bf16[256,128]{1,0:T(8,128)(2,1)S(1)} %get-tuple-element.77), channel_id=1, source_target_pairs={{1,0},{2,1},{3,2},{4,3},{5,4},{6,5},{7,6},{0,7},{9,8},{10,9},{11,1... | collective-permute-start | bytes 196616 | tf_op jit(solution)/shard_map/ppermute | solution.py:566
  23.8 10.1 %collective-permute-start.7 = (bf16[128,1280]{1,0:T(8,128)(2,1)S(1)}, bf16[128,1280]{1,0:T(8,128)(2,1)S(1)}, u32[]{:S(2)}, u32[]{:S(2)}) collective-permute-start(bf16[128,1280]{1,0:T(8,128)(2,1)S(1)} %get-tuple-element.70), channel_id=1, source_target_pairs={{0,8},{1,17},{2,10},{3,19},{4,12},{5,21},{6,14},{7,23},{8,0},{9,25... | collective-permute-start | bytes 983048 | tf_op jit(solution)/shard_map/ppermute | solution.py:510
  25.9 8.1 %collective-permute-start.8 = (bf16[128,1280]{1,0:T(8,128)(2,1)S(1)}, bf16[128,1280]{1,0:T(8,128)(2,1)S(1)}, u32[]{:S(2)}, u32[]{:S(2)}) collective-permute-start(bf16[128,1280]{1,0:T(8,128)(2,1)S(1)} %shard_map.144), channel_id=1, source_target_pairs={{0,16},{1,9},{2,18},{3,11},{4,20},{5,13},{6,22},{7,15},{8,24},{9,1... | collective-permute-start | bytes 983048 | tf_op jit(solution)/shard_map/ppermute | solution.py:510
  34.1 7.2 %collective-permute-start.9 = (bf16[32,1280]{1,0:T(8,128)(2,1)S(1)}, bf16[32,1280]{1,0:T(8,128)(2,1)S(1)}, u32[]{:S(2)}, u32[]{:S(2)}) collective-permute-start(bf16[32,1280]{1,0:T(8,128)(2,1)S(1)} %get-tuple-element.88), channel_id=1, source_target_pairs={{0,6},{1,7},{2,4},{3,5},{4,2},{5,3},{6,0},{7,1},{8,14},{9,15},{10,... | collective-permute-start | bytes 245768 | tf_op jit(solution)/shard_map/ppermute | solution.py:499
  35.1 8.9 %collective-permute-start.10 = (bf16[32,1280]{1,0:T(8,128)(2,1)S(1)}, bf16[32,1280]{1,0:T(8,128)(2,1)S(1)}, u32[]{:S(2)}, u32[]{:S(2)}) collective-permute-start(bf16[32,1280]{1,0:T(8,128)(2,1)S(1)} %get-tuple-element.89), channel_id=1, source_target_pairs={{0,4},{1,5},{2,6},{3,7},{4,0},{5,1},{6,2},{7,3},{8,12},{9,13},{10,... | collective-permute-start | bytes 245768 | tf_op jit(solution)/shard_map/ppermute | solution.py:499
  35.1 8.9 %collective-permute-start.11 = (bf16[32,1280]{1,0:T(8,128)(2,1)S(1)}, bf16[32,1280]{1,0:T(8,128)(2,1)S(1)}, u32[]{:S(2)}, u32[]{:S(2)}) collective-permute-start(bf16[32,1280]{1,0:T(8,128)(2,1)S(1)} %get-tuple-element.90), channel_id=1, source_target_pairs={{0,2},{1,3},{2,0},{3,1},{4,6},{5,7},{6,4},{7,5},{8,10},{9,11},{10,... | collective-permute-start | bytes 245768 | tf_op jit(solution)/shard_map/ppermute | solution.py:499
  44.1 7.3 %collective-permute-start.14 = (bf16[32,1280]{1,0:T(8,128)(2,1)S(1)}, bf16[32,1280]{1,0:T(8,128)(2,1)S(1)}, u32[]{:S(2)}, u32[]{:S(2)}) collective-permute-start(bf16[32,1280]{1,0:T(8,128)(2,1)S(1)} %shard_map.147.refs_0_), channel_id=1, source_target_pairs={{0,6},{1,7},{2,4},{3,5},{4,2},{5,3},{6,0},{7,1},{8,14},{9,15},{10,... | collective-permute-start | bytes 245768 | tf_op jit(solution)/shard_map/ppermute | solution.py:499
  45.7 8.2 %collective-permute-start.13 = (bf16[32,1280]{1,0:T(8,128)(2,1)S(1)}, bf16[32,1280]{1,0:T(8,128)(2,1)S(1)}, u32[]{:S(2)}, u32[]{:S(2)}) collective-permute-start(bf16[32,1280]{1,0:T(8,128)(2,1)S(1)} %shard_map.147.refs_0_), channel_id=1, source_target_pairs={{0,4},{1,5},{2,6},{3,7},{4,0},{5,1},{6,2},{7,3},{8,12},{9,13},{10,... | collective-permute-start | bytes 245768 | tf_op jit(solution)/shard_map/ppermute | solution.py:499
  45.7 8.2 %collective-permute-start.12 = (bf16[32,1280]{1,0:T(8,128)(2,1)S(1)}, bf16[32,1280]{1,0:T(8,128)(2,1)S(1)}, u32[]{:S(2)}, u32[]{:S(2)}) collective-permute-start(bf16[32,1280]{1,0:T(8,128)(2,1)S(1)} %shard_map.147.refs_0_), channel_id=1, source_target_pairs={{0,2},{1,3},{2,0},{3,1},{4,6},{5,7},{6,4},{7,5},{8,10},{9,11},{10,... | collective-permute-start | bytes 245768 | tf_op jit(solution)/shard_map/ppermute | solution.py:499
  54.0 7.1 %collective-permute-start.15 = (bf16[128,640]{1,0:T(8,128)(2,1)S(1)}, bf16[128,640]{1,0:T(8,128)(2,1)S(1)}, u32[]{:S(2)}, u32[]{:S(2)}) collective-permute-start(bf16[128,640]{1,0:T(8,128)(2,1)S(1)} %get-tuple-element.91.refs_0_), channel_id=1, source_target_pairs={{0,8},{8,0},{16,24},{24,16},{1,9},{9,1},{17,25},{25,17},{2,10},{10... | collective-permute-start | bytes 491528 | tf_op jit(solution)/shard_map/ppermute | solution.py:499
  54.4 8.2 %collective-permute-start.19 = (bf16[128,640]{1,0:T(8,128)(2,1)S(1)}, bf16[128,640]{1,0:T(8,128)(2,1)S(1)}, u32[]{:S(2)}, u32[]{:S(2)}) collective-permute-start(bf16[128,640]{1,0:T(8,128)(2,1)S(1)} %get-tuple-element.92.refs_4_), channel_id=1, source_target_pairs={{0,16},{8,24},{16,0},{24,8},{1,17},{9,25},{17,1},{25,9},{2,18},{10... | collective-permute-start | bytes 491528 | tf_op jit(solution)/shard_map/ppermute | solution.py:499
  56.0 8.9 %collective-permute-start.16 = (bf16[128,640]{1,0:T(8,128)(2,1)S(1)}, bf16[128,640]{1,0:T(8,128)(2,1)S(1)}, u32[]{:S(2)}, u32[]{:S(2)}) collective-permute-start(bf16[128,640]{1,0:T(8,128)(2,1)S(1)} %get-tuple-element.91.refs_0_), channel_id=1, source_target_pairs={{0,16},{8,24},{16,0},{24,8},{1,17},{9,25},{17,1},{25,9},{2,18},{10... | collective-permute-start | bytes 491528 | tf_op jit(solution)/shard_map/ppermute | solution.py:499
  56.4 8.6 %collective-permute-start.18 = (bf16[128,640]{1,0:T(8,128)(2,1)S(1)}, bf16[128,640]{1,0:T(8,128)(2,1)S(1)}, u32[]{:S(2)}, u32[]{:S(2)}) collective-permute-start(bf16[128,640]{1,0:T(8,128)(2,1)S(1)} %get-tuple-element.92.refs_4_), channel_id=1, source_target_pairs={{0,8},{8,0},{16,24},{24,16},{1,9},{9,1},{17,25},{25,17},{2,10},{10... | collective-permute-start | bytes 491528 | tf_op jit(solution)/shard_map/ppermute | solution.py:499
  61.1 6.2 %collective-permute-start.17 = (bf16[128,640]{1,0:T(8,128)(2,1)S(1)}, bf16[128,640]{1,0:T(8,128)(2,1)S(1)}, u32[]{:S(2)}, u32[]{:S(2)}) collective-permute-start(bf16[128,640]{1,0:T(8,128)(2,1)S(1)} %collective-permute-done.15.refs_1_), channel_id=1, source_target_pairs={{0,16},{8,24},{16,0},{24,8},{1,17},{9,25},{17,1},{25,9},{2,18},{10... | collective-permute-start | bytes 491528 | tf_op jit(solution)/shard_map/ppermute | solution.py:499
  62.6 5.3 %collective-permute-start.20 = (bf16[128,640]{1,0:T(8,128)(2,1)S(1)}, bf16[128,640]{1,0:T(8,128)(2,1)S(1)}, u32[]{:S(2)}, u32[]{:S(2)}) collective-permute-start(bf16[128,640]{1,0:T(8,128)(2,1)S(1)} %collective-permute-done.19.refs_6_), channel_id=1, source_target_pairs={{0,8},{8,0},{16,24},{24,16},{1,9},{9,1},{17,25},{25,17},{2,10},{10... | collective-permute-start | bytes 491528 | tf_op jit(solution)/shard_map/ppermute | solution.py:499
  68.0 3.1 %collective-permute-start.21 = (bf16[512,1280]{1,0:T(8,128)(2,1)S(1)}, bf16[512,1280]{1,0:T(8,128)(2,1)S(1)}, u32[]{:S(2)}, u32[]{:S(2)}) collective-permute-start(bf16[512,1280]{1,0:T(8,128)(2,1)S(1)} %shard_map.149.mid_half.small_half), channel_id=1, source_target_pairs={{0,1},{1,0},{2,3},{3,2},{4,5},{5,4},{6,7},{7,6},{8,9},{9,8},{10,11... | collective-permute-start | bytes 3932168 | tf_op jit(solution)/shard_map/ppermute | solution.py:499

commit v14 on v12

--- a/solution.py
+++ b/solution.py
@@ -389,6 +389,7 @@
 
 CORE = ("horiz", 0, 2)
 CHIPS = ("horiz", 1, 4)
+NEAR, FAR = ("horiz", 1, 2), ("horiz", 2, 2)
 MEMBERS = ("ens", 0, 4)
 MEMBER_LOW, MEMBER_HIGH = ("ens", 0, 2), ("ens", 1, 2)
 
@@ -460,7 +461,7 @@
 def final(rows, other, before, fields):
     half, columns = rows.shape
     units = 2 * half
-    block = units // 4
+    block = units // 2
 
     def place():
         core = lax.axis_index("horiz") % 2
@@ -538,13 +539,19 @@
     )(*[piece for group in groups for piece in group])
 
 
-def reduce_to(terms, stage):
-    parts = add(terms, stage)
-    return [parts[0]] + exchange(parts[:0:-1], stage)[::-1]
-
-
-def collect(piece, stage):
-    return [piece] + exchange([piece] * (stage[2] - 1), stage)
+def reduce_chips(terms):
+    own, both, far, near = add(terms, CHIPS)
+    (got_both,) = exchange([both], NEAR)
+    (got_near,) = exchange([near], NEAR)
+    (got_far,) = exchange(add([far, got_both], None), FAR)
+    return [own, got_near, got_far]
+
+
+def collect_chips(piece):
+    (got_far,) = exchange([piece], FAR)
+    (got_near,) = exchange([piece], NEAR)
+    (got_both,) = exchange([got_far], NEAR)
+    return [piece, got_near, got_far, got_both]
 
 
 def tie(*values):
@@ -643,8 +650,8 @@
     terms, grad_rows = tie(terms, grad_rows)
 
     if lax.axis_size("horiz") == 8:
-        terms = reduce_to(terms, CHIPS)
-        halves = join([collect(add(terms, None, factor)[0], CHIPS)], CHIPS, cuts=2)
+        terms = reduce_chips(terms)
+        halves = join([collect_chips(add(terms, None, factor)[0])], CHIPS, cuts=2)
     else:
         halves = jnp.split(over_all_chips(add(terms, None)[0], factor), 2, axis=1)
     (own,) = join(collect_members(*halves), MEMBERS)

time: 73.2 us -> 74.6 us (1.019)
  waiting for transfers between devices: 25.2 us -> 31 us
  starting transfers between devices: 27.7 us -> 24 us
  Pallas kernels: 15.6 us -> 14.8 us
    ppermute x15, waiting for transfers between devices: 20 us -> 25.8 us  [exchange(): sent[k] = lax.ppermute(arrays[k - 1], axis, route)]
    ppermute x15, starting transfers between devices: 15.7 us -> 12.1 us  [exchange(): sent[k] = lax.ppermute(arrays[k - 1], axis, route)]
    pallas_call x2, Pallas kernels: 4.47 us -> 3.64 us  [final(): pl.pallas_call(final_kernel, grid=(units // block,), out_shape=[jax.Shape...]
    pallas_call x13 -> x14, Pallas kernels: 11.1 us -> 11.2 us  [run(): pl.pallas_call(functools.partial(kernel, **names), out_shape=[jax.ShapeDt...]
  transfers between devices with their start and end apart: 22 -> 22, of which waited for: 12 -> 14; matrix products, arithmetic and copies ran while one was open for 3% -> 3% of each run, Pallas kernels for 12% -> 11%
where the time goes in v14:
time: 74.6 us; the launch traced here: 74.4 us
  waiting for transfers between devices  31 us (42%)
  starting transfers between devices  24 us (32%)
  Pallas kernels  14.8 us (20%)
  local copies, waits for them, and re-layouts  1.92 us (3%)
  between operations  1.53 us (2%)
  other arithmetic  1.1 us (1%)
    ppermute x15, waiting for transfers between devices, exchange(): sent[k] = lax.ppermute(arrays[k - 1], axis, route)  25.8 us
    ppermute x15, starting transfers between devices, exchange(): sent[k] = lax.ppermute(arrays[k - 1], axis, route)  12.1 us
    pallas_call x14, Pallas kernels, run(): pl.pallas_call(functools.partial(kernel, **names), out_shape=[jax.ShapeDt...  11.2 us
    ppermute x2, starting transfers between devices, to_neighbours(): lax.ppermute(downward, axis, backward)  7.52 us
    ppermute x3, waiting for transfers between devices, to_member(): return lax.ppermute(array, ('ens', 'horiz'), route)  4.86 us
    ppermute x3, starting transfers between devices, to_member(): return lax.ppermute(array, ('ens', 'horiz'), route)  3.8 us
    pallas_call x2, Pallas kernels, final(): pl.pallas_call(final_kernel, grid=(units // block,), out_shape=[jax.Shape...  3.64 us
    unnamed x14, local copies, waits for them, and re-layouts  1.86 us
  transfers between devices with their start and end apart: 22, of which 14 were waited for; matrix products, arithmetic and copies ran while one was open for 3% of the time, Pallas kernels for 11%

profile of v14, /device:TPU:0, one launch (start us, length us, event | category | flops | bytes accessed | tf_op | source)
XLA Modules:
  0.0 74.4 jit_solution(2876900605515407068)
XLA Ops:
  0.6 1.0 %pad_maximum_fusion.1 = f32[130,4,128]{2,1,0:T(4,128)S(1)} fusion(f32[2,4,128]{2,1,0:T(4,128)} %param.12, f32[128,4,128]{2,1,0:T(4,128)} %bitcast.16), kind=kLoop, calls=%fused_computation.1 | loop fusion | flops 66560 | bytes 532480 | tf_op jit(solution)/shard_map/concatenate | solution.py:582
  2.2 4.1 %collective-permute-start.1 = (bf16[272,128]{1,0:T(8,128)(2,1)S(1)}, bf16[272,128]{1,0:T(8,128)(2,1)S(1)}, u32[]{:S(2)}, u32[]{:S(2)}) collective-permute-start(bf16[272,128]{1,0:T(8,128)(2,1)S(1)} %get-tuple-element.53), channel_id=1, source_target_pairs={{1,0},{2,1},{3,2},{4,3},{5,4},{6,5},{7,6},{0,7},{9,8},{10,9},{11,1... | collective-permute-start | bytes 208904 | tf_op jit(solution)/shard_map/ppermute | solution.py:571
  7.0 1.8 %constant_dynamic-update-slice_fusion.1 = bf16[1024,1152]{1,0:T(8,128)(2,1)S(1)} fusion(bf16[1024,1024]{1,0:T(8,128)(2,1)} %param.18), kind=kLoop, calls=%fused_computation.3 | loop fusion | bytes 4194304
  9.0 0.8 %shard_map.138 = (f32[3,128,128]{2,1,0:T(8,128)S(1)}, f32[32,384]{1,0:T(8,128)S(1)}, f32[32,384]{1,0:T(8,128)S(1)}, f32[32,384]{1,0:T(8,128)S(1)}) custom-call(s32[1,1]{1,0:T(1,128)S(6)} %copy.26.count_ref, f32[640,128]{1,0:T(8,128)S(1)} %bitcast.14, s32[3,128]{1,0:T(4,128)S(1)} %get-tuple-element.100.cols_ref, s32[3,128]{1,0:T(4,128)S(1)} %get-tuple-element.99.mask_ref), custom_call_target="tpu_custom_call" | custom-call | bytes 30000000 | tf_op jit(solution)/shard_map/pallas_call | solution.py:27
  9.9 4.0 %shard_map.139 = (f32[4,128,128]{2,1,0:T(8,128)S(1)}, bf16[128,384]{1,0:T(8,128)(2,1)S(1)}, bf16[1024,384]{1,0:T(8,128)(2,1)}, bf16[1024,384]{1,0:T(8,128)(2,1)S...) custom-call(f32[520,128]{1,0:T(8,128)S(1)} %bitcast.12, ...), custom_call_target="tpu_custom_call" | custom-call | bytes 15000000 | tf_op jit(solution)/shard_map/pallas_call | solution.py:27
  13.8 2.1 %shard_map.140 = (bf16[1024,384]{1,0:T(8,128)(2,1)S(1)}, bf16[512,256]{1,0:T(8,128)(2,1)S(1)}, bf16[512,256]{1,0:T(8,128)(2,1)S(1)}) custom-call(bf16[128,384]{1,0:T(8,128)(2,1)S(1)} %get-tuple-element.57.x_ref, bf16[1024,384]{1,0:T(8,128)(2,1)S(1)} %get-tuple-element.72.act_two_ref, bf16[1024,384]{1,0:T(8,128)(2,1)S(1)} %get-tuple-element.59.delta_two_ref, ...), custom_call_target="tpu_custom_call" | custom-call | bytes 4000000 | tf_op jit(solution)/shard_map/pallas_call | solution.py:27
  15.9 0.6 collective-permute-start.3
  16.4 0.6 shard_map.141
  17.0 0.6 collective-permute-done.3.got_small
  17.9 2.0 %collective-permute-start.4 = (bf16[128,1280]{1,0:T(8,128)(2,1)S(1)}, bf16[128,1280]{1,0:T(8,128)(2,1)S(1)}, u32[]{:S(2)}, u32[]{:S(2)}) collective-permute-start(bf16[128,1280]{1,0:T(8,128)(2,1)S(1)} %get-tuple-element.65), channel_id=1, source_target_pairs={{0,8},{1,17},{2,10},{3,19},{4,12},{5,21},{6,14},{7,23},{8,0},{9,25... | collective-permute-start | bytes 983048 | tf_op jit(solution)/shard_map/ppermute | solution.py:509
  20.0 3.4 %collective-permute-start.6 = (bf16[256,128]{1,0:T(8,128)(2,1)S(1)}, bf16[256,128]{1,0:T(8,128)(2,1)S(1)}, u32[]{:S(2)}, u32[]{:S(2)}) collective-permute-start(bf16[256,128]{1,0:T(8,128)(2,1)S(1)} %get-tuple-element.77), channel_id=1, source_target_pairs={{1,0},{2,1},{3,2},{4,3},{5,4},{6,5},{7,6},{0,7},{9,8},{10,9},{11,1... | collective-permute-start | bytes 196616 | tf_op jit(solution)/shard_map/ppermute | solution.py:571
  23.6 1.6 %shard_map.143 = f32[512,128]{1,0:T(8,128)} custom-call(s32[1,1]{1,0:T(1,128)S(6)} %copy.26.count_ref, f32[4,128,128]{2,1,0:T(8,128)S(1)} %get-tuple-element.66.moved_ref, s32[3,128]{1,0:T(4,128)S(1)} %get-tuple-element.100.cols_ref, s32[3,128]{1,0:T(4,128)S(1)} %get-tuple-element.99.mask_ref, bf16[128,384]{1,0:T(8,128)(2,1)S(1)} %get-tuple-element.57.x_ref, ...), custom_call_target="tpu_custom_call" | custom-call | tf_op jit(solution)/shard_map/pallas_call | solution.py:27
  25.5 1.7 %collective-permute-start.8 = (bf16[128,1280]{1,0:T(8,128)(2,1)S(1)}, bf16[128,1280]{1,0:T(8,128)(2,1)S(1)}, u32[]{:S(2)}, u32[]{:S(2)}) collective-permute-start(bf16[128,1280]{1,0:T(8,128)(2,1)S(1)} %shard_map.144), channel_id=1, source_target_pairs={{0,16},{1,9},{2,18},{3,11},{4,20},{5,13},{6,22},{7,15},{8,24},{9,1... | collective-permute-start | bytes 983048 | tf_op jit(solution)/shard_map/ppermute | solution.py:509
  27.3 1.5 %shard_map.145 = f32[512,128]{1,0:T(8,128)} custom-call(f32[4,128,128]{2,1,0:T(8,128)S(1)} %get-tuple-element.80.field_ref, bf16[256,128]{1,0:T(8,128)(2,1)S(1)} %collective-permute-done.5.low_ref, bf16[256,128]{1,0:T(8,128)(2,1)S(1)} %collective-permute-done.6.high_ref, bf16[272,128]{1,0:T(8,128)(2,1)S(1)} %collective-permute-done.low_ref.low_mix_ref, ...), custom_call_target="tpu_custom_call" | custom-call | tf_op jit(solution)/shard_map/pallas_call | solution.py:27
  28.7 4.9 %collective-permute-done.7.refs_1_ = bf16[128,1280]{1,0:T(8,128)(2,1)S(1)} collective-permute-done((bf16[128,1280]{1,0:T(8,128)(2,1)S(1)}, bf16[128,1280]{1,0:T(8,128)(2,1)S(1)}, u32[]{:S(2)}, u32[]{:S(2)}) %collective-permute-start.7) | collective-permute-done | bytes 327712 | tf_op jit(solution)/shard_map/ppermute | solution.py:509
  33.8 2.0 %collective-permute-start.9 = (bf16[32,1280]{1,0:T(8,128)(2,1)S(1)}, bf16[32,1280]{1,0:T(8,128)(2,1)S(1)}, u32[]{:S(2)}, u32[]{:S(2)}) collective-permute-start(bf16[32,1280]{1,0:T(8,128)(2,1)S(1)} %get-tuple-element.88), channel_id=1, source_target_pairs={{0,2},{1,3},{2,0},{3,1},{4,6},{5,7},{6,4},{7,5},{8,10},{9,11},{10,... | collective-permute-start | bytes 245768 | tf_op jit(solution)/shard_map/ppermute | solution.py:498
  35.8 3.2 %collective-permute-done.10.refs_1_ = bf16[32,1280]{1,0:T(8,128)(2,1)S(1)} collective-permute-done((bf16[32,1280]{1,0:T(8,128)(2,1)S(1)}, bf16[32,1280]{1,0:T(8,128)(2,1)S(1)}, u32[]{:S(2)}, u32[]{:S(2)}) %collective-permute-start.10) | collective-permute-done | bytes 81952 | tf_op jit(solution)/shard_map/ppermute | solution.py:498
  39.2 1.0 %collective-permute-done.9.refs_1_ = bf16[32,1280]{1,0:T(8,128)(2,1)S(1)} collective-permute-done((bf16[32,1280]{1,0:T(8,128)(2,1)S(1)}, bf16[32,1280]{1,0:T(8,128)(2,1)S(1)}, u32[]{:S(2)}, u32[]{:S(2)}) %collective-permute-start.9) | collective-permute-done | bytes 81952 | tf_op jit(solution)/shard_map/ppermute | solution.py:498
  40.2 4.8 %collective-permute-done.11.refs_2_ = bf16[32,1280]{1,0:T(8,128)(2,1)S(1)} collective-permute-done((bf16[32,1280]{1,0:T(8,128)(2,1)S(1)}, bf16[32,1280]{1,0:T(8,128)(2,1)S(1)}, u32[]{:S(2)}, u32[]{:S(2)}) %collective-permute-start.11) | collective-permute-done | bytes 81952 | tf_op jit(solution)/shard_map/ppermute | solution.py:498
  45.1 2.2 %collective-permute-start.12 = (bf16[32,1280]{1,0:T(8,128)(2,1)S(1)}, bf16[32,1280]{1,0:T(8,128)(2,1)S(1)}, u32[]{:S(2)}, u32[]{:S(2)}) collective-permute-start(bf16[32,1280]{1,0:T(8,128)(2,1)S(1)} %shard_map.148.refs_0_), channel_id=1, source_target_pairs={{0,2},{1,3},{2,0},{3,1},{4,6},{5,7},{6,4},{7,5},{8,10},{9,11},{10,... | collective-permute-start | bytes 245768 | tf_op jit(solution)/shard_map/ppermute | solution.py:498
  47.3 3.4 %collective-permute-done.13.refs_2_ = bf16[32,1280]{1,0:T(8,128)(2,1)S(1)} collective-permute-done((bf16[32,1280]{1,0:T(8,128)(2,1)S(1)}, bf16[32,1280]{1,0:T(8,128)(2,1)S(1)}, u32[]{:S(2)}, u32[]{:S(2)}) %collective-permute-start.13) | collective-permute-done | bytes 81952 | tf_op jit(solution)/shard_map/ppermute | solution.py:498
  50.8 4.3 %collective-permute-done.14.refs_3_ = bf16[32,1280]{1,0:T(8,128)(2,1)S(1)} collective-permute-done((bf16[32,1280]{1,0:T(8,128)(2,1)S(1)}, bf16[32,1280]{1,0:T(8,128)(2,1)S(1)}, u32[]{:S(2)}, u32[]{:S(2)}) %collective-permute-start.14) | collective-permute-done | bytes 81952 | tf_op jit(solution)/shard_map/ppermute | solution.py:498
  55.4 1.8 %collective-permute-start.19 = (bf16[128,640]{1,0:T(8,128)(2,1)S(1)}, bf16[128,640]{1,0:T(8,128)(2,1)S(1)}, u32[]{:S(2)}, u32[]{:S(2)}) collective-permute-start(bf16[128,640]{1,0:T(8,128)(2,1)S(1)} %get-tuple-element.92.refs_4_), channel_id=1, source_target_pairs={{0,16},{8,24},{16,0},{24,8},{1,17},{9,25},{17,1},{25,9},{2,18},{10... | collective-permute-start | bytes 491528 | tf_op jit(solution)/shard_map/ppermute | solution.py:498
  57.4 1.8 %collective-permute-start.18 = (bf16[128,640]{1,0:T(8,128)(2,1)S(1)}, bf16[128,640]{1,0:T(8,128)(2,1)S(1)}, u32[]{:S(2)}, u32[]{:S(2)}) collective-permute-start(bf16[128,640]{1,0:T(8,128)(2,1)S(1)} %get-tuple-element.92.refs_4_), channel_id=1, source_target_pairs={{0,8},{8,0},{16,24},{24,16},{1,9},{9,1},{17,25},{25,17},{2,10},{10... | collective-permute-start | bytes 491528 | tf_op jit(solution)/shard_map/ppermute | solution.py:498
  59.2 2.2 %collective-permute-done.15.refs_1_ = bf16[128,640]{1,0:T(8,128)(2,1)S(1)} collective-permute-done((bf16[128,640]{1,0:T(8,128)(2,1)S(1)}, bf16[128,640]{1,0:T(8,128)(2,1)S(1)}, u32[]{:S(2)}, u32[]{:S(2)}) %collective-permute-start.15) | collective-permute-done | bytes 163872 | tf_op jit(solution)/shard_map/ppermute | solution.py:498
  61.4 2.6 %collective-permute-start.17 = (bf16[128,640]{1,0:T(8,128)(2,1)S(1)}, bf16[128,640]{1,0:T(8,128)(2,1)S(1)}, u32[]{:S(2)}, u32[]{:S(2)}) collective-permute-start(bf16[128,640]{1,0:T(8,128)(2,1)S(1)} %collective-permute-done.15.refs_1_), channel_id=1, source_target_pairs={{0,16},{8,24},{16,0},{24,8},{1,17},{9,25},{17,1},{25,9},{2,18},{10... | collective-permute-start | bytes 491528 | tf_op jit(solution)/shard_map/ppermute | solution.py:498
  64.3 0.8 %collective-permute-done.16.refs_2_ = bf16[128,640]{1,0:T(8,128)(2,1)S(1)} collective-permute-done((bf16[128,640]{1,0:T(8,128)(2,1)S(1)}, bf16[128,640]{1,0:T(8,128)(2,1)S(1)}, u32[]{:S(2)}, u32[]{:S(2)}) %collective-permute-start.16) | collective-permute-done | bytes 163872 | tf_op jit(solution)/shard_map/ppermute | solution.py:498
  65.1 2.2 %collective-permute-done.17.refs_3_ = bf16[128,640]{1,0:T(8,128)(2,1)S(1)} collective-permute-done((bf16[128,640]{1,0:T(8,128)(2,1)S(1)}, bf16[128,640]{1,0:T(8,128)(2,1)S(1)}, u32[]{:S(2)}, u32[]{:S(2)}) %collective-permute-start.17) | collective-permute-done | bytes 163872 | tf_op jit(solution)/shard_map/ppermute | solution.py:498
  67.3 2.0 %collective-permute-done.20.refs_7_ = bf16[128,640]{1,0:T(8,128)(2,1)S(1)} collective-permute-done((bf16[128,640]{1,0:T(8,128)(2,1)S(1)}, bf16[128,640]{1,0:T(8,128)(2,1)S(1)}, u32[]{:S(2)}, u32[]{:S(2)}) %collective-permute-start.20) | collective-permute-done | bytes 163872 | tf_op jit(solution)/shard_map/ppermute | solution.py:498
  69.5 1.8 %shard_map.151 = (f32[1024,1024]{1,0:T(8,128)}, f32[1024,128]{1,0:T(8,128)}, f32[128,1024]{1,0:T(8,128)}) custom-call(bf16[512,1280]{1,0:T(8,128)(2,1)S(1)} %shard_map.150.mid_half.small_half, bf16[512,1280]{1,0:T(8,128)(2,1)S(1)} %shard_map.150.mid_half.small_half), custom_call_target="tpu_custom_call" | custom-call | tf_op jit(solution)/shard_map/pallas_call | solution.py:470
  71.4 1.2 %collective-permute-done.21.mid_half.small_half = bf16[512,1280]{1,0:T(8,128)(2,1)S(1)} collective-permute-done((bf16[512,1280]{1,0:T(8,128)(2,1)S(1)}, bf16[512,1280]{1,0:T(8,128)(2,1)S(1)}, u32[]{:S(2)}, u32[]{:S(2)}) %collective-permute-start.21) | collective-permute-done | bytes 1310752 | tf_op jit(solution)/shard_map/ppermute | solution.py:498
  72.6 1.8 %shard_map.152 = (f32[1024,1024]{1,0:T(8,128)}, f32[1024,128]{1,0:T(8,128)}, f32[128,1024]{1,0:T(8,128)}) custom-call(bf16[512,1280]{1,0:T(8,128)(2,1)S(1)} %collective-permute-done.21.mid_half.small_half, bf16[512,1280]{1,0:T(8,128)(2,1)S(1)} %collective-permute-done.21.mid_half.small_half, ...), custom_call_target="tpu_custom_call", output_to_operand_aliasing={{0}: (2, {}), {1}: (3, {}), {2}: (4, {})} | custom-call | tf_op jit(solution)/shard_map/pallas_call | solution.py:470
  (45 shorter events, 3.3 us)
Async XLA Ops:
  1.7 7.2 %copy-start.4 = (s32[1,1,3,128]{3,1,2,0:T(1,128)S(1)}, s32[1,1,3,128]{3,1,2,0:T(1,128)}, u32[]{:S(2)}) copy-start(s32[1,1,3,128]{3,1,2,0:T(1,128)} %param.15) | copy-start | bytes 4612
  1.7 7.2 %copy-start.5 = (s32[1,1,3,128]{3,1,2,0:T(1,128)S(1)}, s32[1,1,3,128]{3,1,2,0:T(1,128)}, u32[]{:S(2)}) copy-start(s32[1,1,3,128]{3,1,2,0:T(1,128)} %param.14) | copy-start | bytes 4612
  1.7 7.2 %copy-start.1 = (f32[1,128,4,128]{3,2,1,0:T(4,128)S(1)}, f32[1,128,4,128]{3,2,1,0:T(4,128)}, u32[]{:S(2)}) copy-start(f32[1,128,4,128]{3,2,1,0:T(4,128)} %param.13) | copy-start | bytes 786436
  1.7 7.2 %copy-start.3 = (f32[1,32,4,128]{3,2,1,0:T(4,128)S(1)}, f32[1,32,4,128]{3,2,1,0:T(4,128)}, u32[]{:S(2)}) copy-start(f32[1,32,4,128]{3,2,1,0:T(4,128)} %param.11) | copy-start | bytes 196612
  1.7 8.1 %collective-permute-start = (bf16[272,128]{1,0:T(8,128)(2,1)S(1)}, bf16[272,128]{1,0:T(8,128)(2,1)S(1)}, u32[]{:S(2)}, u32[]{:S(2)}) collective-permute-start(bf16[272,128]{1,0:T(8,128)(2,1)S(1)} %get-tuple-element.52), channel_id=1, source_target_pairs={{0,1},{1,2},{2,3},{3,4},{4,5},{5,6},{6,7},{7,0},{8,9},{9,10},{10,1... | collective-permute-start | bytes 208904 | tf_op jit(solution)/shard_map/ppermute | solution.py:571
  2.2 7.6 %collective-permute-start.1 = (bf16[272,128]{1,0:T(8,128)(2,1)S(1)}, bf16[272,128]{1,0:T(8,128)(2,1)S(1)}, u32[]{:S(2)}, u32[]{:S(2)}) collective-permute-start(bf16[272,128]{1,0:T(8,128)(2,1)S(1)} %get-tuple-element.53), channel_id=1, source_target_pairs={{1,0},{2,1},{3,2},{4,3},{5,4},{6,5},{7,6},{0,7},{9,8},{10,9},{11,1... | collective-permute-start | bytes 208904 | tf_op jit(solution)/shard_map/ppermute | solution.py:571
  7.0 2.7 %copy-start.2 = (bf16[1024,128]{1,0:T(8,128)(2,1)S(1)}, bf16[1024,128]{1,0:T(8,128)(2,1)}, u32[]{:S(2)}) copy-start(bf16[1024,128]{1,0:T(8,128)(2,1)} %param.17) | copy-start | bytes 786436
  7.0 2.8 %copy-start = (bf16[128,1024]{1,0:T(8,128)(2,1)S(1)}, bf16[128,1024]{1,0:T(8,128)(2,1)}, u32[]{:S(2)}) copy-start(bf16[128,1024]{1,0:T(8,128)(2,1)} %w_out_ref.3) | copy-start | bytes 786436
  13.8 3.8 %collective-permute-start.2 = (bf16[512,1024]{1,0:T(8,128)(2,1)S(1)}, bf16[512,1024]{1,0:T(8,128)(2,1)S(1)}, u32[]{:S(2)}, u32[]{:S(2)}) collective-permute-start(bf16[512,1024]{1,0:T(8,128)(2,1)S(1)} %get-tuple-element.56), channel_id=1, source_target_pairs={{0,1},{1,0},{2,3},{3,2},{4,5},{5,4},{6,7},{7,6},{8,9},{9,8},{10,11... | collective-permute-start | bytes 3145736 | tf_op jit(solution)/shard_map/ppermute | solution.py:498
  15.9 1.7 %collective-permute-start.3 = (bf16[512,256]{1,0:T(8,128)(2,1)S(1)}, bf16[512,256]{1,0:T(8,128)(2,1)S(1)}, u32[]{:S(2)}, u32[]{:S(2)}) collective-permute-start(bf16[512,256]{1,0:T(8,128)(2,1)S(1)} %get-tuple-element.61), channel_id=1, source_target_pairs={{0,1},{1,0},{2,3},{3,2},{4,5},{5,4},{6,7},{7,6},{8,9},{9,8},{10,11... | collective-permute-start | bytes 786440 | tf_op jit(solution)/shard_map/ppermute | solution.py:498
  17.9 7.5 %collective-permute-start.4 = (bf16[128,1280]{1,0:T(8,128)(2,1)S(1)}, bf16[128,1280]{1,0:T(8,128)(2,1)S(1)}, u32[]{:S(2)}, u32[]{:S(2)}) collective-permute-start(bf16[128,1280]{1,0:T(8,128)(2,1)S(1)} %get-tuple-element.65), channel_id=1, source_target_pairs={{0,8},{1,17},{2,10},{3,19},{4,12},{5,21},{6,14},{7,23},{8,0},{9,25... | collective-permute-start | bytes 983048 | tf_op jit(solution)/shard_map/ppermute | solution.py:509
  19.9 5.5 %collective-permute-start.5 = (bf16[256,128]{1,0:T(8,128)(2,1)S(1)}, bf16[256,128]{1,0:T(8,128)(2,1)S(1)}, u32[]{:S(2)}, u32[]{:S(2)}) collective-permute-start(bf16[256,128]{1,0:T(8,128)(2,1)S(1)} %get-tuple-element.76), channel_id=1, source_target_pairs={{0,1},{1,2},{2,3},{3,4},{4,5},{5,6},{6,7},{7,0},{8,9},{9,10},{10,1... | collective-permute-start | bytes 196616 | tf_op jit(solution)/shard_map/ppermute | solution.py:571
  20.0 5.4 %collective-permute-start.6 = (bf16[256,128]{1,0:T(8,128)(2,1)S(1)}, bf16[256,128]{1,0:T(8,128)(2,1)S(1)}, u32[]{:S(2)}, u32[]{:S(2)}) collective-permute-start(bf16[256,128]{1,0:T(8,128)(2,1)S(1)} %get-tuple-element.77), channel_id=1, source_target_pairs={{1,0},{2,1},{3,2},{4,3},{5,4},{6,5},{7,6},{0,7},{9,8},{10,9},{11,1... | collective-permute-start | bytes 196616 | tf_op jit(solution)/shard_map/ppermute | solution.py:571
  23.5 10.1 %collective-permute-start.7 = (bf16[128,1280]{1,0:T(8,128)(2,1)S(1)}, bf16[128,1280]{1,0:T(8,128)(2,1)S(1)}, u32[]{:S(2)}, u32[]{:S(2)}) collective-permute-start(bf16[128,1280]{1,0:T(8,128)(2,1)S(1)} %get-tuple-element.70), channel_id=1, source_target_pairs={{0,8},{1,17},{2,10},{3,19},{4,12},{5,21},{6,14},{7,23},{8,0},{9,25... | collective-permute-start | bytes 983048 | tf_op jit(solution)/shard_map/ppermute | solution.py:509
  25.5 8.1 %collective-permute-start.8 = (bf16[128,1280]{1,0:T(8,128)(2,1)S(1)}, bf16[128,1280]{1,0:T(8,128)(2,1)S(1)}, u32[]{:S(2)}, u32[]{:S(2)}) collective-permute-start(bf16[128,1280]{1,0:T(8,128)(2,1)S(1)} %shard_map.144), channel_id=1, source_target_pairs={{0,16},{1,9},{2,18},{3,11},{4,20},{5,13},{6,22},{7,15},{8,24},{9,1... | collective-permute-start | bytes 983048 | tf_op jit(solution)/shard_map/ppermute | solution.py:509
  33.7 5.3 %collective-permute-start.10 = (bf16[32,1280]{1,0:T(8,128)(2,1)S(1)}, bf16[32,1280]{1,0:T(8,128)(2,1)S(1)}, u32[]{:S(2)}, u32[]{:S(2)}) collective-permute-start(bf16[32,1280]{1,0:T(8,128)(2,1)S(1)} %get-tuple-element.90), channel_id=1, source_target_pairs={{0,2},{1,3},{2,0},{3,1},{4,6},{5,7},{6,4},{7,5},{8,10},{9,11},{10,... | collective-permute-start | bytes 245768 | tf_op jit(solution)/shard_map/ppermute | solution.py:498
  33.8 6.4 %collective-permute-start.9 = (bf16[32,1280]{1,0:T(8,128)(2,1)S(1)}, bf16[32,1280]{1,0:T(8,128)(2,1)S(1)}, u32[]{:S(2)}, u32[]{:S(2)}) collective-permute-start(bf16[32,1280]{1,0:T(8,128)(2,1)S(1)} %get-tuple-element.88), channel_id=1, source_target_pairs={{0,2},{1,3},{2,0},{3,1},{4,6},{5,7},{6,4},{7,5},{8,10},{9,11},{10,... | collective-permute-start | bytes 245768 | tf_op jit(solution)/shard_map/ppermute | solution.py:498
  39.1 5.9 %collective-permute-start.11 = (bf16[32,1280]{1,0:T(8,128)(2,1)S(1)}, bf16[32,1280]{1,0:T(8,128)(2,1)S(1)}, u32[]{:S(2)}, u32[]{:S(2)}) collective-permute-start(bf16[32,1280]{1,0:T(8,128)(2,1)S(1)} %shard_map.147), channel_id=1, source_target_pairs={{0,4},{1,5},{2,6},{3,7},{4,0},{5,1},{6,2},{7,3},{8,12},{9,13},{10,... | collective-permute-start | bytes 245768 | tf_op jit(solution)/shard_map/ppermute | solution.py:498
  45.0 5.6 %collective-permute-start.13 = (bf16[32,1280]{1,0:T(8,128)(2,1)S(1)}, bf16[32,1280]{1,0:T(8,128)(2,1)S(1)}, u32[]{:S(2)}, u32[]{:S(2)}) collective-permute-start(bf16[32,1280]{1,0:T(8,128)(2,1)S(1)} %shard_map.148.refs_0_), channel_id=1, source_target_pairs={{0,4},{1,5},{2,6},{3,7},{4,0},{5,1},{6,2},{7,3},{8,12},{9,13},{10,... | collective-permute-start | bytes 245768 | tf_op jit(solution)/shard_map/ppermute | solution.py:498
  45.1 5.7 %collective-permute-start.12 = (bf16[32,1280]{1,0:T(8,128)(2,1)S(1)}, bf16[32,1280]{1,0:T(8,128)(2,1)S(1)}, u32[]{:S(2)}, u32[]{:S(2)}) collective-permute-start(bf16[32,1280]{1,0:T(8,128)(2,1)S(1)} %shard_map.148.refs_0_), channel_id=1, source_target_pairs={{0,2},{1,3},{2,0},{3,1},{4,6},{5,7},{6,4},{7,5},{8,10},{9,11},{10,... | collective-permute-start | bytes 245768 | tf_op jit(solution)/shard_map/ppermute | solution.py:498
  50.6 4.4 %collective-permute-start.14 = (bf16[32,1280]{1,0:T(8,128)(2,1)S(1)}, bf16[32,1280]{1,0:T(8,128)(2,1)S(1)}, u32[]{:S(2)}, u32[]{:S(2)}) collective-permute-start(bf16[32,1280]{1,0:T(8,128)(2,1)S(1)} %collective-permute-done.13.refs_2_), channel_id=1, source_target_pairs={{0,2},{1,3},{2,0},{3,1},{4,6},{5,7},{6,4},{7,5},{8,10},{9,11},{10,... | collective-permute-start | bytes 245768 | tf_op jit(solution)/shard_map/ppermute | solution.py:498
  55.1 6.3 %collective-permute-start.15 = (bf16[128,640]{1,0:T(8,128)(2,1)S(1)}, bf16[128,640]{1,0:T(8,128)(2,1)S(1)}, u32[]{:S(2)}, u32[]{:S(2)}) collective-permute-start(bf16[128,640]{1,0:T(8,128)(2,1)S(1)} %get-tuple-element.91.refs_0_), channel_id=1, source_target_pairs={{0,8},{8,0},{16,24},{24,16},{1,9},{9,1},{17,25},{25,17},{2,10},{10... | collective-permute-start | bytes 491528 | tf_op jit(solution)/shard_map/ppermute | solution.py:498
  55.4 8.6 %collective-permute-start.19 = (bf16[128,640]{1,0:T(8,128)(2,1)S(1)}, bf16[128,640]{1,0:T(8,128)(2,1)S(1)}, u32[]{:S(2)}, u32[]{:S(2)}) collective-permute-start(bf16[128,640]{1,0:T(8,128)(2,1)S(1)} %get-tuple-element.92.refs_4_), channel_id=1, source_target_pairs={{0,16},{8,24},{16,0},{24,8},{1,17},{9,25},{17,1},{25,9},{2,18},{10... | collective-permute-start | bytes 491528 | tf_op jit(solution)/shard_map/ppermute | solution.py:498
  57.2 8.0 %collective-permute-start.16 = (bf16[128,640]{1,0:T(8,128)(2,1)S(1)}, bf16[128,640]{1,0:T(8,128)(2,1)S(1)}, u32[]{:S(2)}, u32[]{:S(2)}) collective-permute-start(bf16[128,640]{1,0:T(8,128)(2,1)S(1)} %get-tuple-element.91.refs_0_), channel_id=1, source_target_pairs={{0,16},{8,24},{16,0},{24,8},{1,17},{9,25},{17,1},{25,9},{2,18},{10... | collective-permute-start | bytes 491528 | tf_op jit(solution)/shard_map/ppermute | solution.py:498
  57.4 7.7 %collective-permute-start.18 = (bf16[128,640]{1,0:T(8,128)(2,1)S(1)}, bf16[128,640]{1,0:T(8,128)(2,1)S(1)}, u32[]{:S(2)}, u32[]{:S(2)}) collective-permute-start(bf16[128,640]{1,0:T(8,128)(2,1)S(1)} %get-tuple-element.92.refs_4_), channel_id=1, source_target_pairs={{0,8},{8,0},{16,24},{24,16},{1,9},{9,1},{17,25},{25,17},{2,10},{10... | collective-permute-start | bytes 491528 | tf_op jit(solution)/shard_map/ppermute | solution.py:498
  61.4 5.9 %collective-permute-start.17 = (bf16[128,640]{1,0:T(8,128)(2,1)S(1)}, bf16[128,640]{1,0:T(8,128)(2,1)S(1)}, u32[]{:S(2)}, u32[]{:S(2)}) collective-permute-start(bf16[128,640]{1,0:T(8,128)(2,1)S(1)} %collective-permute-done.15.refs_1_), channel_id=1, source_target_pairs={{0,16},{8,24},{16,0},{24,8},{1,17},{9,25},{17,1},{25,9},{2,18},{10... | collective-permute-start | bytes 491528 | tf_op jit(solution)/shard_map/ppermute | solution.py:498
  64.0 5.3 %collective-permute-start.20 = (bf16[128,640]{1,0:T(8,128)(2,1)S(1)}, bf16[128,640]{1,0:T(8,128)(2,1)S(1)}, u32[]{:S(2)}, u32[]{:S(2)}) collective-permute-start(bf16[128,640]{1,0:T(8,128)(2,1)S(1)} %collective-permute-done.19.refs_6_), channel_id=1, source_target_pairs={{0,8},{8,0},{16,24},{24,16},{1,9},{9,1},{17,25},{25,17},{2,10},{10... | collective-permute-start | bytes 491528 | tf_op jit(solution)/shard_map/ppermute | solution.py:498
  69.5 3.1 %collective-permute-start.21 = (bf16[512,1280]{1,0:T(8,128)(2,1)S(1)}, bf16[512,1280]{1,0:T(8,128)(2,1)S(1)}, u32[]{:S(2)}, u32[]{:S(2)}) collective-permute-start(bf16[512,1280]{1,0:T(8,128)(2,1)S(1)} %shard_map.150.mid_half.small_half), channel_id=1, source_target_pairs={{0,1},{1,0},{2,3},{3,2},{4,5},{5,4},{6,7},{7,6},{8,9},{9,8},{10,11... | collective-permute-start | bytes 3932168 | tf_op jit(solution)/shard_map/ppermute | solution.py:498

commit v15 on v14

--- a/solution.py
+++ b/solution.py
@@ -389,7 +389,6 @@
 
 CORE = ("horiz", 0, 2)
 CHIPS = ("horiz", 1, 4)
-NEAR, FAR = ("horiz", 1, 2), ("horiz", 2, 2)
 MEMBERS = ("ens", 0, 4)
 MEMBER_LOW, MEMBER_HIGH = ("ens", 0, 2), ("ens", 1, 2)
 
@@ -397,6 +396,12 @@
 def position(stage):
     axis, shift, parts = stage
     return lax.axis_index(axis) // (1 << shift) % parts
+
+
+def partner(stage, index):
+    parts = stage[2]
+    offset = jnp.where(lax.axis_index("horiz") % 2 == 0, -index % parts, index)
+    return position(stage) ^ offset
 
 
 def sum_kernel(*refs, terms, stage, factor):
@@ -405,7 +410,7 @@
     for index, out_ref in enumerate(outs):
         here = pl.ds(0, rows)
         if stage is not None:
-            start = (position(stage) ^ (-index % len(outs))) * rows
+            start = partner(stage, index) * rows
             here = pl.ds(pl.multiple_of(start, rows), rows)
         total = ins[0][here, :].astype(F32)
         for ref in ins[1:]:
@@ -420,7 +425,8 @@
     width = outs[0].shape[1]
     part = min(width, columns)
     for k in range(count):
-        here = pl.ds(pl.multiple_of((position(stage) ^ k) * rows, rows), rows)
+        place = partner(stage, k) if stage == CHIPS else position(stage) ^ k
+        here = pl.ds(pl.multiple_of(place * rows, rows), rows)
         for group in range(groups):
             for start in range(0, columns, part):
                 first = group * columns + start
@@ -539,19 +545,24 @@
     )(*[piece for group in groups for piece in group])
 
 
+def to_chips(arrays):
+    _, shift, parts = CHIPS
+    count = lax.axis_size("horiz")
+    received = []
+    for index, array in enumerate(arrays, 1):
+        offsets = [-index % parts, index]
+        route = [(i, i ^ (offsets[i % 2] << shift)) for i in range(count)]
+        received.append(lax.ppermute(array, "horiz", route))
+    return received
+
+
 def reduce_chips(terms):
-    own, both, far, near = add(terms, CHIPS)
-    (got_both,) = exchange([both], NEAR)
-    (got_near,) = exchange([near], NEAR)
-    (got_far,) = exchange(add([far, got_both], None), FAR)
-    return [own, got_near, got_far]
+    parts = add(terms, CHIPS)
+    return [parts[0]] + to_chips(parts[1:])
 
 
 def collect_chips(piece):
-    (got_far,) = exchange([piece], FAR)
-    (got_near,) = exchange([piece], NEAR)
-    (got_both,) = exchange([got_far], NEAR)
-    return [piece, got_near, got_far, got_both]
+    return [piece] + to_chips([piece] * (CHIPS[2] - 1))
 
 
 def tie(*values):

time: 74.6 us -> 71.8 us (0.962)
  waiting for transfers between devices: 31 us -> 23.1 us
  starting transfers between devices: 24 us -> 29.1 us
    ppermute x15 -> x9, waiting for transfers between devices: 25.8 us -> 8.21 us  [exchange(): sent[k] = lax.ppermute(arrays[k - 1], axis, route)]
    ppermute x0 -> x6, waiting for transfers between devices: none -> 9.74 us  [to_chips(): received.append(lax.ppermute(array, 'horiz', route))]
    ppermute x0 -> x6, starting transfers between devices: none -> 8.9 us  [to_chips(): received.append(lax.ppermute(array, 'horiz', route))]
    ppermute x15 -> x9, starting transfers between devices: 12.1 us -> 8.27 us  [exchange(): sent[k] = lax.ppermute(arrays[k - 1], axis, route)]
    pallas_call x14 -> x13, Pallas kernels: 11.2 us -> 11.1 us  [run(): pl.pallas_call(functools.partial(kernel, **names), out_shape=[jax.ShapeDt...]
  transfers between devices with their start and end apart: 22 -> 22, of which waited for: 14 -> 13; matrix products, arithmetic and copies ran while one was open for 3% -> 3% of each run, Pallas kernels for 11% -> 12%
where the time goes in v15:
time: 71.8 us; the launch traced here: 71.6 us
  starting transfers between devices  29.1 us (41%)
  waiting for transfers between devices  23.1 us (32%)
  Pallas kernels  14.8 us (21%)
  local copies, waits for them, and re-layouts  1.92 us (3%)
  between operations  1.52 us (2%)
  other arithmetic  1.1 us (2%)
    pallas_call x13, Pallas kernels, run(): pl.pallas_call(functools.partial(kernel, **names), out_shape=[jax.ShapeDt...  11.1 us
    ppermute x6, waiting for transfers between devices, to_chips(): received.append(lax.ppermute(array, 'horiz', route))  9.74 us
    ppermute x6, starting transfers between devices, to_chips(): received.append(lax.ppermute(array, 'horiz', route))  8.9 us
    ppermute x9, starting transfers between devices, exchange(): sent[k] = lax.ppermute(arrays[k - 1], axis, route)  8.27 us
    ppermute x9, waiting for transfers between devices, exchange(): sent[k] = lax.ppermute(arrays[k - 1], axis, route)  8.21 us
    ppermute x2, starting transfers between devices, to_neighbours(): lax.ppermute(downward, axis, backward)  7.52 us
    ppermute x3, waiting for transfers between devices, to_member(): return lax.ppermute(array, ('ens', 'horiz'), route)  4.86 us
    ppermute x3, starting transfers between devices, to_member(): return lax.ppermute(array, ('ens', 'horiz'), route)  3.8 us
  transfers between devices with their start and end apart: 22, of which 13 were waited for; matrix products, arithmetic and copies ran while one was open for 3% of the time, Pallas kernels for 12%

profile of v15, /device:TPU:0, one launch (start us, length us, event | category | flops | bytes accessed | tf_op | source)
XLA Modules:
  0.0 71.6 jit_solution(9374750939631172436)
XLA Ops:
  0.6 1.0 %pad_maximum_fusion.1 = f32[130,4,128]{2,1,0:T(4,128)S(1)} fusion(f32[2,4,128]{2,1,0:T(4,128)} %param.12, f32[128,4,128]{2,1,0:T(4,128)} %bitcast.16), kind=kLoop, calls=%fused_computation.1 | loop fusion | flops 66560 | bytes 532480 | tf_op jit(solution)/shard_map/concatenate | solution.py:593
  2.2 4.1 %collective-permute-start.1 = (bf16[272,128]{1,0:T(8,128)(2,1)S(1)}, bf16[272,128]{1,0:T(8,128)(2,1)S(1)}, u32[]{:S(2)}, u32[]{:S(2)}) collective-permute-start(bf16[272,128]{1,0:T(8,128)(2,1)S(1)} %get-tuple-element.53), channel_id=1, source_target_pairs={{1,0},{2,1},{3,2},{4,3},{5,4},{6,5},{7,6},{0,7},{9,8},{10,9},{11,1... | collective-permute-start | bytes 208904 | tf_op jit(solution)/shard_map/ppermute | solution.py:582
  7.0 1.8 %constant_dynamic-update-slice_fusion.1 = bf16[1024,1152]{1,0:T(8,128)(2,1)S(1)} fusion(bf16[1024,1024]{1,0:T(8,128)(2,1)} %param.18), kind=kLoop, calls=%fused_computation.3 | loop fusion | bytes 4194304
  9.0 0.8 %shard_map.138 = (f32[3,128,128]{2,1,0:T(8,128)S(1)}, f32[32,384]{1,0:T(8,128)S(1)}, f32[32,384]{1,0:T(8,128)S(1)}, f32[32,384]{1,0:T(8,128)S(1)}) custom-call(s32[1,1]{1,0:T(1,128)S(6)} %copy.26.count_ref, f32[640,128]{1,0:T(8,128)S(1)} %bitcast.14, s32[3,128]{1,0:T(4,128)S(1)} %get-tuple-element.100.cols_ref, s32[3,128]{1,0:T(4,128)S(1)} %get-tuple-element.99.mask_ref), custom_call_target="tpu_custom_call" | custom-call | bytes 30000000 | tf_op jit(solution)/shard_map/pallas_call | solution.py:27
  9.9 4.0 %shard_map.139 = (f32[4,128,128]{2,1,0:T(8,128)S(1)}, bf16[128,384]{1,0:T(8,128)(2,1)S(1)}, bf16[1024,384]{1,0:T(8,128)(2,1)}, bf16[1024,384]{1,0:T(8,128)(2,1)S...) custom-call(f32[520,128]{1,0:T(8,128)S(1)} %bitcast.12, ...), custom_call_target="tpu_custom_call" | custom-call | bytes 15000000 | tf_op jit(solution)/shard_map/pallas_call | solution.py:27
  13.8 2.1 %shard_map.140 = (bf16[1024,384]{1,0:T(8,128)(2,1)S(1)}, bf16[512,256]{1,0:T(8,128)(2,1)S(1)}, bf16[512,256]{1,0:T(8,128)(2,1)S(1)}) custom-call(bf16[128,384]{1,0:T(8,128)(2,1)S(1)} %get-tuple-element.57.x_ref, bf16[1024,384]{1,0:T(8,128)(2,1)S(1)} %get-tuple-element.72.act_two_ref, bf16[1024,384]{1,0:T(8,128)(2,1)S(1)} %get-tuple-element.59.delta_two_ref, ...), custom_call_target="tpu_custom_call" | custom-call | bytes 4000000 | tf_op jit(solution)/shard_map/pallas_call | solution.py:27
  17.9 2.0 %collective-permute-start.4 = (bf16[128,1280]{1,0:T(8,128)(2,1)S(1)}, bf16[128,1280]{1,0:T(8,128)(2,1)S(1)}, u32[]{:S(2)}, u32[]{:S(2)}) collective-permute-start(bf16[128,1280]{1,0:T(8,128)(2,1)S(1)} %get-tuple-element.65), channel_id=1, source_target_pairs={{0,8},{1,17},{2,10},{3,19},{4,12},{5,21},{6,14},{7,23},{8,0},{9,25... | collective-permute-start | bytes 983048 | tf_op jit(solution)/shard_map/ppermute | solution.py:515
  20.0 3.4 %collective-permute-start.6 = (bf16[256,128]{1,0:T(8,128)(2,1)S(1)}, bf16[256,128]{1,0:T(8,128)(2,1)S(1)}, u32[]{:S(2)}, u32[]{:S(2)}) collective-permute-start(bf16[256,128]{1,0:T(8,128)(2,1)S(1)} %get-tuple-element.77), channel_id=1, source_target_pairs={{1,0},{2,1},{3,2},{4,3},{5,4},{6,5},{7,6},{0,7},{9,8},{10,9},{11,1... | collective-permute-start | bytes 196616 | tf_op jit(solution)/shard_map/ppermute | solution.py:582
  23.6 1.6 %shard_map.143 = f32[512,128]{1,0:T(8,128)} custom-call(s32[1,1]{1,0:T(1,128)S(6)} %copy.26.count_ref, f32[4,128,128]{2,1,0:T(8,128)S(1)} %get-tuple-element.66.moved_ref, s32[3,128]{1,0:T(4,128)S(1)} %get-tuple-element.100.cols_ref, s32[3,128]{1,0:T(4,128)S(1)} %get-tuple-element.99.mask_ref, bf16[128,384]{1,0:T(8,128)(2,1)S(1)} %get-tuple-element.57.x_ref, ...), custom_call_target="tpu_custom_call" | custom-call | tf_op jit(solution)/shard_map/pallas_call | solution.py:27
  25.5 1.7 %collective-permute-start.8 = (bf16[128,1280]{1,0:T(8,128)(2,1)S(1)}, bf16[128,1280]{1,0:T(8,128)(2,1)S(1)}, u32[]{:S(2)}, u32[]{:S(2)}) collective-permute-start(bf16[128,1280]{1,0:T(8,128)(2,1)S(1)} %shard_map.144), channel_id=1, source_target_pairs={{0,16},{1,9},{2,18},{3,11},{4,20},{5,13},{6,22},{7,15},{8,24},{9,1... | collective-permute-start | bytes 983048 | tf_op jit(solution)/shard_map/ppermute | solution.py:515
  27.3 1.5 %shard_map.145 = f32[512,128]{1,0:T(8,128)} custom-call(f32[4,128,128]{2,1,0:T(8,128)S(1)} %get-tuple-element.80.field_ref, bf16[256,128]{1,0:T(8,128)(2,1)S(1)} %collective-permute-done.5.low_ref, bf16[256,128]{1,0:T(8,128)(2,1)S(1)} %collective-permute-done.6.high_ref, bf16[272,128]{1,0:T(8,128)(2,1)S(1)} %collective-permute-done.low_ref.low_mix_ref, ...), custom_call_target="tpu_custom_call" | custom-call | tf_op jit(solution)/shard_map/pallas_call | solution.py:27
  28.7 4.9 %collective-permute-done.7.refs_1_ = bf16[128,1280]{1,0:T(8,128)(2,1)S(1)} collective-permute-done((bf16[128,1280]{1,0:T(8,128)(2,1)S(1)}, bf16[128,1280]{1,0:T(8,128)(2,1)S(1)}, u32[]{:S(2)}, u32[]{:S(2)}) %collective-permute-start.7) | collective-permute-done | bytes 327712 | tf_op jit(solution)/shard_map/ppermute | solution.py:515
  33.7 1.0 %collective-permute-start.9 = (bf16[32,1280]{1,0:T(8,128)(2,1)S(1)}, bf16[32,1280]{1,0:T(8,128)(2,1)S(1)}, u32[]{:S(2)}, u32[]{:S(2)}) collective-permute-start(bf16[32,1280]{1,0:T(8,128)(2,1)S(1)} %get-tuple-element.88), channel_id=1, source_target_pairs={{0,6},{1,3},{2,4},{3,1},{4,2},{5,7},{6,0},{7,5},{8,14},{9,11},{10,... | collective-permute-start | bytes 245768 | tf_op jit(solution)/shard_map/ppermute | solution.py:555
  34.8 3.4 %collective-permute-start.11 = (bf16[32,1280]{1,0:T(8,128)(2,1)S(1)}, bf16[32,1280]{1,0:T(8,128)(2,1)S(1)}, u32[]{:S(2)}, u32[]{:S(2)}) collective-permute-start(bf16[32,1280]{1,0:T(8,128)(2,1)S(1)} %get-tuple-element.90), channel_id=1, source_target_pairs={{0,2},{1,7},{2,0},{3,5},{4,6},{5,3},{6,4},{7,1},{8,10},{9,15},{10,... | collective-permute-start | bytes 245768 | tf_op jit(solution)/shard_map/ppermute | solution.py:555
  38.2 2.8 %collective-permute-done.9.refs_1_ = bf16[32,1280]{1,0:T(8,128)(2,1)S(1)} collective-permute-done((bf16[32,1280]{1,0:T(8,128)(2,1)S(1)}, bf16[32,1280]{1,0:T(8,128)(2,1)S(1)}, u32[]{:S(2)}, u32[]{:S(2)}) %collective-permute-start.9) | collective-permute-done | bytes 81952 | tf_op jit(solution)/shard_map/ppermute | solution.py:555
  41.0 2.7 %collective-permute-done.10.refs_2_ = bf16[32,1280]{1,0:T(8,128)(2,1)S(1)} collective-permute-done((bf16[32,1280]{1,0:T(8,128)(2,1)S(1)}, bf16[32,1280]{1,0:T(8,128)(2,1)S(1)}, u32[]{:S(2)}, u32[]{:S(2)}) %collective-permute-start.10) | collective-permute-done | bytes 81952 | tf_op jit(solution)/shard_map/ppermute | solution.py:555
  43.9 2.2 %collective-permute-start.13 = (bf16[32,1280]{1,0:T(8,128)(2,1)S(1)}, bf16[32,1280]{1,0:T(8,128)(2,1)S(1)}, u32[]{:S(2)}, u32[]{:S(2)}) collective-permute-start(bf16[32,1280]{1,0:T(8,128)(2,1)S(1)} %shard_map.147.refs_0_), channel_id=1, source_target_pairs={{0,4},{1,5},{2,6},{3,7},{4,0},{5,1},{6,2},{7,3},{8,12},{9,13},{10,... | collective-permute-start | bytes 245768 | tf_op jit(solution)/shard_map/ppermute | solution.py:555
  46.1 2.2 %collective-permute-start.12 = (bf16[32,1280]{1,0:T(8,128)(2,1)S(1)}, bf16[32,1280]{1,0:T(8,128)(2,1)S(1)}, u32[]{:S(2)}, u32[]{:S(2)}) collective-permute-start(bf16[32,1280]{1,0:T(8,128)(2,1)S(1)} %shard_map.147.refs_0_), channel_id=1, source_target_pairs={{0,6},{1,3},{2,4},{3,1},{4,2},{5,7},{6,0},{7,5},{8,14},{9,11},{10,... | collective-permute-start | bytes 245768 | tf_op jit(solution)/shard_map/ppermute | solution.py:555
  48.3 2.3 %collective-permute-done.14.refs_3_ = bf16[32,1280]{1,0:T(8,128)(2,1)S(1)} collective-permute-done((bf16[32,1280]{1,0:T(8,128)(2,1)S(1)}, bf16[32,1280]{1,0:T(8,128)(2,1)S(1)}, u32[]{:S(2)}, u32[]{:S(2)}) %collective-permute-start.14) | collective-permute-done | bytes 81952 | tf_op jit(solution)/shard_map/ppermute | solution.py:555
  50.5 0.6 collective-permute-done.13.refs_2_
  51.2 1.3 %collective-permute-done.12.refs_1_ = bf16[32,1280]{1,0:T(8,128)(2,1)S(1)} collective-permute-done((bf16[32,1280]{1,0:T(8,128)(2,1)S(1)}, bf16[32,1280]{1,0:T(8,128)(2,1)S(1)}, u32[]{:S(2)}, u32[]{:S(2)}) %collective-permute-start.12) | collective-permute-done | bytes 81952 | tf_op jit(solution)/shard_map/ppermute | solution.py:555
  52.5 1.3 %collective-permute-start.15 = (bf16[128,640]{1,0:T(8,128)(2,1)S(1)}, bf16[128,640]{1,0:T(8,128)(2,1)S(1)}, u32[]{:S(2)}, u32[]{:S(2)}) collective-permute-start(bf16[128,640]{1,0:T(8,128)(2,1)S(1)} %get-tuple-element.91.refs_0_), channel_id=1, source_target_pairs={{0,8},{8,0},{16,24},{24,16},{1,9},{9,1},{17,25},{25,17},{2,10},{10... | collective-permute-start | bytes 491528 | tf_op jit(solution)/shard_map/ppermute | solution.py:504
  53.8 1.6 %collective-permute-start.19 = (bf16[128,640]{1,0:T(8,128)(2,1)S(1)}, bf16[128,640]{1,0:T(8,128)(2,1)S(1)}, u32[]{:S(2)}, u32[]{:S(2)}) collective-permute-start(bf16[128,640]{1,0:T(8,128)(2,1)S(1)} %get-tuple-element.92.refs_4_), channel_id=1, source_target_pairs={{0,16},{8,24},{16,0},{24,8},{1,17},{9,25},{17,1},{25,9},{2,18},{10... | collective-permute-start | bytes 491528 | tf_op jit(solution)/shard_map/ppermute | solution.py:504
  55.8 0.7 %collective-permute-start.18 = (bf16[128,640]{1,0:T(8,128)(2,1)S(1)}, bf16[128,640]{1,0:T(8,128)(2,1)S(1)}, u32[]{:S(2)}, u32[]{:S(2)}) collective-permute-start(bf16[128,640]{1,0:T(8,128)(2,1)S(1)} %get-tuple-element.92.refs_4_), channel_id=1, source_target_pairs={{0,8},{8,0},{16,24},{24,16},{1,9},{9,1},{17,25},{25,17},{2,10},{10... | collective-permute-start | bytes 491528 | tf_op jit(solution)/shard_map/ppermute | solution.py:504
  56.6 2.3 %collective-permute-done.15.refs_1_ = bf16[128,640]{1,0:T(8,128)(2,1)S(1)} collective-permute-done((bf16[128,640]{1,0:T(8,128)(2,1)S(1)}, bf16[128,640]{1,0:T(8,128)(2,1)S(1)}, u32[]{:S(2)}, u32[]{:S(2)}) %collective-permute-start.15) | collective-permute-done | bytes 163872 | tf_op jit(solution)/shard_map/ppermute | solution.py:504
  58.9 2.4 %collective-permute-start.17 = (bf16[128,640]{1,0:T(8,128)(2,1)S(1)}, bf16[128,640]{1,0:T(8,128)(2,1)S(1)}, u32[]{:S(2)}, u32[]{:S(2)}) collective-permute-start(bf16[128,640]{1,0:T(8,128)(2,1)S(1)} %collective-permute-done.15.refs_1_), channel_id=1, source_target_pairs={{0,16},{8,24},{16,0},{24,8},{1,17},{9,25},{17,1},{25,9},{2,18},{10... | collective-permute-start | bytes 491528 | tf_op jit(solution)/shard_map/ppermute | solution.py:504
  61.2 1.2 %collective-permute-start.20 = (bf16[128,640]{1,0:T(8,128)(2,1)S(1)}, bf16[128,640]{1,0:T(8,128)(2,1)S(1)}, u32[]{:S(2)}, u32[]{:S(2)}) collective-permute-start(bf16[128,640]{1,0:T(8,128)(2,1)S(1)} %collective-permute-done.19.refs_6_), channel_id=1, source_target_pairs={{0,8},{8,0},{16,24},{24,16},{1,9},{9,1},{17,25},{25,17},{2,10},{10... | collective-permute-start | bytes 491528 | tf_op jit(solution)/shard_map/ppermute | solution.py:504
  62.7 1.9 %collective-permute-done.17.refs_3_ = bf16[128,640]{1,0:T(8,128)(2,1)S(1)} collective-permute-done((bf16[128,640]{1,0:T(8,128)(2,1)S(1)}, bf16[128,640]{1,0:T(8,128)(2,1)S(1)}, u32[]{:S(2)}, u32[]{:S(2)}) %collective-permute-start.17) | collective-permute-done | bytes 163872 | tf_op jit(solution)/shard_map/ppermute | solution.py:504
  64.5 2.0 %collective-permute-done.20.refs_7_ = bf16[128,640]{1,0:T(8,128)(2,1)S(1)} collective-permute-done((bf16[128,640]{1,0:T(8,128)(2,1)S(1)}, bf16[128,640]{1,0:T(8,128)(2,1)S(1)}, u32[]{:S(2)}, u32[]{:S(2)}) %collective-permute-start.20) | collective-permute-done | bytes 163872 | tf_op jit(solution)/shard_map/ppermute | solution.py:504
  66.8 1.8 %shard_map.150 = (f32[1024,1024]{1,0:T(8,128)}, f32[1024,128]{1,0:T(8,128)}, f32[128,1024]{1,0:T(8,128)}) custom-call(bf16[512,1280]{1,0:T(8,128)(2,1)S(1)} %shard_map.149.mid_half.small_half, bf16[512,1280]{1,0:T(8,128)(2,1)S(1)} %shard_map.149.mid_half.small_half), custom_call_target="tpu_custom_call" | custom-call | tf_op jit(solution)/shard_map/pallas_call | solution.py:476
  68.6 1.2 %collective-permute-done.21.mid_half.small_half = bf16[512,1280]{1,0:T(8,128)(2,1)S(1)} collective-permute-done((bf16[512,1280]{1,0:T(8,128)(2,1)S(1)}, bf16[512,1280]{1,0:T(8,128)(2,1)S(1)}, u32[]{:S(2)}, u32[]{:S(2)}) %collective-permute-start.21) | collective-permute-done | bytes 1310752 | tf_op jit(solution)/shard_map/ppermute | solution.py:504
  69.8 1.8 %shard_map.151 = (f32[1024,1024]{1,0:T(8,128)}, f32[1024,128]{1,0:T(8,128)}, f32[128,1024]{1,0:T(8,128)}) custom-call(bf16[512,1280]{1,0:T(8,128)(2,1)S(1)} %collective-permute-done.21.mid_half.small_half, bf16[512,1280]{1,0:T(8,128)(2,1)S(1)} %collective-permute-done.21.mid_half.small_half, ...), custom_call_target="tpu_custom_call", output_to_operand_aliasing={{0}: (2, {}), {1}: (3, {}), {2}: (4, {})} | custom-call | tf_op jit(solution)/shard_map/pallas_call | solution.py:476
  (44 shorter events, 4.6 us)
Async XLA Ops:
  1.7 7.2 %copy-start.4 = (s32[1,1,3,128]{3,1,2,0:T(1,128)S(1)}, s32[1,1,3,128]{3,1,2,0:T(1,128)}, u32[]{:S(2)}) copy-start(s32[1,1,3,128]{3,1,2,0:T(1,128)} %param.15) | copy-start | bytes 4612
  1.7 7.2 %copy-start.5 = (s32[1,1,3,128]{3,1,2,0:T(1,128)S(1)}, s32[1,1,3,128]{3,1,2,0:T(1,128)}, u32[]{:S(2)}) copy-start(s32[1,1,3,128]{3,1,2,0:T(1,128)} %param.14) | copy-start | bytes 4612
  1.7 7.2 %copy-start.1 = (f32[1,128,4,128]{3,2,1,0:T(4,128)S(1)}, f32[1,128,4,128]{3,2,1,0:T(4,128)}, u32[]{:S(2)}) copy-start(f32[1,128,4,128]{3,2,1,0:T(4,128)} %param.13) | copy-start | bytes 786436
  1.7 7.2 %copy-start.3 = (f32[1,32,4,128]{3,2,1,0:T(4,128)S(1)}, f32[1,32,4,128]{3,2,1,0:T(4,128)}, u32[]{:S(2)}) copy-start(f32[1,32,4,128]{3,2,1,0:T(4,128)} %param.11) | copy-start | bytes 196612
  1.7 8.1 %collective-permute-start = (bf16[272,128]{1,0:T(8,128)(2,1)S(1)}, bf16[272,128]{1,0:T(8,128)(2,1)S(1)}, u32[]{:S(2)}, u32[]{:S(2)}) collective-permute-start(bf16[272,128]{1,0:T(8,128)(2,1)S(1)} %get-tuple-element.52), channel_id=1, source_target_pairs={{0,1},{1,2},{2,3},{3,4},{4,5},{5,6},{6,7},{7,0},{8,9},{9,10},{10,1... | collective-permute-start | bytes 208904 | tf_op jit(solution)/shard_map/ppermute | solution.py:582
  2.2 7.6 %collective-permute-start.1 = (bf16[272,128]{1,0:T(8,128)(2,1)S(1)}, bf16[272,128]{1,0:T(8,128)(2,1)S(1)}, u32[]{:S(2)}, u32[]{:S(2)}) collective-permute-start(bf16[272,128]{1,0:T(8,128)(2,1)S(1)} %get-tuple-element.53), channel_id=1, source_target_pairs={{1,0},{2,1},{3,2},{4,3},{5,4},{6,5},{7,6},{0,7},{9,8},{10,9},{11,1... | collective-permute-start | bytes 208904 | tf_op jit(solution)/shard_map/ppermute | solution.py:582
  7.0 2.7 %copy-start.2 = (bf16[1024,128]{1,0:T(8,128)(2,1)S(1)}, bf16[1024,128]{1,0:T(8,128)(2,1)}, u32[]{:S(2)}) copy-start(bf16[1024,128]{1,0:T(8,128)(2,1)} %param.17) | copy-start | bytes 786436
  7.0 2.8 %copy-start = (bf16[128,1024]{1,0:T(8,128)(2,1)S(1)}, bf16[128,1024]{1,0:T(8,128)(2,1)}, u32[]{:S(2)}) copy-start(bf16[128,1024]{1,0:T(8,128)(2,1)} %w_out_ref.3) | copy-start | bytes 786436
  13.8 3.8 %collective-permute-start.2 = (bf16[512,1024]{1,0:T(8,128)(2,1)S(1)}, bf16[512,1024]{1,0:T(8,128)(2,1)S(1)}, u32[]{:S(2)}, u32[]{:S(2)}) collective-permute-start(bf16[512,1024]{1,0:T(8,128)(2,1)S(1)} %get-tuple-element.56), channel_id=1, source_target_pairs={{0,1},{1,0},{2,3},{3,2},{4,5},{5,4},{6,7},{7,6},{8,9},{9,8},{10,11... | collective-permute-start | bytes 3145736 | tf_op jit(solution)/shard_map/ppermute | solution.py:504
  15.9 1.7 %collective-permute-start.3 = (bf16[512,256]{1,0:T(8,128)(2,1)S(1)}, bf16[512,256]{1,0:T(8,128)(2,1)S(1)}, u32[]{:S(2)}, u32[]{:S(2)}) collective-permute-start(bf16[512,256]{1,0:T(8,128)(2,1)S(1)} %get-tuple-element.61), channel_id=1, source_target_pairs={{0,1},{1,0},{2,3},{3,2},{4,5},{5,4},{6,7},{7,6},{8,9},{9,8},{10,11... | collective-permute-start | bytes 786440 | tf_op jit(solution)/shard_map/ppermute | solution.py:504
  17.9 7.5 %collective-permute-start.4 = (bf16[128,1280]{1,0:T(8,128)(2,1)S(1)}, bf16[128,1280]{1,0:T(8,128)(2,1)S(1)}, u32[]{:S(2)}, u32[]{:S(2)}) collective-permute-start(bf16[128,1280]{1,0:T(8,128)(2,1)S(1)} %get-tuple-element.65), channel_id=1, source_target_pairs={{0,8},{1,17},{2,10},{3,19},{4,12},{5,21},{6,14},{7,23},{8,0},{9,25... | collective-permute-start | bytes 983048 | tf_op jit(solution)/shard_map/ppermute | solution.py:515
  19.9 5.5 %collective-permute-start.5 = (bf16[256,128]{1,0:T(8,128)(2,1)S(1)}, bf16[256,128]{1,0:T(8,128)(2,1)S(1)}, u32[]{:S(2)}, u32[]{:S(2)}) collective-permute-start(bf16[256,128]{1,0:T(8,128)(2,1)S(1)} %get-tuple-element.76), channel_id=1, source_target_pairs={{0,1},{1,2},{2,3},{3,4},{4,5},{5,6},{6,7},{7,0},{8,9},{9,10},{10,1... | collective-permute-start | bytes 196616 | tf_op jit(solution)/shard_map/ppermute | solution.py:582
  20.0 5.4 %collective-permute-start.6 = (bf16[256,128]{1,0:T(8,128)(2,1)S(1)}, bf16[256,128]{1,0:T(8,128)(2,1)S(1)}, u32[]{:S(2)}, u32[]{:S(2)}) collective-permute-start(bf16[256,128]{1,0:T(8,128)(2,1)S(1)} %get-tuple-element.77), channel_id=1, source_target_pairs={{1,0},{2,1},{3,2},{4,3},{5,4},{6,5},{7,6},{0,7},{9,8},{10,9},{11,1... | collective-permute-start | bytes 196616 | tf_op jit(solution)/shard_map/ppermute | solution.py:582
  23.5 10.1 %collective-permute-start.7 = (bf16[128,1280]{1,0:T(8,128)(2,1)S(1)}, bf16[128,1280]{1,0:T(8,128)(2,1)S(1)}, u32[]{:S(2)}, u32[]{:S(2)}) collective-permute-start(bf16[128,1280]{1,0:T(8,128)(2,1)S(1)} %get-tuple-element.70), channel_id=1, source_target_pairs={{0,8},{1,17},{2,10},{3,19},{4,12},{5,21},{6,14},{7,23},{8,0},{9,25... | collective-permute-start | bytes 983048 | tf_op jit(solution)/shard_map/ppermute | solution.py:515
  25.5 8.1 %collective-permute-start.8 = (bf16[128,1280]{1,0:T(8,128)(2,1)S(1)}, bf16[128,1280]{1,0:T(8,128)(2,1)S(1)}, u32[]{:S(2)}, u32[]{:S(2)}) collective-permute-start(bf16[128,1280]{1,0:T(8,128)(2,1)S(1)} %shard_map.144), channel_id=1, source_target_pairs={{0,16},{1,9},{2,18},{3,11},{4,20},{5,13},{6,22},{7,15},{8,24},{9,1... | collective-permute-start | bytes 983048 | tf_op jit(solution)/shard_map/ppermute | solution.py:515
  33.7 7.3 %collective-permute-start.9 = (bf16[32,1280]{1,0:T(8,128)(2,1)S(1)}, bf16[32,1280]{1,0:T(8,128)(2,1)S(1)}, u32[]{:S(2)}, u32[]{:S(2)}) collective-permute-start(bf16[32,1280]{1,0:T(8,128)(2,1)S(1)} %get-tuple-element.88), channel_id=1, source_target_pairs={{0,6},{1,3},{2,4},{3,1},{4,2},{5,7},{6,0},{7,5},{8,14},{9,11},{10,... | collective-permute-start | bytes 245768 | tf_op jit(solution)/shard_map/ppermute | solution.py:555
  34.8 9.0 %collective-permute-start.10 = (bf16[32,1280]{1,0:T(8,128)(2,1)S(1)}, bf16[32,1280]{1,0:T(8,128)(2,1)S(1)}, u32[]{:S(2)}, u32[]{:S(2)}) collective-permute-start(bf16[32,1280]{1,0:T(8,128)(2,1)S(1)} %get-tuple-element.89), channel_id=1, source_target_pairs={{0,4},{1,5},{2,6},{3,7},{4,0},{5,1},{6,2},{7,3},{8,12},{9,13},{10,... | collective-permute-start | bytes 245768 | tf_op jit(solution)/shard_map/ppermute | solution.py:555
  34.8 9.0 %collective-permute-start.11 = (bf16[32,1280]{1,0:T(8,128)(2,1)S(1)}, bf16[32,1280]{1,0:T(8,128)(2,1)S(1)}, u32[]{:S(2)}, u32[]{:S(2)}) collective-permute-start(bf16[32,1280]{1,0:T(8,128)(2,1)S(1)} %get-tuple-element.90), channel_id=1, source_target_pairs={{0,2},{1,7},{2,0},{3,5},{4,6},{5,3},{6,4},{7,1},{8,10},{9,15},{10,... | collective-permute-start | bytes 245768 | tf_op jit(solution)/shard_map/ppermute | solution.py:555
  43.8 6.7 %collective-permute-start.14 = (bf16[32,1280]{1,0:T(8,128)(2,1)S(1)}, bf16[32,1280]{1,0:T(8,128)(2,1)S(1)}, u32[]{:S(2)}, u32[]{:S(2)}) collective-permute-start(bf16[32,1280]{1,0:T(8,128)(2,1)S(1)} %shard_map.147.refs_0_), channel_id=1, source_target_pairs={{0,2},{1,7},{2,0},{3,5},{4,6},{5,3},{6,4},{7,1},{8,10},{9,15},{10,... | collective-permute-start | bytes 245768 | tf_op jit(solution)/shard_map/ppermute | solution.py:555
  43.9 7.3 %collective-permute-start.13 = (bf16[32,1280]{1,0:T(8,128)(2,1)S(1)}, bf16[32,1280]{1,0:T(8,128)(2,1)S(1)}, u32[]{:S(2)}, u32[]{:S(2)}) collective-permute-start(bf16[32,1280]{1,0:T(8,128)(2,1)S(1)} %shard_map.147.refs_0_), channel_id=1, source_target_pairs={{0,4},{1,5},{2,6},{3,7},{4,0},{5,1},{6,2},{7,3},{8,12},{9,13},{10,... | collective-permute-start | bytes 245768 | tf_op jit(solution)/shard_map/ppermute | solution.py:555
  46.1 6.3 %collective-permute-start.12 = (bf16[32,1280]{1,0:T(8,128)(2,1)S(1)}, bf16[32,1280]{1,0:T(8,128)(2,1)S(1)}, u32[]{:S(2)}, u32[]{:S(2)}) collective-permute-start(bf16[32,1280]{1,0:T(8,128)(2,1)S(1)} %shard_map.147.refs_0_), channel_id=1, source_target_pairs={{0,6},{1,3},{2,4},{3,1},{4,2},{5,7},{6,0},{7,5},{8,14},{9,11},{10,... | collective-permute-start | bytes 245768 | tf_op jit(solution)/shard_map/ppermute | solution.py:555
  52.5 6.4 %collective-permute-start.15 = (bf16[128,640]{1,0:T(8,128)(2,1)S(1)}, bf16[128,640]{1,0:T(8,128)(2,1)S(1)}, u32[]{:S(2)}, u32[]{:S(2)}) collective-permute-start(bf16[128,640]{1,0:T(8,128)(2,1)S(1)} %get-tuple-element.91.refs_0_), channel_id=1, source_target_pairs={{0,8},{8,0},{16,24},{24,16},{1,9},{9,1},{17,25},{25,17},{2,10},{10... | collective-permute-start | bytes 491528 | tf_op jit(solution)/shard_map/ppermute | solution.py:504
  53.8 7.4 %collective-permute-start.19 = (bf16[128,640]{1,0:T(8,128)(2,1)S(1)}, bf16[128,640]{1,0:T(8,128)(2,1)S(1)}, u32[]{:S(2)}, u32[]{:S(2)}) collective-permute-start(bf16[128,640]{1,0:T(8,128)(2,1)S(1)} %get-tuple-element.92.refs_4_), channel_id=1, source_target_pairs={{0,16},{8,24},{16,0},{24,8},{1,17},{9,25},{17,1},{25,9},{2,18},{10... | collective-permute-start | bytes 491528 | tf_op jit(solution)/shard_map/ppermute | solution.py:504
  55.4 7.3 %collective-permute-start.16 = (bf16[128,640]{1,0:T(8,128)(2,1)S(1)}, bf16[128,640]{1,0:T(8,128)(2,1)S(1)}, u32[]{:S(2)}, u32[]{:S(2)}) collective-permute-start(bf16[128,640]{1,0:T(8,128)(2,1)S(1)} %get-tuple-element.91.refs_0_), channel_id=1, source_target_pairs={{0,16},{8,24},{16,0},{24,8},{1,17},{9,25},{17,1},{25,9},{2,18},{10... | collective-permute-start | bytes 491528 | tf_op jit(solution)/shard_map/ppermute | solution.py:504
  55.8 6.8 %collective-permute-start.18 = (bf16[128,640]{1,0:T(8,128)(2,1)S(1)}, bf16[128,640]{1,0:T(8,128)(2,1)S(1)}, u32[]{:S(2)}, u32[]{:S(2)}) collective-permute-start(bf16[128,640]{1,0:T(8,128)(2,1)S(1)} %get-tuple-element.92.refs_4_), channel_id=1, source_target_pairs={{0,8},{8,0},{16,24},{24,16},{1,9},{9,1},{17,25},{25,17},{2,10},{10... | collective-permute-start | bytes 491528 | tf_op jit(solution)/shard_map/ppermute | solution.py:504
  58.9 5.7 %collective-permute-start.17 = (bf16[128,640]{1,0:T(8,128)(2,1)S(1)}, bf16[128,640]{1,0:T(8,128)(2,1)S(1)}, u32[]{:S(2)}, u32[]{:S(2)}) collective-permute-start(bf16[128,640]{1,0:T(8,128)(2,1)S(1)} %collective-permute-done.15.refs_1_), channel_id=1, source_target_pairs={{0,16},{8,24},{16,0},{24,8},{1,17},{9,25},{17,1},{25,9},{2,18},{10... | collective-permute-start | bytes 491528 | tf_op jit(solution)/shard_map/ppermute | solution.py:504
  61.2 5.3 %collective-permute-start.20 = (bf16[128,640]{1,0:T(8,128)(2,1)S(1)}, bf16[128,640]{1,0:T(8,128)(2,1)S(1)}, u32[]{:S(2)}, u32[]{:S(2)}) collective-permute-start(bf16[128,640]{1,0:T(8,128)(2,1)S(1)} %collective-permute-done.19.refs_6_), channel_id=1, source_target_pairs={{0,8},{8,0},{16,24},{24,16},{1,9},{9,1},{17,25},{25,17},{2,10},{10... | collective-permute-start | bytes 491528 | tf_op jit(solution)/shard_map/ppermute | solution.py:504
  66.7 3.1 %collective-permute-start.21 = (bf16[512,1280]{1,0:T(8,128)(2,1)S(1)}, bf16[512,1280]{1,0:T(8,128)(2,1)S(1)}, u32[]{:S(2)}, u32[]{:S(2)}) collective-permute-start(bf16[512,1280]{1,0:T(8,128)(2,1)S(1)} %shard_map.149.mid_half.small_half), channel_id=1, source_target_pairs={{0,1},{1,0},{2,3},{3,2},{4,5},{5,4},{6,7},{7,6},{8,9},{9,8},{10,11... | collective-permute-start | bytes 3932168 | tf_op jit(solution)/shard_map/ppermute | solution.py:504

commit v16 on v15

--- a/solution.py
+++ b/solution.py
@@ -425,7 +425,7 @@
     width = outs[0].shape[1]
     part = min(width, columns)
     for k in range(count):
-        place = partner(stage, k) if stage == CHIPS else position(stage) ^ k
+        place = partner(stage, k) if stage == CHIPS else member_order()[k]
         here = pl.ds(pl.multiple_of(place * rows, rows), rows)
         for group in range(groups):
             for start in range(0, columns, part):
@@ -516,13 +516,13 @@
 
 
 def collect_members(one, two):
-    (low_one,) = exchange([one], MEMBER_LOW)
-    (high_two,) = exchange([two], MEMBER_HIGH)
-    (high_one,) = exchange([one], MEMBER_HIGH)
-    (low_two,) = exchange([two], MEMBER_LOW)
-    (far_one,) = exchange([low_one], MEMBER_HIGH)
-    (far_two,) = exchange([high_two], MEMBER_LOW)
-    return [one, low_one, high_one, far_one], [two, low_two, high_two, far_two]
+    first_one = to_member(one, 0)
+    second_two = to_member(two, 1)
+    second_one = to_member(one, 1)
+    first_two = to_member(two, 0)
+    far_one = to_member(first_one, 1)
+    far_two = to_member(second_two, 0)
+    return [one, first_one, second_one, far_one], [two, first_two, second_two, far_two]
 
 
 def add(terms, stage, factor=1.0):

time: 71.8 us -> 71.9 us (level)
  waiting for transfers between devices: 23.1 us -> 24 us
  starting transfers between devices: 29.1 us -> 28.3 us
    ppermute x9 -> x3, starting transfers between devices: 8.27 us -> 0.63 us  [exchange(): sent[k] = lax.ppermute(arrays[k - 1], axis, route)]
    ppermute x3 -> x9, waiting for transfers between devices: 4.86 us -> 12.2 us  [to_member(): return lax.ppermute(array, ('ens', 'horiz'), route)]
    ppermute x3 -> x9, starting transfers between devices: 3.8 us -> 10.7 us  [to_member(): return lax.ppermute(array, ('ens', 'horiz'), route)]
    ppermute x9 -> x3, waiting for transfers between devices: 8.21 us -> 1.78 us  [exchange(): sent[k] = lax.ppermute(arrays[k - 1], axis, route)]
where the time goes in v16:
time: 71.9 us; the launch traced here: 71.7 us
  starting transfers between devices  28.3 us (39%)
  waiting for transfers between devices  24 us (33%)
  Pallas kernels  14.8 us (21%)
  local copies, waits for them, and re-layouts  1.92 us (3%)
  between operations  1.52 us (2%)
  other arithmetic  1.1 us (2%)
    ppermute x9, waiting for transfers between devices, to_member(): return lax.ppermute(array, ('ens', 'horiz'), route)  12.2 us
    pallas_call x13, Pallas kernels, run(): pl.pallas_call(functools.partial(kernel, **names), out_shape=[jax.ShapeDt...  11.1 us
    ppermute x9, starting transfers between devices, to_member(): return lax.ppermute(array, ('ens', 'horiz'), route)  10.7 us
    ppermute x6, waiting for transfers between devices, to_chips(): received.append(lax.ppermute(array, 'horiz', route))  9.74 us
    ppermute x6, starting transfers between devices, to_chips(): received.append(lax.ppermute(array, 'horiz', route))  8.9 us
    ppermute x2, starting transfers between devices, to_neighbours(): lax.ppermute(downward, axis, backward)  7.52 us
    pallas_call x2, Pallas kernels, final(): pl.pallas_call(final_kernel, grid=(units // block,), out_shape=[jax.Shape...  3.64 us
    unnamed x14, local copies, waits for them, and re-layouts  1.86 us
  transfers between devices with their start and end apart: 22, of which 13 were waited for; matrix products, arithmetic and copies ran while one was open for 3% of the time, Pallas kernels for 12%

profile of v16, /device:TPU:0, one launch (start us, length us, event | category | flops | bytes accessed | tf_op | source)
XLA Modules:
  0.0 71.7 jit_solution(15917434014211767223)
XLA Ops:
  0.6 1.0 %pad_maximum_fusion.1 = f32[130,4,128]{2,1,0:T(4,128)S(1)} fusion(f32[2,4,128]{2,1,0:T(4,128)} %param.12, f32[128,4,128]{2,1,0:T(4,128)} %bitcast.16), kind=kLoop, calls=%fused_computation.1 | loop fusion | flops 66560 | bytes 532480 | tf_op jit(solution)/shard_map/concatenate | solution.py:593
  2.2 4.1 %collective-permute-start.1 = (bf16[272,128]{1,0:T(8,128)(2,1)S(1)}, bf16[272,128]{1,0:T(8,128)(2,1)S(1)}, u32[]{:S(2)}, u32[]{:S(2)}) collective-permute-start(bf16[272,128]{1,0:T(8,128)(2,1)S(1)} %get-tuple-element.53), channel_id=1, source_target_pairs={{1,0},{2,1},{3,2},{4,3},{5,4},{6,5},{7,6},{0,7},{9,8},{10,9},{11,1... | collective-permute-start | bytes 208904 | tf_op jit(solution)/shard_map/ppermute | solution.py:582
  7.0 1.8 %constant_dynamic-update-slice_fusion.1 = bf16[1024,1152]{1,0:T(8,128)(2,1)S(1)} fusion(bf16[1024,1024]{1,0:T(8,128)(2,1)} %param.18), kind=kLoop, calls=%fused_computation.3 | loop fusion | bytes 4194304
  9.0 0.8 %shard_map.138 = (f32[3,128,128]{2,1,0:T(8,128)S(1)}, f32[32,384]{1,0:T(8,128)S(1)}, f32[32,384]{1,0:T(8,128)S(1)}, f32[32,384]{1,0:T(8,128)S(1)}) custom-call(s32[1,1]{1,0:T(1,128)S(6)} %copy.26.count_ref, f32[640,128]{1,0:T(8,128)S(1)} %bitcast.14, s32[3,128]{1,0:T(4,128)S(1)} %get-tuple-element.100.cols_ref, s32[3,128]{1,0:T(4,128)S(1)} %get-tuple-element.99.mask_ref), custom_call_target="tpu_custom_call" | custom-call | bytes 30000000 | tf_op jit(solution)/shard_map/pallas_call | solution.py:27
  9.9 4.0 %shard_map.139 = (f32[4,128,128]{2,1,0:T(8,128)S(1)}, bf16[128,384]{1,0:T(8,128)(2,1)S(1)}, bf16[1024,384]{1,0:T(8,128)(2,1)}, bf16[1024,384]{1,0:T(8,128)(2,1)S...) custom-call(f32[520,128]{1,0:T(8,128)S(1)} %bitcast.12, ...), custom_call_target="tpu_custom_call" | custom-call | bytes 15000000 | tf_op jit(solution)/shard_map/pallas_call | solution.py:27
  13.8 2.1 %shard_map.140 = (bf16[1024,384]{1,0:T(8,128)(2,1)S(1)}, bf16[512,256]{1,0:T(8,128)(2,1)S(1)}, bf16[512,256]{1,0:T(8,128)(2,1)S(1)}) custom-call(bf16[128,384]{1,0:T(8,128)(2,1)S(1)} %get-tuple-element.57.x_ref, bf16[1024,384]{1,0:T(8,128)(2,1)S(1)} %get-tuple-element.72.act_two_ref, bf16[1024,384]{1,0:T(8,128)(2,1)S(1)} %get-tuple-element.59.delta_two_ref, ...), custom_call_target="tpu_custom_call" | custom-call | bytes 4000000 | tf_op jit(solution)/shard_map/pallas_call | solution.py:27
  17.9 2.0 %collective-permute-start.4 = (bf16[128,1280]{1,0:T(8,128)(2,1)S(1)}, bf16[128,1280]{1,0:T(8,128)(2,1)S(1)}, u32[]{:S(2)}, u32[]{:S(2)}) collective-permute-start(bf16[128,1280]{1,0:T(8,128)(2,1)S(1)} %get-tuple-element.65), channel_id=1, source_target_pairs={{0,8},{1,17},{2,10},{3,19},{4,12},{5,21},{6,14},{7,23},{8,0},{9,25... | collective-permute-start | bytes 983048 | tf_op jit(solution)/shard_map/ppermute | solution.py:515
  20.0 3.4 %collective-permute-start.6 = (bf16[256,128]{1,0:T(8,128)(2,1)S(1)}, bf16[256,128]{1,0:T(8,128)(2,1)S(1)}, u32[]{:S(2)}, u32[]{:S(2)}) collective-permute-start(bf16[256,128]{1,0:T(8,128)(2,1)S(1)} %get-tuple-element.77), channel_id=1, source_target_pairs={{1,0},{2,1},{3,2},{4,3},{5,4},{6,5},{7,6},{0,7},{9,8},{10,9},{11,1... | collective-permute-start | bytes 196616 | tf_op jit(solution)/shard_map/ppermute | solution.py:582
  23.6 1.6 %shard_map.143 = f32[512,128]{1,0:T(8,128)} custom-call(s32[1,1]{1,0:T(1,128)S(6)} %copy.26.count_ref, f32[4,128,128]{2,1,0:T(8,128)S(1)} %get-tuple-element.66.moved_ref, s32[3,128]{1,0:T(4,128)S(1)} %get-tuple-element.100.cols_ref, s32[3,128]{1,0:T(4,128)S(1)} %get-tuple-element.99.mask_ref, bf16[128,384]{1,0:T(8,128)(2,1)S(1)} %get-tuple-element.57.x_ref, ...), custom_call_target="tpu_custom_call" | custom-call | tf_op jit(solution)/shard_map/pallas_call | solution.py:27
  25.5 1.7 %collective-permute-start.8 = (bf16[128,1280]{1,0:T(8,128)(2,1)S(1)}, bf16[128,1280]{1,0:T(8,128)(2,1)S(1)}, u32[]{:S(2)}, u32[]{:S(2)}) collective-permute-start(bf16[128,1280]{1,0:T(8,128)(2,1)S(1)} %shard_map.144), channel_id=1, source_target_pairs={{0,16},{1,9},{2,18},{3,11},{4,20},{5,13},{6,22},{7,15},{8,24},{9,1... | collective-permute-start | bytes 983048 | tf_op jit(solution)/shard_map/ppermute | solution.py:515
  27.3 1.5 %shard_map.145 = f32[512,128]{1,0:T(8,128)} custom-call(f32[4,128,128]{2,1,0:T(8,128)S(1)} %get-tuple-element.80.field_ref, bf16[256,128]{1,0:T(8,128)(2,1)S(1)} %collective-permute-done.5.low_ref, bf16[256,128]{1,0:T(8,128)(2,1)S(1)} %collective-permute-done.6.high_ref, bf16[272,128]{1,0:T(8,128)(2,1)S(1)} %collective-permute-done.low_ref.low_mix_ref, ...), custom_call_target="tpu_custom_call" | custom-call | tf_op jit(solution)/shard_map/pallas_call | solution.py:27
  28.7 4.9 %collective-permute-done.7.refs_1_ = bf16[128,1280]{1,0:T(8,128)(2,1)S(1)} collective-permute-done((bf16[128,1280]{1,0:T(8,128)(2,1)S(1)}, bf16[128,1280]{1,0:T(8,128)(2,1)S(1)}, u32[]{:S(2)}, u32[]{:S(2)}) %collective-permute-start.7) | collective-permute-done | bytes 327712 | tf_op jit(solution)/shard_map/ppermute | solution.py:515
  33.7 1.0 %collective-permute-start.9 = (bf16[32,1280]{1,0:T(8,128)(2,1)S(1)}, bf16[32,1280]{1,0:T(8,128)(2,1)S(1)}, u32[]{:S(2)}, u32[]{:S(2)}) collective-permute-start(bf16[32,1280]{1,0:T(8,128)(2,1)S(1)} %get-tuple-element.88), channel_id=1, source_target_pairs={{0,6},{1,3},{2,4},{3,1},{4,2},{5,7},{6,0},{7,5},{8,14},{9,11},{10,... | collective-permute-start | bytes 245768 | tf_op jit(solution)/shard_map/ppermute | solution.py:555
  34.8 3.4 %collective-permute-start.11 = (bf16[32,1280]{1,0:T(8,128)(2,1)S(1)}, bf16[32,1280]{1,0:T(8,128)(2,1)S(1)}, u32[]{:S(2)}, u32[]{:S(2)}) collective-permute-start(bf16[32,1280]{1,0:T(8,128)(2,1)S(1)} %get-tuple-element.90), channel_id=1, source_target_pairs={{0,2},{1,7},{2,0},{3,5},{4,6},{5,3},{6,4},{7,1},{8,10},{9,15},{10,... | collective-permute-start | bytes 245768 | tf_op jit(solution)/shard_map/ppermute | solution.py:555
  38.2 2.8 %collective-permute-done.9.refs_1_ = bf16[32,1280]{1,0:T(8,128)(2,1)S(1)} collective-permute-done((bf16[32,1280]{1,0:T(8,128)(2,1)S(1)}, bf16[32,1280]{1,0:T(8,128)(2,1)S(1)}, u32[]{:S(2)}, u32[]{:S(2)}) %collective-permute-start.9) | collective-permute-done | bytes 81952 | tf_op jit(solution)/shard_map/ppermute | solution.py:555
  41.0 2.7 %collective-permute-done.10.refs_2_ = bf16[32,1280]{1,0:T(8,128)(2,1)S(1)} collective-permute-done((bf16[32,1280]{1,0:T(8,128)(2,1)S(1)}, bf16[32,1280]{1,0:T(8,128)(2,1)S(1)}, u32[]{:S(2)}, u32[]{:S(2)}) %collective-permute-start.10) | collective-permute-done | bytes 81952 | tf_op jit(solution)/shard_map/ppermute | solution.py:555
  43.9 2.2 %collective-permute-start.13 = (bf16[32,1280]{1,0:T(8,128)(2,1)S(1)}, bf16[32,1280]{1,0:T(8,128)(2,1)S(1)}, u32[]{:S(2)}, u32[]{:S(2)}) collective-permute-start(bf16[32,1280]{1,0:T(8,128)(2,1)S(1)} %shard_map.147.refs_0_), channel_id=1, source_target_pairs={{0,4},{1,5},{2,6},{3,7},{4,0},{5,1},{6,2},{7,3},{8,12},{9,13},{10,... | collective-permute-start | bytes 245768 | tf_op jit(solution)/shard_map/ppermute | solution.py:555
  46.1 2.2 %collective-permute-start.12 = (bf16[32,1280]{1,0:T(8,128)(2,1)S(1)}, bf16[32,1280]{1,0:T(8,128)(2,1)S(1)}, u32[]{:S(2)}, u32[]{:S(2)}) collective-permute-start(bf16[32,1280]{1,0:T(8,128)(2,1)S(1)} %shard_map.147.refs_0_), channel_id=1, source_target_pairs={{0,6},{1,3},{2,4},{3,1},{4,2},{5,7},{6,0},{7,5},{8,14},{9,11},{10,... | collective-permute-start | bytes 245768 | tf_op jit(solution)/shard_map/ppermute | solution.py:555
  48.3 2.3 %collective-permute-done.14.refs_3_ = bf16[32,1280]{1,0:T(8,128)(2,1)S(1)} collective-permute-done((bf16[32,1280]{1,0:T(8,128)(2,1)S(1)}, bf16[32,1280]{1,0:T(8,128)(2,1)S(1)}, u32[]{:S(2)}, u32[]{:S(2)}) %collective-permute-start.14) | collective-permute-done | bytes 81952 | tf_op jit(solution)/shard_map/ppermute | solution.py:555
  51.2 1.3 %collective-permute-done.12.refs_1_ = bf16[32,1280]{1,0:T(8,128)(2,1)S(1)} collective-permute-done((bf16[32,1280]{1,0:T(8,128)(2,1)S(1)}, bf16[32,1280]{1,0:T(8,128)(2,1)S(1)}, u32[]{:S(2)}, u32[]{:S(2)}) %collective-permute-start.12) | collective-permute-done | bytes 81952 | tf_op jit(solution)/shard_map/ppermute | solution.py:555
  52.5 1.3 %collective-permute-start.15 = (bf16[128,640]{1,0:T(8,128)(2,1)S(1)}, bf16[128,640]{1,0:T(8,128)(2,1)S(1)}, u32[]{:S(2)}, u32[]{:S(2)}) collective-permute-start(bf16[128,640]{1,0:T(8,128)(2,1)S(1)} %get-tuple-element.91.refs_0_), channel_id=1, source_target_pairs={{0,8},{1,17},{2,10},{3,19},{4,12},{5,21},{6,14},{7,23},{8,0},{9,25... | collective-permute-start | bytes 491528 | tf_op jit(solution)/shard_map/ppermute | solution.py:515
  53.8 1.5 %collective-permute-start.19 = (bf16[128,640]{1,0:T(8,128)(2,1)S(1)}, bf16[128,640]{1,0:T(8,128)(2,1)S(1)}, u32[]{:S(2)}, u32[]{:S(2)}) collective-permute-start(bf16[128,640]{1,0:T(8,128)(2,1)S(1)} %get-tuple-element.92.refs_4_), channel_id=1, source_target_pairs={{0,16},{1,9},{2,18},{3,11},{4,20},{5,13},{6,22},{7,15},{8,24},{9,1... | collective-permute-start | bytes 491528 | tf_op jit(solution)/shard_map/ppermute | solution.py:515
  55.8 0.7 %collective-permute-start.18 = (bf16[128,640]{1,0:T(8,128)(2,1)S(1)}, bf16[128,640]{1,0:T(8,128)(2,1)S(1)}, u32[]{:S(2)}, u32[]{:S(2)}) collective-permute-start(bf16[128,640]{1,0:T(8,128)(2,1)S(1)} %get-tuple-element.92.refs_4_), channel_id=1, source_target_pairs={{0,8},{1,17},{2,10},{3,19},{4,12},{5,21},{6,14},{7,23},{8,0},{9,25... | collective-permute-start | bytes 491528 | tf_op jit(solution)/shard_map/ppermute | solution.py:515
  56.6 3.1 %collective-permute-done.15.refs_1_ = bf16[128,640]{1,0:T(8,128)(2,1)S(1)} collective-permute-done((bf16[128,640]{1,0:T(8,128)(2,1)S(1)}, bf16[128,640]{1,0:T(8,128)(2,1)S(1)}, u32[]{:S(2)}, u32[]{:S(2)}) %collective-permute-start.15) | collective-permute-done | bytes 163872 | tf_op jit(solution)/shard_map/ppermute | solution.py:515
  59.6 1.7 %collective-permute-start.17 = (bf16[128,640]{1,0:T(8,128)(2,1)S(1)}, bf16[128,640]{1,0:T(8,128)(2,1)S(1)}, u32[]{:S(2)}, u32[]{:S(2)}) collective-permute-start(bf16[128,640]{1,0:T(8,128)(2,1)S(1)} %collective-permute-done.15.refs_1_), channel_id=1, source_target_pairs={{0,16},{1,9},{2,18},{3,11},{4,20},{5,13},{6,22},{7,15},{8,24},{9,1... | collective-permute-start | bytes 491528 | tf_op jit(solution)/shard_map/ppermute | solution.py:515
  61.3 1.0 %collective-permute-start.20 = (bf16[128,640]{1,0:T(8,128)(2,1)S(1)}, bf16[128,640]{1,0:T(8,128)(2,1)S(1)}, u32[]{:S(2)}, u32[]{:S(2)}) collective-permute-start(bf16[128,640]{1,0:T(8,128)(2,1)S(1)} %collective-permute-done.19.refs_6_), channel_id=1, source_target_pairs={{0,8},{1,17},{2,10},{3,19},{4,12},{5,21},{6,14},{7,23},{8,0},{9,25... | collective-permute-start | bytes 491528 | tf_op jit(solution)/shard_map/ppermute | solution.py:515
  62.4 0.9 %collective-permute-done.16.refs_2_ = bf16[128,640]{1,0:T(8,128)(2,1)S(1)} collective-permute-done((bf16[128,640]{1,0:T(8,128)(2,1)S(1)}, bf16[128,640]{1,0:T(8,128)(2,1)S(1)}, u32[]{:S(2)}, u32[]{:S(2)}) %collective-permute-start.16) | collective-permute-done | bytes 163872 | tf_op jit(solution)/shard_map/ppermute | solution.py:515
  63.3 1.8 %collective-permute-done.17.refs_3_ = bf16[128,640]{1,0:T(8,128)(2,1)S(1)} collective-permute-done((bf16[128,640]{1,0:T(8,128)(2,1)S(1)}, bf16[128,640]{1,0:T(8,128)(2,1)S(1)}, u32[]{:S(2)}, u32[]{:S(2)}) %collective-permute-start.17) | collective-permute-done | bytes 163872 | tf_op jit(solution)/shard_map/ppermute | solution.py:515
  65.1 1.6 %collective-permute-done.20.refs_7_ = bf16[128,640]{1,0:T(8,128)(2,1)S(1)} collective-permute-done((bf16[128,640]{1,0:T(8,128)(2,1)S(1)}, bf16[128,640]{1,0:T(8,128)(2,1)S(1)}, u32[]{:S(2)}, u32[]{:S(2)}) %collective-permute-start.20) | collective-permute-done | bytes 163872 | tf_op jit(solution)/shard_map/ppermute | solution.py:515
  66.9 1.8 %shard_map.150 = (f32[1024,1024]{1,0:T(8,128)}, f32[1024,128]{1,0:T(8,128)}, f32[128,1024]{1,0:T(8,128)}) custom-call(bf16[512,1280]{1,0:T(8,128)(2,1)S(1)} %shard_map.149.mid_half.small_half, bf16[512,1280]{1,0:T(8,128)(2,1)S(1)} %shard_map.149.mid_half.small_half), custom_call_target="tpu_custom_call" | custom-call | tf_op jit(solution)/shard_map/pallas_call | solution.py:476
  68.7 1.2 %collective-permute-done.21.mid_half.small_half = bf16[512,1280]{1,0:T(8,128)(2,1)S(1)} collective-permute-done((bf16[512,1280]{1,0:T(8,128)(2,1)S(1)}, bf16[512,1280]{1,0:T(8,128)(2,1)S(1)}, u32[]{:S(2)}, u32[]{:S(2)}) %collective-permute-start.21) | collective-permute-done | bytes 1310752 | tf_op jit(solution)/shard_map/ppermute | solution.py:504
  69.9 1.8 %shard_map.151 = (f32[1024,1024]{1,0:T(8,128)}, f32[1024,128]{1,0:T(8,128)}, f32[128,1024]{1,0:T(8,128)}) custom-call(bf16[512,1280]{1,0:T(8,128)(2,1)S(1)} %collective-permute-done.21.mid_half.small_half, bf16[512,1280]{1,0:T(8,128)(2,1)S(1)} %collective-permute-done.21.mid_half.small_half, ...), custom_call_target="tpu_custom_call", output_to_operand_aliasing={{0}: (2, {}), {1}: (3, {}), {2}: (4, {})} | custom-call | tf_op jit(solution)/shard_map/pallas_call | solution.py:476
  (44 shorter events, 5.0 us)
Async XLA Ops:
  1.7 7.2 %copy-start.4 = (s32[1,1,3,128]{3,1,2,0:T(1,128)S(1)}, s32[1,1,3,128]{3,1,2,0:T(1,128)}, u32[]{:S(2)}) copy-start(s32[1,1,3,128]{3,1,2,0:T(1,128)} %param.15) | copy-start | bytes 4612
  1.7 7.2 %copy-start.5 = (s32[1,1,3,128]{3,1,2,0:T(1,128)S(1)}, s32[1,1,3,128]{3,1,2,0:T(1,128)}, u32[]{:S(2)}) copy-start(s32[1,1,3,128]{3,1,2,0:T(1,128)} %param.14) | copy-start | bytes 4612
  1.7 7.2 %copy-start.1 = (f32[1,128,4,128]{3,2,1,0:T(4,128)S(1)}, f32[1,128,4,128]{3,2,1,0:T(4,128)}, u32[]{:S(2)}) copy-start(f32[1,128,4,128]{3,2,1,0:T(4,128)} %param.13) | copy-start | bytes 786436
  1.7 7.2 %copy-start.3 = (f32[1,32,4,128]{3,2,1,0:T(4,128)S(1)}, f32[1,32,4,128]{3,2,1,0:T(4,128)}, u32[]{:S(2)}) copy-start(f32[1,32,4,128]{3,2,1,0:T(4,128)} %param.11) | copy-start | bytes 196612
  1.7 8.1 %collective-permute-start = (bf16[272,128]{1,0:T(8,128)(2,1)S(1)}, bf16[272,128]{1,0:T(8,128)(2,1)S(1)}, u32[]{:S(2)}, u32[]{:S(2)}) collective-permute-start(bf16[272,128]{1,0:T(8,128)(2,1)S(1)} %get-tuple-element.52), channel_id=1, source_target_pairs={{0,1},{1,2},{2,3},{3,4},{4,5},{5,6},{6,7},{7,0},{8,9},{9,10},{10,1... | collective-permute-start | bytes 208904 | tf_op jit(solution)/shard_map/ppermute | solution.py:582
  2.2 7.6 %collective-permute-start.1 = (bf16[272,128]{1,0:T(8,128)(2,1)S(1)}, bf16[272,128]{1,0:T(8,128)(2,1)S(1)}, u32[]{:S(2)}, u32[]{:S(2)}) collective-permute-start(bf16[272,128]{1,0:T(8,128)(2,1)S(1)} %get-tuple-element.53), channel_id=1, source_target_pairs={{1,0},{2,1},{3,2},{4,3},{5,4},{6,5},{7,6},{0,7},{9,8},{10,9},{11,1... | collective-permute-start | bytes 208904 | tf_op jit(solution)/shard_map/ppermute | solution.py:582
  7.0 2.7 %copy-start.2 = (bf16[1024,128]{1,0:T(8,128)(2,1)S(1)}, bf16[1024,128]{1,0:T(8,128)(2,1)}, u32[]{:S(2)}) copy-start(bf16[1024,128]{1,0:T(8,128)(2,1)} %param.17) | copy-start | bytes 786436
  7.0 2.8 %copy-start = (bf16[128,1024]{1,0:T(8,128)(2,1)S(1)}, bf16[128,1024]{1,0:T(8,128)(2,1)}, u32[]{:S(2)}) copy-start(bf16[128,1024]{1,0:T(8,128)(2,1)} %w_out_ref.3) | copy-start | bytes 786436
  13.8 3.8 %collective-permute-start.2 = (bf16[512,1024]{1,0:T(8,128)(2,1)S(1)}, bf16[512,1024]{1,0:T(8,128)(2,1)S(1)}, u32[]{:S(2)}, u32[]{:S(2)}) collective-permute-start(bf16[512,1024]{1,0:T(8,128)(2,1)S(1)} %get-tuple-element.56), channel_id=1, source_target_pairs={{0,1},{1,0},{2,3},{3,2},{4,5},{5,4},{6,7},{7,6},{8,9},{9,8},{10,11... | collective-permute-start | bytes 3145736 | tf_op jit(solution)/shard_map/ppermute | solution.py:504
  15.9 1.7 %collective-permute-start.3 = (bf16[512,256]{1,0:T(8,128)(2,1)S(1)}, bf16[512,256]{1,0:T(8,128)(2,1)S(1)}, u32[]{:S(2)}, u32[]{:S(2)}) collective-permute-start(bf16[512,256]{1,0:T(8,128)(2,1)S(1)} %get-tuple-element.61), channel_id=1, source_target_pairs={{0,1},{1,0},{2,3},{3,2},{4,5},{5,4},{6,7},{7,6},{8,9},{9,8},{10,11... | collective-permute-start | bytes 786440 | tf_op jit(solution)/shard_map/ppermute | solution.py:504
  17.9 7.5 %collective-permute-start.4 = (bf16[128,1280]{1,0:T(8,128)(2,1)S(1)}, bf16[128,1280]{1,0:T(8,128)(2,1)S(1)}, u32[]{:S(2)}, u32[]{:S(2)}) collective-permute-start(bf16[128,1280]{1,0:T(8,128)(2,1)S(1)} %get-tuple-element.65), channel_id=1, source_target_pairs={{0,8},{1,17},{2,10},{3,19},{4,12},{5,21},{6,14},{7,23},{8,0},{9,25... | collective-permute-start | bytes 983048 | tf_op jit(solution)/shard_map/ppermute | solution.py:515
  19.9 5.5 %collective-permute-start.5 = (bf16[256,128]{1,0:T(8,128)(2,1)S(1)}, bf16[256,128]{1,0:T(8,128)(2,1)S(1)}, u32[]{:S(2)}, u32[]{:S(2)}) collective-permute-start(bf16[256,128]{1,0:T(8,128)(2,1)S(1)} %get-tuple-element.76), channel_id=1, source_target_pairs={{0,1},{1,2},{2,3},{3,4},{4,5},{5,6},{6,7},{7,0},{8,9},{9,10},{10,1... | collective-permute-start | bytes 196616 | tf_op jit(solution)/shard_map/ppermute | solution.py:582
  20.0 5.4 %collective-permute-start.6 = (bf16[256,128]{1,0:T(8,128)(2,1)S(1)}, bf16[256,128]{1,0:T(8,128)(2,1)S(1)}, u32[]{:S(2)}, u32[]{:S(2)}) collective-permute-start(bf16[256,128]{1,0:T(8,128)(2,1)S(1)} %get-tuple-element.77), channel_id=1, source_target_pairs={{1,0},{2,1},{3,2},{4,3},{5,4},{6,5},{7,6},{0,7},{9,8},{10,9},{11,1... | collective-permute-start | bytes 196616 | tf_op jit(solution)/shard_map/ppermute | solution.py:582
  23.5 10.1 %collective-permute-start.7 = (bf16[128,1280]{1,0:T(8,128)(2,1)S(1)}, bf16[128,1280]{1,0:T(8,128)(2,1)S(1)}, u32[]{:S(2)}, u32[]{:S(2)}) collective-permute-start(bf16[128,1280]{1,0:T(8,128)(2,1)S(1)} %get-tuple-element.70), channel_id=1, source_target_pairs={{0,8},{1,17},{2,10},{3,19},{4,12},{5,21},{6,14},{7,23},{8,0},{9,25... | collective-permute-start | bytes 983048 | tf_op jit(solution)/shard_map/ppermute | solution.py:515
  25.5 8.1 %collective-permute-start.8 = (bf16[128,1280]{1,0:T(8,128)(2,1)S(1)}, bf16[128,1280]{1,0:T(8,128)(2,1)S(1)}, u32[]{:S(2)}, u32[]{:S(2)}) collective-permute-start(bf16[128,1280]{1,0:T(8,128)(2,1)S(1)} %shard_map.144), channel_id=1, source_target_pairs={{0,16},{1,9},{2,18},{3,11},{4,20},{5,13},{6,22},{7,15},{8,24},{9,1... | collective-permute-start | bytes 983048 | tf_op jit(solution)/shard_map/ppermute | solution.py:515
  33.7 7.3 %collective-permute-start.9 = (bf16[32,1280]{1,0:T(8,128)(2,1)S(1)}, bf16[32,1280]{1,0:T(8,128)(2,1)S(1)}, u32[]{:S(2)}, u32[]{:S(2)}) collective-permute-start(bf16[32,1280]{1,0:T(8,128)(2,1)S(1)} %get-tuple-element.88), channel_id=1, source_target_pairs={{0,6},{1,3},{2,4},{3,1},{4,2},{5,7},{6,0},{7,5},{8,14},{9,11},{10,... | collective-permute-start | bytes 245768 | tf_op jit(solution)/shard_map/ppermute | solution.py:555
  34.8 9.0 %collective-permute-start.10 = (bf16[32,1280]{1,0:T(8,128)(2,1)S(1)}, bf16[32,1280]{1,0:T(8,128)(2,1)S(1)}, u32[]{:S(2)}, u32[]{:S(2)}) collective-permute-start(bf16[32,1280]{1,0:T(8,128)(2,1)S(1)} %get-tuple-element.89), channel_id=1, source_target_pairs={{0,4},{1,5},{2,6},{3,7},{4,0},{5,1},{6,2},{7,3},{8,12},{9,13},{10,... | collective-permute-start | bytes 245768 | tf_op jit(solution)/shard_map/ppermute | solution.py:555
  34.8 9.0 %collective-permute-start.11 = (bf16[32,1280]{1,0:T(8,128)(2,1)S(1)}, bf16[32,1280]{1,0:T(8,128)(2,1)S(1)}, u32[]{:S(2)}, u32[]{:S(2)}) collective-permute-start(bf16[32,1280]{1,0:T(8,128)(2,1)S(1)} %get-tuple-element.90), channel_id=1, source_target_pairs={{0,2},{1,7},{2,0},{3,5},{4,6},{5,3},{6,4},{7,1},{8,10},{9,15},{10,... | collective-permute-start | bytes 245768 | tf_op jit(solution)/shard_map/ppermute | solution.py:555
  43.8 6.7 %collective-permute-start.14 = (bf16[32,1280]{1,0:T(8,128)(2,1)S(1)}, bf16[32,1280]{1,0:T(8,128)(2,1)S(1)}, u32[]{:S(2)}, u32[]{:S(2)}) collective-permute-start(bf16[32,1280]{1,0:T(8,128)(2,1)S(1)} %shard_map.147.refs_0_), channel_id=1, source_target_pairs={{0,2},{1,7},{2,0},{3,5},{4,6},{5,3},{6,4},{7,1},{8,10},{9,15},{10,... | collective-permute-start | bytes 245768 | tf_op jit(solution)/shard_map/ppermute | solution.py:555
  43.9 7.3 %collective-permute-start.13 = (bf16[32,1280]{1,0:T(8,128)(2,1)S(1)}, bf16[32,1280]{1,0:T(8,128)(2,1)S(1)}, u32[]{:S(2)}, u32[]{:S(2)}) collective-permute-start(bf16[32,1280]{1,0:T(8,128)(2,1)S(1)} %shard_map.147.refs_0_), channel_id=1, source_target_pairs={{0,4},{1,5},{2,6},{3,7},{4,0},{5,1},{6,2},{7,3},{8,12},{9,13},{10,... | collective-permute-start | bytes 245768 | tf_op jit(solution)/shard_map/ppermute | solution.py:555
  46.1 6.3 %collective-permute-start.12 = (bf16[32,1280]{1,0:T(8,128)(2,1)S(1)}, bf16[32,1280]{1,0:T(8,128)(2,1)S(1)}, u32[]{:S(2)}, u32[]{:S(2)}) collective-permute-start(bf16[32,1280]{1,0:T(8,128)(2,1)S(1)} %shard_map.147.refs_0_), channel_id=1, source_target_pairs={{0,6},{1,3},{2,4},{3,1},{4,2},{5,7},{6,0},{7,5},{8,14},{9,11},{10,... | collective-permute-start | bytes 245768 | tf_op jit(solution)/shard_map/ppermute | solution.py:555
  52.5 7.2 %collective-permute-start.15 = (bf16[128,640]{1,0:T(8,128)(2,1)S(1)}, bf16[128,640]{1,0:T(8,128)(2,1)S(1)}, u32[]{:S(2)}, u32[]{:S(2)}) collective-permute-start(bf16[128,640]{1,0:T(8,128)(2,1)S(1)} %get-tuple-element.91.refs_0_), channel_id=1, source_target_pairs={{0,8},{1,17},{2,10},{3,19},{4,12},{5,21},{6,14},{7,23},{8,0},{9,25... | collective-permute-start | bytes 491528 | tf_op jit(solution)/shard_map/ppermute | solution.py:515
  53.8 7.5 %collective-permute-start.19 = (bf16[128,640]{1,0:T(8,128)(2,1)S(1)}, bf16[128,640]{1,0:T(8,128)(2,1)S(1)}, u32[]{:S(2)}, u32[]{:S(2)}) collective-permute-start(bf16[128,640]{1,0:T(8,128)(2,1)S(1)} %get-tuple-element.92.refs_4_), channel_id=1, source_target_pairs={{0,16},{1,9},{2,18},{3,11},{4,20},{5,13},{6,22},{7,15},{8,24},{9,1... | collective-permute-start | bytes 491528 | tf_op jit(solution)/shard_map/ppermute | solution.py:515
  55.4 8.0 %collective-permute-start.16 = (bf16[128,640]{1,0:T(8,128)(2,1)S(1)}, bf16[128,640]{1,0:T(8,128)(2,1)S(1)}, u32[]{:S(2)}, u32[]{:S(2)}) collective-permute-start(bf16[128,640]{1,0:T(8,128)(2,1)S(1)} %get-tuple-element.91.refs_0_), channel_id=1, source_target_pairs={{0,16},{1,9},{2,18},{3,11},{4,20},{5,13},{6,22},{7,15},{8,24},{9,1... | collective-permute-start | bytes 491528 | tf_op jit(solution)/shard_map/ppermute | solution.py:515
  55.8 7.5 %collective-permute-start.18 = (bf16[128,640]{1,0:T(8,128)(2,1)S(1)}, bf16[128,640]{1,0:T(8,128)(2,1)S(1)}, u32[]{:S(2)}, u32[]{:S(2)}) collective-permute-start(bf16[128,640]{1,0:T(8,128)(2,1)S(1)} %get-tuple-element.92.refs_4_), channel_id=1, source_target_pairs={{0,8},{1,17},{2,10},{3,19},{4,12},{5,21},{6,14},{7,23},{8,0},{9,25... | collective-permute-start | bytes 491528 | tf_op jit(solution)/shard_map/ppermute | solution.py:515
  59.6 5.4 %collective-permute-start.17 = (bf16[128,640]{1,0:T(8,128)(2,1)S(1)}, bf16[128,640]{1,0:T(8,128)(2,1)S(1)}, u32[]{:S(2)}, u32[]{:S(2)}) collective-permute-start(bf16[128,640]{1,0:T(8,128)(2,1)S(1)} %collective-permute-done.15.refs_1_), channel_id=1, source_target_pairs={{0,16},{1,9},{2,18},{3,11},{4,20},{5,13},{6,22},{7,15},{8,24},{9,1... | collective-permute-start | bytes 491528 | tf_op jit(solution)/shard_map/ppermute | solution.py:515
  61.3 5.3 %collective-permute-start.20 = (bf16[128,640]{1,0:T(8,128)(2,1)S(1)}, bf16[128,640]{1,0:T(8,128)(2,1)S(1)}, u32[]{:S(2)}, u32[]{:S(2)}) collective-permute-start(bf16[128,640]{1,0:T(8,128)(2,1)S(1)} %collective-permute-done.19.refs_6_), channel_id=1, source_target_pairs={{0,8},{1,17},{2,10},{3,19},{4,12},{5,21},{6,14},{7,23},{8,0},{9,25... | collective-permute-start | bytes 491528 | tf_op jit(solution)/shard_map/ppermute | solution.py:515
  66.8 3.1 %collective-permute-start.21 = (bf16[512,1280]{1,0:T(8,128)(2,1)S(1)}, bf16[512,1280]{1,0:T(8,128)(2,1)S(1)}, u32[]{:S(2)}, u32[]{:S(2)}) collective-permute-start(bf16[512,1280]{1,0:T(8,128)(2,1)S(1)} %shard_map.149.mid_half.small_half), channel_id=1, source_target_pairs={{0,1},{1,0},{2,3},{3,2},{4,5},{5,4},{6,7},{7,6},{8,9},{9,8},{10,11... | collective-permute-start | bytes 3932168 | tf_op jit(solution)/shard_map/ppermute | solution.py:504

commit v17 on v16

--- a/solution.py
+++ b/solution.py
@@ -10,6 +10,7 @@
 
 DYN_STEPS = 2
 BLOCK = 256
+LAYER_BLOCK = 128
 PACK_ROWS = 16
 VMEM_LIMIT = 32 * 1024 * 1024
 F32 = jnp.float32
@@ -249,24 +250,24 @@
     sources = jnp.concatenate(rows, axis=1).astype(BF16)
     x_now = jnp.dot(sources, spread, preferred_element_type=F32).astype(BF16)
     x_ref[...] = x_now
-    for start in range(0, units, BLOCK):
-        pre_one = jnp.dot(weights_ref[start : start + BLOCK, units:], x_now, preferred_element_type=F32)
-        act_one_ref[start : start + BLOCK, :] = (pre_one * sigmoid(pre_one)).astype(BF16)
+    for start in range(0, units, LAYER_BLOCK):
+        pre_one = jnp.dot(weights_ref[start : start + LAYER_BLOCK, units:], x_now, preferred_element_type=F32)
+        act_one_ref[start : start + LAYER_BLOCK, :] = (pre_one * sigmoid(pre_one)).astype(BF16)
     adj_half = join_tiles(adj_ref).astype(BF16)
-    for start in range(0, units, BLOCK):
+    for start in range(0, units, LAYER_BLOCK):
         pre_two = jnp.dot(
-            weights_ref[start : start + BLOCK, :units], act_one_ref[...], preferred_element_type=F32
+            weights_ref[start : start + LAYER_BLOCK, :units], act_one_ref[...], preferred_element_type=F32
         )
         sigma_val = sigmoid(pre_two)
-        act_two_ref[start : start + BLOCK, :] = (pre_two * sigma_val).astype(BF16)
+        act_two_ref[start : start + LAYER_BLOCK, :] = (pre_two * sigma_val).astype(BF16)
         back_two = lax.dot_general(
-            w_out_ref[:, start : start + BLOCK],
+            w_out_ref[:, start : start + LAYER_BLOCK],
             adj_half,
             CONTRACT_FIRST,
             preferred_element_type=F32,
         )
         slope = sigma_val * (1.0 + pre_two * (1.0 - sigma_val))
-        delta_two_ref[start : start + BLOCK, :] = (back_two * slope).astype(BF16)
+        delta_two_ref[start : start + LAYER_BLOCK, :] = (back_two * slope).astype(BF16)
     weight_product(delta_two_ref, act_one_ref[...], keep_ref, send_ref, 0)
 
 
@@ -283,17 +284,17 @@
     fields = x_ref.shape[0]
     units = weights_ref.shape[0]
     x_now = x_ref[...]
-    for start in range(0, units, BLOCK):
+    for start in range(0, units, LAYER_BLOCK):
         back_one = lax.dot_general(
-            weights_ref[:, start : start + BLOCK],
+            weights_ref[:, start : start + LAYER_BLOCK],
             delta_two_ref[...],
             CONTRACT_FIRST,
             preferred_element_type=F32,
         )
-        pre_one = jnp.dot(weights_ref[start : start + BLOCK, units:], x_now, preferred_element_type=F32)
+        pre_one = jnp.dot(weights_ref[start : start + LAYER_BLOCK, units:], x_now, preferred_element_type=F32)
         sigma_val = sigmoid(pre_one)
         slope = sigma_val * (1.0 + pre_one * (1.0 - sigma_val))
-        delta_one_ref[start : start + BLOCK, :] = (back_one * slope).astype(BF16)
+        delta_one_ref[start : start + LAYER_BLOCK, :] = (back_one * slope).astype(BF16)
     weight_product(delta_one_ref, x_now, keep_ref, send_ref, 0)
     weight_product(act_two_ref, join_tiles(adj_ref).astype(BF16), keep_ref, send_ref, fields)
 
@@ -467,7 +468,7 @@
 def final(rows, other, before, fields):
     half, columns = rows.shape
     units = 2 * half
-    block = units // 2
+    block = units
 
     def place():
         core = lax.axis_index("horiz") % 2

time: 71.9 us -> 71.3 us (level)
  Pallas kernels: 14.8 us -> 13.9 us
  transfers between devices with their start and end apart: 22 -> 22, of which waited for: 13 -> 13; matrix products, arithmetic and copies ran while one was open for 3% -> 3% of each run, Pallas kernels for 12% -> 11%
where the time goes in v17:
time: 71.3 us; the launch traced here: 71.2 us
  starting transfers between devices  28.5 us (40%)
  waiting for transfers between devices  24.2 us (34%)
  Pallas kernels  13.9 us (19%)
  local copies, waits for them, and re-layouts  1.92 us (3%)
  between operations  1.53 us (2%)
  other arithmetic  1.1 us (2%)
    ppermute x9, waiting for transfers between devices, to_member(): return lax.ppermute(array, ('ens', 'horiz'), route)  12.1 us
    ppermute x9, starting transfers between devices, to_member(): return lax.ppermute(array, ('ens', 'horiz'), route)  10.8 us
    pallas_call x13, Pallas kernels, run(): pl.pallas_call(functools.partial(kernel, **names), out_shape=[jax.ShapeDt...  10.7 us
    ppermute x6, waiting for transfers between devices, to_chips(): received.append(lax.ppermute(array, 'horiz', route))  9.73 us
    ppermute x6, starting transfers between devices, to_chips(): received.append(lax.ppermute(array, 'horiz', route))  8.9 us
    ppermute x2, starting transfers between devices, to_neighbours(): lax.ppermute(downward, axis, backward)  7.52 us
    pallas_call x2, Pallas kernels, final(): pl.pallas_call(final_kernel, grid=(units // block,), out_shape=[jax.Shape...  3.16 us
    ppermute x3, waiting for transfers between devices, exchange(): sent[k] = lax.ppermute(arrays[k - 1], axis, route)  2.05 us
  transfers between devices with their start and end apart: 22, of which 13 were waited for; matrix products, arithmetic and copies ran while one was open for 3% of the time, Pallas kernels for 11%

profile of v17, /device:TPU:0, one launch (start us, length us, event | category | flops | bytes accessed | tf_op | source)
XLA Modules:
  0.0 71.2 jit_solution(9839395506677169092)
XLA Ops:
  0.6 1.0 %pad_maximum_fusion.1 = f32[130,4,128]{2,1,0:T(4,128)S(1)} fusion(f32[2,4,128]{2,1,0:T(4,128)} %param.12, f32[128,4,128]{2,1,0:T(4,128)} %bitcast.16), kind=kLoop, calls=%fused_computation.1 | loop fusion | flops 66560 | bytes 532480 | tf_op jit(solution)/shard_map/concatenate | solution.py:594
  2.2 4.1 %collective-permute-start.1 = (bf16[272,128]{1,0:T(8,128)(2,1)S(1)}, bf16[272,128]{1,0:T(8,128)(2,1)S(1)}, u32[]{:S(2)}, u32[]{:S(2)}) collective-permute-start(bf16[272,128]{1,0:T(8,128)(2,1)S(1)} %get-tuple-element.53), channel_id=1, source_target_pairs={{1,0},{2,1},{3,2},{4,3},{5,4},{6,5},{7,6},{0,7},{9,8},{10,9},{11,1... | collective-permute-start | bytes 208904 | tf_op jit(solution)/shard_map/ppermute | solution.py:583
  7.0 1.8 %constant_dynamic-update-slice_fusion.1 = bf16[1024,1152]{1,0:T(8,128)(2,1)S(1)} fusion(bf16[1024,1024]{1,0:T(8,128)(2,1)} %param.18), kind=kLoop, calls=%fused_computation.3 | loop fusion | bytes 4194304
  9.0 0.8 %shard_map.138 = (f32[3,128,128]{2,1,0:T(8,128)S(1)}, f32[32,384]{1,0:T(8,128)S(1)}, f32[32,384]{1,0:T(8,128)S(1)}, f32[32,384]{1,0:T(8,128)S(1)}) custom-call(s32[1,1]{1,0:T(1,128)S(6)} %copy.26.count_ref, f32[640,128]{1,0:T(8,128)S(1)} %bitcast.14, s32[3,128]{1,0:T(4,128)S(1)} %get-tuple-element.100.cols_ref, s32[3,128]{1,0:T(4,128)S(1)} %get-tuple-element.99.mask_ref), custom_call_target="tpu_custom_call" | custom-call | bytes 30000000 | tf_op jit(solution)/shard_map/pallas_call | solution.py:28
  9.9 3.6 %shard_map.139 = (f32[4,128,128]{2,1,0:T(8,128)S(1)}, bf16[128,384]{1,0:T(8,128)(2,1)S(1)}, bf16[1024,384]{1,0:T(8,128)(2,1)}, bf16[1024,384]{1,0:T(8,128)(2,1)S...) custom-call(f32[520,128]{1,0:T(8,128)S(1)} %bitcast.12, ...), custom_call_target="tpu_custom_call" | custom-call | bytes 15000000 | tf_op jit(solution)/shard_map/pallas_call | solution.py:28
  13.5 2.0 %shard_map.140 = (bf16[1024,384]{1,0:T(8,128)(2,1)S(1)}, bf16[512,256]{1,0:T(8,128)(2,1)S(1)}, bf16[512,256]{1,0:T(8,128)(2,1)S(1)}) custom-call(bf16[128,384]{1,0:T(8,128)(2,1)S(1)} %get-tuple-element.57.x_ref, bf16[1024,384]{1,0:T(8,128)(2,1)S(1)} %get-tuple-element.72.act_two_ref, bf16[1024,384]{1,0:T(8,128)(2,1)S(1)} %get-tuple-element.59.delta_two_ref, ...), custom_call_target="tpu_custom_call" | custom-call | bytes 4000000 | tf_op jit(solution)/shard_map/pallas_call | solution.py:28
  17.6 2.0 %collective-permute-start.4 = (bf16[128,1280]{1,0:T(8,128)(2,1)S(1)}, bf16[128,1280]{1,0:T(8,128)(2,1)S(1)}, u32[]{:S(2)}, u32[]{:S(2)}) collective-permute-start(bf16[128,1280]{1,0:T(8,128)(2,1)S(1)} %get-tuple-element.65), channel_id=1, source_target_pairs={{0,8},{1,17},{2,10},{3,19},{4,12},{5,21},{6,14},{7,23},{8,0},{9,25... | collective-permute-start | bytes 983048 | tf_op jit(solution)/shard_map/ppermute | solution.py:516
  19.7 3.4 %collective-permute-start.6 = (bf16[256,128]{1,0:T(8,128)(2,1)S(1)}, bf16[256,128]{1,0:T(8,128)(2,1)S(1)}, u32[]{:S(2)}, u32[]{:S(2)}) collective-permute-start(bf16[256,128]{1,0:T(8,128)(2,1)S(1)} %get-tuple-element.77), channel_id=1, source_target_pairs={{1,0},{2,1},{3,2},{4,3},{5,4},{6,5},{7,6},{0,7},{9,8},{10,9},{11,1... | collective-permute-start | bytes 196616 | tf_op jit(solution)/shard_map/ppermute | solution.py:583
  23.2 1.6 %shard_map.143 = f32[512,128]{1,0:T(8,128)} custom-call(s32[1,1]{1,0:T(1,128)S(6)} %copy.26.count_ref, f32[4,128,128]{2,1,0:T(8,128)S(1)} %get-tuple-element.66.moved_ref, s32[3,128]{1,0:T(4,128)S(1)} %get-tuple-element.100.cols_ref, s32[3,128]{1,0:T(4,128)S(1)} %get-tuple-element.99.mask_ref, bf16[128,384]{1,0:T(8,128)(2,1)S(1)} %get-tuple-element.57.x_ref, ...), custom_call_target="tpu_custom_call" | custom-call | tf_op jit(solution)/shard_map/pallas_call | solution.py:28
  25.2 1.7 %collective-permute-start.8 = (bf16[128,1280]{1,0:T(8,128)(2,1)S(1)}, bf16[128,1280]{1,0:T(8,128)(2,1)S(1)}, u32[]{:S(2)}, u32[]{:S(2)}) collective-permute-start(bf16[128,1280]{1,0:T(8,128)(2,1)S(1)} %shard_map.144), channel_id=1, source_target_pairs={{0,16},{1,9},{2,18},{3,11},{4,20},{5,13},{6,22},{7,15},{8,24},{9,1... | collective-permute-start | bytes 983048 | tf_op jit(solution)/shard_map/ppermute | solution.py:516
  26.9 1.5 %shard_map.145 = f32[512,128]{1,0:T(8,128)} custom-call(f32[4,128,128]{2,1,0:T(8,128)S(1)} %get-tuple-element.80.field_ref, bf16[256,128]{1,0:T(8,128)(2,1)S(1)} %collective-permute-done.5.low_ref, bf16[256,128]{1,0:T(8,128)(2,1)S(1)} %collective-permute-done.6.high_ref, bf16[272,128]{1,0:T(8,128)(2,1)S(1)} %collective-permute-done.low_ref.low_mix_ref, ...), custom_call_target="tpu_custom_call" | custom-call | tf_op jit(solution)/shard_map/pallas_call | solution.py:28
  28.4 4.8 %collective-permute-done.7.refs_1_ = bf16[128,1280]{1,0:T(8,128)(2,1)S(1)} collective-permute-done((bf16[128,1280]{1,0:T(8,128)(2,1)S(1)}, bf16[128,1280]{1,0:T(8,128)(2,1)S(1)}, u32[]{:S(2)}, u32[]{:S(2)}) %collective-permute-start.7) | collective-permute-done | bytes 327712 | tf_op jit(solution)/shard_map/ppermute | solution.py:516
  33.4 1.0 %collective-permute-start.9 = (bf16[32,1280]{1,0:T(8,128)(2,1)S(1)}, bf16[32,1280]{1,0:T(8,128)(2,1)S(1)}, u32[]{:S(2)}, u32[]{:S(2)}) collective-permute-start(bf16[32,1280]{1,0:T(8,128)(2,1)S(1)} %get-tuple-element.88), channel_id=1, source_target_pairs={{0,6},{1,3},{2,4},{3,1},{4,2},{5,7},{6,0},{7,5},{8,14},{9,11},{10,... | collective-permute-start | bytes 245768 | tf_op jit(solution)/shard_map/ppermute | solution.py:556
  34.4 3.4 %collective-permute-start.11 = (bf16[32,1280]{1,0:T(8,128)(2,1)S(1)}, bf16[32,1280]{1,0:T(8,128)(2,1)S(1)}, u32[]{:S(2)}, u32[]{:S(2)}) collective-permute-start(bf16[32,1280]{1,0:T(8,128)(2,1)S(1)} %get-tuple-element.90), channel_id=1, source_target_pairs={{0,2},{1,7},{2,0},{3,5},{4,6},{5,3},{6,4},{7,1},{8,10},{9,15},{10,... | collective-permute-start | bytes 245768 | tf_op jit(solution)/shard_map/ppermute | solution.py:556
  37.9 2.8 %collective-permute-done.9.refs_1_ = bf16[32,1280]{1,0:T(8,128)(2,1)S(1)} collective-permute-done((bf16[32,1280]{1,0:T(8,128)(2,1)S(1)}, bf16[32,1280]{1,0:T(8,128)(2,1)S(1)}, u32[]{:S(2)}, u32[]{:S(2)}) %collective-permute-start.9) | collective-permute-done | bytes 81952 | tf_op jit(solution)/shard_map/ppermute | solution.py:556
  40.7 2.7 %collective-permute-done.10.refs_2_ = bf16[32,1280]{1,0:T(8,128)(2,1)S(1)} collective-permute-done((bf16[32,1280]{1,0:T(8,128)(2,1)S(1)}, bf16[32,1280]{1,0:T(8,128)(2,1)S(1)}, u32[]{:S(2)}, u32[]{:S(2)}) %collective-permute-start.10) | collective-permute-done | bytes 81952 | tf_op jit(solution)/shard_map/ppermute | solution.py:556
  43.6 2.2 %collective-permute-start.13 = (bf16[32,1280]{1,0:T(8,128)(2,1)S(1)}, bf16[32,1280]{1,0:T(8,128)(2,1)S(1)}, u32[]{:S(2)}, u32[]{:S(2)}) collective-permute-start(bf16[32,1280]{1,0:T(8,128)(2,1)S(1)} %shard_map.147.refs_0_), channel_id=1, source_target_pairs={{0,4},{1,5},{2,6},{3,7},{4,0},{5,1},{6,2},{7,3},{8,12},{9,13},{10,... | collective-permute-start | bytes 245768 | tf_op jit(solution)/shard_map/ppermute | solution.py:556
  45.8 2.2 %collective-permute-start.12 = (bf16[32,1280]{1,0:T(8,128)(2,1)S(1)}, bf16[32,1280]{1,0:T(8,128)(2,1)S(1)}, u32[]{:S(2)}, u32[]{:S(2)}) collective-permute-start(bf16[32,1280]{1,0:T(8,128)(2,1)S(1)} %shard_map.147.refs_0_), channel_id=1, source_target_pairs={{0,6},{1,3},{2,4},{3,1},{4,2},{5,7},{6,0},{7,5},{8,14},{9,11},{10,... | collective-permute-start | bytes 245768 | tf_op jit(solution)/shard_map/ppermute | solution.py:556
  48.0 2.3 %collective-permute-done.14.refs_3_ = bf16[32,1280]{1,0:T(8,128)(2,1)S(1)} collective-permute-done((bf16[32,1280]{1,0:T(8,128)(2,1)S(1)}, bf16[32,1280]{1,0:T(8,128)(2,1)S(1)}, u32[]{:S(2)}, u32[]{:S(2)}) %collective-permute-start.14) | collective-permute-done | bytes 81952 | tf_op jit(solution)/shard_map/ppermute | solution.py:556
  50.9 1.3 %collective-permute-done.12.refs_1_ = bf16[32,1280]{1,0:T(8,128)(2,1)S(1)} collective-permute-done((bf16[32,1280]{1,0:T(8,128)(2,1)S(1)}, bf16[32,1280]{1,0:T(8,128)(2,1)S(1)}, u32[]{:S(2)}, u32[]{:S(2)}) %collective-permute-start.12) | collective-permute-done | bytes 81952 | tf_op jit(solution)/shard_map/ppermute | solution.py:556
  52.2 1.3 %collective-permute-start.15 = (bf16[128,640]{1,0:T(8,128)(2,1)S(1)}, bf16[128,640]{1,0:T(8,128)(2,1)S(1)}, u32[]{:S(2)}, u32[]{:S(2)}) collective-permute-start(bf16[128,640]{1,0:T(8,128)(2,1)S(1)} %get-tuple-element.91.refs_0_), channel_id=1, source_target_pairs={{0,8},{1,17},{2,10},{3,19},{4,12},{5,21},{6,14},{7,23},{8,0},{9,25... | collective-permute-start | bytes 491528 | tf_op jit(solution)/shard_map/ppermute | solution.py:516
  53.4 1.6 %collective-permute-start.19 = (bf16[128,640]{1,0:T(8,128)(2,1)S(1)}, bf16[128,640]{1,0:T(8,128)(2,1)S(1)}, u32[]{:S(2)}, u32[]{:S(2)}) collective-permute-start(bf16[128,640]{1,0:T(8,128)(2,1)S(1)} %get-tuple-element.92.refs_4_), channel_id=1, source_target_pairs={{0,16},{1,9},{2,18},{3,11},{4,20},{5,13},{6,22},{7,15},{8,24},{9,1... | collective-permute-start | bytes 491528 | tf_op jit(solution)/shard_map/ppermute | solution.py:516
  55.5 0.8 %collective-permute-start.18 = (bf16[128,640]{1,0:T(8,128)(2,1)S(1)}, bf16[128,640]{1,0:T(8,128)(2,1)S(1)}, u32[]{:S(2)}, u32[]{:S(2)}) collective-permute-start(bf16[128,640]{1,0:T(8,128)(2,1)S(1)} %get-tuple-element.92.refs_4_), channel_id=1, source_target_pairs={{0,8},{1,17},{2,10},{3,19},{4,12},{5,21},{6,14},{7,23},{8,0},{9,25... | collective-permute-start | bytes 491528 | tf_op jit(solution)/shard_map/ppermute | solution.py:516
  56.3 3.1 %collective-permute-done.15.refs_1_ = bf16[128,640]{1,0:T(8,128)(2,1)S(1)} collective-permute-done((bf16[128,640]{1,0:T(8,128)(2,1)S(1)}, bf16[128,640]{1,0:T(8,128)(2,1)S(1)}, u32[]{:S(2)}, u32[]{:S(2)}) %collective-permute-start.15) | collective-permute-done | bytes 163872 | tf_op jit(solution)/shard_map/ppermute | solution.py:516
  59.3 1.7 %collective-permute-start.17 = (bf16[128,640]{1,0:T(8,128)(2,1)S(1)}, bf16[128,640]{1,0:T(8,128)(2,1)S(1)}, u32[]{:S(2)}, u32[]{:S(2)}) collective-permute-start(bf16[128,640]{1,0:T(8,128)(2,1)S(1)} %collective-permute-done.15.refs_1_), channel_id=1, source_target_pairs={{0,16},{1,9},{2,18},{3,11},{4,20},{5,13},{6,22},{7,15},{8,24},{9,1... | collective-permute-start | bytes 491528 | tf_op jit(solution)/shard_map/ppermute | solution.py:516
  61.0 1.1 %collective-permute-start.20 = (bf16[128,640]{1,0:T(8,128)(2,1)S(1)}, bf16[128,640]{1,0:T(8,128)(2,1)S(1)}, u32[]{:S(2)}, u32[]{:S(2)}) collective-permute-start(bf16[128,640]{1,0:T(8,128)(2,1)S(1)} %collective-permute-done.19.refs_6_), channel_id=1, source_target_pairs={{0,8},{1,17},{2,10},{3,19},{4,12},{5,21},{6,14},{7,23},{8,0},{9,25... | collective-permute-start | bytes 491528 | tf_op jit(solution)/shard_map/ppermute | solution.py:516
  62.2 0.8 %collective-permute-done.16.refs_2_ = bf16[128,640]{1,0:T(8,128)(2,1)S(1)} collective-permute-done((bf16[128,640]{1,0:T(8,128)(2,1)S(1)}, bf16[128,640]{1,0:T(8,128)(2,1)S(1)}, u32[]{:S(2)}, u32[]{:S(2)}) %collective-permute-start.16) | collective-permute-done | bytes 163872 | tf_op jit(solution)/shard_map/ppermute | solution.py:516
  63.0 1.8 %collective-permute-done.17.refs_3_ = bf16[128,640]{1,0:T(8,128)(2,1)S(1)} collective-permute-done((bf16[128,640]{1,0:T(8,128)(2,1)S(1)}, bf16[128,640]{1,0:T(8,128)(2,1)S(1)}, u32[]{:S(2)}, u32[]{:S(2)}) %collective-permute-start.17) | collective-permute-done | bytes 163872 | tf_op jit(solution)/shard_map/ppermute | solution.py:516
  64.8 1.6 %collective-permute-done.20.refs_7_ = bf16[128,640]{1,0:T(8,128)(2,1)S(1)} collective-permute-done((bf16[128,640]{1,0:T(8,128)(2,1)S(1)}, bf16[128,640]{1,0:T(8,128)(2,1)S(1)}, u32[]{:S(2)}, u32[]{:S(2)}) %collective-permute-start.20) | collective-permute-done | bytes 163872 | tf_op jit(solution)/shard_map/ppermute | solution.py:516
  66.6 1.6 %shard_map.150 = (f32[1024,1024]{1,0:T(8,128)}, f32[1024,128]{1,0:T(8,128)}, f32[128,1024]{1,0:T(8,128)}) custom-call(bf16[512,1280]{1,0:T(8,128)(2,1)S(1)} %shard_map.149.mid_half.small_half, bf16[512,1280]{1,0:T(8,128)(2,1)S(1)} %shard_map.149.mid_half.small_half), custom_call_target="tpu_custom_call" | custom-call | tf_op jit(solution)/shard_map/pallas_call | solution.py:477
  68.1 1.4 %collective-permute-done.21.mid_half.small_half = bf16[512,1280]{1,0:T(8,128)(2,1)S(1)} collective-permute-done((bf16[512,1280]{1,0:T(8,128)(2,1)S(1)}, bf16[512,1280]{1,0:T(8,128)(2,1)S(1)}, u32[]{:S(2)}, u32[]{:S(2)}) %collective-permute-start.21) | collective-permute-done | bytes 1310752 | tf_op jit(solution)/shard_map/ppermute | solution.py:505
  69.6 1.6 %shard_map.151 = (f32[1024,1024]{1,0:T(8,128)}, f32[1024,128]{1,0:T(8,128)}, f32[128,1024]{1,0:T(8,128)}) custom-call(bf16[512,1280]{1,0:T(8,128)(2,1)S(1)} %collective-permute-done.21.mid_half.small_half, bf16[512,1280]{1,0:T(8,128)(2,1)S(1)} %collective-permute-done.21.mid_half.small_half, ...), custom_call_target="tpu_custom_call", output_to_operand_aliasing={{0}: (2, {}), {1}: (3, {}), {2}: (4, {})} | custom-call | tf_op jit(solution)/shard_map/pallas_call | solution.py:477
  (44 shorter events, 5.0 us)
Async XLA Ops:
  1.7 7.2 %copy-start.4 = (s32[1,1,3,128]{3,1,2,0:T(1,128)S(1)}, s32[1,1,3,128]{3,1,2,0:T(1,128)}, u32[]{:S(2)}) copy-start(s32[1,1,3,128]{3,1,2,0:T(1,128)} %param.15) | copy-start | bytes 4612
  1.7 7.2 %copy-start.5 = (s32[1,1,3,128]{3,1,2,0:T(1,128)S(1)}, s32[1,1,3,128]{3,1,2,0:T(1,128)}, u32[]{:S(2)}) copy-start(s32[1,1,3,128]{3,1,2,0:T(1,128)} %param.14) | copy-start | bytes 4612
  1.7 7.2 %copy-start.1 = (f32[1,128,4,128]{3,2,1,0:T(4,128)S(1)}, f32[1,128,4,128]{3,2,1,0:T(4,128)}, u32[]{:S(2)}) copy-start(f32[1,128,4,128]{3,2,1,0:T(4,128)} %param.13) | copy-start | bytes 786436
  1.7 7.2 %copy-start.3 = (f32[1,32,4,128]{3,2,1,0:T(4,128)S(1)}, f32[1,32,4,128]{3,2,1,0:T(4,128)}, u32[]{:S(2)}) copy-start(f32[1,32,4,128]{3,2,1,0:T(4,128)} %param.11) | copy-start | bytes 196612
  1.7 8.1 %collective-permute-start = (bf16[272,128]{1,0:T(8,128)(2,1)S(1)}, bf16[272,128]{1,0:T(8,128)(2,1)S(1)}, u32[]{:S(2)}, u32[]{:S(2)}) collective-permute-start(bf16[272,128]{1,0:T(8,128)(2,1)S(1)} %get-tuple-element.52), channel_id=1, source_target_pairs={{0,1},{1,2},{2,3},{3,4},{4,5},{5,6},{6,7},{7,0},{8,9},{9,10},{10,1... | collective-permute-start | bytes 208904 | tf_op jit(solution)/shard_map/ppermute | solution.py:583
  2.2 7.6 %collective-permute-start.1 = (bf16[272,128]{1,0:T(8,128)(2,1)S(1)}, bf16[272,128]{1,0:T(8,128)(2,1)S(1)}, u32[]{:S(2)}, u32[]{:S(2)}) collective-permute-start(bf16[272,128]{1,0:T(8,128)(2,1)S(1)} %get-tuple-element.53), channel_id=1, source_target_pairs={{1,0},{2,1},{3,2},{4,3},{5,4},{6,5},{7,6},{0,7},{9,8},{10,9},{11,1... | collective-permute-start | bytes 208904 | tf_op jit(solution)/shard_map/ppermute | solution.py:583
  7.0 2.7 %copy-start.2 = (bf16[1024,128]{1,0:T(8,128)(2,1)S(1)}, bf16[1024,128]{1,0:T(8,128)(2,1)}, u32[]{:S(2)}) copy-start(bf16[1024,128]{1,0:T(8,128)(2,1)} %param.17) | copy-start | bytes 786436
  7.0 2.8 %copy-start = (bf16[128,1024]{1,0:T(8,128)(2,1)S(1)}, bf16[128,1024]{1,0:T(8,128)(2,1)}, u32[]{:S(2)}) copy-start(bf16[128,1024]{1,0:T(8,128)(2,1)} %w_out_ref.3) | copy-start | bytes 786436
  13.5 3.8 %collective-permute-start.2 = (bf16[512,1024]{1,0:T(8,128)(2,1)S(1)}, bf16[512,1024]{1,0:T(8,128)(2,1)S(1)}, u32[]{:S(2)}, u32[]{:S(2)}) collective-permute-start(bf16[512,1024]{1,0:T(8,128)(2,1)S(1)} %get-tuple-element.56), channel_id=1, source_target_pairs={{0,1},{1,0},{2,3},{3,2},{4,5},{5,4},{6,7},{7,6},{8,9},{9,8},{10,11... | collective-permute-start | bytes 3145736 | tf_op jit(solution)/shard_map/ppermute | solution.py:505
  15.6 1.7 %collective-permute-start.3 = (bf16[512,256]{1,0:T(8,128)(2,1)S(1)}, bf16[512,256]{1,0:T(8,128)(2,1)S(1)}, u32[]{:S(2)}, u32[]{:S(2)}) collective-permute-start(bf16[512,256]{1,0:T(8,128)(2,1)S(1)} %get-tuple-element.61), channel_id=1, source_target_pairs={{0,1},{1,0},{2,3},{3,2},{4,5},{5,4},{6,7},{7,6},{8,9},{9,8},{10,11... | collective-permute-start | bytes 786440 | tf_op jit(solution)/shard_map/ppermute | solution.py:505
  17.6 7.5 %collective-permute-start.4 = (bf16[128,1280]{1,0:T(8,128)(2,1)S(1)}, bf16[128,1280]{1,0:T(8,128)(2,1)S(1)}, u32[]{:S(2)}, u32[]{:S(2)}) collective-permute-start(bf16[128,1280]{1,0:T(8,128)(2,1)S(1)} %get-tuple-element.65), channel_id=1, source_target_pairs={{0,8},{1,17},{2,10},{3,19},{4,12},{5,21},{6,14},{7,23},{8,0},{9,25... | collective-permute-start | bytes 983048 | tf_op jit(solution)/shard_map/ppermute | solution.py:516
  19.6 5.5 %collective-permute-start.5 = (bf16[256,128]{1,0:T(8,128)(2,1)S(1)}, bf16[256,128]{1,0:T(8,128)(2,1)S(1)}, u32[]{:S(2)}, u32[]{:S(2)}) collective-permute-start(bf16[256,128]{1,0:T(8,128)(2,1)S(1)} %get-tuple-element.76), channel_id=1, source_target_pairs={{0,1},{1,2},{2,3},{3,4},{4,5},{5,6},{6,7},{7,0},{8,9},{9,10},{10,1... | collective-permute-start | bytes 196616 | tf_op jit(solution)/shard_map/ppermute | solution.py:583
  19.7 5.4 %collective-permute-start.6 = (bf16[256,128]{1,0:T(8,128)(2,1)S(1)}, bf16[256,128]{1,0:T(8,128)(2,1)S(1)}, u32[]{:S(2)}, u32[]{:S(2)}) collective-permute-start(bf16[256,128]{1,0:T(8,128)(2,1)S(1)} %get-tuple-element.77), channel_id=1, source_target_pairs={{1,0},{2,1},{3,2},{4,3},{5,4},{6,5},{7,6},{0,7},{9,8},{10,9},{11,1... | collective-permute-start | bytes 196616 | tf_op jit(solution)/shard_map/ppermute | solution.py:583
  23.1 10.1 %collective-permute-start.7 = (bf16[128,1280]{1,0:T(8,128)(2,1)S(1)}, bf16[128,1280]{1,0:T(8,128)(2,1)S(1)}, u32[]{:S(2)}, u32[]{:S(2)}) collective-permute-start(bf16[128,1280]{1,0:T(8,128)(2,1)S(1)} %get-tuple-element.70), channel_id=1, source_target_pairs={{0,8},{1,17},{2,10},{3,19},{4,12},{5,21},{6,14},{7,23},{8,0},{9,25... | collective-permute-start | bytes 983048 | tf_op jit(solution)/shard_map/ppermute | solution.py:516
  25.2 8.1 %collective-permute-start.8 = (bf16[128,1280]{1,0:T(8,128)(2,1)S(1)}, bf16[128,1280]{1,0:T(8,128)(2,1)S(1)}, u32[]{:S(2)}, u32[]{:S(2)}) collective-permute-start(bf16[128,1280]{1,0:T(8,128)(2,1)S(1)} %shard_map.144), channel_id=1, source_target_pairs={{0,16},{1,9},{2,18},{3,11},{4,20},{5,13},{6,22},{7,15},{8,24},{9,1... | collective-permute-start | bytes 983048 | tf_op jit(solution)/shard_map/ppermute | solution.py:516
  33.4 7.3 %collective-permute-start.9 = (bf16[32,1280]{1,0:T(8,128)(2,1)S(1)}, bf16[32,1280]{1,0:T(8,128)(2,1)S(1)}, u32[]{:S(2)}, u32[]{:S(2)}) collective-permute-start(bf16[32,1280]{1,0:T(8,128)(2,1)S(1)} %get-tuple-element.88), channel_id=1, source_target_pairs={{0,6},{1,3},{2,4},{3,1},{4,2},{5,7},{6,0},{7,5},{8,14},{9,11},{10,... | collective-permute-start | bytes 245768 | tf_op jit(solution)/shard_map/ppermute | solution.py:556
  34.4 9.0 %collective-permute-start.10 = (bf16[32,1280]{1,0:T(8,128)(2,1)S(1)}, bf16[32,1280]{1,0:T(8,128)(2,1)S(1)}, u32[]{:S(2)}, u32[]{:S(2)}) collective-permute-start(bf16[32,1280]{1,0:T(8,128)(2,1)S(1)} %get-tuple-element.89), channel_id=1, source_target_pairs={{0,4},{1,5},{2,6},{3,7},{4,0},{5,1},{6,2},{7,3},{8,12},{9,13},{10,... | collective-permute-start | bytes 245768 | tf_op jit(solution)/shard_map/ppermute | solution.py:556
  34.4 9.0 %collective-permute-start.11 = (bf16[32,1280]{1,0:T(8,128)(2,1)S(1)}, bf16[32,1280]{1,0:T(8,128)(2,1)S(1)}, u32[]{:S(2)}, u32[]{:S(2)}) collective-permute-start(bf16[32,1280]{1,0:T(8,128)(2,1)S(1)} %get-tuple-element.90), channel_id=1, source_target_pairs={{0,2},{1,7},{2,0},{3,5},{4,6},{5,3},{6,4},{7,1},{8,10},{9,15},{10,... | collective-permute-start | bytes 245768 | tf_op jit(solution)/shard_map/ppermute | solution.py:556
  43.5 6.7 %collective-permute-start.14 = (bf16[32,1280]{1,0:T(8,128)(2,1)S(1)}, bf16[32,1280]{1,0:T(8,128)(2,1)S(1)}, u32[]{:S(2)}, u32[]{:S(2)}) collective-permute-start(bf16[32,1280]{1,0:T(8,128)(2,1)S(1)} %shard_map.147.refs_0_), channel_id=1, source_target_pairs={{0,2},{1,7},{2,0},{3,5},{4,6},{5,3},{6,4},{7,1},{8,10},{9,15},{10,... | collective-permute-start | bytes 245768 | tf_op jit(solution)/shard_map/ppermute | solution.py:556
  43.6 7.3 %collective-permute-start.13 = (bf16[32,1280]{1,0:T(8,128)(2,1)S(1)}, bf16[32,1280]{1,0:T(8,128)(2,1)S(1)}, u32[]{:S(2)}, u32[]{:S(2)}) collective-permute-start(bf16[32,1280]{1,0:T(8,128)(2,1)S(1)} %shard_map.147.refs_0_), channel_id=1, source_target_pairs={{0,4},{1,5},{2,6},{3,7},{4,0},{5,1},{6,2},{7,3},{8,12},{9,13},{10,... | collective-permute-start | bytes 245768 | tf_op jit(solution)/shard_map/ppermute | solution.py:556
  45.8 6.3 %collective-permute-start.12 = (bf16[32,1280]{1,0:T(8,128)(2,1)S(1)}, bf16[32,1280]{1,0:T(8,128)(2,1)S(1)}, u32[]{:S(2)}, u32[]{:S(2)}) collective-permute-start(bf16[32,1280]{1,0:T(8,128)(2,1)S(1)} %shard_map.147.refs_0_), channel_id=1, source_target_pairs={{0,6},{1,3},{2,4},{3,1},{4,2},{5,7},{6,0},{7,5},{8,14},{9,11},{10,... | collective-permute-start | bytes 245768 | tf_op jit(solution)/shard_map/ppermute | solution.py:556
  52.2 7.2 %collective-permute-start.15 = (bf16[128,640]{1,0:T(8,128)(2,1)S(1)}, bf16[128,640]{1,0:T(8,128)(2,1)S(1)}, u32[]{:S(2)}, u32[]{:S(2)}) collective-permute-start(bf16[128,640]{1,0:T(8,128)(2,1)S(1)} %get-tuple-element.91.refs_0_), channel_id=1, source_target_pairs={{0,8},{1,17},{2,10},{3,19},{4,12},{5,21},{6,14},{7,23},{8,0},{9,25... | collective-permute-start | bytes 491528 | tf_op jit(solution)/shard_map/ppermute | solution.py:516
  53.4 7.6 %collective-permute-start.19 = (bf16[128,640]{1,0:T(8,128)(2,1)S(1)}, bf16[128,640]{1,0:T(8,128)(2,1)S(1)}, u32[]{:S(2)}, u32[]{:S(2)}) collective-permute-start(bf16[128,640]{1,0:T(8,128)(2,1)S(1)} %get-tuple-element.92.refs_4_), channel_id=1, source_target_pairs={{0,16},{1,9},{2,18},{3,11},{4,20},{5,13},{6,22},{7,15},{8,24},{9,1... | collective-permute-start | bytes 491528 | tf_op jit(solution)/shard_map/ppermute | solution.py:516
  55.0 8.0 %collective-permute-start.16 = (bf16[128,640]{1,0:T(8,128)(2,1)S(1)}, bf16[128,640]{1,0:T(8,128)(2,1)S(1)}, u32[]{:S(2)}, u32[]{:S(2)}) collective-permute-start(bf16[128,640]{1,0:T(8,128)(2,1)S(1)} %get-tuple-element.91.refs_0_), channel_id=1, source_target_pairs={{0,16},{1,9},{2,18},{3,11},{4,20},{5,13},{6,22},{7,15},{8,24},{9,1... | collective-permute-start | bytes 491528 | tf_op jit(solution)/shard_map/ppermute | solution.py:516
  55.5 7.5 %collective-permute-start.18 = (bf16[128,640]{1,0:T(8,128)(2,1)S(1)}, bf16[128,640]{1,0:T(8,128)(2,1)S(1)}, u32[]{:S(2)}, u32[]{:S(2)}) collective-permute-start(bf16[128,640]{1,0:T(8,128)(2,1)S(1)} %get-tuple-element.92.refs_4_), channel_id=1, source_target_pairs={{0,8},{1,17},{2,10},{3,19},{4,12},{5,21},{6,14},{7,23},{8,0},{9,25... | collective-permute-start | bytes 491528 | tf_op jit(solution)/shard_map/ppermute | solution.py:516
  59.3 5.4 %collective-permute-start.17 = (bf16[128,640]{1,0:T(8,128)(2,1)S(1)}, bf16[128,640]{1,0:T(8,128)(2,1)S(1)}, u32[]{:S(2)}, u32[]{:S(2)}) collective-permute-start(bf16[128,640]{1,0:T(8,128)(2,1)S(1)} %collective-permute-done.15.refs_1_), channel_id=1, source_target_pairs={{0,16},{1,9},{2,18},{3,11},{4,20},{5,13},{6,22},{7,15},{8,24},{9,1... | collective-permute-start | bytes 491528 | tf_op jit(solution)/shard_map/ppermute | solution.py:516
  61.0 5.3 %collective-permute-start.20 = (bf16[128,640]{1,0:T(8,128)(2,1)S(1)}, bf16[128,640]{1,0:T(8,128)(2,1)S(1)}, u32[]{:S(2)}, u32[]{:S(2)}) collective-permute-start(bf16[128,640]{1,0:T(8,128)(2,1)S(1)} %collective-permute-done.19.refs_6_), channel_id=1, source_target_pairs={{0,8},{1,17},{2,10},{3,19},{4,12},{5,21},{6,14},{7,23},{8,0},{9,25... | collective-permute-start | bytes 491528 | tf_op jit(solution)/shard_map/ppermute | solution.py:516
  66.5 3.1 %collective-permute-start.21 = (bf16[512,1280]{1,0:T(8,128)(2,1)S(1)}, bf16[512,1280]{1,0:T(8,128)(2,1)S(1)}, u32[]{:S(2)}, u32[]{:S(2)}) collective-permute-start(bf16[512,1280]{1,0:T(8,128)(2,1)S(1)} %shard_map.149.mid_half.small_half), channel_id=1, source_target_pairs={{0,1},{1,0},{2,3},{3,2},{4,5},{5,4},{6,7},{7,6},{8,9},{9,8},{10,11... | collective-permute-start | bytes 3932168 | tf_op jit(solution)/shard_map/ppermute | solution.py:505
